TPU v7x, 256 devices: a whole 4x4x8 slice. The times are simulated.
256 devices in a mesh: grp: 16 (over z, core), dev: 16 (over y, x).
Axes of the slice: x: 4, y: 4, z: 8, core: 2. Of those that a mesh axis runs over, the one named last changes fastest.
Arguments:
- orbitals: bfloat16 [512, 256, 1024], P(('grp', 'dev')), may hold values from -6 to 6
- dens_tiles: bfloat16 [8192, 128, 128], P(('grp', 'dev')), may hold values from -0.005859375 to 0.005859375
- point_coords: float32 [3, 131072], P(None, ('grp', 'dev')), may hold values from 0 to 64
- point_weights: float32 [131072], P(('grp', 'dev')), may hold values from 0.005 to 0.05
- batch_blocks: int32 [512, 8], P(('grp', 'dev')), may hold values from 0 to 8, all different within a row
- tile_owner: int32 [20736, 1], P(('grp', 'dev')), may hold values from 0 to 15; in each aligned block of 81 rows (0 to 80, 81 to 161, ...) at most 9 rows name the same one
- tile_slot: int32 [20736], P(('grp', 'dev')), may hold values from 0 to 31
- batch_atoms: int32 [512, 4], P(('grp', 'dev')), may hold values from 0 to 15, all different within a row
- batch_weights: int32 [512, 4], P(('grp', 'dev')), may hold values from 1 to 8
- atom_grid_index: int32 [3, 256], P(None, 'grp'), may hold values from 0 to 63
Outputs:
- density: float32 [131072], P(('grp', 'dev'))
- potential: float32 [131072], P(('grp', 'dev'))
- ham_tiles: bfloat16 [8192, 128, 128], P(('grp', 'dev'))
Inputs may be any that keep to these rules, and one draw needn't show every extreme that they name: `tile_owner`: in each aligned block of 81 rows (the listed tiles of one device) no owner is named by more than 9 rows, a bound that some block reaches. `batch_blocks`: the 8 blocks of a batch are distinct. `batch_atoms`: the 4 atoms of a batch are distinct.
All inputs are finite; a program needn't handle non-finite values.
Results may differ from a plain program's by a relative error of at most 0.0056.
Values may be sent and summed in bfloat16 or wider, within the bound.
No kernel may reach another device: no remote copies, remote signals or barrier semaphores. Data moves between devices by JAX's collectives and lax.ppermute only.
A program may use at most 64 MiB of HBM per device.

v0:
```python
import math

import jax
import jax.numpy as jnp
from jax import lax
from jax.sharding import PartitionSpec as P

TB = 128
BB = 8
UB = 9
PTS = 256
BAT_DEV = 2
KM = 512
TILE_DEV = 32
GRIDN = 64


TOP_PRECISION = lax.Precision.HIGHEST


def wave_table(count):
    mode_ids = jnp.arange(count // 2, dtype=jnp.int32)
    return jnp.stack([mode_ids % 8, mode_ids // 8 % 8, mode_ids // 64]).astype(jnp.float32)


def kernel_gains(count):
    wave_vecs = wave_table(count)
    squared = jnp.sum(wave_vecs * wave_vecs, axis=0)
    near_gain = 0.1 / (1.0 + 0.1 * squared)
    far_gain = 0.03 / (1.0 + 0.1 * squared)
    return (jnp.concatenate([near_gain, near_gain]), jnp.concatenate([far_gain, far_gain]))


def local_basis(coords, centre_points, wave_vecs, grid_extent):
    displace = coords[:, :, None, :] - centre_points[:, :, :, None]
    phases = jnp.einsum("cbnp,cm->bnpm", displace, wave_vecs, precision=TOP_PRECISION) * (
        2.0 * math.pi / grid_extent
    )
    envelope = jnp.exp(-2.0 * jnp.sum(displace * displace, axis=0) / (grid_extent * grid_extent))
    return envelope[..., None] * jnp.concatenate([jnp.cos(phases), jnp.sin(phases)], axis=-1)


def wave_values(coords, wave_vecs, grid_extent):
    phases = jnp.einsum("cbp,cm->bpm", coords, wave_vecs, precision=TOP_PRECISION) * (
        2.0 * math.pi / grid_extent
    )
    return jnp.concatenate([jnp.cos(phases), jnp.sin(phases)], axis=-1)


def on_device(
    orbitals,
    dens_tiles,
    point_coords,
    point_weights,
    batch_blocks,
    tile_owner,
    tile_slot,
    batch_atoms,
    batch_weights,
    atom_grid_index,
):
    owner_count = lax.axis_size("dev")
    listed = tile_slot.shape[0]
    capacity = max(2, (listed + owner_count - 1) // owner_count * 3 // 2)
    owner_ids = tile_owner[:, 0]
    owner_hot = (owner_ids[:, None] == jnp.arange(owner_count, dtype=jnp.int32)[None, :]).astype(
        jnp.int32
    )
    bucket_rank = jnp.sum(jnp.cumsum(owner_hot, axis=0) * owner_hot, axis=1) - 1
    send_place = owner_ids * capacity + bucket_rank
    outgoing = jnp.full((owner_count * capacity,), -1, jnp.int32).at[send_place].set(tile_slot)
    requested_tiles = lax.all_to_all(outgoing, "dev", split_axis=0, concat_axis=0, tiled=True)
    served = jnp.where(
        (requested_tiles >= 0)[:, None, None],
        dens_tiles[jnp.maximum(requested_tiles, 0)],
        jnp.zeros((), jnp.bfloat16),
    )
    arrived = lax.all_to_all(served, "dev", split_axis=0, concat_axis=0, tiled=True)
    local_tiles = arrived[send_place]
    wave_vecs = wave_table(KM)
    near_gain, far_gain = kernel_gains(KM)
    coords = point_coords.reshape(3, BAT_DEV, PTS)
    weights = point_weights.reshape(BAT_DEV, PTS)
    atom_location = atom_grid_index.astype(jnp.float32)
    atom_onehot_rows = (
        batch_atoms[:, :, None]
        == jnp.arange(atom_grid_index.shape[1], dtype=jnp.int32)[None, None, :]
    ).astype(jnp.float32)
    centre_points = jnp.einsum(
        "dxp,qp->qdx", atom_onehot_rows, atom_location, precision=TOP_PRECISION
    )
    ebasis = local_basis(coords, centre_points, wave_vecs, GRIDN)
    raw_weight = batch_weights.astype(jnp.float32)
    partition = raw_weight / jnp.sum(raw_weight, axis=1, keepdims=True)

    def density_step(unused, inputs):
        orbital, chosen = inputs
        block_index = chosen[:, None] * UB + chosen[None, :]
        dens_block = local_tiles[block_index].transpose(0, 2, 1, 3).reshape(BB * TB, BB * TB)
        product = jnp.dot(orbital, dens_block, preferred_element_type=jnp.float32)
        return (unused, jnp.sum(product * orbital.astype(jnp.float32), axis=1))

    unused, density = lax.scan(density_step, jnp.zeros((), jnp.float32), (orbitals, batch_blocks))
    coeffs = partition[:, :, None] * jnp.einsum(
        "bp,bnpk->bnk", weights * density, ebasis, precision=TOP_PRECISION
    )
    moments_dev = jnp.einsum("bna,bnk->ak", atom_onehot_rows, coeffs, precision=TOP_PRECISION)
    atom_trig = wave_values(atom_location[:, None, :], wave_vecs, GRIDN)[0]
    moments_grp = lax.psum(moments_dev, "dev")
    structure = lax.psum(jnp.dot(moments_grp[:, 0], atom_trig, precision=TOP_PRECISION), "grp")
    coef_near = near_gain[None, :] * moments_grp
    chosen_coef = jnp.einsum("bna,ak->bnk", atom_onehot_rows, coef_near, precision=TOP_PRECISION)
    near_val = jnp.sum(
        partition[:, :, None]
        * jnp.einsum("bnpk,bnk->bnp", ebasis, chosen_coef, precision=TOP_PRECISION),
        axis=1,
    )
    far_val = jnp.einsum(
        "bpk,k->bp",
        wave_values(coords, wave_vecs, GRIDN),
        far_gain * structure,
        precision=TOP_PRECISION,
    )
    potential = near_val + far_val

    def hamilton_step(ham_local, inputs):
        orbital, chosen, scaled_pot = inputs
        scaled_orb = (scaled_pot[:, None] * orbital.astype(jnp.float32)).astype(jnp.bfloat16)
        ham_batch = lax.dot_general(
            orbital, scaled_orb, (((0,), (0,)), ((), ())), preferred_element_type=jnp.float32
        )
        pieces = ham_batch.reshape(BB, TB, BB, TB).transpose(0, 2, 1, 3).reshape(BB * BB, TB, TB)
        block_index = (chosen[:, None] * UB + chosen[None, :]).reshape(-1)
        return (ham_local.at[block_index].add(pieces), None)

    ham_local, unused_out = lax.scan(
        hamilton_step,
        jnp.zeros((listed, TB, TB), jnp.float32),
        (orbitals, batch_blocks, weights * potential),
    )
    ham_out = (
        jnp.zeros((owner_count * capacity, TB, TB), jnp.bfloat16)
        .at[send_place]
        .set(ham_local.astype(jnp.bfloat16))
    )
    returned = lax.all_to_all(ham_out, "dev", split_axis=0, concat_axis=0, tiled=True)
    slot_onehot_rows = (
        jnp.arange(TILE_DEV, dtype=jnp.int32)[:, None] == requested_tiles[None, :]
    ).astype(jnp.bfloat16)
    ham_tiles = jnp.dot(
        slot_onehot_rows,
        returned.reshape(owner_count * capacity, TB * TB),
        preferred_element_type=jnp.float32,
    )
    return (
        density.reshape(-1),
        potential.reshape(-1),
        ham_tiles.reshape(TILE_DEV, TB, TB).astype(jnp.bfloat16),
    )


def solution(mesh):
    in_specs = (
        P(("grp", "dev"), None, None),
        P(("grp", "dev"), None, None),
        P(None, ("grp", "dev")),
        P(("grp", "dev")),
        P(("grp", "dev"), None),
        P(("grp", "dev"), None),
        P(("grp", "dev")),
        P(("grp", "dev"), None),
        P(("grp", "dev"), None),
        P(None, "grp"),
    )
    out_specs = (P(("grp", "dev")), P(("grp", "dev")), P(("grp", "dev"), None, None))
    return jax.shard_map(
        on_device, mesh=mesh, in_specs=in_specs, out_specs=out_specs, check_vma=False
    )
```

profile of v0, /device:TPU:2, one launch (start us, length us, event | category | flops | bytes accessed | tf_op | source)
XLA Modules:
  0.0 367.5 jit_solution(4640356351945402682)
XLA Ops:
  0.6 0.8 fusion.30
  1.6 0.8 select_reduce_fusion
  2.4 0.7 fusion.59
  3.1 1.0 scatter_custom_fusion.1
  4.1 13.5 %all_to_all.22 = s32[16,9,1]{1,2,0:T(1,128)S(1)} all-to-all(s32[16,9,1]{1,2,0:T(1,128)S(1)} %bitcast.176), channel_id=1, replica_groups=mesh['grp'=16,'dev'=16] {'dev'}, dimensions={0} | all-to-all | bytes 1152 | tf_op jit(solution)/shard_map/all_to_all | solution.py:72
  17.6 0.5 broadcast.362
  18.1 0.7 fusion.69
  19.0 7.5 %gather_fusion.1 = bf16[144,128,128]{2,1,0:T(8,128)(2,1)} fusion(bf16[32,128,128]{2,1,0:T(8,128)(2,1)S(1)} %copy-done, s32[1024]{0:T(1024)S(1)} %pad_clamp_fusion.2), kind=kCustom, calls=%fused_computation.1 | custom fusion | bytes 9437760 | tf_op jit(solution)/shard_map/gather | solution.py:75
  26.6 4.9 %broadcast_select_fusion = bf16[144,128,128]{2,1,0:T(8,128)(2,1)} fusion(bf16[144,128,128]{2,1,0:T(8,128)(2,1)} %gather_fusion.1, pred[144]{0:T(512)(128)(4,1)S(1)} %broadcast_compare_fusion), kind=kLoop, calls=%fused_computation.31 | loop fusion | flops 2359296 | bytes 9437328 | tf_op jit(solution)/shard_map/jit(_where)/select_n | solution.py:73
  31.5 5.9 %all-to-all-start.1 = ((bf16[144,128,128]{2,1,0:T(8,128)(2,1)}), bf16[144,128,128]{2,1,0:T(8,128)(2,1)}, u32[]{:S(2)}, u32[]{:S(2)}) async-start(bf16[144,128,128]{2,1,0:T(8,128)(2,1)} %broadcast_select_fusion), calls=%async_computation.1 | async-start | bytes 9437184 | tf_op jit(solution)/shard_map/all_to_all | solution.py:78
  37.4 0.2 convolution_bitcast_fusion.2
  38.0 0.3 cosine_bitcast_fusion.1
  38.5 3.4 cosine_bitcast_fusion
  41.9 11.3 %multiply_cosine_fusion = (f32[2,4,256,256]{2,3,1,0:T(8,128)}, f32[2,4,256,256]{2,3,1,0:T(8,128)}) fusion(s32[1,256]{1,0:T(1,128)S(1)} %get-tuple-element.127, s32[1,256]{1,0:T(1,128)S(1)} %get-tuple-element.128, s32[1,256]{1,0:T(1,128)S(1)} %and_select_fusion.3, f32[3,2,4]{0,2,1:T(4,128)S(1)} %copy.36, f32[3,2,256]{2,0,1:T(4,128)S(1)} %bitcast.175), kind=kOutput, calls=%fused_computation.38 | convolution fusion | flops 19407104 | bytes 4203616 | tf_op jit(solution)/shard_map/cbnp,cm->bnpm/dot_general | solution.py:36
  53.3 47.8 %all-to-all-done.1 = bf16[144,128,128]{2,1,0:T(8,128)(2,1)} async-done(((bf16[144,128,128]{2,1,0:T(8,128)(2,1)}), bf16[144,128,128]{2,1,0:T(8,128)(2,1)}, u32[]{:S(2)}, u32[]{:S(2)}) %all-to-all-start.1) | async-done | bytes 4718624 | tf_op jit(solution)/shard_map/all_to_all | solution.py:78
  101.0 4.9 %gather_fusion.2 = bf16[81,128,128]{2,1,0:T(8,128)(2,1)} fusion(bf16[144,128,128]{2,1,0:T(8,128)(2,1)} %all-to-all-done.1, s32[1024]{0:T(1024)S(1)} %pad_clamp_fusion.1), kind=kCustom, calls=%fused_computation.2 | custom fusion | bytes 5308740 | tf_op jit(solution)/shard_map/gather | solution.py:79
  105.9 10.3 %while.20 = (s32[]{:T(128)}, f32[2,256]{1,0:T(2,128)S(1)}, bf16[2,256,1024]{2,1,0:T(8,128)(2,1)}, s32[2,8]{1,0:T(2,128)S(1)}, bf16[81,128,128]{2,1,0:T(8,128)(2,1)}, /*index=5*/s32[]{:T(128)}, s32[]{:T(128)}) while((s32[]{:T(128)}, f32[2,256]{1,0:T(2,128)S(1)}, bf16[2,256,1024]{2,1,0:T(8,128)(2,1)}, s32[2,8]{1,0:T(2,128)S(1)}, ...), condition=%wide.region_5.6_spmd, body=%wide.region_3.5_spmd.sunk | while | flops 537658368 | bytes 15738385 | solution.py:103
  106.1 2.7 gather_fusion
  108.8 1.4 copy.89
  110.2 0.8 fusion.89
  111.2 2.7 gather_fusion
  114.0 1.4 copy.89
  115.3 0.8 fusion.89
  116.2 5.9 %fusion.18 = f32[2,1,4,512]{3,1,2,0:T(1,128)S(1)} fusion(f32[2,4,256,256]{2,3,1,0:T(8,128)} %get-tuple-element.118, f32[2,4,256,256]{2,3,1,0:T(8,128)} %get-tuple-element.117, f32[2,4,256]{2,1,0:T(4,128)S(1)} %multiply_exponential_fusion, f32[2,256,1,1]{1,0,2,3:T(2,128)S(1)} %multiply_bitcast_fusion), kind=kOutput, calls=%fused_computation.34 | convolution fusion | flops 14680064 | bytes 4220928 | tf_op jit(solution)/shard_map/bp,bnpk->bnk/dot_general | solution.py:104
  122.1 0.3 convolution_bitcast_fusion
  122.4 70.5 %psum.14 = f32[16,512]{1,0:T(8,128)S(1)} all-reduce(f32[16,512]{1,0:T(8,128)S(1)} %convolution_bitcast_fusion), channel_id=1, replica_groups=mesh['grp'=16,'dev'=16] {'dev'}, use_global_device_ids=true, to_apply=%region_9.10 | all-reduce | flops 8192 | bytes 65536 | tf_op jit(solution)/shard_map/psum | solution.py:109
  193.0 0.1 fusion.32
  193.1 26.3 %psum.15 = f32[512]{0:T(512)S(1)} all-reduce(f32[512]{0:T(512)S(1)} %bitcast.180), channel_id=1, replica_groups=mesh['grp'=16,'dev'=16] {'grp'}, use_global_device_ids=true, to_apply=%region_11.12 | all-reduce | flops 512 | bytes 4096 | tf_op jit(solution)/shard_map/psum | solution.py:110
  219.5 0.2 convolution_bitcast_fusion.1
  219.7 4.1 %fusion.17 = f32[2,4,1,256]{3,2,1,0:T(1,128)S(1)} fusion(f32[2,4,256,256]{2,3,1,0:T(8,128)} %get-tuple-element.118, f32[2,4,256,256]{2,3,1,0:T(8,128)S(1)} %copy-done.1, f32[2,4,256]{2,1,0:T(4,128)S(1)} %multiply_exponential_fusion, f32[2,4,512,1]{2,1,0,3:T(4,128)S(1)} %convolution_bitcast_fusion.1), kind=kOutput, calls=%fused_computation.33 | convolution fusion | flops 14680064 | bytes 4227072 | tf_op jit(solution)/shard_map/bnpk,bnk->bnp/dot_general | solution.py:115
  223.8 0.6 fusion.24
  224.5 3.0 broadcast_in_dim.33
  227.5 33.9 %while.21 = (s32[]{:T(128)}, f32[81,128,128]{2,1,0:T(8,128)}, s32[2,8]{1,0:T(2,128)S(1)}, bf16[2,256,1024]{2,1,0:T(8,128)(2,1)S(1)}, f32[2,256]{1,0:T(2,128)S(1)}, /*index=5*/s32[]{:T(128)}) while((s32[]{:T(128)}, f32[81,128,128]{2,1,0:T(8,128)}, s32[2,8]{1,0:T(2,128)S(1)}, bf16[2,256,1024]{2,1,0:T(8,128)(2,1)S(1)}, ...), condition=%wide.region_14.15_spmd, body=%wide.region_12.14_spmd.sunk | while | flops 538706176 | bytes 20976368 | solution.py:136
  227.5 0.2 copy.90
  227.9 2.8 fusion.93
  230.8 13.7 %scatter_fusion = f32[81,128,128]{2,1,0:T(8,128)} fusion(f32[81,128,128]{2,1,0:T(8,128)} %get-tuple-element.227, s32[64]{0:T(128)S(1)} %fusion.92, f32[64,128,128]{2,1,0:T(8,128)} %bitcast.167), kind=kCustom, calls=%fused_computation.3.clone.1 | custom fusion | flops 1048576 | bytes 12583168 | tf_op jit(solution)/shard_map/while/body/eval_jaxpr/scatter-add | solution.py:134
  244.5 0.2 copy.90
  244.8 2.8 fusion.93
  247.7 13.7 %scatter_fusion = f32[81,128,128]{2,1,0:T(8,128)} fusion(f32[81,128,128]{2,1,0:T(8,128)} %get-tuple-element.227, s32[64]{0:T(128)S(1)} %fusion.92, f32[64,128,128]{2,1,0:T(8,128)} %bitcast.167), kind=kCustom, calls=%fused_computation.3.clone.1 | custom fusion | flops 1048576 | bytes 12583168 | tf_op jit(solution)/shard_map/while/body/eval_jaxpr/scatter-add | solution.py:134
  261.4 4.6 %convert_element_type.34 = bf16[81,128,128]{2,1,0:T(8,128)(2,1)} convert(f32[81,128,128]{2,1,0:T(8,128)} %get-tuple-element.58) | non-fusion elementwise | flops 1327104 | bytes 7962624 | tf_op jit(solution)/shard_map/convert_element_type | solution.py:144
  266.0 3.3 broadcast_in_dim.32
  269.3 14.4 %scatter_fusion.1 = bf16[144,128,128]{2,1,0:T(8,128)(2,1)} fusion(bf16[144,128,128]{2,1,0:T(8,128)(2,1)} %broadcast_in_dim.32, s32[81]{0:T(128)S(1)} %fusion.59, bf16[81,128,128]{2,1,0:T(8,128)(2,1)} %convert_element_type.34), kind=kCustom, calls=%fused_computation.5 | custom fusion | bytes 7962948 | tf_op jit(solution)/shard_map/scatter | solution.py:144
  283.7 8.8 %all-to-all-start.2 = ((bf16[144,128,128]{2,1,0:T(8,128)(2,1)}), bf16[144,128,128]{2,1,0:T(8,128)(2,1)}, u32[]{:S(2)}, u32[]{:S(2)}) async-start(bf16[144,128,128]{2,1,0:T(8,128)(2,1)} %scatter_fusion.1), calls=%async_computation.2 | async-start | bytes 9437184 | tf_op jit(solution)/shard_map/all_to_all | solution.py:146
  292.6 0.6 copy.52
  293.1 0.6 copy.51
  293.7 67.1 %all-to-all-done.2 = bf16[144,128,128]{2,1,0:T(8,128)(2,1)} async-done(((bf16[144,128,128]{2,1,0:T(8,128)(2,1)}), bf16[144,128,128]{2,1,0:T(8,128)(2,1)}, u32[]{:S(2)}, u32[]{:S(2)}) %all-to-all-start.2) | async-done | bytes 4718624 | tf_op jit(solution)/shard_map/all_to_all | solution.py:146
  360.9 5.3 %fusion.21 = bf16[32,128,128]{2,0,1:T(8,128)(2,1)S(1)} fusion(s32[144]{0:T(256)S(1)} %all_to_all.16, bf16[18,8,128,128]{3,2,1,0:T(8,128)(2,1)} %bitcast.68), kind=kOutput, calls=%fused_computation.39 | convolution fusion | flops 151523840 | bytes 5767744 | tf_op jit(solution)/shard_map/dot_general | solution.py:150
  366.1 1.4 copy.40
  (74 shorter events, 2.2 us)
Async XLA Ops:
  0.6 18.4 %copy-start = (bf16[32,128,128]{2,1,0:T(8,128)(2,1)S(1)}, bf16[32,128,128]{2,1,0:T(8,128)(2,1)}, u32[]{:S(2)}) copy-start(bf16[32,128,128]{2,1,0:T(8,128)(2,1)} %param.15) | copy-start | bytes 3145732
  31.5 5.9 %copy-start.8 = (f32[512]{0:T(512)S(1)}, f32[512]{0:T(512)}, u32[]{:S(2)}) copy-start(f32[512]{0:T(512)} %param.17) | copy-start | bytes 6148
  31.5 6.0 %copy-start.10 = (s32[3,16]{1,0:T(4,128)S(1)}, s32[3,16]{1,0:T(4,128)}, u32[]{:S(2)}) copy-start(s32[3,16]{1,0:T(4,128)} %param.23) | copy-start | bytes 580
  31.5 6.0 %copy-start.11 = (s32[2,4]{1,0:T(2,128)S(1)}, s32[2,4]{1,0:T(2,128)}, u32[]{:S(2)}) copy-start(s32[2,4]{1,0:T(2,128)} %param.21) | copy-start | bytes 100
  31.5 6.4 %copy-start.9 = (s32[2,4]{1,0:T(2,128)S(1)}, s32[2,4]{1,0:T(2,128)}, u32[]{:S(2)}) copy-start(s32[2,4]{1,0:T(2,128)} %param.22) | copy-start | bytes 100
  31.5 6.8 %copy-start.6 = (f32[3,512]{1,0:T(4,128)S(1)}, f32[3,512]{1,0:T(4,128)}, u32[]{:S(2)}) copy-start(f32[3,512]{1,0:T(4,128)} %param.16) | copy-start | bytes 18436
  31.5 69.5 %all-to-all-start.1 = ((bf16[144,128,128]{2,1,0:T(8,128)(2,1)}), bf16[144,128,128]{2,1,0:T(8,128)(2,1)}, u32[]{:S(2)}, u32[]{:S(2)}) async-start(bf16[144,128,128]{2,1,0:T(8,128)(2,1)} %broadcast_select_fusion), calls=%async_computation.1 | async-start | bytes 9437184 | tf_op jit(solution)/shard_map/all_to_all | solution.py:78
  41.9 64.0 %copy-start.7 = (s32[2,8]{1,0:T(2,128)S(1)}, s32[2,8]{1,0:T(2,128)}, u32[]{:S(2)}) copy-start(s32[2,8]{1,0:T(2,128)} %param.18) | copy-start | bytes 196
  108.8 1.4 copy-start.2
  113.9 1.4 copy-start.2
  116.2 103.5 %copy-start.1 = (f32[2,4,256,256]{2,3,1,0:T(8,128)S(1)}, f32[2,4,256,256]{2,3,1,0:T(8,128)}, u32[]{:S(2)}) copy-start(f32[2,4,256,256]{2,3,1,0:T(8,128)} %get-tuple-element.117) | copy-start | bytes 6291460
  219.4 4.4 %copy-start.4 = (f32[2,256,256]{1,2,0:T(8,128)S(1)}, f32[2,256,256]{1,2,0:T(8,128)}, u32[]{:S(2)}) copy-start(f32[2,256,256]{1,2,0:T(8,128)} %get-tuple-element.119) | copy-start | bytes 1572868
  219.4 4.4 %copy-start.5 = (f32[2,256,256]{1,2,0:T(8,128)S(1)}, f32[2,256,256]{1,2,0:T(8,128)}, u32[]{:S(2)}) copy-start(f32[2,256,256]{1,2,0:T(8,128)} %get-tuple-element.120) | copy-start | bytes 1572868
  223.7 3.7 %copy-start.3 = (bf16[2,256,1024]{2,1,0:T(8,128)(2,1)S(1)}, bf16[2,256,1024]{2,1,0:T(8,128)(2,1)}, u32[]{:S(2)}) copy-start(bf16[2,256,1024]{2,1,0:T(8,128)(2,1)} %get-tuple-element.242) | copy-start | bytes 3145732
  283.7 77.1 %all-to-all-start.2 = ((bf16[144,128,128]{2,1,0:T(8,128)(2,1)}), bf16[144,128,128]{2,1,0:T(8,128)(2,1)}, u32[]{:S(2)}, u32[]{:S(2)}) async-start(bf16[144,128,128]{2,1,0:T(8,128)(2,1)} %scatter_fusion.1), calls=%async_computation.2 | async-start | bytes 9437184 | tf_op jit(solution)/shard_map/all_to_all | solution.py:146
where the time goes:
time: 373 us; the launch traced here: 367 us
  waiting for transfers between devices  115 us (31%)
  blocking collectives  110 us (29%)
  local copies, waits for them, and re-layouts  46.7 us (13%)
  other arithmetic  41 us (11%)
  matrix products  38.8 us (10%)
  starting transfers between devices  14.7 us (4%)
    psum x1, blocking collectives, on_device(): moments_grp = lax.psum(moments_dev, 'dev')  70.5 us
    all_to_all x1, waiting for transfers between devices, on_device(): lax.all_to_all(ham_out, 'dev', split_axis=0, concat_axis=0, tiled=True)  67.1 us
    all_to_all x1, waiting for transfers between devices, on_device(): lax.all_to_all(served, 'dev', split_axis=0, concat_axis=0, tiled=True)  47.8 us
    scatter-add x2, other arithmetic, hamilton_step(): return (ham_local.at[block_index].add(pieces), None)  27.3 us
    psum x1, blocking collectives, on_device(): lax.psum(jnp.dot(moments_grp[:, 0], atom_trig, precision=TOP_PRECISION),...  26.3 us
    scatter x1, local copies, waits for them, and re-layouts, on_device(): ham_out = jnp.zeros((owner_count * capacity, TB, TB), jnp.bfloat16).at[se...  14.4 us
    all_to_all x1, blocking collectives, on_device(): lax.all_to_all(outgoing, 'dev', split_axis=0, concat_axis=0, tiled=True)  13.5 us
    dot_general x1, matrix products, local_basis(): jnp.einsum('cbnp,cm->bnpm', displace, wave_vecs, precision=TOP_PRECISION)  11.3 us
  transfers between devices with their start and end apart: 2, of which 2 were waited for; matrix products, arithmetic and copies ran while one was open for 5% of the time, Pallas kernels for 0%

commit v1 on v0

v1 whole, which is shorter than its diff:
```python
import math

import jax
import jax.numpy as jnp
from jax import lax
from jax.experimental import pallas as pl
from jax.experimental.pallas import tpu as pltpu
from jax.sharding import PartitionSpec as P

TB = 128
BB = 8
UB = 9
R = 81
PTS = 256
BAT_DEV = 2
KM = 512
HALF = KM // 2
NEAR = 4
TILE_DEV = 32
GRIDN = 64
ATOM_GRP = 16
DEV_PTS = BAT_DEV * PTS
LISTERS = 4
LIST_PTS = LISTERS * DEV_PTS
NO_TILE = 4 * TILE_DEV
GROUP = 4
LIST_LEN = 96
VMEM_BYTES = 56 * 1024 * 1024

F32 = jnp.float32
BF16 = jnp.bfloat16
TOP_PRECISION = lax.Precision.HIGHEST
NT = (((1,), (1,)), ((), ()))


def swap(array, bits):
    return lax.ppermute(array, "dev", [(d, d ^ bits) for d in range(16)])


def swap_grp(array, bits):
    return lax.ppermute(array, "grp", [(g, g ^ bits) for g in range(16)])


X1, Y1 = 1, 4
X3, Y3 = 3, 12


def wave_table(count):
    mode_ids = jnp.arange(count // 2, dtype=jnp.int32)
    return jnp.stack([mode_ids % 8, mode_ids // 8 % 8, mode_ids // 64]).astype(F32)


def split_bf16(value):
    high = value.astype(BF16)
    return high, (value - high.astype(F32)).astype(BF16)


def wave_kernel(cs_ref, high_ref, low_ref):
    cos_x, sin_x = cs_ref[0:8], cs_ref[8:16]
    for fz in range(4):
        cos_z, sin_z = cs_ref[32 + fz : 33 + fz], cs_ref[40 + fz : 41 + fz]
        for fy in range(0, 8, 2):
            parts_cos, parts_sin = [], []
            for step in range(2):
                cos_y = cs_ref[16 + fy + step : 17 + fy + step]
                sin_y = cs_ref[24 + fy + step : 25 + fy + step]
                cos_yz = cos_y * cos_z - sin_y * sin_z
                sin_yz = sin_y * cos_z + cos_y * sin_z
                parts_cos.append(cos_x * cos_yz - sin_x * sin_yz)
                parts_sin.append(sin_x * cos_yz + cos_x * sin_yz)
            row = fz * 64 + fy * 8
            for base, parts in ((row, parts_cos), (HALF + row, parts_sin)):
                high, low = split_bf16(jnp.concatenate(parts, axis=0))
                high_ref[base : base + 16] = high
                low_ref[base : base + 16] = low


def wave_of_points(coords):
    points = coords.shape[1]
    chunk = 256
    angle = (jnp.arange(8, dtype=F32)[None, :, None] * coords[:, None, :]) * (2.0 * math.pi / GRIDN)
    cs = jnp.stack([jnp.cos(angle), jnp.sin(angle)], axis=1).reshape(48, points)
    out = jax.ShapeDtypeStruct((KM, points), BF16)
    return pl.pallas_call(
        wave_kernel,
        grid=(points // chunk,),
        in_specs=[pl.BlockSpec((48, chunk), lambda i: (0, i))],
        out_specs=[pl.BlockSpec((KM, chunk), lambda i: (0, i))] * 2,
        out_shape=[out, out],
        cost_estimate=pl.CostEstimate(flops=8 * KM * points, bytes_accessed=4 * KM * points, transcendentals=0),
    )(cs)


def list_kernel(tmap_ref, codes_ref, counts_ref):
    for e in range(LISTERS):

        def look(row, state):
            r, count = state

            def column(col, state):
                r, count = state
                tile = tmap_ref[e, r]
                codes_ref[e, count] = tile + row * 256 + col * 4096
                return r + 1, count + jnp.where(tile < NO_TILE, 1, 0)

            return lax.fori_loop(0, UB, column, (r, count))

        r, count = lax.fori_loop(0, UB, look, (0, 0))
        for step in range(GROUP):
            codes_ref[e, count + step] = NO_TILE
        counts_ref[e] = (count + GROUP - 1) // GROUP


def lists_of(tmap):
    smem = pl.BlockSpec(memory_space=pltpu.SMEM)
    return pl.pallas_call(
        list_kernel,
        in_specs=[smem],
        out_specs=[smem, smem],
        out_shape=[
            jax.ShapeDtypeStruct((LISTERS, LIST_LEN), jnp.int32),
            jax.ShapeDtypeStruct((LISTERS,), jnp.int32),
        ],
        cost_estimate=pl.CostEstimate(flops=4000, bytes_accessed=4000, transcendentals=0),
    )(tmap)


def density_kernel(
    tmap_ref,
    blocks_ref,
    own_tile,
    x_tile,
    y_tile,
    low_tile,
    high_tile,
    own_orb,
    x_orb,
    y_orb,
    first_orb,
    second_orb,
    spread_ref,
    weights_ref,
    high_ref,
    low_ref,
    trig_ref,
    out_ref,
    tiles,
    orbs,
    density,
    sems,
):
    copies = [
        pltpu.make_async_copy(own_tile, tiles.at[0:32], sems.at[0]),
        pltpu.make_async_copy(x_tile, tiles.at[32:64], sems.at[1]),
        pltpu.make_async_copy(y_tile, tiles.at[64:96], sems.at[2]),
        pltpu.make_async_copy(low_tile, tiles.at[96:112], sems.at[3]),
        pltpu.make_async_copy(high_tile, tiles.at[112:128], sems.at[4]),
        pltpu.make_async_copy(own_orb, orbs.at[0:2], sems.at[5]),
        pltpu.make_async_copy(x_orb, orbs.at[2:4], sems.at[6]),
        pltpu.make_async_copy(y_orb, orbs.at[4:6], sems.at[7]),
        pltpu.make_async_copy(first_orb, orbs.at[6], sems.at[8]),
        pltpu.make_async_copy(second_orb, orbs.at[7], sems.at[9]),
    ]
    for copy in copies:
        copy.start()
    tiles[NO_TILE] = jnp.zeros((TB, TB), BF16)
    for copy in copies:
        copy.wait()

    def one_batch(batch, unused):
        lister = batch // BAT_DEV
        chosen = [blocks_ref[batch, i] for i in range(BB)]
        total = jnp.zeros((PTS, TB), F32)
        for pair in range(BB // 2):
            columns = []
            for j in (2 * pair, 2 * pair + 1):
                columns.append(
                    jnp.concatenate([tiles[tmap_ref[lister, chosen[i] * UB + chosen[j]]] for i in range(BB)], axis=0)
                )
            product = jnp.dot(orbs[batch], jnp.concatenate(columns, axis=1), preferred_element_type=F32)
            for side in range(2):
                block = orbs[batch, :, (2 * pair + side) * TB : (2 * pair + side + 1) * TB]
                total = total + product[:, side * TB : (side + 1) * TB] * block.astype(F32)
        density[pl.ds(batch, 1), :] = jnp.sum(total.T, axis=0, keepdims=True)
        return unused

    lax.fori_loop(0, LISTERS * BAT_DEV, one_batch, 0)
    weighted = density[...] * weights_ref[...]
    charge = jnp.concatenate(
        [spread_ref[:, b * PTS : (b + 1) * PTS] * weighted[b : b + 1] for b in range(LISTERS * BAT_DEV)], axis=1
    )
    charge_high, charge_low = split_bf16(charge)
    both = lax.dot_general(
        jnp.concatenate([charge_high, charge_low], axis=0), high_ref[...], NT, preferred_element_type=F32
    )
    sums = both[:ATOM_GRP] + both[ATOM_GRP:]
    sums = sums + lax.dot_general(charge_high, low_ref[...], NT, preferred_element_type=F32)
    cos_sum, sin_sum = sums[:, :HALF], sums[:, HALF:]
    cos_atom, sin_atom = trig_ref[:, :HALF], trig_ref[:, HALF:]
    out_ref[0:ATOM_GRP, :HALF] = cos_sum * cos_atom + sin_sum * sin_atom
    out_ref[0:ATOM_GRP, HALF:] = sin_sum * cos_atom - cos_sum * sin_atom
    for e in range(LISTERS):
        for b in range(BAT_DEV):
            out_ref[ATOM_GRP + e : ATOM_GRP + e + 1, b * PTS : (b + 1) * PTS] = density[
                BAT_DEV * e + b : BAT_DEV * e + b + 1
            ]
    out_ref[ATOM_GRP + LISTERS :] = jnp.zeros((8 - LISTERS, KM), F32)


def density_and_moments(tmap, blocks, tiles, orbs, spread, weights, wave_high, wave_low, trig):
    smem = pl.BlockSpec(memory_space=pltpu.SMEM)
    vmem = pl.BlockSpec(memory_space=pltpu.VMEM)
    hbm = pl.BlockSpec(memory_space=pl.ANY)
    return pl.pallas_call(
        density_kernel,
        in_specs=[smem, smem] + [hbm] * 10 + [vmem] * 5,
        out_specs=vmem,
        out_shape=jax.ShapeDtypeStruct((ATOM_GRP + 8, KM), F32),
        scratch_shapes=[
            pltpu.VMEM((NO_TILE + 1, TB, TB), BF16),
            pltpu.VMEM((LISTERS * BAT_DEV, PTS, BB * TB), BF16),
            pltpu.VMEM((LISTERS * BAT_DEV, PTS), F32),
            pltpu.SemaphoreType.DMA((10,)),
        ],
        compiler_params=pltpu.CompilerParams(vmem_limit_bytes=VMEM_BYTES),
        cost_estimate=pl.CostEstimate(flops=5 * 10**9, bytes_accessed=12 * 2**20, transcendentals=0),
    )(tmap, blocks, *tiles, *orbs, spread, weights, wave_high, wave_low, trig)


def ham_kernel(
    codes_ref,
    counts_ref,
    blocks_ref,
    own_orb,
    x_orb,
    y_orb,
    first_orb,
    second_orb,
    moments_ref,
    far_ref,
    near_ref,
    trig_ref,
    spread_ref,
    weights_ref,
    high_ref,
    low_ref,
    pot_ref,
    own_ref,
    x_ref,
    y_ref,
    diag_ref,
    ham,
    orbs,
    turned,
    scaled,
    sems,
):
    copies = []
    for batch in range(LISTERS * BAT_DEV):
        e, b = batch // BAT_DEV, batch % BAT_DEV
        source = (own_orb.at[b], x_orb.at[b], y_orb.at[b], (first_orb, second_orb)[b])[e]
        some = []
        missing = UB * (UB - 1) // 2
        for i in range(BB):
            block = blocks_ref[batch, i]
            missing = missing - block
            some.append(
                pltpu.make_async_copy(
                    source.at[:, i * TB : (i + 1) * TB],
                    orbs.at[e, block, b * PTS : (b + 1) * PTS, :],
                    sems.at[batch, i],
                )
            )
        for copy in some:
            copy.start()
        orbs[e, missing, b * PTS : (b + 1) * PTS, :] = jnp.zeros((PTS, TB), BF16)
        copies.append(some)

    cos_atom, sin_atom = trig_ref[:, :HALF], trig_ref[:, HALF:]
    cos_near = moments_ref[:, :HALF] * near_ref[:, :HALF]
    sin_near = moments_ref[:, HALF:] * near_ref[:, HALF:]
    turned_cos = cos_near * cos_atom - sin_near * sin_atom
    turned_sin = cos_near * sin_atom + sin_near * cos_atom
    coef = jnp.concatenate(
        [
            jnp.concatenate([turned_cos, turned_sin], axis=1),
            jnp.concatenate([far_ref[...], jnp.zeros((ATOM_GRP - 1, KM), F32)], axis=0),
        ],
        axis=0,
    )
    coef_high, coef_low = split_bf16(coef)
    both = jnp.dot(jnp.concatenate([coef_high, coef_low], axis=0), high_ref[...], preferred_element_type=F32)
    values = both[: 2 * ATOM_GRP] + both[2 * ATOM_GRP :]
    values = values + jnp.dot(coef_high, low_ref[...], preferred_element_type=F32)
    pot = jnp.sum(values[:ATOM_GRP] * spread_ref[...], axis=0, keepdims=True) + values[ATOM_GRP : ATOM_GRP + 1]
    pot_ref[...] = pot[:, :DEV_PTS]
    scale = pot * weights_ref[...]

    def clear(t, unused):
        ham[t] = jnp.zeros((TB, TB), F32)
        return unused

    lax.fori_loop(0, NO_TILE, clear, 0)
    for e in range(LISTERS):
        for b in range(BAT_DEV):
            for copy in copies[BAT_DEV * e + b]:
                copy.wait()
        for part in range(DEV_PTS // TB):
            at = e * DEV_PTS + part * TB
            factor = jnp.broadcast_to(scale[:, at : at + TB], (TB, TB)).T
            for block in range(UB):
                piece = orbs[e, block, part * TB : (part + 1) * TB, :]
                scaled[block, part * TB : (part + 1) * TB, :] = (factor * piece.astype(F32)).astype(BF16)
                turned[block, :, part * TB : (part + 1) * TB] = piece.T

        def some_items(step, unused):
            for item in range(GROUP):
                code = codes_ref[e, step * GROUP + item]
                tile = code & 255
                i = (code >> 8) & 15
                j = code >> 12
                ham[tile] += jnp.dot(turned[i], scaled[j], preferred_element_type=F32)
            return unused

        lax.fori_loop(0, counts_ref[e], some_items, 0)
    own_ref[...] = ham[0:32]
    x_ref[...] = ham[32:64].astype(BF16)
    y_ref[...] = ham[64:96].astype(BF16)
    diag_ref[...] = ham[96:128].astype(BF16)


def potential_and_ham(codes, counts, blocks, orbs, moments, far, near, trig, spread, weights, wave_high, wave_low):
    smem = pl.BlockSpec(memory_space=pltpu.SMEM)
    vmem = pl.BlockSpec(memory_space=pltpu.VMEM)
    hbm = pl.BlockSpec(memory_space=pl.ANY)
    part = jax.ShapeDtypeStruct((TILE_DEV, TB, TB), BF16)
    return pl.pallas_call(
        ham_kernel,
        in_specs=[smem] * 3 + [hbm] * 5 + [vmem] * 8,
        out_specs=[vmem] * 5,
        out_shape=[
            jax.ShapeDtypeStruct((1, DEV_PTS), F32),
            jax.ShapeDtypeStruct((TILE_DEV, TB, TB), F32),
            part,
            part,
            part,
        ],
        scratch_shapes=[
            pltpu.VMEM((NO_TILE + 1, TB, TB), F32),
            pltpu.VMEM((LISTERS, UB, DEV_PTS, TB), BF16),
            pltpu.VMEM((UB, TB, DEV_PTS), BF16),
            pltpu.VMEM((UB, DEV_PTS, TB), BF16),
            pltpu.SemaphoreType.DMA((LISTERS * BAT_DEV, BB)),
        ],
        compiler_params=pltpu.CompilerParams(vmem_limit_bytes=VMEM_BYTES),
        cost_estimate=pl.CostEstimate(flops=4 * 10**9, bytes_accessed=16 * 2**20, transcendentals=0),
    )(codes, counts, blocks, *orbs, moments, far, near, trig, spread, weights, wave_high, wave_low)


def on_device(
    orbitals,
    dens_tiles,
    point_coords,
    point_weights,
    batch_blocks,
    tile_owner,
    tile_slot,
    batch_atoms,
    batch_weights,
    atom_grid_index,
):
    me = lax.axis_index("dev").astype(jnp.int32)
    ints = jnp.concatenate(
        [tile_owner[:, 0], tile_slot, batch_blocks.reshape(-1), batch_atoms.reshape(-1), batch_weights.reshape(-1)]
    )
    facts = jnp.concatenate(
        [point_coords, point_weights[None], jnp.pad(ints, (0, DEV_PTS - ints.shape[0])).astype(F32)[None]], axis=0
    )
    half = TILE_DEV // 2
    facts_x, facts_y, facts_diag = swap(facts, X3), swap(facts, Y3), swap(facts, X3 ^ Y3)
    tile_x, tile_y = swap(dens_tiles, X1), swap(dens_tiles, Y1)
    orb_x, orb_y = swap(orbitals, X3), swap(orbitals, Y3)
    tile_low, tile_high = swap(tile_y[:half], X1), swap(tile_x[half:], Y1)
    orb_first, orb_second = swap(orb_y[0], X3), swap(orb_x[1], Y3)

    facts = jnp.stack([facts, facts_x, facts_y, facts_diag], axis=1)
    coords = facts[:3].reshape(3, LIST_PTS)
    weights = facts[3].reshape(LISTERS * BAT_DEV, PTS)
    ints = facts[4].astype(jnp.int32)
    owners, slots = ints[:, :R], ints[:, R : 2 * R]
    at = 2 * R
    blocks = ints[:, at : at + BAT_DEV * BB].reshape(LISTERS * BAT_DEV, BB)
    at = at + BAT_DEV * BB
    atoms = ints[:, at : at + BAT_DEV * NEAR].reshape(LISTERS * BAT_DEV, NEAR)
    at = at + BAT_DEV * NEAR
    raw_weight = facts[4][:, at : at + BAT_DEV * NEAR].reshape(LISTERS * BAT_DEV, NEAR)
    away = owners ^ me
    tmap = jnp.where((away & 10) == 0, ((away & 1) + ((away >> 2) & 1) * 2) * TILE_DEV + slots, NO_TILE)

    wave_vecs = wave_table(KM)
    squared = jnp.sum(wave_vecs * wave_vecs, axis=0)
    near_gain = jnp.tile(0.1 / (1.0 + 0.1 * squared), 2)[None]
    far_gain = jnp.tile(0.03 / (1.0 + 0.1 * squared), 2)[None]
    location = atom_grid_index.astype(F32)
    phases = jnp.einsum("ca,cm->am", location, wave_vecs, precision=TOP_PRECISION) * (2.0 * math.pi / GRIDN)
    trig = jnp.concatenate([jnp.cos(phases), jnp.sin(phases)], axis=1)
    partition = raw_weight / jnp.sum(raw_weight, axis=1, keepdims=True)
    share = jnp.sum(
        jnp.where(
            atoms[None] == jnp.arange(ATOM_GRP, dtype=jnp.int32)[:, None, None],
            partition[None],
            0.0,
        ),
        axis=2,
    )
    displace = coords[:, None, :] - location[:, :, None]
    envelope = jnp.exp(-2.0 * jnp.sum(displace * displace, axis=0) / (GRIDN * GRIDN))
    spread = (envelope.reshape(ATOM_GRP, LISTERS * BAT_DEV, PTS) * share[:, :, None]).reshape(ATOM_GRP, LIST_PTS)
    wave_high, wave_low = wave_of_points(coords)
    codes, counts = lists_of(tmap)

    orbs = (orbitals, orb_x, orb_y, orb_first, orb_second)
    part = density_and_moments(
        tmap,
        blocks,
        (dens_tiles, tile_x, tile_y, tile_low, tile_high),
        orbs,
        spread,
        weights,
        wave_high,
        wave_low,
        trig,
    )
    a = ATOM_GRP
    got = swap(part, X3)
    part = part + jnp.concatenate([got[:a], got[a + 1 : a + 2], got[a : a + 1], got[a + 3 : a + 4], got[a + 2 : a + 3], got[a + 4 :]], axis=0)
    got = swap(part, Y3)
    density = part[a] + got[a + 2]
    moments = part[:a] + got[:a]
    moments = moments + swap(moments, X1)
    moments = moments + swap(moments, Y1)
    structure = jnp.sum(moments[:, :1] * trig, axis=0, keepdims=True)
    for bits in (1, 2, 4, 8):
        structure = structure + swap_grp(structure, bits)

    potential, own, part_x, part_y, part_diag = potential_and_ham(
        codes,
        counts,
        blocks,
        orbs,
        moments,
        far_gain * structure,
        near_gain,
        trig,
        spread,
        weights.reshape(1, LIST_PTS),
        wave_high,
        wave_low,
    )
    low_y = swap(part_diag[:half], X1)
    high_x = swap(part_diag[half:], Y1)
    low_x = swap(part_x[:half], X1)
    high_y = swap(part_y[half:], Y1)
    high_x = swap((part_x[half:].astype(F32) + high_x.astype(F32)).astype(BF16), X1)
    low_y = swap((part_y[:half].astype(F32) + low_y.astype(F32)).astype(BF16), Y1)
    low = own[:half] + low_x.astype(F32) + low_y.astype(F32)
    high = own[half:] + high_x.astype(F32) + high_y.astype(F32)
    return (density, potential.reshape(-1), jnp.concatenate([low, high], axis=0).astype(BF16))


def solution(mesh):
    in_specs = (
        P(("grp", "dev"), None, None),
        P(("grp", "dev"), None, None),
        P(None, ("grp", "dev")),
        P(("grp", "dev")),
        P(("grp", "dev"), None),
        P(("grp", "dev"), None),
        P(("grp", "dev")),
        P(("grp", "dev"), None),
        P(("grp", "dev"), None),
        P(None, "grp"),
    )
    out_specs = (P(("grp", "dev")), P(("grp", "dev")), P(("grp", "dev"), None, None))
    return jax.shard_map(
        on_device, mesh=mesh, in_specs=in_specs, out_specs=out_specs, check_vma=False
    )
```

time: 373 us -> 167 us (0.45)
  blocking collectives: 110 us -> 0 us
  waiting for transfers between devices: 115 us -> 62.5 us
  Pallas kernels: 0 us -> 40 us
  matrix products: 38.8 us -> 0.96 us
  local copies, waits for them, and re-layouts: 46.7 us -> 9.89 us
  other arithmetic: 41 us -> 9.31 us
  starting transfers between devices: 14.7 us -> 41.1 us
    all_to_all x2 -> x0, waiting for transfers between devices: 115 us -> none  [the longest x1 67.1 us: on_device(): lax.all_to_all(ham_out, 'dev', split_axis=0, concat_axis=0, tiled=True)]
    psum x2 -> x0, blocking collectives: 96.8 us -> none  [the longest x1 70.5 us: on_device(): moments_grp = lax.psum(moments_dev, 'dev')]
    ppermute x0 -> x25, waiting for transfers between devices: none -> 62.5 us  [the longest x21 58.2 us: swap(): return lax.ppermute(array, 'dev', [(d, d ^ bits) for d in range(16)])]
    ppermute x0 -> x25, starting transfers between devices: none -> 41.1 us  [the longest x21 28.9 us: swap(): return lax.ppermute(array, 'dev', [(d, d ^ bits) for d in range(16)])]
    pallas_call x0 -> x4, Pallas kernels: none -> 40 us  [the longest x1 15.7 us: potential_and_ham(): pl.pallas_call(ham_kernel, in_specs=[smem] * 3 + [hbm] * 5 + [vmem] * 8,...]
    dot_general x15 -> x1, matrix products: 38.8 us -> 0.96 us  [on_device(): jnp.einsum('ca,cm->am', location, wave_vecs, precision=TOP_PRECISION)]
    scatter-add x2 -> x0, other arithmetic: 27.3 us -> none  [hamilton_step(): return (ham_local.at[block_index].add(pieces), None)]
    gather x6 -> x0, local copies, waits for them, and re-layouts: 20.6 us -> none  [the longest x4 8.14 us: density_step(): local_tiles[block_index].transpose(0, 2, 1, 3).reshape(BB * TB, BB * TB)]
  transfers between devices with their start and end apart: 2 -> 25, of which waited for: 2 -> 19; matrix products, arithmetic and copies ran while one was open for 5% -> 7% of each run, Pallas kernels for 0% -> 6%
where the time goes in v1:
time: 167 us; the launch traced here: 165 us
  waiting for transfers between devices  62.5 us (37%)
  starting transfers between devices  41.1 us (25%)
  Pallas kernels  40 us (24%)
  local copies, waits for them, and re-layouts  9.89 us (6%)
  other arithmetic  9.31 us (6%)
    ppermute x21, waiting for transfers between devices, swap(): return lax.ppermute(array, 'dev', [(d, d ^ bits) for d in range(16)])  58.2 us
    ppermute x21, starting transfers between devices, swap(): return lax.ppermute(array, 'dev', [(d, d ^ bits) for d in range(16)])  28.9 us
    pallas_call x1, Pallas kernels, potential_and_ham(): pl.pallas_call(ham_kernel, in_specs=[smem] * 3 + [hbm] * 5 + [vmem] * 8,...  15.7 us
    pallas_call x1, Pallas kernels, density_and_moments(): pl.pallas_call(density_kernel, in_specs=[smem, smem] + [hbm] * 10 + [vmem...  14 us
    ppermute x4, starting transfers between devices, swap_grp(): return lax.ppermute(array, 'grp', [(g, g ^ bits) for g in range(16)])  12.3 us
    pallas_call x1, Pallas kernels, wave_of_points(): pl.pallas_call(wave_kernel, grid=(points // chunk,), in_specs=[pl.BlockSp...  5.74 us
    pallas_call x1, Pallas kernels, lists_of(): pl.pallas_call(list_kernel, in_specs=[smem], out_specs=[smem, smem], out_...  4.54 us
    ppermute x4, waiting for transfers between devices, swap_grp(): return lax.ppermute(array, 'grp', [(g, g ^ bits) for g in range(16)])  4.34 us
  transfers between devices with their start and end apart: 25, of which 19 were waited for; matrix products, arithmetic and copies ran while one was open for 7% of the time, Pallas kernels for 6%

profile of v1, /device:TPU:2, one launch (start us, length us, event | category | flops | bytes accessed | tf_op | source)
XLA Modules:
  0.0 164.8 jit_solution(18145393057308566580)
XLA Ops:
  0.6 0.8 reshape.183
  1.4 0.8 reshape.184
  2.1 0.8 reshape.185
  2.9 0.7 concatenate.16
  3.7 0.7 fusion.8
  4.4 3.1 %collective-permute-start.1 = (f32[5,512]{1,0:T(8,128)S(1)}, f32[5,512]{1,0:T(8,128)S(1)}, u32[]{:S(2)}, u32[]{:S(2)}) collective-permute-start(f32[5,512]{1,0:T(8,128)S(1)} %get-tuple-element.37), channel_id=1, source_target_pairs={{0,12},{1,13},{2,14},{3,15},{4,8},{5,9},{6,10},{7,11},{8,4},{9,5},... | collective-permute-start | bytes 30728 | tf_op jit(solution)/shard_map/ppermute | solution.py:37
  7.5 1.5 collective-permute-start
  9.2 3.5 %collective-permute-start.3 = (bf16[32,128,128]{2,1,0:T(8,128)(2,1)}, bf16[32,128,128]{2,1,0:T(8,128)(2,1)S(1)}, u32[]{:S(2)}, u32[]{:S(2)}) collective-permute-start(bf16[32,128,128]{2,1,0:T(8,128)(2,1)} %own_tile.1), channel_id=1, source_target_pairs={{0,1},{1,0},{2,3},{3,2},{4,5},{5,4},{6,7},{7,6},{8,9},{9,8},{10,11... | collective-permute-start | bytes 3145736 | tf_op jit(solution)/shard_map/ppermute | solution.py:37
  12.7 1.0 cosine_bitcast_fusion
  15.0 1.4 collective-permute-start.8
  16.4 2.2 %collective-permute-start.7 = (bf16[2,256,1024]{2,1,0:T(8,128)(2,1)}, bf16[2,256,1024]{2,1,0:T(8,128)(2,1)S(1)}, u32[]{:S(2)}, u32[]{:S(2)}) collective-permute-start(bf16[2,256,1024]{2,1,0:T(8,128)(2,1)} %own_orb.3), channel_id=1, source_target_pairs={{0,3},{1,2},{2,1},{3,0},{4,7},{5,6},{6,5},{7,4},{8,11},{9,10},{10,... | collective-permute-start | bytes 3145736 | tf_op jit(solution)/shard_map/ppermute | solution.py:37
  21.8 0.8 pad_maximum_fusion.1
  22.5 5.7 %shard_map.121 = (bf16[512,2048]{1,0:T(8,128)(2,1)}, bf16[512,2048]{1,0:T(8,128)(2,1)}) custom-call(f32[48,2048]{1,0:T(8,128)} %bitcast.37), custom_call_target="tpu_custom_call" | custom-call | flops 8388608 | bytes 4194304 | tf_op jit(solution)/shard_map/pallas_call | solution.py:84
  28.9 4.7 %collective-permute-done.3.x_tile = bf16[32,128,128]{2,1,0:T(8,128)(2,1)S(1)} collective-permute-done((bf16[32,128,128]{2,1,0:T(8,128)(2,1)}, bf16[32,128,128]{2,1,0:T(8,128)(2,1)S(1)}, u32[]{:S(2)}, u32[]{:S(2)}) %collective-permute-start.3) | collective-permute-done | bytes 1048608 | tf_op jit(solution)/shard_map/ppermute | solution.py:37
  34.0 3.0 %collective-permute-done.4.y_tile = bf16[32,128,128]{2,1,0:T(8,128)(2,1)} collective-permute-done((bf16[32,128,128]{2,1,0:T(8,128)(2,1)}, bf16[32,128,128]{2,1,0:T(8,128)(2,1)}, u32[]{:S(2)}, u32[]{:S(2)}) %collective-permute-start.4) | collective-permute-done | bytes 1048608 | tf_op jit(solution)/shard_map/ppermute | solution.py:37
  37.0 1.1 slice.128
  38.7 2.2 %collective-permute-start.9 = (bf16[256,1024]{1,0:T(8,128)(2,1)S(1)}, bf16[256,1024]{1,0:T(8,128)(2,1)S(1)}, u32[]{:S(2)}, u32[]{:S(2)}) collective-permute-start(bf16[256,1024]{1,0:T(8,128)(2,1)S(1)} %slice_bitcast_fusion.1), channel_id=1, source_target_pairs={{0,3},{1,2},{2,1},{3,0},{4,7},{5,6},{6,5},{7,4},{8,11},{9,10},{10,... | collective-permute-start | bytes 1572872 | tf_op jit(solution)/shard_map/ppermute | solution.py:37
  41.7 2.2 %collective-permute-start.10 = (bf16[256,1024]{1,0:T(8,128)(2,1)S(1)}, bf16[256,1024]{1,0:T(8,128)(2,1)S(1)}, u32[]{:S(2)}, u32[]{:S(2)}) collective-permute-start(bf16[256,1024]{1,0:T(8,128)(2,1)S(1)} %slice_bitcast_fusion), channel_id=1, source_target_pairs={{0,12},{1,13},{2,14},{3,15},{4,8},{5,9},{6,10},{7,11},{8,4},{9,5},... | collective-permute-start | bytes 1572872 | tf_op jit(solution)/shard_map/ppermute | solution.py:37
  44.7 1.6 collective-permute-done.6.high_tile
  46.3 1.0 collective-permute-done.5.low_tile
  47.3 4.5 %collective-permute-done.9.first_orb = bf16[256,1024]{1,0:T(8,128)(2,1)S(1)} collective-permute-done((bf16[256,1024]{1,0:T(8,128)(2,1)S(1)}, bf16[256,1024]{1,0:T(8,128)(2,1)S(1)}, u32[]{:S(2)}, u32[]{:S(2)}) %collective-permute-start.9) | collective-permute-done | bytes 524320 | tf_op jit(solution)/shard_map/ppermute | solution.py:37
  51.8 1.7 %collective-permute-done.10.second_orb = bf16[256,1024]{1,0:T(8,128)(2,1)S(1)} collective-permute-done((bf16[256,1024]{1,0:T(8,128)(2,1)S(1)}, bf16[256,1024]{1,0:T(8,128)(2,1)S(1)}, u32[]{:S(2)}, u32[]{:S(2)}) %collective-permute-start.10) | collective-permute-done | bytes 524320 | tf_op jit(solution)/shard_map/ppermute | solution.py:37
  53.6 0.8 copy-done.8
  54.3 14.0 %shard_map.122 = f32[24,512]{1,0:T(8,128)} custom-call(s32[4,81]{1,0:T(4,128)} %fusion.2.tmap_ref, s32[8,8]{1,0:T(8,128)} %reshape.186.blocks_ref, bf16[32,128,128]{2,1,0:T(8,128)(2,1)} %own_tile.1, bf16[32,128,128]{2,1,0:T(8,128)(2,1)} %copy-done.5, bf16[32,128,128]{2,1,0:T(8,128)(2,1)} %collective-permute-done.4.y_tile, bf16[16,128,128]{2,1,0:T(8,128)(2,1)} %copy-done.10, ...), custom_call_target="tpu_custom_call" | custom-call | flops 5000000000 | bytes 12582912 | tf_op jit(solution)/shard_map/pallas_call | solution.py:214
  68.4 1.5 collective-permute-start.11
  69.9 2.9 %collective-permute-done.11 = f32[24,512]{1,0:T(8,128)S(1)} collective-permute-done((f32[24,512]{1,0:T(8,128)}, f32[24,512]{1,0:T(8,128)S(1)}, u32[]{:S(2)}, u32[]{:S(2)}) %collective-permute-start.11) | collective-permute-done | bytes 49184 | tf_op jit(solution)/shard_map/ppermute | solution.py:37
  72.8 0.8 add.111
  73.6 3.0 %collective-permute-start.12 = (f32[24,512]{1,0:T(8,128)S(1)}, f32[24,512]{1,0:T(8,128)S(1)}, u32[]{:S(2)}, u32[]{:S(2)}) collective-permute-start(f32[24,512]{1,0:T(8,128)S(1)} %add.111), channel_id=1, source_target_pairs={{0,12},{1,13},{2,14},{3,15},{4,8},{5,9},{6,10},{7,11},{8,4},{9,5},... | collective-permute-start | bytes 147464 | tf_op jit(solution)/shard_map/ppermute | solution.py:37
  76.6 2.3 %collective-permute-done.12 = f32[24,512]{1,0:T(8,128)S(1)} collective-permute-done((f32[24,512]{1,0:T(8,128)S(1)}, f32[24,512]{1,0:T(8,128)S(1)}, u32[]{:S(2)}, u32[]{:S(2)}) %collective-permute-start.12) | collective-permute-done | bytes 49184 | tf_op jit(solution)/shard_map/ppermute | solution.py:37
  78.9 2.4 %collective-permute-start.13 = (f32[16,512]{1,0:T(8,128)S(1)}, f32[16,512]{1,0:T(8,128)S(1)}, u32[]{:S(2)}, u32[]{:S(2)}) collective-permute-start(f32[16,512]{1,0:T(8,128)S(1)} %slice_add_fusion), channel_id=1, source_target_pairs={{0,1},{1,0},{2,3},{3,2},{4,5},{5,4},{6,7},{7,6},{8,9},{9,8},{10,11... | collective-permute-start | bytes 98312 | tf_op jit(solution)/shard_map/ppermute | solution.py:37
  81.3 1.9 %collective-permute-done.13 = f32[16,512]{1,0:T(8,128)S(1)} collective-permute-done((f32[16,512]{1,0:T(8,128)S(1)}, f32[16,512]{1,0:T(8,128)S(1)}, u32[]{:S(2)}, u32[]{:S(2)}) %collective-permute-start.13) | collective-permute-done | bytes 32800 | tf_op jit(solution)/shard_map/ppermute | solution.py:37
  83.2 3.9 %collective-permute-done.14 = f32[16,512]{1,0:T(8,128)S(1)} collective-permute-done((f32[16,512]{1,0:T(8,128)S(1)}, f32[16,512]{1,0:T(8,128)S(1)}, u32[]{:S(2)}, u32[]{:S(2)}) %collective-permute-start.14) | collective-permute-done | bytes 32800 | tf_op jit(solution)/shard_map/ppermute | solution.py:37
  87.6 1.1 collective-permute-done.15
  88.8 1.9 %collective-permute-start.16 = (f32[1,512]{1,0:T(1,128)S(1)}, f32[1,512]{1,0:T(1,128)S(1)}, u32[]{:S(2)}, u32[]{:S(2)}) collective-permute-start(f32[1,512]{1,0:T(1,128)S(1)} %add.118), channel_id=1, source_target_pairs={{0,32},{16,48},{32,0},{48,16},{64,96},{80,112},{96,64},{112,80},{1... | collective-permute-start | bytes 6152 | tf_op jit(solution)/shard_map/ppermute | solution.py:41
  90.7 1.7 %collective-permute-done.16 = f32[1,512]{1,0:T(1,128)S(1)} collective-permute-done((f32[1,512]{1,0:T(1,128)S(1)}, f32[1,512]{1,0:T(1,128)S(1)}, u32[]{:S(2)}, u32[]{:S(2)}) %collective-permute-start.16) | collective-permute-done | bytes 2080 | tf_op jit(solution)/shard_map/ppermute | solution.py:41
  92.3 3.3 %collective-permute-start.17 = (f32[1,512]{1,0:T(1,128)S(1)}, f32[1,512]{1,0:T(1,128)S(1)}, u32[]{:S(2)}, u32[]{:S(2)}) collective-permute-start(f32[1,512]{1,0:T(1,128)S(1)} %add.119), channel_id=1, source_target_pairs={{0,64},{16,80},{32,96},{48,112},{64,0},{80,16},{96,32},{112,48},{1... | collective-permute-start | bytes 6152 | tf_op jit(solution)/shard_map/ppermute | solution.py:41
  95.6 1.6 collective-permute-done.17
  97.2 6.8 %collective-permute-start.18 = (f32[1,512]{1,0:T(1,128)S(1)}, f32[1,512]{1,0:T(1,128)S(1)}, u32[]{:S(2)}, u32[]{:S(2)}) collective-permute-start(f32[1,512]{1,0:T(1,128)S(1)} %add.120), channel_id=1, source_target_pairs={{0,128},{16,144},{32,160},{48,176},{64,192},{80,208},{96,224},{112... | collective-permute-start | bytes 6152 | tf_op jit(solution)/shard_map/ppermute | solution.py:41
  104.6 4.5 %shard_map.123 = (s32[4,96]{1,0:T(4,128)}, s32[4]{0:T(128)}) custom-call(s32[4,81]{1,0:T(4,128)} %fusion.2.tmap_ref), custom_call_target="tpu_custom_call" | custom-call | flops 4000 | bytes 4000 | tf_op jit(solution)/shard_map/pallas_call | solution.py:116
  110.3 15.7 %shard_map.124 = (f32[1,512]{1,0:T(1,128)}, f32[32,128,128]{2,1,0:T(8,128)}, bf16[32,128,128]{2,1,0:T(8,128)(2,1)}, bf16[32,128,128]{2,1,0:T(8,128)(2,1)}, bf16[32,128,128]{2,1,0:T(8,128)(2,1)}) custom-call(s32[4,96]{1,0:T(4,128)} %get-tuple-element.14.codes_ref, s32[4]{0:T(128)} %get-tuple-element.15.counts_ref, s32[8,8]{1,0:T(8,128)} %reshape.186.blocks_ref, ...), custom_call_target="tpu_custom_call" | custom-call | flops 4000000000 | bytes 16777216 | tf_op jit(solution)/shard_map/pallas_call | solution.py:337
  126.1 1.4 fusion.10
  127.5 1.8 %collective-permute-start.20 = (bf16[16,128,128]{2,1,0:T(8,128)(2,1)S(1)}, bf16[16,128,128]{2,1,0:T(8,128)(2,1)S(1)}, u32[]{:S(2)}, u32[]{:S(2)}) collective-permute-start(bf16[16,128,128]{2,1,0:T(8,128)(2,1)S(1)} %get-tuple-element.25), channel_id=1, source_target_pairs={{0,1},{1,0},{2,3},{3,2},{4,5},{5,4},{6,7},{7,6},{8,9},{9,8},{10,11... | collective-permute-start | bytes 1572872 | tf_op jit(solution)/shard_map/ppermute | solution.py:37
  129.4 2.1 %collective-permute-start.24 = (bf16[16,128,128]{2,1,0:T(8,128)(2,1)S(1)}, bf16[16,128,128]{2,1,0:T(8,128)(2,1)S(1)}, u32[]{:S(2)}, u32[]{:S(2)}) collective-permute-start(bf16[16,128,128]{2,1,0:T(8,128)(2,1)S(1)} %slice.124), channel_id=1, source_target_pairs={{0,4},{1,5},{2,6},{3,7},{4,0},{5,1},{6,2},{7,3},{8,12},{9,13},{10,... | collective-permute-start | bytes 1572872 | tf_op jit(solution)/shard_map/ppermute | solution.py:37
  131.8 10.6 %collective-permute-done.20 = bf16[16,128,128]{2,1,0:T(8,128)(2,1)S(1)} collective-permute-done((bf16[16,128,128]{2,1,0:T(8,128)(2,1)S(1)}, bf16[16,128,128]{2,1,0:T(8,128)(2,1)S(1)}, u32[]{:S(2)}, u32[]{:S(2)}) %collective-permute-start.20) | collective-permute-done | bytes 524320 | tf_op jit(solution)/shard_map/ppermute | solution.py:37
  143.3 0.9 collective-permute-done.22
  145.3 10.1 %collective-permute-done.24 = bf16[16,128,128]{2,1,0:T(8,128)(2,1)S(1)} collective-permute-done((bf16[16,128,128]{2,1,0:T(8,128)(2,1)S(1)}, bf16[16,128,128]{2,1,0:T(8,128)(2,1)S(1)}, u32[]{:S(2)}, u32[]{:S(2)}) %collective-permute-start.24) | collective-permute-done | bytes 524320 | tf_op jit(solution)/shard_map/ppermute | solution.py:37
  155.4 7.8 %collective-permute-done.21 = bf16[16,128,128]{2,1,0:T(8,128)(2,1)S(1)} collective-permute-done((bf16[16,128,128]{2,1,0:T(8,128)(2,1)S(1)}, bf16[16,128,128]{2,1,0:T(8,128)(2,1)S(1)}, u32[]{:S(2)}, u32[]{:S(2)}) %collective-permute-start.21) | collective-permute-done | bytes 524320 | tf_op jit(solution)/shard_map/ppermute | solution.py:37
  163.8 1.1 pad_maximum_fusion
  (100 shorter events, 13.0 us)
Async XLA Ops:
  4.4 10.6 %collective-permute-start.1 = (f32[5,512]{1,0:T(8,128)S(1)}, f32[5,512]{1,0:T(8,128)S(1)}, u32[]{:S(2)}, u32[]{:S(2)}) collective-permute-start(f32[5,512]{1,0:T(8,128)S(1)} %get-tuple-element.37), channel_id=1, source_target_pairs={{0,12},{1,13},{2,14},{3,15},{4,8},{5,9},{6,10},{7,11},{8,4},{9,5},... | collective-permute-start | bytes 30728 | tf_op jit(solution)/shard_map/ppermute | solution.py:37
  7.5 8.9 %collective-permute-start = (f32[5,512]{1,0:T(8,128)S(1)}, f32[5,512]{1,0:T(8,128)S(1)}, u32[]{:S(2)}, u32[]{:S(2)}) collective-permute-start(f32[5,512]{1,0:T(8,128)S(1)} %get-tuple-element.37), channel_id=1, source_target_pairs={{0,3},{1,2},{2,1},{3,0},{4,7},{5,6},{6,5},{7,4},{8,11},{9,10},{10,... | collective-permute-start | bytes 30728 | tf_op jit(solution)/shard_map/ppermute | solution.py:37
  9.0 9.6 %collective-permute-start.2 = (f32[5,512]{1,0:T(8,128)S(1)}, f32[5,512]{1,0:T(8,128)S(1)}, u32[]{:S(2)}, u32[]{:S(2)}) collective-permute-start(f32[5,512]{1,0:T(8,128)S(1)} %get-tuple-element.37), channel_id=1, source_target_pairs={{0,15},{1,14},{2,13},{3,12},{4,11},{5,10},{6,9},{7,8},{8,7},{9,6},... | collective-permute-start | bytes 30728 | tf_op jit(solution)/shard_map/ppermute | solution.py:37
  9.2 24.4 %collective-permute-start.3 = (bf16[32,128,128]{2,1,0:T(8,128)(2,1)}, bf16[32,128,128]{2,1,0:T(8,128)(2,1)S(1)}, u32[]{:S(2)}, u32[]{:S(2)}) collective-permute-start(bf16[32,128,128]{2,1,0:T(8,128)(2,1)} %own_tile.1), channel_id=1, source_target_pairs={{0,1},{1,0},{2,3},{3,2},{4,5},{5,4},{6,7},{7,6},{8,9},{9,8},{10,11... | collective-permute-start | bytes 3145736 | tf_op jit(solution)/shard_map/ppermute | solution.py:37
  12.7 24.3 %collective-permute-start.4 = (bf16[32,128,128]{2,1,0:T(8,128)(2,1)}, bf16[32,128,128]{2,1,0:T(8,128)(2,1)}, u32[]{:S(2)}, u32[]{:S(2)}) collective-permute-start(bf16[32,128,128]{2,1,0:T(8,128)(2,1)} %own_tile.1), channel_id=1, source_target_pairs={{0,4},{1,5},{2,6},{3,7},{4,0},{5,1},{6,2},{7,3},{8,12},{9,13},{10,... | collective-permute-start | bytes 3145736 | tf_op jit(solution)/shard_map/ppermute | solution.py:37
  15.0 23.7 %collective-permute-start.8 = (bf16[2,256,1024]{2,1,0:T(8,128)(2,1)}, bf16[2,256,1024]{2,1,0:T(8,128)(2,1)S(1)}, u32[]{:S(2)}, u32[]{:S(2)}) collective-permute-start(bf16[2,256,1024]{2,1,0:T(8,128)(2,1)} %own_orb.3), channel_id=1, source_target_pairs={{0,12},{1,13},{2,14},{3,15},{4,8},{5,9},{6,10},{7,11},{8,4},{9,5},... | collective-permute-start | bytes 3145736 | tf_op jit(solution)/shard_map/ppermute | solution.py:37
  16.4 25.3 %collective-permute-start.7 = (bf16[2,256,1024]{2,1,0:T(8,128)(2,1)}, bf16[2,256,1024]{2,1,0:T(8,128)(2,1)S(1)}, u32[]{:S(2)}, u32[]{:S(2)}) collective-permute-start(bf16[2,256,1024]{2,1,0:T(8,128)(2,1)} %own_orb.3), channel_id=1, source_target_pairs={{0,3},{1,2},{2,1},{3,0},{4,7},{5,6},{6,5},{7,4},{8,11},{9,10},{10,... | collective-permute-start | bytes 3145736 | tf_op jit(solution)/shard_map/ppermute | solution.py:37
  33.6 10.5 %copy-start.5 = (bf16[32,128,128]{2,1,0:T(8,128)(2,1)}, bf16[32,128,128]{2,1,0:T(8,128)(2,1)S(1)}, u32[]{:S(2)}) copy-start(bf16[32,128,128]{2,1,0:T(8,128)(2,1)S(1)} %collective-permute-done.3.x_tile) | copy-start | bytes 3145732
  33.7 12.6 %collective-permute-start.6 = (bf16[16,128,128]{2,1,0:T(8,128)(2,1)S(1)}, bf16[16,128,128]{2,1,0:T(8,128)(2,1)S(1)}, u32[]{:S(2)}, u32[]{:S(2)}) collective-permute-start(bf16[16,128,128]{2,1,0:T(8,128)(2,1)S(1)} %slice.129), channel_id=1, source_target_pairs={{0,4},{1,5},{2,6},{3,7},{4,0},{5,1},{6,2},{7,3},{8,12},{9,13},{10,... | collective-permute-start | bytes 1572872 | tf_op jit(solution)/shard_map/ppermute | solution.py:37
  38.0 9.3 %collective-permute-start.5 = (bf16[16,128,128]{2,1,0:T(8,128)(2,1)S(1)}, bf16[16,128,128]{2,1,0:T(8,128)(2,1)S(1)}, u32[]{:S(2)}, u32[]{:S(2)}) collective-permute-start(bf16[16,128,128]{2,1,0:T(8,128)(2,1)S(1)} %slice.128), channel_id=1, source_target_pairs={{0,1},{1,0},{2,3},{3,2},{4,5},{5,4},{6,7},{7,6},{8,9},{9,8},{10,11... | collective-permute-start | bytes 1572872 | tf_op jit(solution)/shard_map/ppermute | solution.py:37
  38.7 14.9 %copy-start.3 = (bf16[2,256,1024]{2,1,0:T(8,128)(2,1)}, bf16[2,256,1024]{2,1,0:T(8,128)(2,1)S(1)}, u32[]{:S(2)}) copy-start(bf16[2,256,1024]{2,1,0:T(8,128)(2,1)S(1)} %collective-permute-done.8.y_orb) | copy-start | bytes 3145732
  38.7 13.1 %collective-permute-start.9 = (bf16[256,1024]{1,0:T(8,128)(2,1)S(1)}, bf16[256,1024]{1,0:T(8,128)(2,1)S(1)}, u32[]{:S(2)}, u32[]{:S(2)}) collective-permute-start(bf16[256,1024]{1,0:T(8,128)(2,1)S(1)} %slice_bitcast_fusion.1), channel_id=1, source_target_pairs={{0,3},{1,2},{2,1},{3,0},{4,7},{5,6},{6,5},{7,4},{8,11},{9,10},{10,... | collective-permute-start | bytes 1572872 | tf_op jit(solution)/shard_map/ppermute | solution.py:37
  41.7 11.9 %copy-start.4 = (bf16[2,256,1024]{2,1,0:T(8,128)(2,1)}, bf16[2,256,1024]{2,1,0:T(8,128)(2,1)S(1)}, u32[]{:S(2)}) copy-start(bf16[2,256,1024]{2,1,0:T(8,128)(2,1)S(1)} %collective-permute-done.7.x_orb) | copy-start | bytes 3145732
  41.7 11.8 %collective-permute-start.10 = (bf16[256,1024]{1,0:T(8,128)(2,1)S(1)}, bf16[256,1024]{1,0:T(8,128)(2,1)S(1)}, u32[]{:S(2)}, u32[]{:S(2)}) collective-permute-start(bf16[256,1024]{1,0:T(8,128)(2,1)S(1)} %slice_bitcast_fusion), channel_id=1, source_target_pairs={{0,12},{1,13},{2,14},{3,15},{4,8},{5,9},{6,10},{7,11},{8,4},{9,5},... | collective-permute-start | bytes 1572872 | tf_op jit(solution)/shard_map/ppermute | solution.py:37
  46.3 7.3 %copy-start.9 = (bf16[16,128,128]{2,1,0:T(8,128)(2,1)}, bf16[16,128,128]{2,1,0:T(8,128)(2,1)S(1)}, u32[]{:S(2)}) copy-start(bf16[16,128,128]{2,1,0:T(8,128)(2,1)S(1)} %collective-permute-done.6.high_tile) | copy-start | bytes 1572868
  47.3 6.3 %copy-start.10 = (bf16[16,128,128]{2,1,0:T(8,128)(2,1)}, bf16[16,128,128]{2,1,0:T(8,128)(2,1)S(1)}, u32[]{:S(2)}) copy-start(bf16[16,128,128]{2,1,0:T(8,128)(2,1)S(1)} %collective-permute-done.5.low_tile) | copy-start | bytes 1572868
  51.8 1.8 %copy-start.7 = (bf16[256,1024]{1,0:T(8,128)(2,1)}, bf16[256,1024]{1,0:T(8,128)(2,1)S(1)}, u32[]{:S(2)}) copy-start(bf16[256,1024]{1,0:T(8,128)(2,1)S(1)} %collective-permute-done.9.first_orb) | copy-start | bytes 1572868
  53.6 0.8 copy-start.8
  68.4 4.4 %collective-permute-start.11 = (f32[24,512]{1,0:T(8,128)}, f32[24,512]{1,0:T(8,128)S(1)}, u32[]{:S(2)}, u32[]{:S(2)}) collective-permute-start(f32[24,512]{1,0:T(8,128)} %shard_map.122), channel_id=1, source_target_pairs={{0,3},{1,2},{2,1},{3,0},{4,7},{5,6},{6,5},{7,4},{8,11},{9,10},{10,... | collective-permute-start | bytes 147464 | tf_op jit(solution)/shard_map/ppermute | solution.py:37
  73.6 5.3 %collective-permute-start.12 = (f32[24,512]{1,0:T(8,128)S(1)}, f32[24,512]{1,0:T(8,128)S(1)}, u32[]{:S(2)}, u32[]{:S(2)}) collective-permute-start(f32[24,512]{1,0:T(8,128)S(1)} %add.111), channel_id=1, source_target_pairs={{0,12},{1,13},{2,14},{3,15},{4,8},{5,9},{6,10},{7,11},{8,4},{9,5},... | collective-permute-start | bytes 147464 | tf_op jit(solution)/shard_map/ppermute | solution.py:37
  78.9 4.3 %collective-permute-start.13 = (f32[16,512]{1,0:T(8,128)S(1)}, f32[16,512]{1,0:T(8,128)S(1)}, u32[]{:S(2)}, u32[]{:S(2)}) collective-permute-start(f32[16,512]{1,0:T(8,128)S(1)} %slice_add_fusion), channel_id=1, source_target_pairs={{0,1},{1,0},{2,3},{3,2},{4,5},{5,4},{6,7},{7,6},{8,9},{9,8},{10,11... | collective-permute-start | bytes 98312 | tf_op jit(solution)/shard_map/ppermute | solution.py:37
  83.2 3.9 %collective-permute-start.14 = (f32[16,512]{1,0:T(8,128)S(1)}, f32[16,512]{1,0:T(8,128)S(1)}, u32[]{:S(2)}, u32[]{:S(2)}) collective-permute-start(f32[16,512]{1,0:T(8,128)S(1)} %add.115), channel_id=1, source_target_pairs={{0,4},{1,5},{2,6},{3,7},{4,0},{5,1},{6,2},{7,3},{8,12},{9,13},{10,... | collective-permute-start | bytes 98312 | tf_op jit(solution)/shard_map/ppermute | solution.py:37
  87.2 23.2 %copy-start.6 = (f32[16,512]{1,0:T(8,128)}, f32[16,512]{1,0:T(8,128)S(1)}, u32[]{:S(2)}) copy-start(f32[16,512]{1,0:T(8,128)S(1)} %add.116.moments_ref) | copy-start | bytes 98308
  87.4 1.4 collective-permute-start.15
  88.8 3.6 %collective-permute-start.16 = (f32[1,512]{1,0:T(1,128)S(1)}, f32[1,512]{1,0:T(1,128)S(1)}, u32[]{:S(2)}, u32[]{:S(2)}) collective-permute-start(f32[1,512]{1,0:T(1,128)S(1)} %add.118), channel_id=1, source_target_pairs={{0,32},{16,48},{32,0},{48,16},{64,96},{80,112},{96,64},{112,80},{1... | collective-permute-start | bytes 6152 | tf_op jit(solution)/shard_map/ppermute | solution.py:41
  92.3 4.8 %collective-permute-start.17 = (f32[1,512]{1,0:T(1,128)S(1)}, f32[1,512]{1,0:T(1,128)S(1)}, u32[]{:S(2)}, u32[]{:S(2)}) collective-permute-start(f32[1,512]{1,0:T(1,128)S(1)} %add.119), channel_id=1, source_target_pairs={{0,64},{16,80},{32,96},{48,112},{64,0},{80,16},{96,32},{112,48},{1... | collective-permute-start | bytes 6152 | tf_op jit(solution)/shard_map/ppermute | solution.py:41
  97.2 12.5 %collective-permute-start.18 = (f32[1,512]{1,0:T(1,128)S(1)}, f32[1,512]{1,0:T(1,128)S(1)}, u32[]{:S(2)}, u32[]{:S(2)}) collective-permute-start(f32[1,512]{1,0:T(1,128)S(1)} %add.120), channel_id=1, source_target_pairs={{0,128},{16,144},{32,160},{48,176},{64,192},{80,208},{96,224},{112... | collective-permute-start | bytes 6152 | tf_op jit(solution)/shard_map/ppermute | solution.py:41
  126.0 3.3 %copy-start.1 = (bf16[32,128,128]{2,1,0:T(8,128)(2,1)S(1)}, bf16[32,128,128]{2,1,0:T(8,128)(2,1)}, u32[]{:S(2)}) copy-start(bf16[32,128,128]{2,1,0:T(8,128)(2,1)} %get-tuple-element.18) | copy-start | bytes 3145732
  126.1 3.3 %copy-start.2 = (bf16[32,128,128]{2,1,0:T(8,128)(2,1)S(1)}, bf16[32,128,128]{2,1,0:T(8,128)(2,1)}, u32[]{:S(2)}) copy-start(bf16[32,128,128]{2,1,0:T(8,128)(2,1)} %get-tuple-element.19) | copy-start | bytes 3145732
  127.5 14.9 %collective-permute-start.20 = (bf16[16,128,128]{2,1,0:T(8,128)(2,1)S(1)}, bf16[16,128,128]{2,1,0:T(8,128)(2,1)S(1)}, u32[]{:S(2)}, u32[]{:S(2)}) collective-permute-start(bf16[16,128,128]{2,1,0:T(8,128)(2,1)S(1)} %get-tuple-element.25), channel_id=1, source_target_pairs={{0,1},{1,0},{2,3},{3,2},{4,5},{5,4},{6,7},{7,6},{8,9},{9,8},{10,11... | collective-permute-start | bytes 1572872 | tf_op jit(solution)/shard_map/ppermute | solution.py:37
  129.3 14.9 %collective-permute-start.22 = (bf16[16,128,128]{2,1,0:T(8,128)(2,1)S(1)}, bf16[16,128,128]{2,1,0:T(8,128)(2,1)S(1)}, u32[]{:S(2)}, u32[]{:S(2)}) collective-permute-start(bf16[16,128,128]{2,1,0:T(8,128)(2,1)S(1)} %get-tuple-element.26), channel_id=1, source_target_pairs={{0,4},{1,5},{2,6},{3,7},{4,0},{5,1},{6,2},{7,3},{8,12},{9,13},{10,... | collective-permute-start | bytes 1572872 | tf_op jit(solution)/shard_map/ppermute | solution.py:37
  129.4 33.9 %copy-start = (f32[32,128,128]{2,1,0:T(8,128)S(1)}, f32[32,128,128]{2,1,0:T(8,128)}, u32[]{:S(2)}) copy-start(f32[32,128,128]{2,1,0:T(8,128)} %get-tuple-element.17) | copy-start | bytes 6291460
  129.4 26.0 %collective-permute-start.24 = (bf16[16,128,128]{2,1,0:T(8,128)(2,1)S(1)}, bf16[16,128,128]{2,1,0:T(8,128)(2,1)S(1)}, u32[]{:S(2)}, u32[]{:S(2)}) collective-permute-start(bf16[16,128,128]{2,1,0:T(8,128)(2,1)S(1)} %slice.124), channel_id=1, source_target_pairs={{0,4},{1,5},{2,6},{3,7},{4,0},{5,1},{6,2},{7,3},{8,12},{9,13},{10,... | collective-permute-start | bytes 1572872 | tf_op jit(solution)/shard_map/ppermute | solution.py:37
  131.5 23.9 %collective-permute-start.19 = (bf16[16,128,128]{2,1,0:T(8,128)(2,1)S(1)}, bf16[16,128,128]{2,1,0:T(8,128)(2,1)S(1)}, u32[]{:S(2)}, u32[]{:S(2)}) collective-permute-start(bf16[16,128,128]{2,1,0:T(8,128)(2,1)S(1)} %slice.118), channel_id=1, source_target_pairs={{0,1},{1,0},{2,3},{3,2},{4,5},{5,4},{6,7},{7,6},{8,9},{9,8},{10,11... | collective-permute-start | bytes 1572872 | tf_op jit(solution)/shard_map/ppermute | solution.py:37
  142.6 20.6 %collective-permute-start.21 = (bf16[16,128,128]{2,1,0:T(8,128)(2,1)S(1)}, bf16[16,128,128]{2,1,0:T(8,128)(2,1)S(1)}, u32[]{:S(2)}, u32[]{:S(2)}) collective-permute-start(bf16[16,128,128]{2,1,0:T(8,128)(2,1)S(1)} %add_convert_fusion.3), channel_id=1, source_target_pairs={{0,4},{1,5},{2,6},{3,7},{4,0},{5,1},{6,2},{7,3},{8,12},{9,13},{10,... | collective-permute-start | bytes 1572872 | tf_op jit(solution)/shard_map/ppermute | solution.py:37
  144.3 18.9 %collective-permute-start.23 = (bf16[16,128,128]{2,1,0:T(8,128)(2,1)S(1)}, bf16[16,128,128]{2,1,0:T(8,128)(2,1)S(1)}, u32[]{:S(2)}, u32[]{:S(2)}) collective-permute-start(bf16[16,128,128]{2,1,0:T(8,128)(2,1)S(1)} %add_convert_fusion.1), channel_id=1, source_target_pairs={{0,1},{1,0},{2,3},{3,2},{4,5},{5,4},{6,7},{7,6},{8,9},{9,8},{10,11... | collective-permute-start | bytes 1572872 | tf_op jit(solution)/shard_map/ppermute | solution.py:37

commit v2 on v1

v2 whole, which is shorter than its diff:
```python
import math

import jax
import jax.numpy as jnp
from jax import lax
from jax.experimental import pallas as pl
from jax.experimental.pallas import tpu as pltpu
from jax.sharding import PartitionSpec as P

TB = 128
BB = 8
UB = 9
R = 81
PTS = 256
BAT_DEV = 2
KM = 512
HALF = KM // 2
NEAR = 4
TILE_DEV = 32
GRIDN = 64
ATOM_GRP = 16
DEV_PTS = BAT_DEV * PTS
LISTERS = 4
LIST_PTS = LISTERS * DEV_PTS
NO_TILE = 4 * TILE_DEV
PARTS = TILE_DEV + 2 * (TILE_DEV // 2)
GROUP = 4
LIST_LEN = 32
MIB = 1024 * 1024

F32 = jnp.float32
BF16 = jnp.bfloat16
TOP_PRECISION = lax.Precision.HIGHEST
NT = (((1,), (1,)), ((), ()))


def swap(array, bits):
    return lax.ppermute(array, "dev", [(d, d ^ bits) for d in range(16)])


def swap_grp(array, bits):
    return lax.ppermute(array, "grp", [(g, g ^ bits) for g in range(16)])


X1, Y1 = 1, 4
X3, Y3 = 3, 12
XY = 5


def wave_table(count):
    mode_ids = jnp.arange(count // 2, dtype=jnp.int32)
    return jnp.stack([mode_ids % 8, mode_ids // 8 % 8, mode_ids // 64]).astype(F32)


def split_bf16(value):
    high = value.astype(BF16)
    return high, (value - high.astype(F32)).astype(BF16)


def wave_kernel(cs_ref, high_ref, low_ref):
    cos_x, sin_x = cs_ref[0:8], cs_ref[8:16]
    for fz in range(4):
        cos_z, sin_z = cs_ref[32 + fz : 33 + fz], cs_ref[40 + fz : 41 + fz]
        for fy in range(0, 8, 2):
            parts_cos, parts_sin = [], []
            for step in range(2):
                cos_y = cs_ref[16 + fy + step : 17 + fy + step]
                sin_y = cs_ref[24 + fy + step : 25 + fy + step]
                cos_yz = cos_y * cos_z - sin_y * sin_z
                sin_yz = sin_y * cos_z + cos_y * sin_z
                parts_cos.append(cos_x * cos_yz - sin_x * sin_yz)
                parts_sin.append(sin_x * cos_yz + cos_x * sin_yz)
            row = fz * 64 + fy * 8
            for base, parts in ((row, parts_cos), (HALF + row, parts_sin)):
                high, low = split_bf16(jnp.concatenate(parts, axis=0))
                high_ref[base : base + 16] = high
                low_ref[base : base + 16] = low


def wave_of_points(coords):
    points = coords.shape[1]
    chunk = 256
    angle = (jnp.arange(8, dtype=F32)[None, :, None] * coords[:, None, :]) * (2.0 * math.pi / GRIDN)
    cs = jnp.stack([jnp.cos(angle), jnp.sin(angle)], axis=1).reshape(48, points)
    out = jax.ShapeDtypeStruct((KM, points), BF16)
    return pl.pallas_call(
        wave_kernel,
        grid=(points // chunk,),
        in_specs=[pl.BlockSpec((48, chunk), lambda i: (0, i))],
        out_specs=[pl.BlockSpec((KM, chunk), lambda i: (0, i))] * 2,
        out_shape=[out, out],
        cost_estimate=pl.CostEstimate(flops=8 * KM * points, bytes_accessed=4 * KM * points, transcendentals=0),
    )(cs)


def orbital_copies(own_orb, x_orb, y_orb, diag_orbs, orbs, sems):
    return [
        [pltpu.make_async_copy(own_orb, orbs.at[0:2], sems.at[0])],
        [pltpu.make_async_copy(x_orb, orbs.at[2:4], sems.at[1])],
        [pltpu.make_async_copy(y_orb, orbs.at[4:6], sems.at[2])],
        [
            pltpu.make_async_copy(orb, orbs.at[6 + b] if len(diag_orbs) > 1 else orbs.at[6:8], sems.at[3 + b])
            for b, orb in enumerate(diag_orbs)
        ],
    ]


def density_kernel(
    tmap_ref,
    blocks_ref,
    own_tile,
    x_tile,
    y_tile,
    low_tile,
    high_tile,
    own_orb,
    x_orb,
    y_orb,
    first_orb,
    second_orb,
    spread_ref,
    weights_ref,
    high_hbm,
    low_hbm,
    trig_ref,
    out_ref,
    tiles,
    orbs,
    density,
    high_ref,
    low_ref,
    sems,
):
    half = TILE_DEV // 2
    arrivals = [
        pltpu.make_async_copy(source, tiles.at[at : at + source.shape[0]], sems.at[n])
        for n, (source, at) in enumerate(
            (
                (own_tile, 0),
                (x_tile, TILE_DEV),
                (y_tile, 2 * TILE_DEV),
                (low_tile, 3 * TILE_DEV),
                (high_tile, 3 * TILE_DEV + half),
            )
        )
    ]
    waves = [
        pltpu.make_async_copy(high_hbm, high_ref, sems.at[5]),
        pltpu.make_async_copy(low_hbm, low_ref, sems.at[6]),
    ]
    points = orbital_copies(own_orb, x_orb, y_orb, (first_orb, second_orb), orbs, sems.at[7:12])
    for copy in arrivals + sum(points, []) + waves:
        copy.start()
    tiles[NO_TILE] = jnp.zeros((TB, TB), BF16)
    for copy in arrivals:
        copy.wait()
    for lister in range(LISTERS):
        for copy in points[lister]:
            copy.wait()

        def one_batch(batch, unused, lister=lister):
            chosen = [blocks_ref[batch, i] for i in range(BB)]
            total = jnp.zeros((PTS, TB), F32)
            for pair in range(BB // 2):
                columns = []
                for j in (2 * pair, 2 * pair + 1):
                    columns.append(
                        jnp.concatenate(
                            [tiles[tmap_ref[lister, chosen[i] * UB + chosen[j]]] for i in range(BB)], axis=0
                        )
                    )
                product = jnp.dot(orbs[batch], jnp.concatenate(columns, axis=1), preferred_element_type=F32)
                for side in range(2):
                    block = orbs[batch, :, (2 * pair + side) * TB : (2 * pair + side + 1) * TB]
                    total = total + product[:, side * TB : (side + 1) * TB] * block.astype(F32)
            density[pl.ds(batch, 1), :] = jnp.sum(total.T, axis=0, keepdims=True)
            return unused

        lax.fori_loop(BAT_DEV * lister, BAT_DEV * (lister + 1), one_batch, 0)
    for copy in waves:
        copy.wait()
    weighted = density[...] * weights_ref[...]
    charge = jnp.concatenate(
        [spread_ref[:, b * PTS : (b + 1) * PTS] * weighted[b : b + 1] for b in range(LISTERS * BAT_DEV)], axis=1
    )
    charge_high, charge_low = split_bf16(charge)
    both = lax.dot_general(
        jnp.concatenate([charge_high, charge_low], axis=0), high_ref[...], NT, preferred_element_type=F32
    )
    sums = both[:ATOM_GRP] + both[ATOM_GRP:]
    sums = sums + lax.dot_general(charge_high, low_ref[...], NT, preferred_element_type=F32)
    cos_sum, sin_sum = sums[:, :HALF], sums[:, HALF:]
    cos_atom, sin_atom = trig_ref[:, :HALF], trig_ref[:, HALF:]
    out_ref[0:ATOM_GRP, :HALF] = cos_sum * cos_atom + sin_sum * sin_atom
    out_ref[0:ATOM_GRP, HALF:] = sin_sum * cos_atom - cos_sum * sin_atom
    for e in range(LISTERS):
        for b in range(BAT_DEV):
            out_ref[ATOM_GRP + e : ATOM_GRP + e + 1, b * PTS : (b + 1) * PTS] = density[
                BAT_DEV * e + b : BAT_DEV * e + b + 1
            ]
    out_ref[ATOM_GRP + LISTERS :] = jnp.zeros((8 - LISTERS, KM), F32)


SMEM_SPEC = pl.BlockSpec(memory_space=pltpu.SMEM)
VMEM_SPEC = pl.BlockSpec(memory_space=pltpu.VMEM)
ANY_SPEC = pl.BlockSpec(memory_space=pl.ANY)


def density_and_moments(tmap, blocks, tiles, orbs, spread, weights, wave_high, wave_low, trig):
    return pl.pallas_call(
        density_kernel,
        in_specs=[SMEM_SPEC] * 2 + [ANY_SPEC] * 10 + [VMEM_SPEC] * 2 + [ANY_SPEC] * 2 + [VMEM_SPEC],
        out_specs=VMEM_SPEC,
        out_shape=jax.ShapeDtypeStruct((ATOM_GRP + 8, KM), F32),
        scratch_shapes=[
            pltpu.VMEM((NO_TILE + 1, TB, TB), BF16),
            pltpu.VMEM((LISTERS * BAT_DEV, PTS, BB * TB), BF16),
            pltpu.VMEM((LISTERS * BAT_DEV, PTS), F32),
            pltpu.VMEM((KM, LIST_PTS), BF16),
            pltpu.VMEM((KM, LIST_PTS), BF16),
            pltpu.SemaphoreType.DMA((12,)),
        ],
        compiler_params=pltpu.CompilerParams(vmem_limit_bytes=56 * MIB),
        cost_estimate=pl.CostEstimate(flops=10**6, bytes_accessed=10**4, transcendentals=0),
    )(tmap, blocks, *tiles, *orbs, spread, weights, wave_high, wave_low, trig)


def pack_kernel(coords, weights, owner, slot, blocks, atoms, shares, out_ref, owner_ref, slot_ref, blocks_ref, atoms_ref, shares_ref, sems):
    copies = [
        pltpu.make_async_copy(source, target, sems.at[n])
        for n, (source, target) in enumerate(
            (
                (coords, out_ref.at[0:3]),
                (weights, out_ref.at[3:4]),
                (owner, owner_ref),
                (slot, slot_ref),
                (blocks, blocks_ref),
                (atoms, atoms_ref),
                (shares, shares_ref),
            )
        )
    ]
    out_ref[4:6] = jnp.zeros((2, DEV_PTS), F32)
    for copy in copies:
        copy.start()
    for copy in copies:
        copy.wait()
    out_ref[4:5, :R] = owner_ref[...].astype(F32)
    out_ref[4:5, TB : TB + R] = slot_ref[...].astype(F32)
    for b in range(BAT_DEV):
        out_ref[4:5, (2 + b) * TB : (2 + b) * TB + BB] = blocks_ref[b : b + 1].astype(F32)
        out_ref[5:6, b * TB : b * TB + NEAR] = atoms_ref[b : b + 1].astype(F32)
        out_ref[5:6, (2 + b) * TB : (2 + b) * TB + NEAR] = shares_ref[b : b + 1].astype(F32)


def place_kernel(index_ref, out_ref):
    out_ref[...] = index_ref[...].astype(F32)


def atom_places(index):
    return pl.pallas_call(
        place_kernel,
        in_specs=[VMEM_SPEC],
        out_specs=VMEM_SPEC,
        out_shape=jax.ShapeDtypeStruct(index.shape, F32),
        cost_estimate=pl.CostEstimate(flops=2 * 10**10, bytes_accessed=1000, transcendentals=0),
    )(index)


def packed_facts(*parts):
    return pl.pallas_call(
        pack_kernel,
        in_specs=[ANY_SPEC] * 7,
        out_specs=VMEM_SPEC,
        out_shape=jax.ShapeDtypeStruct((6, DEV_PTS), F32),
        scratch_shapes=[pltpu.VMEM(part.shape, part.dtype) for part in parts[2:]] + [pltpu.SemaphoreType.DMA((7,))],
        compiler_params=pltpu.CompilerParams(vmem_limit_bytes=56 * MIB),
        cost_estimate=pl.CostEstimate(flops=1000, bytes_accessed=1000, transcendentals=0),
    )(*parts)


def add_ham(codes_ref, counts_ref, blocks_ref, copies, orbs, scale, ham, turned, scaled):
    for e in range(LISTERS):
        for copy in copies[e]:
            copy.wait()
        for b in range(BAT_DEV):
            source = orbs.at[BAT_DEV * e + b]
            factors = []
            for part in range(PTS // TB):
                at = e * DEV_PTS + b * PTS + part * TB
                factors.append(jnp.broadcast_to(scale[:, at : at + TB], (TB, TB)).T)
            missing = UB * (UB - 1) // 2
            for i in range(BB):
                block = blocks_ref[BAT_DEV * e + b, i]
                missing = missing - block
                turned[block, :, b * PTS : (b + 1) * PTS] = source[:, i * TB : (i + 1) * TB].T
                for part in range(PTS // TB):
                    piece = source[part * TB : (part + 1) * TB, i * TB : (i + 1) * TB]
                    rows = slice(b * PTS + part * TB, b * PTS + (part + 1) * TB)
                    scaled[block, rows, :] = (factors[part] * piece.astype(F32)).astype(BF16)
            scaled[missing, b * PTS : (b + 1) * PTS, :] = jnp.zeros((PTS, TB), BF16)
            turned[missing, :, b * PTS : (b + 1) * PTS] = jnp.zeros((TB, PTS), BF16)

        def some_items(step, unused):
            for item in range(GROUP):
                code = codes_ref[e, step * GROUP + item]
                tile = code & 255
                i = (code >> 8) & 15
                j = code >> 12
                ham[tile] += jnp.dot(turned[i], scaled[j], preferred_element_type=F32)
            return unused

        lax.fori_loop(0, counts_ref[e], some_items, 0)


def near_kernel(
    codes_ref,
    counts_ref,
    blocks_ref,
    own_orb,
    x_orb,
    y_orb,
    first_orb,
    second_orb,
    moments_ref,
    far_ref,
    near_ref,
    trig_ref,
    spread_ref,
    weights_ref,
    high_hbm,
    low_hbm,
    pot_ref,
    scale_ref,
    ham,
    turned,
    scaled,
    orbs,
    high_ref,
    low_ref,
    sems,
):
    waves = [
        pltpu.make_async_copy(high_hbm, high_ref, sems.at[5]),
        pltpu.make_async_copy(low_hbm, low_ref, sems.at[6]),
    ]
    copies = orbital_copies(own_orb, x_orb, y_orb, (first_orb, second_orb), orbs, sems)
    for copy in waves + sum(copies, []):
        copy.start()

    def clear(t, unused):
        ham[t] = jnp.zeros((TB, TB), F32)
        return unused

    lax.fori_loop(0, PARTS + 1, clear, 0)
    cos_atom, sin_atom = trig_ref[:, :HALF], trig_ref[:, HALF:]
    cos_near = moments_ref[:, :HALF] * near_ref[:, :HALF]
    sin_near = moments_ref[:, HALF:] * near_ref[:, HALF:]
    turned_cos = cos_near * cos_atom - sin_near * sin_atom
    turned_sin = cos_near * sin_atom + sin_near * cos_atom
    coef = jnp.concatenate(
        [
            jnp.concatenate([turned_cos, turned_sin], axis=1),
            jnp.concatenate([far_ref[...], jnp.zeros((ATOM_GRP - 1, KM), F32)], axis=0),
        ],
        axis=0,
    )
    coef_high, coef_low = split_bf16(coef)
    for copy in waves:
        copy.wait()
    both = jnp.dot(jnp.concatenate([coef_high, coef_low], axis=0), high_ref[...], preferred_element_type=F32)
    values = both[: 2 * ATOM_GRP] + both[2 * ATOM_GRP :]
    values = values + jnp.dot(coef_high, low_ref[...], preferred_element_type=F32)
    pot = jnp.sum(values[:ATOM_GRP] * spread_ref[...], axis=0, keepdims=True) + values[ATOM_GRP : ATOM_GRP + 1]
    pot_ref[...] = pot[:, :DEV_PTS]
    scale = pot * weights_ref[...]
    scale_ref[...] = scale
    add_ham(codes_ref, counts_ref, blocks_ref, copies, orbs, scale, ham, turned, scaled)


def potential_and_ham(codes, counts, blocks, orbs, moments, far, near, trig, spread, weights, wave_high, wave_low):
    return pl.pallas_call(
        near_kernel,
        in_specs=[SMEM_SPEC] * 3 + [ANY_SPEC] * 5 + [VMEM_SPEC] * 6 + [ANY_SPEC] * 2,
        out_specs=[VMEM_SPEC] * 3,
        out_shape=[
            jax.ShapeDtypeStruct((1, DEV_PTS), F32),
            jax.ShapeDtypeStruct((1, LIST_PTS), F32),
            jax.ShapeDtypeStruct((PARTS + 1, TB, TB), F32),
        ],
        scratch_shapes=[
            pltpu.VMEM((UB, TB, DEV_PTS), BF16),
            pltpu.VMEM((UB, DEV_PTS, TB), BF16),
            pltpu.VMEM((LISTERS * BAT_DEV, PTS, BB * TB), BF16),
            pltpu.VMEM((KM, LIST_PTS), BF16),
            pltpu.VMEM((KM, LIST_PTS), BF16),
            pltpu.SemaphoreType.DMA((7,)),
        ],
        compiler_params=pltpu.CompilerParams(vmem_limit_bytes=56 * MIB),
        cost_estimate=pl.CostEstimate(flops=10**6, bytes_accessed=10**4, transcendentals=0),
    )(codes, counts, blocks, *orbs, moments, far, near, trig, spread, weights, wave_high, wave_low)


def rest_kernel(
    codes_ref,
    counts_ref,
    blocks_ref,
    own_orb,
    x_orb,
    y_orb,
    diag_orb,
    scale_ref,
    start_ref,
    own_ref,
    x_ref,
    y_ref,
    ham,
    turned,
    scaled,
    orbs,
    sems,
):
    begin = pltpu.make_async_copy(start_ref, ham, sems.at[5])
    copies = orbital_copies(own_orb, x_orb, y_orb, (diag_orb,), orbs, sems)
    for copy in copies[0] + [begin] + sum(copies[1:], []):
        copy.start()
    copies[0].append(begin)
    add_ham(codes_ref, counts_ref, blocks_ref, copies, orbs, scale_ref[...], ham, turned, scaled)
    half = TILE_DEV // 2
    own_ref[...] = ham[:TILE_DEV]
    x_ref[...] = ham[TILE_DEV : TILE_DEV + half].astype(BF16)
    y_ref[...] = ham[TILE_DEV + half : PARTS].astype(BF16)


def rest_of_ham(codes, counts, blocks, orbs, scale, start):
    part = jax.ShapeDtypeStruct((TILE_DEV // 2, TB, TB), BF16)
    return pl.pallas_call(
        rest_kernel,
        in_specs=[SMEM_SPEC] * 3 + [ANY_SPEC] * 4 + [VMEM_SPEC, ANY_SPEC],
        out_specs=[VMEM_SPEC] * 3,
        out_shape=[jax.ShapeDtypeStruct((TILE_DEV, TB, TB), F32), part, part],
        scratch_shapes=[
            pltpu.VMEM((PARTS + 1, TB, TB), F32),
            pltpu.VMEM((UB, TB, DEV_PTS), BF16),
            pltpu.VMEM((UB, DEV_PTS, TB), BF16),
            pltpu.VMEM((LISTERS * BAT_DEV, PTS, BB * TB), BF16),
            pltpu.SemaphoreType.DMA((6,)),
        ],
        compiler_params=pltpu.CompilerParams(vmem_limit_bytes=56 * MIB),
        cost_estimate=pl.CostEstimate(flops=10**6, bytes_accessed=10**4, transcendentals=0),
    )(codes, counts, blocks, *orbs, scale, start)


def lists_of(owners, slots, me):
    half = TILE_DEV // 2
    away = owners ^ me
    mine = (away == 0) | ((away == X1) & (slots < half)) | ((away == Y1) & (slots >= half))
    places = jnp.where(away == 0, slots, TILE_DEV + slots)
    rows = jnp.arange(R, dtype=jnp.int32)
    codes = places + (rows // UB) * 256 + (rows % UB) * 4096
    before = (rows[:, None] < rows[None, :])[None] & mine[:, :, None]
    rank = jnp.sum(before.astype(jnp.int32), axis=1)
    counts = jnp.sum(mine.astype(jnp.int32), axis=1)
    at = jnp.arange(LIST_LEN, dtype=jnp.int32)
    hit = (rank[:, None, :] == at[None, :, None]) & mine[:, None, :]
    listed = jnp.sum(jnp.where(hit, codes[:, None, :], 0), axis=2)
    listed = jnp.where(at[None] < counts[:, None], listed, PARTS)
    return listed, (counts + GROUP - 1) // GROUP


def what_is_listed(rows):
    ints = rows.astype(jnp.int32)
    blocks = ints[:, 2 * TB :].reshape(LISTERS * BAT_DEV, TB)[:, :BB]
    return ints[:, :R], ints[:, TB : TB + R], blocks


def on_device(
    orbitals,
    dens_tiles,
    point_coords,
    point_weights,
    batch_blocks,
    tile_owner,
    tile_slot,
    batch_atoms,
    batch_weights,
    atom_grid_index,
):
    me = lax.axis_index("dev").astype(jnp.int32)

    facts = packed_facts(
        point_coords,
        point_weights[None],
        tile_owner.reshape(1, R),
        tile_slot[None],
        batch_blocks,
        batch_atoms,
        batch_weights,
    )
    facts = (facts, swap(facts, X3), swap(facts, Y3), swap(facts, X3 ^ Y3))
    location, sent, *facts = lax.optimization_barrier((atom_places(atom_grid_index), orbitals, *facts))
    half = TILE_DEV // 2
    tile_x, tile_y = swap(dens_tiles, X1), swap(dens_tiles, Y1)
    orb_x, orb_y = swap(sent, X3), swap(sent, Y3)
    tile_low, tile_high = swap(tile_y[:half], X1), swap(tile_x[half:], Y1)
    orb_first, orb_second = swap(orb_y[0], X3), swap(orb_x[1], Y3)
    orbs = (orbitals, orb_x, orb_y, orb_first, orb_second)

    facts = jnp.stack(facts)
    coords = facts[:, :3].transpose(1, 0, 2).reshape(3, LIST_PTS)
    weights = facts[:, 3].reshape(LISTERS * BAT_DEV, PTS)
    owners, slots, blocks = what_is_listed(facts[:, 4])
    near_by = facts[:, 5].reshape(LISTERS, 2, BAT_DEV, TB)[..., :NEAR].reshape(LISTERS, 2, BAT_DEV, NEAR)
    atoms = near_by[:, 0].reshape(LISTERS * BAT_DEV, NEAR).astype(jnp.int32)
    raw_weight = near_by[:, 1].reshape(LISTERS * BAT_DEV, NEAR)
    away = owners ^ me
    tmap = jnp.where((away & 10) == 0, ((away & 1) + ((away >> 2) & 1) * 2) * TILE_DEV + slots, NO_TILE)
    codes, counts = lists_of(owners, slots, me)

    wave_vecs = wave_table(KM)
    squared = jnp.sum(wave_vecs * wave_vecs, axis=0)
    near_gain = jnp.tile(0.1 / (1.0 + 0.1 * squared), 2)[None]
    far_gain = jnp.tile(0.03 / (1.0 + 0.1 * squared), 2)[None]
    phases = jnp.einsum("ca,cm->am", location, wave_vecs, precision=TOP_PRECISION) * (2.0 * math.pi / GRIDN)
    trig = jnp.concatenate([jnp.cos(phases), jnp.sin(phases)], axis=1)
    partition = raw_weight / jnp.sum(raw_weight, axis=1, keepdims=True)
    share = jnp.sum(
        jnp.where(
            atoms[None] == jnp.arange(ATOM_GRP, dtype=jnp.int32)[:, None, None],
            partition[None],
            0.0,
        ),
        axis=2,
    )
    displace = coords[:, None, :] - location[:, :, None]
    envelope = jnp.exp(-2.0 * jnp.sum(displace * displace, axis=0) / (GRIDN * GRIDN))
    spread = (envelope.reshape(ATOM_GRP, LISTERS * BAT_DEV, PTS) * share[:, :, None]).reshape(ATOM_GRP, LIST_PTS)
    wave_high, wave_low = wave_of_points(coords)
    early, late = (spread, weights, wave_high, wave_low, trig, codes, counts, tmap, blocks), orbitals
    early, late, *unused = lax.optimization_barrier((early, late, tile_low, tile_high, orb_first, orb_second))
    spread, weights, wave_high, wave_low, trig, codes, counts, tmap, blocks = early
    orb_far = swap(late, XY)

    part = density_and_moments(
        tmap,
        blocks,
        (dens_tiles, tile_x, tile_y, tile_low, tile_high),
        orbs,
        spread,
        weights,
        wave_high,
        wave_low,
        trig,
    )
    a = ATOM_GRP
    got = swap(part, X3)
    part = part + jnp.concatenate([got[:a], got[a + 1 : a + 2], got[a : a + 1], got[a + 3 : a + 4], got[a + 2 : a + 3], got[a + 4 :]])
    got = swap(part, Y3)
    density = part[a] + got[a + 2]
    moments, orb_far = lax.optimization_barrier((part[:a] + got[:a], orb_far))
    orb_far_x, orb_far_y = swap(orb_far, X3), swap(orb_far, Y3)
    got = swap(jnp.concatenate([moments, facts[:, 4]]), X1)
    moments = moments + got[:a]
    got = swap(jnp.concatenate([moments, got[a:]]), Y1)
    late_diag, moments = lax.optimization_barrier((jnp.stack([orb_first, orb_second]), moments + got[:a]))
    orbs_far = (orb_far, orb_far_x, orb_far_y, swap(late_diag, XY))
    far_owners, far_slots, far_blocks = what_is_listed(got[a:])
    far_codes, far_counts = lists_of(far_owners, far_slots, me)
    structure = jnp.sum(moments[:, :1] * trig, axis=0, keepdims=True)
    for bits in (1, 2, 4, 8):
        structure = structure + swap_grp(structure, bits)

    potential, scale, ham = potential_and_ham(
        codes,
        counts,
        blocks,
        orbs,
        moments,
        far_gain * structure,
        near_gain,
        trig,
        spread,
        weights.reshape(1, LIST_PTS),
        wave_high,
        wave_low,
    )
    own, part_x, part_y = rest_of_ham(
        far_codes, far_counts, far_blocks, orbs_far, swap(scale, XY), ham
    )
    low = own[:half] + swap(part_x, X1).astype(F32)
    high = own[half:] + swap(part_y, Y1).astype(F32)
    return (density, potential.reshape(-1), jnp.concatenate([low, high], axis=0).astype(BF16))


def solution(mesh):
    in_specs = (
        P(("grp", "dev"), None, None),
        P(("grp", "dev"), None, None),
        P(None, ("grp", "dev")),
        P(("grp", "dev")),
        P(("grp", "dev"), None),
        P(("grp", "dev"), None),
        P(("grp", "dev")),
        P(("grp", "dev"), None),
        P(("grp", "dev"), None),
        P(None, "grp"),
    )
    out_specs = (P(("grp", "dev")), P(("grp", "dev")), P(("grp", "dev"), None, None))
    return jax.shard_map(
        on_device, mesh=mesh, in_specs=in_specs, out_specs=out_specs, check_vma=False
    )
```

time: 167 us -> 152 us (0.910)
  waiting for transfers between devices: 62.5 us -> 37.4 us
  starting transfers between devices: 41.1 us -> 47.1 us
  Pallas kernels: 40 us -> 44.2 us
  other arithmetic: 9.31 us -> 13.5 us
  local copies, waits for them, and re-layouts: 9.89 us -> 6.47 us
    ppermute x21 -> x22, waiting for transfers between devices: 58.2 us -> 33.6 us  [swap(): return lax.ppermute(array, 'dev', [(d, d ^ bits) for d in range(16)])]
    ppermute x21 -> x22, starting transfers between devices: 28.9 us -> 34.9 us  [swap(): return lax.ppermute(array, 'dev', [(d, d ^ bits) for d in range(16)])]
    pallas_call x3 -> x5, Pallas kernels: 34.3 us -> 38.5 us  [the longest x1 12.5 us: potential_and_ham(): pl.pallas_call(near_kernel, in_specs=[SMEM_SPEC] * 3 + [ANY_SPEC] * 5 + [...]
    select_n x0 -> x4, other arithmetic: none -> 2.41 us  [the longest x2 1.31 us: lists_of(): listed = jnp.where(at[None] < counts[:, None], listed, PARTS)]
    another operation x3, other arithmetic: 1.29 us -> 3.23 us  [the longest x2 0.77 us: on_device(): facts = jnp.stack([facts, facts_x, facts_y, facts_diag], axis=1)]
    reshape x5 -> x2, local copies, waits for them, and re-layouts: 3.03 us -> 1.19 us  [what_is_listed(): blocks = ints[:, 2 * TB:].reshape(LISTERS * BAT_DEV, TB)[:, :BB]]
    slice x6 -> x3, local copies, waits for them, and re-layouts: 1.71 us -> 0.01 us  [the longest x2 0.01 us: what_is_listed(): blocks = ints[:, 2 * TB:].reshape(LISTERS * BAT_DEV, TB)[:, :BB]]
  transfers between devices with their start and end apart: 25 -> 26, of which waited for: 19 -> 15; matrix products, arithmetic and copies ran while one was open for 7% -> 11% of each run, Pallas kernels for 6% -> 21%
where the time goes in v2:
time: 152 us; the launch traced here: 150 us
  starting transfers between devices  47.1 us (31%)
  Pallas kernels  44.2 us (29%)
  waiting for transfers between devices  37.4 us (25%)
  other arithmetic  13.5 us (9%)
  local copies, waits for them, and re-layouts  6.47 us (4%)
    ppermute x22, starting transfers between devices, swap(): return lax.ppermute(array, 'dev', [(d, d ^ bits) for d in range(16)])  34.9 us
    ppermute x22, waiting for transfers between devices, swap(): return lax.ppermute(array, 'dev', [(d, d ^ bits) for d in range(16)])  33.6 us
    pallas_call x1, Pallas kernels, potential_and_ham(): pl.pallas_call(near_kernel, in_specs=[SMEM_SPEC] * 3 + [ANY_SPEC] * 5 + [...  12.5 us
    ppermute x4, starting transfers between devices, swap_grp(): return lax.ppermute(array, 'grp', [(g, g ^ bits) for g in range(16)])  12.2 us
    pallas_call x1, Pallas kernels, density_and_moments(): pl.pallas_call(density_kernel, in_specs=[SMEM_SPEC] * 2 + [ANY_SPEC] * 10...  11.9 us
    pallas_call x1, Pallas kernels, rest_of_ham(): pl.pallas_call(rest_kernel, in_specs=[SMEM_SPEC] * 3 + [ANY_SPEC] * 4 + [...  11.3 us
    pallas_call x1, Pallas kernels, wave_of_points(): pl.pallas_call(wave_kernel, grid=(points // chunk,), in_specs=[pl.BlockSp...  5.76 us
    ppermute x4, waiting for transfers between devices, swap_grp(): return lax.ppermute(array, 'grp', [(g, g ^ bits) for g in range(16)])  3.83 us
  transfers between devices with their start and end apart: 26, of which 15 were waited for; matrix products, arithmetic and copies ran while one was open for 11% of the time, Pallas kernels for 21%

profile of v2, /device:TPU:2, one launch (start us, length us, event | category | flops | bytes accessed | tf_op | source)
XLA Modules:
  0.0 150.0 jit_solution(13228778448106078067)
XLA Ops:
  0.6 1.4 shard_map.122
  2.1 4.0 %collective-permute-start.2 = (f32[6,512]{1,0:T(8,128)}, f32[6,512]{1,0:T(8,128)S(1)}, u32[]{:S(2)}, u32[]{:S(2)}) collective-permute-start(f32[6,512]{1,0:T(8,128)} %shard_map.122), channel_id=1, source_target_pairs={{0,15},{1,14},{2,13},{3,12},{4,11},{5,10},{6,9},{7,8},{8,7},{9,6},... | collective-permute-start | bytes 36872 | tf_op jit(solution)/shard_map/ppermute | solution.py:38
  7.2 3.1 %collective-permute-start.5 = (bf16[32,128,128]{2,1,0:T(8,128)(2,1)}, bf16[32,128,128]{2,1,0:T(8,128)(2,1)}, u32[]{:S(2)}, u32[]{:S(2)}) collective-permute-start(bf16[32,128,128]{2,1,0:T(8,128)(2,1)} %own_tile.1), channel_id=1, source_target_pairs={{0,1},{1,0},{2,3},{3,2},{4,5},{5,4},{6,7},{7,6},{8,9},{9,8},{10,11... | collective-permute-start | bytes 3145736 | tf_op jit(solution)/shard_map/ppermute | solution.py:38
  10.4 1.3 shard_map.121
  12.0 0.9 collective-permute-start.9
  12.9 2.7 %collective-permute-start.7 = (bf16[2,256,1024]{2,1,0:T(8,128)(2,1)}, bf16[2,256,1024]{2,1,0:T(8,128)(2,1)S(1)}, u32[]{:S(2)}, u32[]{:S(2)}) collective-permute-start(bf16[2,256,1024]{2,1,0:T(8,128)(2,1)} %own_orb.3), channel_id=1, source_target_pairs={{0,12},{1,13},{2,14},{3,15},{4,8},{5,9},{6,10},{7,11},{8,4},{9,5},... | collective-permute-start | bytes 3145736 | tf_op jit(solution)/shard_map/ppermute | solution.py:38
  15.9 0.7 fusion.1
  16.7 0.8 pad_maximum_fusion.2
  20.0 5.8 %shard_map.123 = (bf16[512,2048]{1,0:T(8,128)(2,1)}, bf16[512,2048]{1,0:T(8,128)(2,1)}) custom-call(f32[48,2048]{1,0:T(8,128)} %bitcast.51), custom_call_target="tpu_custom_call" | custom-call | flops 8388608 | bytes 4194304 | tf_op jit(solution)/shard_map/pallas_call | solution.py:86
  26.5 0.6 fusion.9.codes_ref
  27.4 3.9 %collective-permute-done.3.y_tile = bf16[32,128,128]{2,1,0:T(8,128)(2,1)S(1)} collective-permute-done((bf16[32,128,128]{2,1,0:T(8,128)(2,1)}, bf16[32,128,128]{2,1,0:T(8,128)(2,1)S(1)}, u32[]{:S(2)}, u32[]{:S(2)}) %collective-permute-start.3) | collective-permute-done | bytes 1048608 | tf_op jit(solution)/shard_map/ppermute | solution.py:38
  31.4 1.9 %collective-permute-start.4 = (bf16[16,128,128]{2,1,0:T(8,128)(2,1)S(1)}, bf16[16,128,128]{2,1,0:T(8,128)(2,1)S(1)}, u32[]{:S(2)}, u32[]{:S(2)}) collective-permute-start(bf16[16,128,128]{2,1,0:T(8,128)(2,1)S(1)} %slice.150), channel_id=1, source_target_pairs={{0,1},{1,0},{2,3},{3,2},{4,5},{5,4},{6,7},{7,6},{8,9},{9,8},{10,11... | collective-permute-start | bytes 1572872 | tf_op jit(solution)/shard_map/ppermute | solution.py:38
  33.3 1.1 slice.151
  34.4 1.0 collective-permute-start.6
  35.4 2.5 %collective-permute-start.10 = (bf16[256,1024]{1,0:T(8,128)(2,1)S(1)}, bf16[256,1024]{1,0:T(8,128)(2,1)S(1)}, u32[]{:S(2)}, u32[]{:S(2)}) collective-permute-start(bf16[256,1024]{1,0:T(8,128)(2,1)S(1)} %slice_bitcast_fusion), channel_id=1, source_target_pairs={{0,12},{1,13},{2,14},{3,15},{4,8},{5,9},{6,10},{7,11},{8,4},{9,5},... | collective-permute-start | bytes 1572872 | tf_op jit(solution)/shard_map/ppermute | solution.py:38
  38.4 1.6 %collective-permute-start.8 = (bf16[256,1024]{1,0:T(8,128)(2,1)S(1)}, bf16[256,1024]{1,0:T(8,128)(2,1)S(1)}, u32[]{:S(2)}, u32[]{:S(2)}) collective-permute-start(bf16[256,1024]{1,0:T(8,128)(2,1)S(1)} %slice_bitcast_fusion.1), channel_id=1, source_target_pairs={{0,3},{1,2},{2,1},{3,0},{4,7},{5,6},{6,5},{7,4},{8,11},{9,10},{10,... | collective-permute-start | bytes 1572872 | tf_op jit(solution)/shard_map/ppermute | solution.py:38
  39.9 0.6 pad_maximum_fusion.6.trig_ref
  40.5 0.7 exponential_multiply_fusion.spread_ref
  41.2 2.4 %collective-permute-done.4.low_tile = bf16[16,128,128]{2,1,0:T(8,128)(2,1)S(1)} collective-permute-done((bf16[16,128,128]{2,1,0:T(8,128)(2,1)S(1)}, bf16[16,128,128]{2,1,0:T(8,128)(2,1)S(1)}, u32[]{:S(2)}, u32[]{:S(2)}) %collective-permute-start.4) | collective-permute-done | bytes 524320 | tf_op jit(solution)/shard_map/ppermute | solution.py:38
  43.7 1.4 collective-permute-done.6.high_tile
  45.1 3.7 %collective-permute-done.10.second_orb = bf16[256,1024]{1,0:T(8,128)(2,1)S(1)} collective-permute-done((bf16[256,1024]{1,0:T(8,128)(2,1)S(1)}, bf16[256,1024]{1,0:T(8,128)(2,1)S(1)}, u32[]{:S(2)}, u32[]{:S(2)}) %collective-permute-start.10) | collective-permute-done | bytes 524320 | tf_op jit(solution)/shard_map/ppermute | solution.py:38
  48.8 0.9 collective-permute-done.8.first_orb
  49.6 2.4 %collective-permute-start.13 = (bf16[2,256,1024]{2,1,0:T(8,128)(2,1)}, bf16[2,256,1024]{2,1,0:T(8,128)(2,1)}, u32[]{:S(2)}, u32[]{:S(2)}) collective-permute-start(bf16[2,256,1024]{2,1,0:T(8,128)(2,1)} %own_orb.3), channel_id=1, source_target_pairs={{0,5},{1,4},{2,7},{3,6},{4,1},{5,0},{6,3},{7,2},{8,13},{9,12},{10,... | collective-permute-start | bytes 3145736 | tf_op jit(solution)/shard_map/ppermute | solution.py:38
  52.1 11.9 %shard_map.124 = f32[24,512]{1,0:T(8,128)} custom-call(s32[4,81]{1,0:T(4,128)} %get-tuple-element.39.tmap_ref, s32[8,8]{1,0:T(8,128)} %bitcast.57, bf16[32,128,128]{2,1,0:T(8,128)(2,1)} %own_tile.1, bf16[32,128,128]{2,1,0:T(8,128)(2,1)} %collective-permute-done.5.x_tile, bf16[32,128,128]{2,1,0:T(8,128)(2,1)} %copy-done.4, bf16[16,128,128]{2,1,0:T(8,128)(2,1)} %copy-done.8, ...), custom_call_target="tpu_custom_call" | custom-call | flops 1000000 | bytes 10000 | tf_op jit(solution)/shard_map/pallas_call | solution.py:210
  64.0 2.4 %collective-permute-start.11 = (f32[24,512]{1,0:T(8,128)}, f32[24,512]{1,0:T(8,128)S(1)}, u32[]{:S(2)}, u32[]{:S(2)}) collective-permute-start(f32[24,512]{1,0:T(8,128)} %shard_map.124), channel_id=1, source_target_pairs={{0,3},{1,2},{2,1},{3,0},{4,7},{5,6},{6,5},{7,4},{8,11},{9,10},{10,... | collective-permute-start | bytes 147464 | tf_op jit(solution)/shard_map/ppermute | solution.py:38
  66.5 2.3 %collective-permute-done.11 = f32[24,512]{1,0:T(8,128)S(1)} collective-permute-done((f32[24,512]{1,0:T(8,128)}, f32[24,512]{1,0:T(8,128)S(1)}, u32[]{:S(2)}, u32[]{:S(2)}) %collective-permute-start.11) | collective-permute-done | bytes 49184 | tf_op jit(solution)/shard_map/ppermute | solution.py:38
  68.8 0.8 add.170
  69.6 1.6 %collective-permute-start.12 = (f32[24,512]{1,0:T(8,128)S(1)}, f32[24,512]{1,0:T(8,128)S(1)}, u32[]{:S(2)}, u32[]{:S(2)}) collective-permute-start(f32[24,512]{1,0:T(8,128)S(1)} %add.170), channel_id=1, source_target_pairs={{0,12},{1,13},{2,14},{3,15},{4,8},{5,9},{6,10},{7,11},{8,4},{9,5},... | collective-permute-start | bytes 147464 | tf_op jit(solution)/shard_map/ppermute | solution.py:38
  71.2 3.7 %collective-permute-done.12 = f32[24,512]{1,0:T(8,128)S(1)} collective-permute-done((f32[24,512]{1,0:T(8,128)S(1)}, f32[24,512]{1,0:T(8,128)S(1)}, u32[]{:S(2)}, u32[]{:S(2)}) %collective-permute-start.12) | collective-permute-done | bytes 49184 | tf_op jit(solution)/shard_map/ppermute | solution.py:38
  74.9 3.2 %collective-permute-start.14 = (f32[20,512]{1,0:T(8,128)S(1)}, f32[20,512]{1,0:T(8,128)S(1)}, u32[]{:S(2)}, u32[]{:S(2)}) collective-permute-start(f32[20,512]{1,0:T(8,128)S(1)} %pad_maximum_fusion.4), channel_id=1, source_target_pairs={{0,1},{1,0},{2,3},{3,2},{4,5},{5,4},{6,7},{7,6},{8,9},{9,8},{10,11... | collective-permute-start | bytes 122888 | tf_op jit(solution)/shard_map/ppermute | solution.py:38
  78.7 1.5 collective-permute-done.14
  80.6 1.3 pad_maximum_fusion
  82.5 1.0 collective-permute-start.21
  83.6 1.2 collective-permute-start.20
  85.2 3.3 %collective-permute-start.22 = (bf16[2,256,1024]{2,1,0:T(8,128)(2,1)S(1)}, bf16[2,256,1024]{2,1,0:T(8,128)(2,1)}, u32[]{:S(2)}, u32[]{:S(2)}) collective-permute-start(bf16[2,256,1024]{2,1,0:T(8,128)(2,1)S(1)} %pad_maximum_fusion), channel_id=1, source_target_pairs={{0,5},{1,4},{2,7},{3,6},{4,1},{5,0},{6,3},{7,2},{8,13},{9,12},{10,... | collective-permute-start | bytes 3145736 | tf_op jit(solution)/shard_map/ppermute | solution.py:38
  88.6 2.0 %collective-permute-start.17 = (f32[1,512]{1,0:T(1,128)S(1)}, f32[1,512]{1,0:T(1,128)S(1)}, u32[]{:S(2)}, u32[]{:S(2)}) collective-permute-start(f32[1,512]{1,0:T(1,128)S(1)} %add.177), channel_id=1, source_target_pairs={{0,32},{16,48},{32,0},{48,16},{64,96},{80,112},{96,64},{112,80},{1... | collective-permute-start | bytes 6152 | tf_op jit(solution)/shard_map/ppermute | solution.py:42
  90.8 1.5 %collective-permute-done.17 = f32[1,512]{1,0:T(1,128)S(1)} collective-permute-done((f32[1,512]{1,0:T(1,128)S(1)}, f32[1,512]{1,0:T(1,128)S(1)}, u32[]{:S(2)}, u32[]{:S(2)}) %collective-permute-start.17) | collective-permute-done | bytes 2080 | tf_op jit(solution)/shard_map/ppermute | solution.py:42
  92.3 3.3 %collective-permute-start.18 = (f32[1,512]{1,0:T(1,128)S(1)}, f32[1,512]{1,0:T(1,128)S(1)}, u32[]{:S(2)}, u32[]{:S(2)}) collective-permute-start(f32[1,512]{1,0:T(1,128)S(1)} %add.178), channel_id=1, source_target_pairs={{0,64},{16,80},{32,96},{48,112},{64,0},{80,16},{96,32},{112,48},{1... | collective-permute-start | bytes 6152 | tf_op jit(solution)/shard_map/ppermute | solution.py:42
  95.7 1.4 collective-permute-done.18
  97.1 6.8 %collective-permute-start.19 = (f32[1,512]{1,0:T(1,128)S(1)}, f32[1,512]{1,0:T(1,128)S(1)}, u32[]{:S(2)}, u32[]{:S(2)}) collective-permute-start(f32[1,512]{1,0:T(1,128)S(1)} %add.179), channel_id=1, source_target_pairs={{0,128},{16,144},{32,160},{48,176},{64,192},{80,208},{96,224},{112... | collective-permute-start | bytes 6152 | tf_op jit(solution)/shard_map/ppermute | solution.py:42
  104.0 0.7 fusion.10.codes_ref
  104.6 0.9 collective-permute-done.19
  106.1 12.5 %shard_map.125 = (f32[1,512]{1,0:T(1,128)}, f32[1,2048]{1,0:T(1,128)}, f32[65,128,128]{2,1,0:T(8,128)}) custom-call(s32[4,32]{1,0:T(4,128)} %fusion.9.codes_ref, s32[4]{0:T(128)} %and_select_fusion.5.counts_ref, s32[8,8]{1,0:T(8,128)} %bitcast.58, bf16[2,256,1024]{2,1,0:T(8,128)(2,1)} %own_orb.3, bf16[2,256,1024]{2,1,0:T(8,128)(2,1)} %copy-done, ...), custom_call_target="tpu_custom_call" | custom-call | flops 1000000 | bytes 10000 | tf_op jit(solution)/shard_map/pallas_call | solution.py:382
  120.1 3.4 %collective-permute-done.23.scale_ref = f32[1,2048]{1,0:T(1,128)S(1)} collective-permute-done((f32[1,2048]{1,0:T(1,128)}, f32[1,2048]{1,0:T(1,128)S(1)}, u32[]{:S(2)}, u32[]{:S(2)}) %collective-permute-start.23) | collective-permute-done | bytes 8224 | tf_op jit(solution)/shard_map/ppermute | solution.py:38
  124.8 11.3 %shard_map.126 = (f32[32,128,128]{2,1,0:T(8,128)}, bf16[16,128,128]{2,1,0:T(8,128)(2,1)}, bf16[16,128,128]{2,1,0:T(8,128)(2,1)}) custom-call(s32[4,32]{1,0:T(4,128)} %fusion.10.codes_ref, s32[4]{0:T(128)} %and_select_fusion.4.counts_ref, s32[8,8]{1,0:T(8,128)} %bitcast.60, bf16[2,256,1024]{2,1,0:T(8,128)(2,1)} %collective-permute-done.13.own_orb, ...), custom_call_target="tpu_custom_call" | custom-call | flops 1000000 | bytes 10000 | tf_op jit(solution)/shard_map/pallas_call | solution.py:437
  137.1 9.9 %collective-permute-done.24 = bf16[16,128,128]{2,1,0:T(8,128)(2,1)S(1)} collective-permute-done((bf16[16,128,128]{2,1,0:T(8,128)(2,1)}, bf16[16,128,128]{2,1,0:T(8,128)(2,1)S(1)}, u32[]{:S(2)}, u32[]{:S(2)}) %collective-permute-start.24) | collective-permute-done | bytes 524320 | tf_op jit(solution)/shard_map/ppermute | solution.py:38
  147.0 1.9 %add_convert_fusion.1 = (bf16[16,128,128]{2,1,0:T(8,128)(2,1)S(1)}, bf16[16,128,128]{2,1,0:T(8,128)(2,1)S(1)}) fusion(bf16[16,128,128]{2,1,0:T(8,128)(2,1)S(1)} %collective-permute-done.24, f32[32,128,128]{2,1,0:T(8,128)} %get-tuple-element.56, bf16[16,128,128]{2,1,0:T(8,128)(2,1)S(1)} %collective-permute-done.25), kind=kLoop, calls=%fused_computation.4 | loop fusion | flops 1572864 | bytes 4194304 | tf_op jit(solution)/shard_map/convert
  148.9 1.1 pad_maximum_fusion.1
  (121 shorter events, 12.8 us)
Async XLA Ops:
  2.1 9.6 %collective-permute-start.2 = (f32[6,512]{1,0:T(8,128)}, f32[6,512]{1,0:T(8,128)S(1)}, u32[]{:S(2)}, u32[]{:S(2)}) collective-permute-start(f32[6,512]{1,0:T(8,128)} %shard_map.122), channel_id=1, source_target_pairs={{0,15},{1,14},{2,13},{3,12},{4,11},{5,10},{6,9},{7,8},{8,7},{9,6},... | collective-permute-start | bytes 36872 | tf_op jit(solution)/shard_map/ppermute | solution.py:38
  6.1 5.6 %collective-permute-start.1 = (f32[6,512]{1,0:T(8,128)}, f32[6,512]{1,0:T(8,128)S(1)}, u32[]{:S(2)}, u32[]{:S(2)}) collective-permute-start(f32[6,512]{1,0:T(8,128)} %shard_map.122), channel_id=1, source_target_pairs={{0,12},{1,13},{2,14},{3,15},{4,8},{5,9},{6,10},{7,11},{8,4},{9,5},... | collective-permute-start | bytes 36872 | tf_op jit(solution)/shard_map/ppermute | solution.py:38
  6.3 5.4 %collective-permute-start = (f32[6,512]{1,0:T(8,128)}, f32[6,512]{1,0:T(8,128)S(1)}, u32[]{:S(2)}, u32[]{:S(2)}) collective-permute-start(f32[6,512]{1,0:T(8,128)} %shard_map.122), channel_id=1, source_target_pairs={{0,3},{1,2},{2,1},{3,0},{4,7},{5,6},{6,5},{7,4},{8,11},{9,10},{10,... | collective-permute-start | bytes 36872 | tf_op jit(solution)/shard_map/ppermute | solution.py:38
  6.9 24.5 %collective-permute-start.3 = (bf16[32,128,128]{2,1,0:T(8,128)(2,1)}, bf16[32,128,128]{2,1,0:T(8,128)(2,1)S(1)}, u32[]{:S(2)}, u32[]{:S(2)}) collective-permute-start(bf16[32,128,128]{2,1,0:T(8,128)(2,1)} %own_tile.1), channel_id=1, source_target_pairs={{0,4},{1,5},{2,6},{3,7},{4,0},{5,1},{6,2},{7,3},{8,12},{9,13},{10,... | collective-permute-start | bytes 3145736 | tf_op jit(solution)/shard_map/ppermute | solution.py:38
  7.2 26.0 %collective-permute-start.5 = (bf16[32,128,128]{2,1,0:T(8,128)(2,1)}, bf16[32,128,128]{2,1,0:T(8,128)(2,1)}, u32[]{:S(2)}, u32[]{:S(2)}) collective-permute-start(bf16[32,128,128]{2,1,0:T(8,128)(2,1)} %own_tile.1), channel_id=1, source_target_pairs={{0,1},{1,0},{2,3},{3,2},{4,5},{5,4},{6,7},{7,6},{8,9},{9,8},{10,11... | collective-permute-start | bytes 3145736 | tf_op jit(solution)/shard_map/ppermute | solution.py:38
  10.4 1.3 copy-start.12
  11.7 14.1 %copy-start.13 = (f32[3,16]{1,0:T(4,128)S(1)}, f32[3,16]{1,0:T(4,128)}, u32[]{:S(2)}) copy-start(f32[3,16]{1,0:T(4,128)} %shard_map.121) | copy-start | bytes 580
  12.0 23.4 %collective-permute-start.9 = (bf16[2,256,1024]{2,1,0:T(8,128)(2,1)}, bf16[2,256,1024]{2,1,0:T(8,128)(2,1)S(1)}, u32[]{:S(2)}, u32[]{:S(2)}) collective-permute-start(bf16[2,256,1024]{2,1,0:T(8,128)(2,1)} %own_orb.3), channel_id=1, source_target_pairs={{0,3},{1,2},{2,1},{3,0},{4,7},{5,6},{6,5},{7,4},{8,11},{9,10},{10,... | collective-permute-start | bytes 3145736 | tf_op jit(solution)/shard_map/ppermute | solution.py:38
  12.9 25.4 %collective-permute-start.7 = (bf16[2,256,1024]{2,1,0:T(8,128)(2,1)}, bf16[2,256,1024]{2,1,0:T(8,128)(2,1)S(1)}, u32[]{:S(2)}, u32[]{:S(2)}) collective-permute-start(bf16[2,256,1024]{2,1,0:T(8,128)(2,1)} %own_orb.3), channel_id=1, source_target_pairs={{0,12},{1,13},{2,14},{3,15},{4,8},{5,9},{6,10},{7,11},{8,4},{9,5},... | collective-permute-start | bytes 3145736 | tf_op jit(solution)/shard_map/ppermute | solution.py:38
  31.3 7.0 %copy-start.4 = (bf16[32,128,128]{2,1,0:T(8,128)(2,1)}, bf16[32,128,128]{2,1,0:T(8,128)(2,1)S(1)}, u32[]{:S(2)}) copy-start(bf16[32,128,128]{2,1,0:T(8,128)(2,1)S(1)} %collective-permute-done.3.y_tile) | copy-start | bytes 3145732
  31.4 12.3 %collective-permute-start.4 = (bf16[16,128,128]{2,1,0:T(8,128)(2,1)S(1)}, bf16[16,128,128]{2,1,0:T(8,128)(2,1)S(1)}, u32[]{:S(2)}, u32[]{:S(2)}) collective-permute-start(bf16[16,128,128]{2,1,0:T(8,128)(2,1)S(1)} %slice.150), channel_id=1, source_target_pairs={{0,1},{1,0},{2,3},{3,2},{4,5},{5,4},{6,7},{7,6},{8,9},{9,8},{10,11... | collective-permute-start | bytes 1572872 | tf_op jit(solution)/shard_map/ppermute | solution.py:38
  34.4 10.7 %collective-permute-start.6 = (bf16[16,128,128]{2,1,0:T(8,128)(2,1)S(1)}, bf16[16,128,128]{2,1,0:T(8,128)(2,1)S(1)}, u32[]{:S(2)}, u32[]{:S(2)}) collective-permute-start(bf16[16,128,128]{2,1,0:T(8,128)(2,1)S(1)} %slice.151), channel_id=1, source_target_pairs={{0,4},{1,5},{2,6},{3,7},{4,0},{5,1},{6,2},{7,3},{8,12},{9,13},{10,... | collective-permute-start | bytes 1572872 | tf_op jit(solution)/shard_map/ppermute | solution.py:38
  35.4 16.7 %copy-start = (bf16[2,256,1024]{2,1,0:T(8,128)(2,1)}, bf16[2,256,1024]{2,1,0:T(8,128)(2,1)S(1)}, u32[]{:S(2)}) copy-start(bf16[2,256,1024]{2,1,0:T(8,128)(2,1)S(1)} %collective-permute-done.9.x_orb) | copy-start | bytes 3145732
  35.4 13.3 %collective-permute-start.10 = (bf16[256,1024]{1,0:T(8,128)(2,1)S(1)}, bf16[256,1024]{1,0:T(8,128)(2,1)S(1)}, u32[]{:S(2)}, u32[]{:S(2)}) collective-permute-start(bf16[256,1024]{1,0:T(8,128)(2,1)S(1)} %slice_bitcast_fusion), channel_id=1, source_target_pairs={{0,12},{1,13},{2,14},{3,15},{4,8},{5,9},{6,10},{7,11},{8,4},{9,5},... | collective-permute-start | bytes 1572872 | tf_op jit(solution)/shard_map/ppermute | solution.py:38
  38.3 13.8 %copy-start.1 = (bf16[2,256,1024]{2,1,0:T(8,128)(2,1)}, bf16[2,256,1024]{2,1,0:T(8,128)(2,1)S(1)}, u32[]{:S(2)}) copy-start(bf16[2,256,1024]{2,1,0:T(8,128)(2,1)S(1)} %collective-permute-done.7.y_orb) | copy-start | bytes 3145732
  38.4 11.3 %collective-permute-start.8 = (bf16[256,1024]{1,0:T(8,128)(2,1)S(1)}, bf16[256,1024]{1,0:T(8,128)(2,1)S(1)}, u32[]{:S(2)}, u32[]{:S(2)}) collective-permute-start(bf16[256,1024]{1,0:T(8,128)(2,1)S(1)} %slice_bitcast_fusion.1), channel_id=1, source_target_pairs={{0,3},{1,2},{2,1},{3,0},{4,7},{5,6},{6,5},{7,4},{8,11},{9,10},{10,... | collective-permute-start | bytes 1572872 | tf_op jit(solution)/shard_map/ppermute | solution.py:38
  43.6 8.4 %copy-start.8 = (bf16[16,128,128]{2,1,0:T(8,128)(2,1)}, bf16[16,128,128]{2,1,0:T(8,128)(2,1)S(1)}, u32[]{:S(2)}) copy-start(bf16[16,128,128]{2,1,0:T(8,128)(2,1)S(1)} %collective-permute-done.4.low_tile) | copy-start | bytes 1572868
  45.1 7.0 %copy-start.9 = (bf16[16,128,128]{2,1,0:T(8,128)(2,1)}, bf16[16,128,128]{2,1,0:T(8,128)(2,1)S(1)}, u32[]{:S(2)}) copy-start(bf16[16,128,128]{2,1,0:T(8,128)(2,1)S(1)} %collective-permute-done.6.high_tile) | copy-start | bytes 1572868
  48.8 3.4 %copy-start.2 = (bf16[256,1024]{1,0:T(8,128)(2,1)}, bf16[256,1024]{1,0:T(8,128)(2,1)S(1)}, u32[]{:S(2)}) copy-start(bf16[256,1024]{1,0:T(8,128)(2,1)S(1)} %collective-permute-done.10.second_orb) | copy-start | bytes 1572868
  49.6 2.5 %copy-start.3 = (bf16[256,1024]{1,0:T(8,128)(2,1)}, bf16[256,1024]{1,0:T(8,128)(2,1)S(1)}, u32[]{:S(2)}) copy-start(bf16[256,1024]{1,0:T(8,128)(2,1)S(1)} %collective-permute-done.8.first_orb) | copy-start | bytes 1572868
  49.6 25.3 %collective-permute-start.13 = (bf16[2,256,1024]{2,1,0:T(8,128)(2,1)}, bf16[2,256,1024]{2,1,0:T(8,128)(2,1)}, u32[]{:S(2)}, u32[]{:S(2)}) collective-permute-start(bf16[2,256,1024]{2,1,0:T(8,128)(2,1)} %own_orb.3), channel_id=1, source_target_pairs={{0,5},{1,4},{2,7},{3,6},{4,1},{5,0},{6,3},{7,2},{8,13},{9,12},{10,... | collective-permute-start | bytes 3145736 | tf_op jit(solution)/shard_map/ppermute | solution.py:38
  64.0 17.9 %copy-start.11 = (f32[8,256]{1,0:T(8,128)S(1)}, f32[8,256]{1,0:T(8,128)}, u32[]{:S(2)}) copy-start(f32[8,256]{1,0:T(8,128)} %reshape_squeeze.12.weights_ref) | copy-start | bytes 24580
  64.0 21.0 %copy-start.7 = (f32[16,512]{1,0:T(8,128)S(1)}, f32[16,512]{1,0:T(8,128)}, u32[]{:S(2)}) copy-start(f32[16,512]{1,0:T(8,128)} %pad_maximum_fusion.6.trig_ref) | copy-start | bytes 98308
  64.0 4.7 %collective-permute-start.11 = (f32[24,512]{1,0:T(8,128)}, f32[24,512]{1,0:T(8,128)S(1)}, u32[]{:S(2)}, u32[]{:S(2)}) collective-permute-start(f32[24,512]{1,0:T(8,128)} %shard_map.124), channel_id=1, source_target_pairs={{0,3},{1,2},{2,1},{3,0},{4,7},{5,6},{6,5},{7,4},{8,11},{9,10},{10,... | collective-permute-start | bytes 147464 | tf_op jit(solution)/shard_map/ppermute | solution.py:38
  69.6 5.3 %collective-permute-start.12 = (f32[24,512]{1,0:T(8,128)S(1)}, f32[24,512]{1,0:T(8,128)S(1)}, u32[]{:S(2)}, u32[]{:S(2)}) collective-permute-start(f32[24,512]{1,0:T(8,128)S(1)} %add.170), channel_id=1, source_target_pairs={{0,12},{1,13},{2,14},{3,15},{4,8},{5,9},{6,10},{7,11},{8,4},{9,5},... | collective-permute-start | bytes 147464 | tf_op jit(solution)/shard_map/ppermute | solution.py:38
  74.9 5.3 %collective-permute-start.14 = (f32[20,512]{1,0:T(8,128)S(1)}, f32[20,512]{1,0:T(8,128)S(1)}, u32[]{:S(2)}, u32[]{:S(2)}) collective-permute-start(f32[20,512]{1,0:T(8,128)S(1)} %pad_maximum_fusion.4), channel_id=1, source_target_pairs={{0,1},{1,0},{2,3},{3,2},{4,5},{5,4},{6,7},{7,6},{8,9},{9,8},{10,11... | collective-permute-start | bytes 122888 | tf_op jit(solution)/shard_map/ppermute | solution.py:38
  80.2 4.5 %collective-permute-start.15 = (f32[20,512]{1,0:T(8,128)S(1)}, f32[20,512]{1,0:T(8,128)S(1)}, u32[]{:S(2)}, u32[]{:S(2)}) collective-permute-start(f32[20,512]{1,0:T(8,128)S(1)} %pad_maximum_fusion.5), channel_id=1, source_target_pairs={{0,4},{1,5},{2,6},{3,7},{4,0},{5,1},{6,2},{7,3},{8,12},{9,13},{10,... | collective-permute-start | bytes 122888 | tf_op jit(solution)/shard_map/ppermute | solution.py:38
  82.5 41.0 %collective-permute-start.21 = (bf16[2,256,1024]{2,1,0:T(8,128)(2,1)}, bf16[2,256,1024]{2,1,0:T(8,128)(2,1)S(1)}, u32[]{:S(2)}, u32[]{:S(2)}) collective-permute-start(bf16[2,256,1024]{2,1,0:T(8,128)(2,1)} %collective-permute-done.13.own_orb), channel_id=1, source_target_pairs={{0,12},{1,13},{2,14},{3,15},{4,8},{5,9},{6,10},{7,11},{8,4},{9,5},... | collective-permute-start | bytes 3145736 | tf_op jit(solution)/shard_map/ppermute | solution.py:38
  83.6 39.9 %collective-permute-start.20 = (bf16[2,256,1024]{2,1,0:T(8,128)(2,1)}, bf16[2,256,1024]{2,1,0:T(8,128)(2,1)S(1)}, u32[]{:S(2)}, u32[]{:S(2)}) collective-permute-start(bf16[2,256,1024]{2,1,0:T(8,128)(2,1)} %collective-permute-done.13.own_orb), channel_id=1, source_target_pairs={{0,3},{1,2},{2,1},{3,0},{4,7},{5,6},{6,5},{7,4},{8,11},{9,10},{10,... | collective-permute-start | bytes 3145736 | tf_op jit(solution)/shard_map/ppermute | solution.py:38
  84.8 21.3 %copy-start.10 = (f32[16,512]{1,0:T(8,128)}, f32[16,512]{1,0:T(8,128)S(1)}, u32[]{:S(2)}) copy-start(f32[16,512]{1,0:T(8,128)S(1)} %slice_add_fusion.moments_ref) | copy-start | bytes 98308
  85.1 3.5 %collective-permute-start.16 = (f32[1,512]{1,0:T(1,128)S(1)}, f32[1,512]{1,0:T(1,128)S(1)}, u32[]{:S(2)}, u32[]{:S(2)}) collective-permute-start(f32[1,512]{1,0:T(1,128)S(1)} %bitcast.64), channel_id=1, source_target_pairs={{0,16},{16,0},{32,48},{48,32},{64,80},{80,64},{96,112},{112,96},{1... | collective-permute-start | bytes 6152 | tf_op jit(solution)/shard_map/ppermute | solution.py:42
  85.2 38.3 %collective-permute-start.22 = (bf16[2,256,1024]{2,1,0:T(8,128)(2,1)S(1)}, bf16[2,256,1024]{2,1,0:T(8,128)(2,1)}, u32[]{:S(2)}, u32[]{:S(2)}) collective-permute-start(bf16[2,256,1024]{2,1,0:T(8,128)(2,1)S(1)} %pad_maximum_fusion), channel_id=1, source_target_pairs={{0,5},{1,4},{2,7},{3,6},{4,1},{5,0},{6,3},{7,2},{8,13},{9,12},{10,... | collective-permute-start | bytes 3145736 | tf_op jit(solution)/shard_map/ppermute | solution.py:38
  88.6 3.7 %collective-permute-start.17 = (f32[1,512]{1,0:T(1,128)S(1)}, f32[1,512]{1,0:T(1,128)S(1)}, u32[]{:S(2)}, u32[]{:S(2)}) collective-permute-start(f32[1,512]{1,0:T(1,128)S(1)} %add.177), channel_id=1, source_target_pairs={{0,32},{16,48},{32,0},{48,16},{64,96},{80,112},{96,64},{112,80},{1... | collective-permute-start | bytes 6152 | tf_op jit(solution)/shard_map/ppermute | solution.py:42
  92.3 4.8 %collective-permute-start.18 = (f32[1,512]{1,0:T(1,128)S(1)}, f32[1,512]{1,0:T(1,128)S(1)}, u32[]{:S(2)}, u32[]{:S(2)}) collective-permute-start(f32[1,512]{1,0:T(1,128)S(1)} %add.178), channel_id=1, source_target_pairs={{0,64},{16,80},{32,96},{48,112},{64,0},{80,16},{96,32},{112,48},{1... | collective-permute-start | bytes 6152 | tf_op jit(solution)/shard_map/ppermute | solution.py:42
  97.1 8.4 %collective-permute-start.19 = (f32[1,512]{1,0:T(1,128)S(1)}, f32[1,512]{1,0:T(1,128)S(1)}, u32[]{:S(2)}, u32[]{:S(2)}) collective-permute-start(f32[1,512]{1,0:T(1,128)S(1)} %add.179), channel_id=1, source_target_pairs={{0,128},{16,144},{32,160},{48,176},{64,192},{80,208},{96,224},{112... | collective-permute-start | bytes 6152 | tf_op jit(solution)/shard_map/ppermute | solution.py:42
  118.6 4.8 %collective-permute-start.23 = (f32[1,2048]{1,0:T(1,128)}, f32[1,2048]{1,0:T(1,128)S(1)}, u32[]{:S(2)}, u32[]{:S(2)}) collective-permute-start(f32[1,2048]{1,0:T(1,128)} %get-tuple-element.54), channel_id=1, source_target_pairs={{0,5},{1,4},{2,7},{3,6},{4,1},{5,0},{6,3},{7,2},{8,13},{9,12},{10,... | collective-permute-start | bytes 24584 | tf_op jit(solution)/shard_map/ppermute | solution.py:38
  123.5 0.6 copy-start.14
  123.5 1.0 copy-start.5
  123.5 1.3 copy-start.6
  136.2 10.8 %collective-permute-start.24 = (bf16[16,128,128]{2,1,0:T(8,128)(2,1)}, bf16[16,128,128]{2,1,0:T(8,128)(2,1)S(1)}, u32[]{:S(2)}, u32[]{:S(2)}) collective-permute-start(bf16[16,128,128]{2,1,0:T(8,128)(2,1)} %get-tuple-element.57), channel_id=1, source_target_pairs={{0,1},{1,0},{2,3},{3,2},{4,5},{5,4},{6,7},{7,6},{8,9},{9,8},{10,11... | collective-permute-start | bytes 1572872 | tf_op jit(solution)/shard_map/ppermute | solution.py:38
  136.3 10.8 %collective-permute-start.25 = (bf16[16,128,128]{2,1,0:T(8,128)(2,1)}, bf16[16,128,128]{2,1,0:T(8,128)(2,1)S(1)}, u32[]{:S(2)}, u32[]{:S(2)}) collective-permute-start(bf16[16,128,128]{2,1,0:T(8,128)(2,1)} %get-tuple-element.58), channel_id=1, source_target_pairs={{0,4},{1,5},{2,6},{3,7},{4,0},{5,1},{6,2},{7,3},{8,12},{9,13},{10,... | collective-permute-start | bytes 1572872 | tf_op jit(solution)/shard_map/ppermute | solution.py:38

commit v3 on v2

--- a/solution.py
+++ b/solution.py
@@ -1,3 +1,4 @@
+import functools
 import math
 
 import jax
@@ -123,7 +124,9 @@
     high_hbm,
     low_hbm,
     trig_ref,
+    rows_ref,
     out_ref,
+    diag_out,
     tiles,
     orbs,
     density,
@@ -157,6 +160,9 @@
     for lister in range(LISTERS):
         for copy in points[lister]:
             copy.wait()
+        if lister == LISTERS - 1:
+            onward = pltpu.make_async_copy(orbs.at[6:8], diag_out, sems.at[12])
+            onward.start()
 
         def one_batch(batch, unused, lister=lister):
             chosen = [blocks_ref[batch, i] for i in range(BB)]
@@ -198,7 +204,8 @@
             out_ref[ATOM_GRP + e : ATOM_GRP + e + 1, b * PTS : (b + 1) * PTS] = density[
                 BAT_DEV * e + b : BAT_DEV * e + b + 1
             ]
-    out_ref[ATOM_GRP + LISTERS :] = jnp.zeros((8 - LISTERS, KM), F32)
+    out_ref[ATOM_GRP + LISTERS :] = rows_ref[...]
+    onward.wait()
 
 
 SMEM_SPEC = pl.BlockSpec(memory_space=pltpu.SMEM)
@@ -206,23 +213,26 @@
 ANY_SPEC = pl.BlockSpec(memory_space=pl.ANY)
 
 
-def density_and_moments(tmap, blocks, tiles, orbs, spread, weights, wave_high, wave_low, trig):
+def density_and_moments(tmap, blocks, tiles, orbs, spread, weights, wave_high, wave_low, trig, rows):
     return pl.pallas_call(
         density_kernel,
-        in_specs=[SMEM_SPEC] * 2 + [ANY_SPEC] * 10 + [VMEM_SPEC] * 2 + [ANY_SPEC] * 2 + [VMEM_SPEC],
-        out_specs=VMEM_SPEC,
-        out_shape=jax.ShapeDtypeStruct((ATOM_GRP + 8, KM), F32),
+        in_specs=[SMEM_SPEC] * 2 + [ANY_SPEC] * 10 + [VMEM_SPEC] * 2 + [ANY_SPEC] * 2 + [VMEM_SPEC] * 2,
+        out_specs=[VMEM_SPEC, ANY_SPEC],
+        out_shape=[
+            jax.ShapeDtypeStruct((ATOM_GRP + 8, KM), F32),
+            jax.ShapeDtypeStruct((BAT_DEV, PTS, BB * TB), BF16),
+        ],
         scratch_shapes=[
             pltpu.VMEM((NO_TILE + 1, TB, TB), BF16),
             pltpu.VMEM((LISTERS * BAT_DEV, PTS, BB * TB), BF16),
             pltpu.VMEM((LISTERS * BAT_DEV, PTS), F32),
             pltpu.VMEM((KM, LIST_PTS), BF16),
             pltpu.VMEM((KM, LIST_PTS), BF16),
-            pltpu.SemaphoreType.DMA((12,)),
+            pltpu.SemaphoreType.DMA((13,)),
         ],
         compiler_params=pltpu.CompilerParams(vmem_limit_bytes=56 * MIB),
         cost_estimate=pl.CostEstimate(flops=10**6, bytes_accessed=10**4, transcendentals=0),
-    )(tmap, blocks, *tiles, *orbs, spread, weights, wave_high, wave_low, trig)
+    )(tmap, blocks, *tiles, *orbs, spread, weights, wave_high, wave_low, trig, rows)
 
 
 def pack_kernel(coords, weights, owner, slot, blocks, atoms, shares, out_ref, owner_ref, slot_ref, blocks_ref, atoms_ref, shares_ref, sems):
@@ -313,46 +323,9 @@
         lax.fori_loop(0, counts_ref[e], some_items, 0)
 
 
-def near_kernel(
-    codes_ref,
-    counts_ref,
-    blocks_ref,
-    own_orb,
-    x_orb,
-    y_orb,
-    first_orb,
-    second_orb,
-    moments_ref,
-    far_ref,
-    near_ref,
-    trig_ref,
-    spread_ref,
-    weights_ref,
-    high_hbm,
-    low_hbm,
-    pot_ref,
-    scale_ref,
-    ham,
-    turned,
-    scaled,
-    orbs,
-    high_ref,
-    low_ref,
-    sems,
+def potential_kernel(
+    moments_ref, far_ref, near_ref, trig_ref, spread_ref, weights_ref, high_ref, low_ref, pot_ref, scale_ref
 ):
-    waves = [
-        pltpu.make_async_copy(high_hbm, high_ref, sems.at[5]),
-        pltpu.make_async_copy(low_hbm, low_ref, sems.at[6]),
-    ]
-    copies = orbital_copies(own_orb, x_orb, y_orb, (first_orb, second_orb), orbs, sems)
-    for copy in waves + sum(copies, []):
-        copy.start()
-
-    def clear(t, unused):
-        ham[t] = jnp.zeros((TB, TB), F32)
-        return unused
-
-    lax.fori_loop(0, PARTS + 1, clear, 0)
     cos_atom, sin_atom = trig_ref[:, :HALF], trig_ref[:, HALF:]
     cos_near = moments_ref[:, :HALF] * near_ref[:, :HALF]
     sin_near = moments_ref[:, HALF:] * near_ref[:, HALF:]
@@ -366,96 +339,94 @@
         axis=0,
     )
     coef_high, coef_low = split_bf16(coef)
-    for copy in waves:
-        copy.wait()
     both = jnp.dot(jnp.concatenate([coef_high, coef_low], axis=0), high_ref[...], preferred_element_type=F32)
     values = both[: 2 * ATOM_GRP] + both[2 * ATOM_GRP :]
     values = values + jnp.dot(coef_high, low_ref[...], preferred_element_type=F32)
     pot = jnp.sum(values[:ATOM_GRP] * spread_ref[...], axis=0, keepdims=True) + values[ATOM_GRP : ATOM_GRP + 1]
     pot_ref[...] = pot[:, :DEV_PTS]
-    scale = pot * weights_ref[...]
-    scale_ref[...] = scale
-    add_ham(codes_ref, counts_ref, blocks_ref, copies, orbs, scale, ham, turned, scaled)
-
-
-def potential_and_ham(codes, counts, blocks, orbs, moments, far, near, trig, spread, weights, wave_high, wave_low):
+    scale_ref[...] = pot * weights_ref[...]
+
+
+def potential_of(moments, far, near, trig, spread, weights, wave_high, wave_low):
     return pl.pallas_call(
-        near_kernel,
-        in_specs=[SMEM_SPEC] * 3 + [ANY_SPEC] * 5 + [VMEM_SPEC] * 6 + [ANY_SPEC] * 2,
-        out_specs=[VMEM_SPEC] * 3,
-        out_shape=[
-            jax.ShapeDtypeStruct((1, DEV_PTS), F32),
-            jax.ShapeDtypeStruct((1, LIST_PTS), F32),
-            jax.ShapeDtypeStruct((PARTS + 1, TB, TB), F32),
-        ],
+        potential_kernel,
+        in_specs=[VMEM_SPEC] * 8,
+        out_specs=[VMEM_SPEC] * 2,
+        out_shape=[jax.ShapeDtypeStruct((1, DEV_PTS), F32), jax.ShapeDtypeStruct((1, LIST_PTS), F32)],
+        compiler_params=pltpu.CompilerParams(vmem_limit_bytes=16 * MIB),
+        cost_estimate=pl.CostEstimate(flops=10**6, bytes_accessed=10**4, transcendentals=0),
+    )(moments, far, near, trig, spread, weights, wave_high, wave_low)
+
+
+def ham_kernel(n_starts, n_outs, codes_ref, counts_ref, blocks_ref, scale_ref, *refs):
+    n_orbs = len(refs) - n_starts - n_outs - 5
+    orb_refs, refs = refs[:n_orbs], refs[n_orbs:]
+    starts, outs, (ham, turned, scaled, orbs, sems) = refs[:n_starts], refs[n_starts : n_starts + n_outs], refs[-5:]
+    tiles = ham.shape[0] - 1
+    copies = orbital_copies(*orb_refs[:3], orb_refs[3:], orbs, sems)
+    for start in starts:
+        copies[0].append(pltpu.make_async_copy(start, ham.at[0:tiles], sems.at[5]))
+    for copy in sum(copies, []):
+        copy.start()
+    if n_starts == 0:
+
+        def clear(t, unused):
+            ham[t] = jnp.zeros((TB, TB), F32)
+            return unused
+
+        lax.fori_loop(0, tiles, clear, 0)
+    add_ham(codes_ref, counts_ref, blocks_ref, copies, orbs, scale_ref[...], ham, turned, scaled)
+    at = 0
+    for out in outs:
+        out[...] = ham[at : at + out.shape[0]].astype(out.dtype)
+        at = at + out.shape[0]
+
+
+def ham_terms(codes, counts, blocks, scale, orbs, starts, outs, flops):
+    tiles = sum(count for count, unused in outs)
+    return pl.pallas_call(
+        functools.partial(ham_kernel, len(starts), len(outs)),
+        in_specs=[SMEM_SPEC] * 3 + [VMEM_SPEC] + [ANY_SPEC] * (len(orbs) + len(starts)),
+        out_specs=[VMEM_SPEC] * len(outs),
+        out_shape=[jax.ShapeDtypeStruct((count, TB, TB), dtype) for count, dtype in outs],
         scratch_shapes=[
-            pltpu.VMEM((UB, TB, DEV_PTS), BF16),
-            pltpu.VMEM((UB, DEV_PTS, TB), BF16),
-            pltpu.VMEM((LISTERS * BAT_DEV, PTS, BB * TB), BF16),
-            pltpu.VMEM((KM, LIST_PTS), BF16),
-            pltpu.VMEM((KM, LIST_PTS), BF16),
-            pltpu.SemaphoreType.DMA((7,)),
-        ],
-        compiler_params=pltpu.CompilerParams(vmem_limit_bytes=56 * MIB),
-        cost_estimate=pl.CostEstimate(flops=10**6, bytes_accessed=10**4, transcendentals=0),
-    )(codes, counts, blocks, *orbs, moments, far, near, trig, spread, weights, wave_high, wave_low)
-
-
-def rest_kernel(
-    codes_ref,
-    counts_ref,
-    blocks_ref,
-    own_orb,
-    x_orb,
-    y_orb,
-    diag_orb,
-    scale_ref,
-    start_ref,
-    own_ref,
-    x_ref,
-    y_ref,
-    ham,
-    turned,
-    scaled,
-    orbs,
-    sems,
-):
-    begin = pltpu.make_async_copy(start_ref, ham, sems.at[5])
-    copies = orbital_copies(own_orb, x_orb, y_orb, (diag_orb,), orbs, sems)
-    for copy in copies[0] + [begin] + sum(copies[1:], []):
-        copy.start()
-    copies[0].append(begin)
-    add_ham(codes_ref, counts_ref, blocks_ref, copies, orbs, scale_ref[...], ham, turned, scaled)
-    half = TILE_DEV // 2
-    own_ref[...] = ham[:TILE_DEV]
-    x_ref[...] = ham[TILE_DEV : TILE_DEV + half].astype(BF16)
-    y_ref[...] = ham[TILE_DEV + half : PARTS].astype(BF16)
-
-
-def rest_of_ham(codes, counts, blocks, orbs, scale, start):
-    part = jax.ShapeDtypeStruct((TILE_DEV // 2, TB, TB), BF16)
-    return pl.pallas_call(
-        rest_kernel,
-        in_specs=[SMEM_SPEC] * 3 + [ANY_SPEC] * 4 + [VMEM_SPEC, ANY_SPEC],
-        out_specs=[VMEM_SPEC] * 3,
-        out_shape=[jax.ShapeDtypeStruct((TILE_DEV, TB, TB), F32), part, part],
-        scratch_shapes=[
-            pltpu.VMEM((PARTS + 1, TB, TB), F32),
+            pltpu.VMEM((tiles + 1, TB, TB), F32),
             pltpu.VMEM((UB, TB, DEV_PTS), BF16),
             pltpu.VMEM((UB, DEV_PTS, TB), BF16),
             pltpu.VMEM((LISTERS * BAT_DEV, PTS, BB * TB), BF16),
             pltpu.SemaphoreType.DMA((6,)),
         ],
         compiler_params=pltpu.CompilerParams(vmem_limit_bytes=56 * MIB),
+        cost_estimate=pl.CostEstimate(flops=flops, bytes_accessed=10**4, transcendentals=0),
+    )(codes, counts, blocks, scale, *orbs, *starts)
+
+
+def final_kernel(own_ref, x_ref, y_ref, out_ref):
+    half = TILE_DEV // 2
+    step = half // 2
+    got = jnp.where(pl.program_id(0) < half // step, x_ref[...].astype(F32), y_ref[...].astype(F32))
+    out_ref[...] = (own_ref[...] + got).astype(BF16)
+
+
+def final_tiles(own, got_x, got_y):
+    step = TILE_DEV // 4
+    block = (step, TB, TB)
+    return pl.pallas_call(
+        final_kernel,
+        grid=(4,),
+        in_specs=[
+            pl.BlockSpec(block, lambda t: (t, 0, 0)),
+            pl.BlockSpec(block, lambda t: (jnp.minimum(t, 1), 0, 0)),
+            pl.BlockSpec(block, lambda t: (jnp.maximum(t - 2, 0), 0, 0)),
+        ],
+        out_specs=pl.BlockSpec(block, lambda t: (t, 0, 0)),
+        out_shape=jax.ShapeDtypeStruct((TILE_DEV, TB, TB), BF16),
+        compiler_params=pltpu.CompilerParams(vmem_limit_bytes=16 * MIB),
         cost_estimate=pl.CostEstimate(flops=10**6, bytes_accessed=10**4, transcendentals=0),
-    )(codes, counts, blocks, *orbs, scale, start)
-
-
-def lists_of(owners, slots, me):
-    half = TILE_DEV // 2
-    away = owners ^ me
-    mine = (away == 0) | ((away == X1) & (slots < half)) | ((away == Y1) & (slots >= half))
-    places = jnp.where(away == 0, slots, TILE_DEV + slots)
+    )(own, got_x, got_y)
+
+
+def kept_of(mine, places):
     rows = jnp.arange(R, dtype=jnp.int32)
     codes = places + (rows // UB) * 256 + (rows % UB) * 4096
     before = (rows[:, None] < rows[None, :])[None] & mine[:, :, None]
@@ -464,8 +435,21 @@
     at = jnp.arange(LIST_LEN, dtype=jnp.int32)
     hit = (rank[:, None, :] == at[None, :, None]) & mine[:, None, :]
     listed = jnp.sum(jnp.where(hit, codes[:, None, :], 0), axis=2)
-    listed = jnp.where(at[None] < counts[:, None], listed, PARTS)
-    return listed, (counts + GROUP - 1) // GROUP
+    return listed, counts, at
+
+
+def lists_of(owners, slots, me):
+    half = TILE_DEV // 2
+    away = owners ^ me
+    own = away == 0
+    shared = ((away == X1) & (slots < half)) | ((away == Y1) & (slots >= half))
+    found = []
+    for mine in (own | shared, own, shared):
+        place = jnp.where(own, slots, TILE_DEV + slots) if len(found) == 0 else slots
+        listed, counts, at = kept_of(mine, place)
+        dummy = PARTS if len(found) == 0 else TILE_DEV
+        found.append((jnp.where(at[None] < counts[:, None], listed, dummy), (counts + GROUP - 1) // GROUP))
+    return found
 
 
 def what_is_listed(rows):
@@ -498,10 +482,10 @@
         batch_weights,
     )
     facts = (facts, swap(facts, X3), swap(facts, Y3), swap(facts, X3 ^ Y3))
-    location, sent, *facts = lax.optimization_barrier((atom_places(atom_grid_index), orbitals, *facts))
+    location, sent, *facts = lax.optimization_barrier((atom_places(atom_grid_index), dens_tiles, *facts))
     half = TILE_DEV // 2
-    tile_x, tile_y = swap(dens_tiles, X1), swap(dens_tiles, Y1)
-    orb_x, orb_y = swap(sent, X3), swap(sent, Y3)
+    tile_x, tile_y = swap(sent, X1), swap(sent, Y1)
+    orb_x, orb_y = swap(orbitals, X3), swap(orbitals, Y3)
     tile_low, tile_high = swap(tile_y[:half], X1), swap(tile_x[half:], Y1)
     orb_first, orb_second = swap(orb_y[0], X3), swap(orb_x[1], Y3)
     orbs = (orbitals, orb_x, orb_y, orb_first, orb_second)
@@ -515,7 +499,7 @@
     raw_weight = near_by[:, 1].reshape(LISTERS * BAT_DEV, NEAR)
     away = owners ^ me
     tmap = jnp.where((away & 10) == 0, ((away & 1) + ((away >> 2) & 1) * 2) * TILE_DEV + slots, NO_TILE)
-    codes, counts = lists_of(owners, slots, me)
+    codes, counts = lists_of(owners, slots, me)[0]
 
     wave_vecs = wave_table(KM)
     squared = jnp.sum(wave_vecs * wave_vecs, axis=0)
@@ -541,7 +525,7 @@
     spread, weights, wave_high, wave_low, trig, codes, counts, tmap, blocks = early
     orb_far = swap(late, XY)
 
-    part = density_and_moments(
+    part, orb_diag = density_and_moments(
         tmap,
         blocks,
         (dens_tiles, tile_x, tile_y, tile_low, tile_high),
@@ -551,30 +535,30 @@
         wave_high,
         wave_low,
         trig,
+        facts[:, 4],
     )
     a = ATOM_GRP
     got = swap(part, X3)
-    part = part + jnp.concatenate([got[:a], got[a + 1 : a + 2], got[a : a + 1], got[a + 3 : a + 4], got[a + 2 : a + 3], got[a + 4 :]])
+    order = (a + 1, a, a + 3, a + 2)
+    part = part + jnp.concatenate([got[:a]] + [got[r : r + 1] for r in order] + [jnp.zeros((LISTERS, KM), F32)])
     got = swap(part, Y3)
     density = part[a] + got[a + 2]
     moments, orb_far = lax.optimization_barrier((part[:a] + got[:a], orb_far))
     orb_far_x, orb_far_y = swap(orb_far, X3), swap(orb_far, Y3)
-    got = swap(jnp.concatenate([moments, facts[:, 4]]), X1)
+    got = swap(jnp.concatenate([moments, part[a + LISTERS :]]), X1)
     moments = moments + got[:a]
     got = swap(jnp.concatenate([moments, got[a:]]), Y1)
-    late_diag, moments = lax.optimization_barrier((jnp.stack([orb_first, orb_second]), moments + got[:a]))
-    orbs_far = (orb_far, orb_far_x, orb_far_y, swap(late_diag, XY))
+    orb_diag, moments = lax.optimization_barrier((orb_diag, moments + got[:a]))
+    orbs_far = (orb_far, orb_far_x, orb_far_y, swap(orb_diag, XY))
     far_owners, far_slots, far_blocks = what_is_listed(got[a:])
-    far_codes, far_counts = lists_of(far_owners, far_slots, me)
+    unused, (own_codes, own_counts), (far_codes, far_counts) = lists_of(far_owners, far_slots, me)
     structure = jnp.sum(moments[:, :1] * trig, axis=0, keepdims=True)
     for bits in (1, 2, 4, 8):
         structure = structure + swap_grp(structure, bits)
-
-    potential, scale, ham = potential_and_ham(
-        codes,
-        counts,
-        blocks,
-        orbs,
+    structure, own_codes, own_counts, far_codes, far_counts, far_blocks = lax.optimization_barrier(
+        (structure, own_codes, own_counts, far_codes, far_counts, far_blocks)
+    )
+    potential, scale = potential_of(
         moments,
         far_gain * structure,
         near_gain,
@@ -584,12 +568,18 @@
         wave_high,
         wave_low,
     )
-    own, part_x, part_y = rest_of_ham(
-        far_codes, far_counts, far_blocks, orbs_far, swap(scale, XY), ham
-    )
-    low = own[:half] + swap(part_x, X1).astype(F32)
-    high = own[half:] + swap(part_y, Y1).astype(F32)
-    return (density, potential.reshape(-1), jnp.concatenate([low, high], axis=0).astype(BF16))
+    far_scale = swap(scale, XY)
+    own, shared = ham_terms(
+        codes, counts, blocks, scale, orbs, (), ((TILE_DEV, F32), (TILE_DEV, F32)), 2 * 10**10
+    )
+    half = TILE_DEV // 2
+    part_x, part_y = ham_terms(
+        far_codes, far_counts, far_blocks, far_scale, orbs_far, (shared,), ((half, BF16), (half, BF16)), 10**6
+    )
+    (own,) = ham_terms(
+        own_codes, own_counts, far_blocks, far_scale, orbs_far, (own,), ((TILE_DEV, F32),), 2 * 10**10
+    )
+    return (density, potential.reshape(-1), final_tiles(own, swap(part_x, X1), swap(part_y, Y1)))
 
 
 def solution(mesh):

time: 152 us -> 167 us (1.099)
  waiting for transfers between devices: 37.4 us -> 49.6 us
  Pallas kernels: 44.2 us -> 52.6 us
  starting transfers between devices: 47.1 us -> 42.3 us
  local copies, waits for them, and re-layouts: 6.47 us -> 9.04 us
  other arithmetic: 13.5 us -> 11.4 us
    ppermute x22, waiting for transfers between devices: 33.6 us -> 47.7 us  [swap(): return lax.ppermute(array, 'dev', [(d, d ^ bits) for d in range(16)])]
    pallas_call x2 -> x5, Pallas kernels: 23.9 us -> 32.2 us  [the longest x3 29.3 us: ham_terms(): pl.pallas_call(functools.partial(ham_kernel, len(starts), len(outs)), in_...]
    ppermute x22, starting transfers between devices: 34.9 us -> 30.2 us  [swap(): return lax.ppermute(array, 'dev', [(d, d ^ bits) for d in range(16)])]
    another operation x2 -> x0, other arithmetic: 3.18 us -> none
    unnamed x38 -> x44, local copies, waits for them, and re-layouts: 2.61 us -> 5.01 us
    ppermute x4, waiting for transfers between devices: 3.83 us -> 1.97 us  [swap_grp(): return lax.ppermute(array, 'grp', [(g, g ^ bits) for g in range(16)])]
    select_n x4 -> x6, other arithmetic: 2.41 us -> 3.7 us  [the longest x3 2.01 us: lists_of(): jnp.where(at[None] < counts[:, None], listed, dummy)]
  transfers between devices with their start and end apart: 26 -> 26, of which waited for: 15 -> 15; matrix products, arithmetic and copies ran while one was open for 11% -> 9% of each run, Pallas kernels for 21% -> 25%
where the time goes in v3:
time: 167 us; the launch traced here: 166 us
  Pallas kernels  52.6 us (31%)
  waiting for transfers between devices  49.6 us (30%)
  starting transfers between devices  42.3 us (25%)
  other arithmetic  11.4 us (7%)
  local copies, waits for them, and re-layouts  9.04 us (5%)
    ppermute x22, waiting for transfers between devices, swap(): return lax.ppermute(array, 'dev', [(d, d ^ bits) for d in range(16)])  47.7 us
    ppermute x22, starting transfers between devices, swap(): return lax.ppermute(array, 'dev', [(d, d ^ bits) for d in range(16)])  30.2 us
    pallas_call x3, Pallas kernels, ham_terms(): pl.pallas_call(functools.partial(ham_kernel, len(starts), len(outs)), in_...  29.3 us
    ppermute x4, starting transfers between devices, swap_grp(): return lax.ppermute(array, 'grp', [(g, g ^ bits) for g in range(16)])  12.2 us
    pallas_call x1, Pallas kernels, density_and_moments(): pl.pallas_call(density_kernel, in_specs=[SMEM_SPEC] * 2 + [ANY_SPEC] * 10...  12 us
    pallas_call x1, Pallas kernels, wave_of_points(): pl.pallas_call(wave_kernel, grid=(points // chunk,), in_specs=[pl.BlockSp...  5.74 us
    unnamed x44, local copies, waits for them, and re-layouts  5.01 us
  transfers between devices with their start and end apart: 26, of which 15 were waited for; matrix products, arithmetic and copies ran while one was open for 9% of the time, Pallas kernels for 25%

profile of v3, /device:TPU:2, one launch (start us, length us, event | category | flops | bytes accessed | tf_op | source)
XLA Modules:
  0.0 166.4 jit_solution(7961693456275467552)
XLA Ops:
  0.6 1.4 shard_map.122
  2.1 1.6 collective-permute-start
  3.7 3.0 %collective-permute-start.1 = (f32[6,512]{1,0:T(8,128)}, f32[6,512]{1,0:T(8,128)S(1)}, u32[]{:S(2)}, u32[]{:S(2)}) collective-permute-start(f32[6,512]{1,0:T(8,128)} %shard_map.122), channel_id=1, source_target_pairs={{0,12},{1,13},{2,14},{3,15},{4,8},{5,9},{6,10},{7,11},{8,4},{9,5},... | collective-permute-start | bytes 36872 | tf_op jit(solution)/shard_map/ppermute | solution.py:39
  6.9 1.5 collective-permute-start.9
  8.4 3.0 %collective-permute-start.7 = (bf16[2,256,1024]{2,1,0:T(8,128)(2,1)}, bf16[2,256,1024]{2,1,0:T(8,128)(2,1)S(1)}, u32[]{:S(2)}, u32[]{:S(2)}) collective-permute-start(bf16[2,256,1024]{2,1,0:T(8,128)(2,1)} %refs_0_.1), channel_id=1, source_target_pairs={{0,12},{1,13},{2,14},{3,15},{4,8},{5,9},{6,10},{7,11},{8,4},{9,5},... | collective-permute-start | bytes 3145736 | tf_op jit(solution)/shard_map/ppermute | solution.py:39
  11.4 1.3 shard_map.121
  13.9 3.1 %collective-permute-start.5 = (bf16[32,128,128]{2,1,0:T(8,128)(2,1)}, bf16[32,128,128]{2,1,0:T(8,128)(2,1)}, u32[]{:S(2)}, u32[]{:S(2)}) collective-permute-start(bf16[32,128,128]{2,1,0:T(8,128)(2,1)} %own_tile.1), channel_id=1, source_target_pairs={{0,1},{1,0},{2,3},{3,2},{4,5},{5,4},{6,7},{7,6},{8,9},{9,8},{10,11... | collective-permute-start | bytes 3145736 | tf_op jit(solution)/shard_map/ppermute | solution.py:39
  18.6 0.8 pad_maximum_fusion
  19.4 0.8 multiply_reduce_fusion
  22.1 5.7 %shard_map.123 = (bf16[512,2048]{1,0:T(8,128)(2,1)}, bf16[512,2048]{1,0:T(8,128)(2,1)}) custom-call(f32[48,2048]{1,0:T(8,128)} %bitcast.49), custom_call_target="tpu_custom_call" | custom-call | flops 8388608 | bytes 4194304 | tf_op jit(solution)/shard_map/pallas_call | solution.py:87
  29.6 1.8 %collective-permute-done.9.x_orb.refs_1_ = bf16[2,256,1024]{2,1,0:T(8,128)(2,1)S(1)} collective-permute-done((bf16[2,256,1024]{2,1,0:T(8,128)(2,1)}, bf16[2,256,1024]{2,1,0:T(8,128)(2,1)S(1)}, u32[]{:S(2)}, u32[]{:S(2)}) %collective-permute-start.9) | collective-permute-done | bytes 1048608 | tf_op jit(solution)/shard_map/ppermute | solution.py:39
  31.5 3.0 %collective-permute-start.10 = (bf16[256,1024]{1,0:T(8,128)(2,1)S(1)}, bf16[256,1024]{1,0:T(8,128)(2,1)S(1)}, u32[]{:S(2)}, u32[]{:S(2)}) collective-permute-start(bf16[256,1024]{1,0:T(8,128)(2,1)S(1)} %slice_bitcast_fusion), channel_id=1, source_target_pairs={{0,12},{1,13},{2,14},{3,15},{4,8},{5,9},{6,10},{7,11},{8,4},{9,5},... | collective-permute-start | bytes 1572872 | tf_op jit(solution)/shard_map/ppermute | solution.py:39
  34.5 1.6 collective-permute-start.8
  36.1 1.3 collective-permute-done.3.y_tile
  37.4 3.1 %collective-permute-start.4 = (bf16[16,128,128]{2,1,0:T(8,128)(2,1)S(1)}, bf16[16,128,128]{2,1,0:T(8,128)(2,1)S(1)}, u32[]{:S(2)}, u32[]{:S(2)}) collective-permute-start(bf16[16,128,128]{2,1,0:T(8,128)(2,1)S(1)} %slice.142), channel_id=1, source_target_pairs={{0,1},{1,0},{2,3},{3,2},{4,5},{5,4},{6,7},{7,6},{8,9},{9,8},{10,11... | collective-permute-start | bytes 1572872 | tf_op jit(solution)/shard_map/ppermute | solution.py:39
  40.6 1.1 slice.143
  41.6 1.1 collective-permute-start.6
  44.1 1.0 collective-permute-done.10.second_orb.refs_4_
  45.1 1.4 collective-permute-done.8.first_orb.refs_3_
  46.5 3.5 %collective-permute-done.4.low_tile = bf16[16,128,128]{2,1,0:T(8,128)(2,1)S(1)} collective-permute-done((bf16[16,128,128]{2,1,0:T(8,128)(2,1)S(1)}, bf16[16,128,128]{2,1,0:T(8,128)(2,1)S(1)}, u32[]{:S(2)}, u32[]{:S(2)}) %collective-permute-start.4) | collective-permute-done | bytes 524320 | tf_op jit(solution)/shard_map/ppermute | solution.py:39
  50.0 13.9 %collective-permute-done.6.high_tile = bf16[16,128,128]{2,1,0:T(8,128)(2,1)S(1)} collective-permute-done((bf16[16,128,128]{2,1,0:T(8,128)(2,1)S(1)}, bf16[16,128,128]{2,1,0:T(8,128)(2,1)S(1)}, u32[]{:S(2)}, u32[]{:S(2)}) %collective-permute-start.6) | collective-permute-done | bytes 524320 | tf_op jit(solution)/shard_map/ppermute | solution.py:39
  64.0 0.7 copy-done.13
  64.7 12.0 %shard_map.124 = (f32[24,512]{1,0:T(8,128)}, bf16[2,256,1024]{2,1,0:T(8,128)(2,1)}) custom-call(s32[4,81]{1,0:T(4,128)} %get-tuple-element.47.tmap_ref, s32[8,8]{1,0:T(8,128)} %bitcast.55, bf16[32,128,128]{2,1,0:T(8,128)(2,1)} %own_tile.1, bf16[32,128,128]{2,1,0:T(8,128)(2,1)} %collective-permute-done.5.x_tile, bf16[32,128,128]{2,1,0:T(8,128)(2,1)} %copy-done.8, ...), custom_call_target="tpu_custom_call" | custom-call | flops 1000000 | bytes 10000 | tf_op jit(solution)/shard_map/pallas_call | solution.py:217
  76.8 4.9 %collective-permute-done.11 = f32[24,512]{1,0:T(8,128)S(1)} collective-permute-done((f32[24,512]{1,0:T(8,128)}, f32[24,512]{1,0:T(8,128)S(1)}, u32[]{:S(2)}, u32[]{:S(2)}) %collective-permute-start.11) | collective-permute-done | bytes 49184 | tf_op jit(solution)/shard_map/ppermute | solution.py:39
  81.8 0.8 add.176
  82.6 5.9 %collective-permute-done.12 = f32[24,512]{1,0:T(8,128)S(1)} collective-permute-done((f32[24,512]{1,0:T(8,128)S(1)}, f32[24,512]{1,0:T(8,128)S(1)}, u32[]{:S(2)}, u32[]{:S(2)}) %collective-permute-start.12) | collective-permute-done | bytes 49184 | tf_op jit(solution)/shard_map/ppermute | solution.py:39
  88.5 1.7 %collective-permute-start.14 = (f32[20,512]{1,0:T(8,128)S(1)}, f32[20,512]{1,0:T(8,128)S(1)}, u32[]{:S(2)}, u32[]{:S(2)}) collective-permute-start(f32[20,512]{1,0:T(8,128)S(1)} %pad_maximum_fusion.2), channel_id=1, source_target_pairs={{0,1},{1,0},{2,3},{3,2},{4,5},{5,4},{6,7},{7,6},{8,9},{9,8},{10,11... | collective-permute-start | bytes 122888 | tf_op jit(solution)/shard_map/ppermute | solution.py:39
  90.2 2.5 %collective-permute-done.14 = f32[20,512]{1,0:T(8,128)S(1)} collective-permute-done((f32[20,512]{1,0:T(8,128)S(1)}, f32[20,512]{1,0:T(8,128)S(1)}, u32[]{:S(2)}, u32[]{:S(2)}) %collective-permute-start.14) | collective-permute-done | bytes 40992 | tf_op jit(solution)/shard_map/ppermute | solution.py:39
  92.7 0.8 collective-permute-start.15
  94.7 2.2 %collective-permute-done.15 = f32[20,512]{1,0:T(8,128)S(1)} collective-permute-done((f32[20,512]{1,0:T(8,128)S(1)}, f32[20,512]{1,0:T(8,128)S(1)}, u32[]{:S(2)}, u32[]{:S(2)}) %collective-permute-start.15) | collective-permute-done | bytes 40992 | tf_op jit(solution)/shard_map/ppermute | solution.py:39
  98.7 2.0 %collective-permute-start.17 = (f32[1,512]{1,0:T(1,128)S(1)}, f32[1,512]{1,0:T(1,128)S(1)}, u32[]{:S(2)}, u32[]{:S(2)}) collective-permute-start(f32[1,512]{1,0:T(1,128)S(1)} %add.183), channel_id=1, source_target_pairs={{0,32},{16,48},{32,0},{48,16},{64,96},{80,112},{96,64},{112,80},{1... | collective-permute-start | bytes 6152 | tf_op jit(solution)/shard_map/ppermute | solution.py:43
  101.4 1.0 collective-permute-done.17
  102.4 3.3 %collective-permute-start.18 = (f32[1,512]{1,0:T(1,128)S(1)}, f32[1,512]{1,0:T(1,128)S(1)}, u32[]{:S(2)}, u32[]{:S(2)}) collective-permute-start(f32[1,512]{1,0:T(1,128)S(1)} %add.184), channel_id=1, source_target_pairs={{0,64},{16,80},{32,96},{48,112},{64,0},{80,16},{96,32},{112,48},{1... | collective-permute-start | bytes 6152 | tf_op jit(solution)/shard_map/ppermute | solution.py:43
  106.3 1.0 collective-permute-done.18
  107.2 6.8 %collective-permute-start.19 = (f32[1,512]{1,0:T(1,128)S(1)}, f32[1,512]{1,0:T(1,128)S(1)}, u32[]{:S(2)}, u32[]{:S(2)}) collective-permute-start(f32[1,512]{1,0:T(1,128)S(1)} %add.185), channel_id=1, source_target_pairs={{0,128},{16,144},{32,160},{48,176},{64,192},{80,208},{96,224},{112... | collective-permute-start | bytes 6152 | tf_op jit(solution)/shard_map/ppermute | solution.py:43
  115.2 2.1 %collective-permute-start.23 = (bf16[2,256,1024]{2,1,0:T(8,128)(2,1)}, bf16[2,256,1024]{2,1,0:T(8,128)(2,1)S(1)}, u32[]{:S(2)}, u32[]{:S(2)}) collective-permute-start(bf16[2,256,1024]{2,1,0:T(8,128)(2,1)} %get-tuple-element.66), channel_id=1, source_target_pairs={{0,5},{1,4},{2,7},{3,6},{4,1},{5,0},{6,3},{7,2},{8,13},{9,12},{10,... | collective-permute-start | bytes 3145736 | tf_op jit(solution)/shard_map/ppermute | solution.py:39
  117.4 1.6 copy-done.1
  119.0 1.2 shard_map.125
  120.2 0.8 collective-permute-start.20
  121.0 11.2 %shard_map.126 = (f32[32,128,128]{2,1,0:T(8,128)}, f32[32,128,128]{2,1,0:T(8,128)}) custom-call(s32[4,32]{1,0:T(4,128)} %fusion.8.codes_ref, s32[4]{0:T(128)} %and_select_fusion.6.counts_ref, s32[8,8]{1,0:T(8,128)} %bitcast.56, f32[1,2048]{1,0:T(1,128)} %copy-done.5, bf16[2,256,1024]{2,1,0:T(8,128)(2,1)} %refs_0_.1, bf16[2,256,1024]{2,1,0:T(8,128)(2,1)} %copy-done.6, ...), custom_call_target="tpu_custom_call" | custom-call | flops 20000000000 | bytes 10000 | tf_op jit(solution)/shard_map/pallas_call | solution.py:387
  132.2 8.1 %collective-permute-done.20.scale_ref = f32[1,2048]{1,0:T(1,128)S(1)} collective-permute-done((f32[1,2048]{1,0:T(1,128)S(1)}, f32[1,2048]{1,0:T(1,128)S(1)}, u32[]{:S(2)}, u32[]{:S(2)}) %collective-permute-start.20) | collective-permute-done | bytes 8224 | tf_op jit(solution)/shard_map/ppermute | solution.py:39
  141.3 8.3 %shard_map.128 = (bf16[16,128,128]{2,1,0:T(8,128)(2,1)}, bf16[16,128,128]{2,1,0:T(8,128)(2,1)}) custom-call(s32[4,32]{1,0:T(4,128)} %fusion.10.codes_ref, s32[4]{0:T(128)} %and_select_fusion.4.counts_ref, s32[8,8]{1,0:T(8,128)} %bitcast.59, f32[1,2048]{1,0:T(1,128)} %copy-done.16, bf16[2,256,1024]{2,1,0:T(8,128)(2,1)} %collective-permute-done.13.refs_0_, ...), custom_call_target="tpu_custom_call" | custom-call | flops 1000000 | bytes 10000 | tf_op jit(solution)/shard_map/pallas_call | solution.py:387
  149.6 1.1 collective-permute-start.24
  150.7 1.7 %collective-permute-start.25 = (bf16[16,128,128]{2,1,0:T(8,128)(2,1)}, bf16[16,128,128]{2,1,0:T(8,128)(2,1)S(1)}, u32[]{:S(2)}, u32[]{:S(2)}) collective-permute-start(bf16[16,128,128]{2,1,0:T(8,128)(2,1)} %get-tuple-element.74), channel_id=1, source_target_pairs={{0,4},{1,5},{2,6},{3,7},{4,0},{5,1},{6,2},{7,3},{8,12},{9,13},{10,... | collective-permute-start | bytes 1572872 | tf_op jit(solution)/shard_map/ppermute | solution.py:39
  152.4 9.8 %shard_map.127.own_ref = f32[32,128,128]{2,1,0:T(8,128)} custom-call(s32[4,32]{1,0:T(4,128)} %fusion.9.codes_ref, s32[4]{0:T(128)} %and_select_fusion.5.counts_ref, s32[8,8]{1,0:T(8,128)} %bitcast.60, f32[1,2048]{1,0:T(1,128)} %copy-done.16, bf16[2,256,1024]{2,1,0:T(8,128)(2,1)} %collective-permute-done.13.refs_0_, ...), custom_call_target="tpu_custom_call" | custom-call | flops 20000000000 | bytes 10000 | tf_op jit(solution)/shard_map/pallas_call | solution.py:387
  162.2 0.9 collective-permute-done.25.y_ref
  163.1 1.6 copy-done.2
  164.7 1.7 shard_map.129
  (131 shorter events, 14.7 us)
Async XLA Ops:
  2.1 10.6 %collective-permute-start = (f32[6,512]{1,0:T(8,128)}, f32[6,512]{1,0:T(8,128)S(1)}, u32[]{:S(2)}, u32[]{:S(2)}) collective-permute-start(f32[6,512]{1,0:T(8,128)} %shard_map.122), channel_id=1, source_target_pairs={{0,3},{1,2},{2,1},{3,0},{4,7},{5,6},{6,5},{7,4},{8,11},{9,10},{10,... | collective-permute-start | bytes 36872 | tf_op jit(solution)/shard_map/ppermute | solution.py:39
  3.7 9.1 %collective-permute-start.1 = (f32[6,512]{1,0:T(8,128)}, f32[6,512]{1,0:T(8,128)S(1)}, u32[]{:S(2)}, u32[]{:S(2)}) collective-permute-start(f32[6,512]{1,0:T(8,128)} %shard_map.122), channel_id=1, source_target_pairs={{0,12},{1,13},{2,14},{3,15},{4,8},{5,9},{6,10},{7,11},{8,4},{9,5},... | collective-permute-start | bytes 36872 | tf_op jit(solution)/shard_map/ppermute | solution.py:39
  6.7 6.3 %collective-permute-start.2 = (f32[6,512]{1,0:T(8,128)}, f32[6,512]{1,0:T(8,128)S(1)}, u32[]{:S(2)}, u32[]{:S(2)}) collective-permute-start(f32[6,512]{1,0:T(8,128)} %shard_map.122), channel_id=1, source_target_pairs={{0,15},{1,14},{2,13},{3,12},{4,11},{5,10},{6,9},{7,8},{8,7},{9,6},... | collective-permute-start | bytes 36872 | tf_op jit(solution)/shard_map/ppermute | solution.py:39
  6.9 24.5 %collective-permute-start.9 = (bf16[2,256,1024]{2,1,0:T(8,128)(2,1)}, bf16[2,256,1024]{2,1,0:T(8,128)(2,1)S(1)}, u32[]{:S(2)}, u32[]{:S(2)}) collective-permute-start(bf16[2,256,1024]{2,1,0:T(8,128)(2,1)} %refs_0_.1), channel_id=1, source_target_pairs={{0,3},{1,2},{2,1},{3,0},{4,7},{5,6},{6,5},{7,4},{8,11},{9,10},{10,... | collective-permute-start | bytes 3145736 | tf_op jit(solution)/shard_map/ppermute | solution.py:39
  8.4 26.1 %collective-permute-start.7 = (bf16[2,256,1024]{2,1,0:T(8,128)(2,1)}, bf16[2,256,1024]{2,1,0:T(8,128)(2,1)S(1)}, u32[]{:S(2)}, u32[]{:S(2)}) collective-permute-start(bf16[2,256,1024]{2,1,0:T(8,128)(2,1)} %refs_0_.1), channel_id=1, source_target_pairs={{0,12},{1,13},{2,14},{3,15},{4,8},{5,9},{6,10},{7,11},{8,4},{9,5},... | collective-permute-start | bytes 3145736 | tf_op jit(solution)/shard_map/ppermute | solution.py:39
  11.4 1.6 copy-start.15
  12.7 16.6 %copy-start.17 = (f32[3,16]{1,0:T(4,128)S(1)}, f32[3,16]{1,0:T(4,128)}, u32[]{:S(2)}) copy-start(f32[3,16]{1,0:T(4,128)} %shard_map.121) | copy-start | bytes 580
  13.8 23.6 %collective-permute-start.3 = (bf16[32,128,128]{2,1,0:T(8,128)(2,1)}, bf16[32,128,128]{2,1,0:T(8,128)(2,1)S(1)}, u32[]{:S(2)}, u32[]{:S(2)}) collective-permute-start(bf16[32,128,128]{2,1,0:T(8,128)(2,1)} %own_tile.1), channel_id=1, source_target_pairs={{0,4},{1,5},{2,6},{3,7},{4,0},{5,1},{6,2},{7,3},{8,12},{9,13},{10,... | collective-permute-start | bytes 3145736 | tf_op jit(solution)/shard_map/ppermute | solution.py:39
  13.9 26.6 %collective-permute-start.5 = (bf16[32,128,128]{2,1,0:T(8,128)(2,1)}, bf16[32,128,128]{2,1,0:T(8,128)(2,1)}, u32[]{:S(2)}, u32[]{:S(2)}) collective-permute-start(bf16[32,128,128]{2,1,0:T(8,128)(2,1)} %own_tile.1), channel_id=1, source_target_pairs={{0,1},{1,0},{2,3},{3,2},{4,5},{5,4},{6,7},{7,6},{8,9},{9,8},{10,11... | collective-permute-start | bytes 3145736 | tf_op jit(solution)/shard_map/ppermute | solution.py:39
  31.4 10.2 %copy-start.6 = (bf16[2,256,1024]{2,1,0:T(8,128)(2,1)}, bf16[2,256,1024]{2,1,0:T(8,128)(2,1)S(1)}, u32[]{:S(2)}) copy-start(bf16[2,256,1024]{2,1,0:T(8,128)(2,1)S(1)} %collective-permute-done.9.x_orb.refs_1_) | copy-start | bytes 3145732
  31.5 13.6 %collective-permute-start.10 = (bf16[256,1024]{1,0:T(8,128)(2,1)S(1)}, bf16[256,1024]{1,0:T(8,128)(2,1)S(1)}, u32[]{:S(2)}, u32[]{:S(2)}) collective-permute-start(bf16[256,1024]{1,0:T(8,128)(2,1)S(1)} %slice_bitcast_fusion), channel_id=1, source_target_pairs={{0,12},{1,13},{2,14},{3,15},{4,8},{5,9},{6,10},{7,11},{8,4},{9,5},... | collective-permute-start | bytes 1572872 | tf_op jit(solution)/shard_map/ppermute | solution.py:39
  34.5 29.5 %copy-start.7 = (bf16[2,256,1024]{2,1,0:T(8,128)(2,1)}, bf16[2,256,1024]{2,1,0:T(8,128)(2,1)S(1)}, u32[]{:S(2)}) copy-start(bf16[2,256,1024]{2,1,0:T(8,128)(2,1)S(1)} %collective-permute-done.7.y_orb.refs_2_) | copy-start | bytes 3145732
  34.5 12.0 %collective-permute-start.8 = (bf16[256,1024]{1,0:T(8,128)(2,1)S(1)}, bf16[256,1024]{1,0:T(8,128)(2,1)S(1)}, u32[]{:S(2)}, u32[]{:S(2)}) collective-permute-start(bf16[256,1024]{1,0:T(8,128)(2,1)S(1)} %slice_bitcast_fusion.1), channel_id=1, source_target_pairs={{0,3},{1,2},{2,1},{3,0},{4,7},{5,6},{6,5},{7,4},{8,11},{9,10},{10,... | collective-permute-start | bytes 1572872 | tf_op jit(solution)/shard_map/ppermute | solution.py:39
  37.4 26.5 %copy-start.8 = (bf16[32,128,128]{2,1,0:T(8,128)(2,1)}, bf16[32,128,128]{2,1,0:T(8,128)(2,1)S(1)}, u32[]{:S(2)}) copy-start(bf16[32,128,128]{2,1,0:T(8,128)(2,1)S(1)} %collective-permute-done.3.y_tile) | copy-start | bytes 3145732
  37.4 12.6 %collective-permute-start.4 = (bf16[16,128,128]{2,1,0:T(8,128)(2,1)S(1)}, bf16[16,128,128]{2,1,0:T(8,128)(2,1)S(1)}, u32[]{:S(2)}, u32[]{:S(2)}) collective-permute-start(bf16[16,128,128]{2,1,0:T(8,128)(2,1)S(1)} %slice.142), channel_id=1, source_target_pairs={{0,1},{1,0},{2,3},{3,2},{4,5},{5,4},{6,7},{7,6},{8,9},{9,8},{10,11... | collective-permute-start | bytes 1572872 | tf_op jit(solution)/shard_map/ppermute | solution.py:39
  41.6 22.3 %collective-permute-start.6 = (bf16[16,128,128]{2,1,0:T(8,128)(2,1)S(1)}, bf16[16,128,128]{2,1,0:T(8,128)(2,1)S(1)}, u32[]{:S(2)}, u32[]{:S(2)}) collective-permute-start(bf16[16,128,128]{2,1,0:T(8,128)(2,1)S(1)} %slice.143), channel_id=1, source_target_pairs={{0,4},{1,5},{2,6},{3,7},{4,0},{5,1},{6,2},{7,3},{8,12},{9,13},{10,... | collective-permute-start | bytes 1572872 | tf_op jit(solution)/shard_map/ppermute | solution.py:39
  45.1 18.9 %copy-start.10 = (bf16[256,1024]{1,0:T(8,128)(2,1)}, bf16[256,1024]{1,0:T(8,128)(2,1)S(1)}, u32[]{:S(2)}) copy-start(bf16[256,1024]{1,0:T(8,128)(2,1)S(1)} %collective-permute-done.10.second_orb.refs_4_) | copy-start | bytes 1572868
  46.5 17.5 %copy-start.11 = (bf16[256,1024]{1,0:T(8,128)(2,1)}, bf16[256,1024]{1,0:T(8,128)(2,1)S(1)}, u32[]{:S(2)}) copy-start(bf16[256,1024]{1,0:T(8,128)(2,1)S(1)} %collective-permute-done.8.first_orb.refs_3_) | copy-start | bytes 1572868
  50.0 13.9 %copy-start.12 = (bf16[16,128,128]{2,1,0:T(8,128)(2,1)}, bf16[16,128,128]{2,1,0:T(8,128)(2,1)S(1)}, u32[]{:S(2)}) copy-start(bf16[16,128,128]{2,1,0:T(8,128)(2,1)S(1)} %collective-permute-done.4.low_tile) | copy-start | bytes 1572868
  63.9 0.8 copy-start.13
  63.9 24.6 %collective-permute-start.13 = (bf16[2,256,1024]{2,1,0:T(8,128)(2,1)}, bf16[2,256,1024]{2,1,0:T(8,128)(2,1)}, u32[]{:S(2)}, u32[]{:S(2)}) collective-permute-start(bf16[2,256,1024]{2,1,0:T(8,128)(2,1)} %refs_0_.1), channel_id=1, source_target_pairs={{0,5},{1,4},{2,7},{3,6},{4,1},{5,0},{6,3},{7,2},{8,13},{9,12},{10,... | collective-permute-start | bytes 3145736 | tf_op jit(solution)/shard_map/ppermute | solution.py:39
  64.7 25.5 %copy-start.14 = (f32[8,256]{1,0:T(8,128)S(1)}, f32[8,256]{1,0:T(8,128)}, u32[]{:S(2)}) copy-start(f32[8,256]{1,0:T(8,128)} %reshape_squeeze.12.weights_ref) | copy-start | bytes 24580
  64.7 32.7 %copy-start.4 = (f32[16,512]{1,0:T(8,128)S(1)}, f32[16,512]{1,0:T(8,128)}, u32[]{:S(2)}) copy-start(f32[16,512]{1,0:T(8,128)} %pad_maximum_fusion.4.trig_ref) | copy-start | bytes 98308
  64.7 52.7 %copy-start = (bf16[512,2048]{1,0:T(8,128)(2,1)S(1)}, bf16[512,2048]{1,0:T(8,128)(2,1)}, u32[]{:S(2)}) copy-start(bf16[512,2048]{1,0:T(8,128)(2,1)} %get-tuple-element.51.high_hbm.high_ref) | copy-start | bytes 6291460
  64.7 52.7 %copy-start.3 = (f32[16,2048]{1,0:T(8,128)S(1)}, f32[16,2048]{1,0:T(8,128)}, u32[]{:S(2)}) copy-start(f32[16,2048]{1,0:T(8,128)} %exponential_multiply_fusion.spread_ref) | copy-start | bytes 393220
  76.7 5.0 %collective-permute-start.11 = (f32[24,512]{1,0:T(8,128)}, f32[24,512]{1,0:T(8,128)S(1)}, u32[]{:S(2)}, u32[]{:S(2)}) collective-permute-start(f32[24,512]{1,0:T(8,128)} %get-tuple-element.54), channel_id=1, source_target_pairs={{0,3},{1,2},{2,1},{3,0},{4,7},{5,6},{6,5},{7,4},{8,11},{9,10},{10,... | collective-permute-start | bytes 147464 | tf_op jit(solution)/shard_map/ppermute | solution.py:39
  82.6 5.9 %collective-permute-start.12 = (f32[24,512]{1,0:T(8,128)S(1)}, f32[24,512]{1,0:T(8,128)S(1)}, u32[]{:S(2)}, u32[]{:S(2)}) collective-permute-start(f32[24,512]{1,0:T(8,128)S(1)} %add.176), channel_id=1, source_target_pairs={{0,12},{1,13},{2,14},{3,15},{4,8},{5,9},{6,10},{7,11},{8,4},{9,5},... | collective-permute-start | bytes 147464 | tf_op jit(solution)/shard_map/ppermute | solution.py:39
  88.5 4.2 %collective-permute-start.14 = (f32[20,512]{1,0:T(8,128)S(1)}, f32[20,512]{1,0:T(8,128)S(1)}, u32[]{:S(2)}, u32[]{:S(2)}) collective-permute-start(f32[20,512]{1,0:T(8,128)S(1)} %pad_maximum_fusion.2), channel_id=1, source_target_pairs={{0,1},{1,0},{2,3},{3,2},{4,5},{5,4},{6,7},{7,6},{8,9},{9,8},{10,11... | collective-permute-start | bytes 122888 | tf_op jit(solution)/shard_map/ppermute | solution.py:39
  92.7 4.2 %collective-permute-start.15 = (f32[20,512]{1,0:T(8,128)S(1)}, f32[20,512]{1,0:T(8,128)S(1)}, u32[]{:S(2)}, u32[]{:S(2)}) collective-permute-start(f32[20,512]{1,0:T(8,128)S(1)} %pad_maximum_fusion.3), channel_id=1, source_target_pairs={{0,4},{1,5},{2,6},{3,7},{4,0},{5,1},{6,2},{7,3},{8,12},{9,13},{10,... | collective-permute-start | bytes 122888 | tf_op jit(solution)/shard_map/ppermute | solution.py:39
  94.1 46.3 %collective-permute-start.21 = (bf16[2,256,1024]{2,1,0:T(8,128)(2,1)}, bf16[2,256,1024]{2,1,0:T(8,128)(2,1)}, u32[]{:S(2)}, u32[]{:S(2)}) collective-permute-start(bf16[2,256,1024]{2,1,0:T(8,128)(2,1)} %collective-permute-done.13.refs_0_), channel_id=1, source_target_pairs={{0,3},{1,2},{2,1},{3,0},{4,7},{5,6},{6,5},{7,4},{8,11},{9,10},{10,... | collective-permute-start | bytes 3145736 | tf_op jit(solution)/shard_map/ppermute | solution.py:39
  94.1 46.3 %collective-permute-start.22 = (bf16[2,256,1024]{2,1,0:T(8,128)(2,1)}, bf16[2,256,1024]{2,1,0:T(8,128)(2,1)}, u32[]{:S(2)}, u32[]{:S(2)}) collective-permute-start(bf16[2,256,1024]{2,1,0:T(8,128)(2,1)} %collective-permute-done.13.refs_0_), channel_id=1, source_target_pairs={{0,12},{1,13},{2,14},{3,15},{4,8},{5,9},{6,10},{7,11},{8,4},{9,5},... | collective-permute-start | bytes 3145736 | tf_op jit(solution)/shard_map/ppermute | solution.py:39
  97.5 1.2 collective-permute-start.16
  98.7 3.7 %collective-permute-start.17 = (f32[1,512]{1,0:T(1,128)S(1)}, f32[1,512]{1,0:T(1,128)S(1)}, u32[]{:S(2)}, u32[]{:S(2)}) collective-permute-start(f32[1,512]{1,0:T(1,128)S(1)} %add.183), channel_id=1, source_target_pairs={{0,32},{16,48},{32,0},{48,16},{64,96},{80,112},{96,64},{112,80},{1... | collective-permute-start | bytes 6152 | tf_op jit(solution)/shard_map/ppermute | solution.py:43
  102.4 4.8 %collective-permute-start.18 = (f32[1,512]{1,0:T(1,128)S(1)}, f32[1,512]{1,0:T(1,128)S(1)}, u32[]{:S(2)}, u32[]{:S(2)}) collective-permute-start(f32[1,512]{1,0:T(1,128)S(1)} %add.184), channel_id=1, source_target_pairs={{0,64},{16,80},{32,96},{48,112},{64,0},{80,16},{96,32},{112,48},{1... | collective-permute-start | bytes 6152 | tf_op jit(solution)/shard_map/ppermute | solution.py:43
  107.2 10.1 %collective-permute-start.19 = (f32[1,512]{1,0:T(1,128)S(1)}, f32[1,512]{1,0:T(1,128)S(1)}, u32[]{:S(2)}, u32[]{:S(2)}) collective-permute-start(f32[1,512]{1,0:T(1,128)S(1)} %add.185), channel_id=1, source_target_pairs={{0,128},{16,144},{32,160},{48,176},{64,192},{80,208},{96,224},{112... | collective-permute-start | bytes 6152 | tf_op jit(solution)/shard_map/ppermute | solution.py:43
  115.2 25.1 %collective-permute-start.23 = (bf16[2,256,1024]{2,1,0:T(8,128)(2,1)}, bf16[2,256,1024]{2,1,0:T(8,128)(2,1)S(1)}, u32[]{:S(2)}, u32[]{:S(2)}) collective-permute-start(bf16[2,256,1024]{2,1,0:T(8,128)(2,1)} %get-tuple-element.66), channel_id=1, source_target_pairs={{0,5},{1,4},{2,7},{3,6},{4,1},{5,0},{6,3},{7,2},{8,13},{9,12},{10,... | collective-permute-start | bytes 3145736 | tf_op jit(solution)/shard_map/ppermute | solution.py:39
  117.4 1.6 copy-start.1
  120.2 0.8 copy-start.5
  120.2 20.1 %collective-permute-start.20 = (f32[1,2048]{1,0:T(1,128)S(1)}, f32[1,2048]{1,0:T(1,128)S(1)}, u32[]{:S(2)}, u32[]{:S(2)}) collective-permute-start(f32[1,2048]{1,0:T(1,128)S(1)} %get-tuple-element.64.scale_ref), channel_id=1, source_target_pairs={{0,5},{1,4},{2,7},{3,6},{4,1},{5,0},{6,3},{7,2},{8,13},{9,12},{10,... | collective-permute-start | bytes 24584 | tf_op jit(solution)/shard_map/ppermute | solution.py:39
  140.3 0.6 copy-start.16
  140.3 1.0 copy-start.9
  149.6 12.6 %collective-permute-start.24 = (bf16[16,128,128]{2,1,0:T(8,128)(2,1)}, bf16[16,128,128]{2,1,0:T(8,128)(2,1)S(1)}, u32[]{:S(2)}, u32[]{:S(2)}) collective-permute-start(bf16[16,128,128]{2,1,0:T(8,128)(2,1)} %get-tuple-element.73), channel_id=1, source_target_pairs={{0,1},{1,0},{2,3},{3,2},{4,5},{5,4},{6,7},{7,6},{8,9},{9,8},{10,11... | collective-permute-start | bytes 1572872 | tf_op jit(solution)/shard_map/ppermute | solution.py:39
  150.7 12.4 %collective-permute-start.25 = (bf16[16,128,128]{2,1,0:T(8,128)(2,1)}, bf16[16,128,128]{2,1,0:T(8,128)(2,1)S(1)}, u32[]{:S(2)}, u32[]{:S(2)}) collective-permute-start(bf16[16,128,128]{2,1,0:T(8,128)(2,1)} %get-tuple-element.74), channel_id=1, source_target_pairs={{0,4},{1,5},{2,6},{3,7},{4,0},{5,1},{6,2},{7,3},{8,12},{9,13},{10,... | collective-permute-start | bytes 1572872 | tf_op jit(solution)/shard_map/ppermute | solution.py:39
  163.1 1.6 copy-start.2

commit v4 on v3

--- a/solution.py
+++ b/solution.py
@@ -106,7 +106,38 @@
     ]
 
 
-def density_kernel(
+def tile_copies(own_tile, x_tile, y_tile, low_tile, high_tile, tiles, sems):
+    half = TILE_DEV // 2
+    sources = (
+        (own_tile, 0),
+        (x_tile, TILE_DEV),
+        (y_tile, 2 * TILE_DEV),
+        (low_tile, 3 * TILE_DEV),
+        (high_tile, 3 * TILE_DEV + half),
+    )
+    return [
+        pltpu.make_async_copy(source, tiles.at[at : at + source.shape[0]], sems.at[n])
+        for n, (source, at) in enumerate(sources)
+    ]
+
+
+def batch_density(tmap_ref, blocks_ref, tiles, lister, batch, orb):
+    chosen = [blocks_ref[batch, i] for i in range(BB)]
+    total = jnp.zeros((PTS, TB), F32)
+    for pair in range(BB // 2):
+        columns = []
+        for j in (2 * pair, 2 * pair + 1):
+            columns.append(
+                jnp.concatenate([tiles[tmap_ref[lister, chosen[i] * UB + chosen[j]]] for i in range(BB)], axis=0)
+            )
+        product = jnp.dot(orb[...], jnp.concatenate(columns, axis=1), preferred_element_type=F32)
+        for side in range(2):
+            block = orb[:, (2 * pair + side) * TB : (2 * pair + side + 1) * TB]
+            total = total + product[:, side * TB : (side + 1) * TB] * block.astype(F32)
+    return jnp.sum(total.T, axis=0, keepdims=True)
+
+
+def first_density_kernel(
     tmap_ref,
     blocks_ref,
     own_tile,
@@ -117,8 +148,59 @@
     own_orb,
     x_orb,
     y_orb,
+    out_ref,
+    tiles,
+    orbs,
+    sems,
+):
+    arrivals = tile_copies(own_tile, x_tile, y_tile, low_tile, high_tile, tiles, sems)
+    points = orbital_copies(own_orb, x_orb, y_orb, (), orbs, sems.at[5:8])
+    for copy in arrivals + sum(points, []):
+        copy.start()
+    tiles[NO_TILE] = jnp.zeros((TB, TB), BF16)
+    out_ref[...] = jnp.zeros(out_ref.shape, F32)
+    for copy in arrivals:
+        copy.wait()
+    for lister in range(LISTERS - 1):
+        for copy in points[lister]:
+            copy.wait()
+
+        def one_batch(batch, unused, lister=lister):
+            out_ref[pl.ds(batch, 1), :] = batch_density(
+                tmap_ref, blocks_ref, tiles, lister, batch, orbs.at[batch]
+            )
+            return unused
+
+        lax.fori_loop(BAT_DEV * lister, BAT_DEV * (lister + 1), one_batch, 0)
+
+
+def first_density(tmap, blocks, tiles, orbs):
+    return pl.pallas_call(
+        first_density_kernel,
+        in_specs=[SMEM_SPEC] * 2 + [ANY_SPEC] * 8,
+        out_specs=VMEM_SPEC,
+        out_shape=jax.ShapeDtypeStruct((LISTERS * BAT_DEV, PTS), F32),
+        scratch_shapes=[
+            pltpu.VMEM((NO_TILE + 1, TB, TB), BF16),
+            pltpu.VMEM(((LISTERS - 1) * BAT_DEV, PTS, BB * TB), BF16),
+            pltpu.SemaphoreType.DMA((8,)),
+        ],
+        compiler_params=pltpu.CompilerParams(vmem_limit_bytes=56 * MIB),
+        cost_estimate=pl.CostEstimate(flops=2 * 10**10, bytes_accessed=10**4, transcendentals=0),
+    )(tmap, blocks, *tiles, *orbs[:3])
+
+
+def density_kernel(
+    tmap_ref,
+    blocks_ref,
+    own_tile,
+    x_tile,
+    y_tile,
+    low_tile,
+    high_tile,
     first_orb,
     second_orb,
+    before_ref,
     spread_ref,
     weights_ref,
     high_hbm,
@@ -134,55 +216,32 @@
     low_ref,
     sems,
 ):
-    half = TILE_DEV // 2
-    arrivals = [
-        pltpu.make_async_copy(source, tiles.at[at : at + source.shape[0]], sems.at[n])
-        for n, (source, at) in enumerate(
-            (
-                (own_tile, 0),
-                (x_tile, TILE_DEV),
-                (y_tile, 2 * TILE_DEV),
-                (low_tile, 3 * TILE_DEV),
-                (high_tile, 3 * TILE_DEV + half),
-            )
-        )
-    ]
+    arrivals = tile_copies(own_tile, x_tile, y_tile, low_tile, high_tile, tiles, sems)
     waves = [
         pltpu.make_async_copy(high_hbm, high_ref, sems.at[5]),
         pltpu.make_async_copy(low_hbm, low_ref, sems.at[6]),
     ]
-    points = orbital_copies(own_orb, x_orb, y_orb, (first_orb, second_orb), orbs, sems.at[7:12])
-    for copy in arrivals + sum(points, []) + waves:
+    points = [
+        pltpu.make_async_copy(first_orb, orbs.at[0], sems.at[7]),
+        pltpu.make_async_copy(second_orb, orbs.at[1], sems.at[8]),
+    ]
+    for copy in arrivals + points + waves:
         copy.start()
     tiles[NO_TILE] = jnp.zeros((TB, TB), BF16)
-    for copy in arrivals:
+    density[...] = before_ref[...]
+    for copy in arrivals + points:
         copy.wait()
-    for lister in range(LISTERS):
-        for copy in points[lister]:
-            copy.wait()
-        if lister == LISTERS - 1:
-            onward = pltpu.make_async_copy(orbs.at[6:8], diag_out, sems.at[12])
-            onward.start()
-
-        def one_batch(batch, unused, lister=lister):
-            chosen = [blocks_ref[batch, i] for i in range(BB)]
-            total = jnp.zeros((PTS, TB), F32)
-            for pair in range(BB // 2):
-                columns = []
-                for j in (2 * pair, 2 * pair + 1):
-                    columns.append(
-                        jnp.concatenate(
-                            [tiles[tmap_ref[lister, chosen[i] * UB + chosen[j]]] for i in range(BB)], axis=0
-                        )
-                    )
-                product = jnp.dot(orbs[batch], jnp.concatenate(columns, axis=1), preferred_element_type=F32)
-                for side in range(2):
-                    block = orbs[batch, :, (2 * pair + side) * TB : (2 * pair + side + 1) * TB]
-                    total = total + product[:, side * TB : (side + 1) * TB] * block.astype(F32)
-            density[pl.ds(batch, 1), :] = jnp.sum(total.T, axis=0, keepdims=True)
-            return unused
-
-        lax.fori_loop(BAT_DEV * lister, BAT_DEV * (lister + 1), one_batch, 0)
+    onward = pltpu.make_async_copy(orbs, diag_out, sems.at[9])
+    onward.start()
+
+    def one_batch(b, unused):
+        batch = BAT_DEV * (LISTERS - 1) + b
+        density[pl.ds(batch, 1), :] = batch_density(
+            tmap_ref, blocks_ref, tiles, LISTERS - 1, batch, orbs.at[b]
+        )
+        return unused
+
+    lax.fori_loop(0, BAT_DEV, one_batch, 0)
     for copy in waves:
         copy.wait()
     weighted = density[...] * weights_ref[...]
@@ -213,10 +272,10 @@
 ANY_SPEC = pl.BlockSpec(memory_space=pl.ANY)
 
 
-def density_and_moments(tmap, blocks, tiles, orbs, spread, weights, wave_high, wave_low, trig, rows):
+def density_and_moments(tmap, blocks, tiles, orbs, before, spread, weights, wave_high, wave_low, trig, rows):
     return pl.pallas_call(
         density_kernel,
-        in_specs=[SMEM_SPEC] * 2 + [ANY_SPEC] * 10 + [VMEM_SPEC] * 2 + [ANY_SPEC] * 2 + [VMEM_SPEC] * 2,
+        in_specs=[SMEM_SPEC] * 2 + [ANY_SPEC] * 7 + [VMEM_SPEC] * 3 + [ANY_SPEC] * 2 + [VMEM_SPEC] * 2,
         out_specs=[VMEM_SPEC, ANY_SPEC],
         out_shape=[
             jax.ShapeDtypeStruct((ATOM_GRP + 8, KM), F32),
@@ -224,15 +283,15 @@
         ],
         scratch_shapes=[
             pltpu.VMEM((NO_TILE + 1, TB, TB), BF16),
-            pltpu.VMEM((LISTERS * BAT_DEV, PTS, BB * TB), BF16),
+            pltpu.VMEM((BAT_DEV, PTS, BB * TB), BF16),
             pltpu.VMEM((LISTERS * BAT_DEV, PTS), F32),
             pltpu.VMEM((KM, LIST_PTS), BF16),
             pltpu.VMEM((KM, LIST_PTS), BF16),
-            pltpu.SemaphoreType.DMA((13,)),
+            pltpu.SemaphoreType.DMA((10,)),
         ],
         compiler_params=pltpu.CompilerParams(vmem_limit_bytes=56 * MIB),
         cost_estimate=pl.CostEstimate(flops=10**6, bytes_accessed=10**4, transcendentals=0),
-    )(tmap, blocks, *tiles, *orbs, spread, weights, wave_high, wave_low, trig, rows)
+    )(tmap, blocks, *tiles, *orbs[3:], before, spread, weights, wave_high, wave_low, trig, rows)
 
 
 def pack_kernel(coords, weights, owner, slot, blocks, atoms, shares, out_ref, owner_ref, slot_ref, blocks_ref, atoms_ref, shares_ref, sems):
@@ -482,10 +541,10 @@
         batch_weights,
     )
     facts = (facts, swap(facts, X3), swap(facts, Y3), swap(facts, X3 ^ Y3))
-    location, sent, *facts = lax.optimization_barrier((atom_places(atom_grid_index), dens_tiles, *facts))
+    location, sent, *facts = lax.optimization_barrier((atom_places(atom_grid_index), orbitals, *facts))
     half = TILE_DEV // 2
-    tile_x, tile_y = swap(sent, X1), swap(sent, Y1)
-    orb_x, orb_y = swap(orbitals, X3), swap(orbitals, Y3)
+    tile_x, tile_y = swap(dens_tiles, X1), swap(dens_tiles, Y1)
+    orb_x, orb_y = swap(sent, X3), swap(sent, Y3)
     tile_low, tile_high = swap(tile_y[:half], X1), swap(tile_x[half:], Y1)
     orb_first, orb_second = swap(orb_y[0], X3), swap(orb_x[1], Y3)
     orbs = (orbitals, orb_x, orb_y, orb_first, orb_second)
@@ -520,22 +579,16 @@
     envelope = jnp.exp(-2.0 * jnp.sum(displace * displace, axis=0) / (GRIDN * GRIDN))
     spread = (envelope.reshape(ATOM_GRP, LISTERS * BAT_DEV, PTS) * share[:, :, None]).reshape(ATOM_GRP, LIST_PTS)
     wave_high, wave_low = wave_of_points(coords)
-    early, late = (spread, weights, wave_high, wave_low, trig, codes, counts, tmap, blocks), orbitals
-    early, late, *unused = lax.optimization_barrier((early, late, tile_low, tile_high, orb_first, orb_second))
+    first_tmap, first_blocks = tmap, blocks
+    early = (spread, weights, wave_high, wave_low, trig, codes, counts, tmap, blocks)
+
+    tiles = (dens_tiles, tile_x, tile_y, tile_low, tile_high)
+    before = first_density(first_tmap, first_blocks, tiles, orbs)
+    early, late, *unused = lax.optimization_barrier((early, orbitals, before, tile_low, tile_high, orb_first, orb_second))
     spread, weights, wave_high, wave_low, trig, codes, counts, tmap, blocks = early
     orb_far = swap(late, XY)
-
     part, orb_diag = density_and_moments(
-        tmap,
-        blocks,
-        (dens_tiles, tile_x, tile_y, tile_low, tile_high),
-        orbs,
-        spread,
-        weights,
-        wave_high,
-        wave_low,
-        trig,
-        facts[:, 4],
+        tmap, blocks, tiles, orbs, before, spread, weights, wave_high, wave_low, trig, facts[:, 4]
     )
     a = ATOM_GRP
     got = swap(part, X3)
@@ -553,11 +606,12 @@
     far_owners, far_slots, far_blocks = what_is_listed(got[a:])
     unused, (own_codes, own_counts), (far_codes, far_counts) = lists_of(far_owners, far_slots, me)
     structure = jnp.sum(moments[:, :1] * trig, axis=0, keepdims=True)
-    for bits in (1, 2, 4, 8):
+    for bits in (1, 2, 4):
         structure = structure + swap_grp(structure, bits)
     structure, own_codes, own_counts, far_codes, far_counts, far_blocks = lax.optimization_barrier(
         (structure, own_codes, own_counts, far_codes, far_counts, far_blocks)
     )
+    structure = structure + swap_grp(structure, 8)
     potential, scale = potential_of(
         moments,
         far_gain * structure,
@@ -570,7 +624,7 @@
     )
     far_scale = swap(scale, XY)
     own, shared = ham_terms(
-        codes, counts, blocks, scale, orbs, (), ((TILE_DEV, F32), (TILE_DEV, F32)), 2 * 10**10
+        codes, counts, blocks, scale, orbs, (), ((TILE_DEV, F32), (TILE_DEV, F32)), 10**6
     )
     half = TILE_DEV // 2
     part_x, part_y = ham_terms(

time: 167 us -> 154 us (0.922)
  waiting for transfers between devices: 49.6 us -> 28.4 us
  starting transfers between devices: 42.3 us -> 46.5 us
    ppermute x22, waiting for transfers between devices: 47.7 us -> 25.3 us  [swap(): return lax.ppermute(array, 'dev', [(d, d ^ bits) for d in range(16)])]
    ppermute x22, starting transfers between devices: 30.2 us -> 34.4 us  [swap(): return lax.ppermute(array, 'dev', [(d, d ^ bits) for d in range(16)])]
    pallas_call x1 -> x2, Pallas kernels: 12 us -> 15.9 us  [the longest x1 8.73 us: first_density(): pl.pallas_call(first_density_kernel, in_specs=[SMEM_SPEC] * 2 + [ANY_SPEC...]
    pallas_call x3, Pallas kernels: 29.3 us -> 26.7 us  [ham_terms(): pl.pallas_call(functools.partial(ham_kernel, len(starts), len(outs)), in_...]
    slice x2, local copies, waits for them, and re-layouts: 1.11 us -> 2.78 us  [on_device(): tile_low, tile_high = (swap(tile_y[:half], X1), swap(tile_x[half:], Y1))]
    unnamed x44 -> x42, local copies, waits for them, and re-layouts: 5.01 us -> 4.46 us
  transfers between devices with their start and end apart: 26 -> 26, of which waited for: 15 -> 11; matrix products, arithmetic and copies ran while one was open for 9% -> 12% of each run, Pallas kernels for 25% -> 28%
where the time goes in v4:
time: 154 us; the launch traced here: 152 us
  Pallas kernels  53.9 us (35%)
  starting transfers between devices  46.5 us (30%)
  waiting for transfers between devices  28.4 us (18%)
  other arithmetic  12.1 us (8%)
  local copies, waits for them, and re-layouts  10.1 us (7%)
    ppermute x22, starting transfers between devices, swap(): return lax.ppermute(array, 'dev', [(d, d ^ bits) for d in range(16)])  34.4 us
    pallas_call x3, Pallas kernels, ham_terms(): pl.pallas_call(functools.partial(ham_kernel, len(starts), len(outs)), in_...  26.7 us
    ppermute x22, waiting for transfers between devices, swap(): return lax.ppermute(array, 'dev', [(d, d ^ bits) for d in range(16)])  25.3 us
    ppermute x4, starting transfers between devices, swap_grp(): return lax.ppermute(array, 'grp', [(g, g ^ bits) for g in range(16)])  12.2 us
    pallas_call x1, Pallas kernels, first_density(): pl.pallas_call(first_density_kernel, in_specs=[SMEM_SPEC] * 2 + [ANY_SPEC...  8.73 us
    pallas_call x1, Pallas kernels, density_and_moments(): pl.pallas_call(density_kernel, in_specs=[SMEM_SPEC] * 2 + [ANY_SPEC] * 7...  7.2 us
    pallas_call x1, Pallas kernels, wave_of_points(): pl.pallas_call(wave_kernel, grid=(points // chunk,), in_specs=[pl.BlockSp...  5.74 us
    unnamed x42, local copies, waits for them, and re-layouts  4.46 us
  transfers between devices with their start and end apart: 26, of which 11 were waited for; matrix products, arithmetic and copies ran while one was open for 12% of the time, Pallas kernels for 28%

profile of v4, /device:TPU:2, one launch (start us, length us, event | category | flops | bytes accessed | tf_op | source)
XLA Modules:
  0.0 152.4 jit_solution(12975958731861637312)
XLA Ops:
  0.6 1.4 shard_map.122
  2.1 1.6 %collective-permute-start = (f32[6,512]{1,0:T(8,128)}, f32[6,512]{1,0:T(8,128)S(1)}, u32[]{:S(2)}, u32[]{:S(2)}) collective-permute-start(f32[6,512]{1,0:T(8,128)} %shard_map.122), channel_id=1, source_target_pairs={{0,3},{1,2},{2,1},{3,0},{4,7},{5,6},{6,5},{7,4},{8,11},{9,10},{10,... | collective-permute-start | bytes 36872 | tf_op jit(solution)/shard_map/ppermute | solution.py:39
  3.7 3.0 %collective-permute-start.1 = (f32[6,512]{1,0:T(8,128)}, f32[6,512]{1,0:T(8,128)S(1)}, u32[]{:S(2)}, u32[]{:S(2)}) collective-permute-start(f32[6,512]{1,0:T(8,128)} %shard_map.122), channel_id=1, source_target_pairs={{0,12},{1,13},{2,14},{3,15},{4,8},{5,9},{6,10},{7,11},{8,4},{9,5},... | collective-permute-start | bytes 36872 | tf_op jit(solution)/shard_map/ppermute | solution.py:39
  7.2 3.1 %collective-permute-start.3 = (bf16[32,128,128]{2,1,0:T(8,128)(2,1)}, bf16[32,128,128]{2,1,0:T(8,128)(2,1)}, u32[]{:S(2)}, u32[]{:S(2)}) collective-permute-start(bf16[32,128,128]{2,1,0:T(8,128)(2,1)} %own_tile.3), channel_id=1, source_target_pairs={{0,1},{1,0},{2,3},{3,2},{4,5},{5,4},{6,7},{7,6},{8,9},{9,8},{10,11... | collective-permute-start | bytes 3145736 | tf_op jit(solution)/shard_map/ppermute | solution.py:39
  10.4 1.3 shard_map.121
  11.7 1.0 collective-permute-done.2
  13.3 2.0 %collective-permute-start.8 = (bf16[2,256,1024]{2,1,0:T(8,128)(2,1)}, bf16[2,256,1024]{2,1,0:T(8,128)(2,1)S(1)}, u32[]{:S(2)}, u32[]{:S(2)}) collective-permute-start(bf16[2,256,1024]{2,1,0:T(8,128)(2,1)} %refs_0_.1), channel_id=1, source_target_pairs={{0,12},{1,13},{2,14},{3,15},{4,8},{5,9},{6,10},{7,11},{8,4},{9,5},... | collective-permute-start | bytes 3145736 | tf_op jit(solution)/shard_map/ppermute | solution.py:39
  16.5 0.7 fusion.1
  18.8 0.8 pad_maximum_fusion
  20.4 0.8 multiply_reduce_fusion
  22.4 8.8 %collective-permute-done.4.y_tile = bf16[32,128,128]{2,1,0:T(8,128)(2,1)S(1)} collective-permute-done((bf16[32,128,128]{2,1,0:T(8,128)(2,1)}, bf16[32,128,128]{2,1,0:T(8,128)(2,1)S(1)}, u32[]{:S(2)}, u32[]{:S(2)}) %collective-permute-start.4) | collective-permute-done | bytes 1048608 | tf_op jit(solution)/shard_map/ppermute | solution.py:39
  31.2 0.9 slice.142
  32.1 1.8 %collective-permute-start.5 = (bf16[16,128,128]{2,1,0:T(8,128)(2,1)}, bf16[16,128,128]{2,1,0:T(8,128)(2,1)}, u32[]{:S(2)}, u32[]{:S(2)}) collective-permute-start(bf16[16,128,128]{2,1,0:T(8,128)(2,1)} %slice.142), channel_id=1, source_target_pairs={{0,1},{1,0},{2,3},{3,2},{4,5},{5,4},{6,7},{7,6},{8,9},{9,8},{10,11... | collective-permute-start | bytes 1572872 | tf_op jit(solution)/shard_map/ppermute | solution.py:39
  33.9 1.9 %slice.143 = bf16[16,128,128]{2,1,0:T(8,128)(2,1)} slice(bf16[32,128,128]{2,1,0:T(8,128)(2,1)} %collective-permute-done.3.x_tile), slice={[16:32], [0:128], [0:128]} | slice | bytes 1048576 | tf_op jit(solution)/shard_map/slice | solution.py:548
  37.9 5.7 %shard_map.123 = (bf16[512,2048]{1,0:T(8,128)(2,1)}, bf16[512,2048]{1,0:T(8,128)(2,1)}) custom-call(f32[48,2048]{1,0:T(8,128)} %bitcast.49), custom_call_target="tpu_custom_call" | custom-call | flops 8388608 | bytes 4194304 | tf_op jit(solution)/shard_map/pallas_call | solution.py:87
  43.7 3.0 %collective-permute-start.10 = (bf16[256,1024]{1,0:T(8,128)(2,1)S(1)}, bf16[256,1024]{1,0:T(8,128)(2,1)S(1)}, u32[]{:S(2)}, u32[]{:S(2)}) collective-permute-start(bf16[256,1024]{1,0:T(8,128)(2,1)S(1)} %slice_bitcast_fusion), channel_id=1, source_target_pairs={{0,12},{1,13},{2,14},{3,15},{4,8},{5,9},{6,10},{7,11},{8,4},{9,5},... | collective-permute-start | bytes 1572872 | tf_op jit(solution)/shard_map/ppermute | solution.py:39
  46.7 2.2 %collective-permute-start.9 = (bf16[256,1024]{1,0:T(8,128)(2,1)S(1)}, bf16[256,1024]{1,0:T(8,128)(2,1)S(1)}, u32[]{:S(2)}, u32[]{:S(2)}) collective-permute-start(bf16[256,1024]{1,0:T(8,128)(2,1)S(1)} %slice_bitcast_fusion.1), channel_id=1, source_target_pairs={{0,3},{1,2},{2,1},{3,0},{4,7},{5,6},{6,5},{7,4},{8,11},{9,10},{10,... | collective-permute-start | bytes 1572872 | tf_op jit(solution)/shard_map/ppermute | solution.py:39
  49.0 8.7 %shard_map.124.before_ref = f32[8,256]{1,0:T(8,128)} custom-call(s32[4,81]{1,0:T(4,128)} %get-tuple-element.47.tmap_ref, s32[8,8]{1,0:T(8,128)} %bitcast.55, bf16[32,128,128]{2,1,0:T(8,128)(2,1)} %own_tile.3, bf16[32,128,128]{2,1,0:T(8,128)(2,1)} %collective-permute-done.3.x_tile, bf16[32,128,128]{2,1,0:T(8,128)(2,1)} %copy-done.8, ...), custom_call_target="tpu_custom_call" | custom-call | flops 20000000000 | bytes 10000 | tf_op jit(solution)/shard_map/pallas_call | solution.py:178
  57.7 0.9 collective-permute-done.9.first_orb.refs_3_
  58.6 1.4 collective-permute-start.13
  60.1 7.2 %shard_map.125 = (f32[24,512]{1,0:T(8,128)}, bf16[2,256,1024]{2,1,0:T(8,128)(2,1)}) custom-call(s32[4,81]{1,0:T(4,128)} %get-tuple-element.47.tmap_ref, s32[8,8]{1,0:T(8,128)} %bitcast.56, bf16[32,128,128]{2,1,0:T(8,128)(2,1)} %own_tile.3, bf16[32,128,128]{2,1,0:T(8,128)(2,1)} %collective-permute-done.3.x_tile, bf16[32,128,128]{2,1,0:T(8,128)(2,1)} %copy-done.8, ...), custom_call_target="tpu_custom_call" | custom-call | flops 1000000 | bytes 10000 | tf_op jit(solution)/shard_map/pallas_call | solution.py:276
  67.3 2.2 %collective-permute-start.11 = (f32[24,512]{1,0:T(8,128)}, f32[24,512]{1,0:T(8,128)S(1)}, u32[]{:S(2)}, u32[]{:S(2)}) collective-permute-start(f32[24,512]{1,0:T(8,128)} %get-tuple-element.54), channel_id=1, source_target_pairs={{0,3},{1,2},{2,1},{3,0},{4,7},{5,6},{6,5},{7,4},{8,11},{9,10},{10,... | collective-permute-start | bytes 147464 | tf_op jit(solution)/shard_map/ppermute | solution.py:39
  69.5 2.3 %collective-permute-done.11 = f32[24,512]{1,0:T(8,128)S(1)} collective-permute-done((f32[24,512]{1,0:T(8,128)}, f32[24,512]{1,0:T(8,128)S(1)}, u32[]{:S(2)}, u32[]{:S(2)}) %collective-permute-start.11) | collective-permute-done | bytes 49184 | tf_op jit(solution)/shard_map/ppermute | solution.py:39
  71.8 0.8 add.176
  72.7 0.9 collective-permute-start.12
  73.6 4.4 %collective-permute-done.12 = f32[24,512]{1,0:T(8,128)S(1)} collective-permute-done((f32[24,512]{1,0:T(8,128)S(1)}, f32[24,512]{1,0:T(8,128)S(1)}, u32[]{:S(2)}, u32[]{:S(2)}) %collective-permute-start.12) | collective-permute-done | bytes 49184 | tf_op jit(solution)/shard_map/ppermute | solution.py:39
  78.6 3.8 %collective-permute-done.13.refs_0_ = bf16[2,256,1024]{2,1,0:T(8,128)(2,1)S(1)} collective-permute-done((bf16[2,256,1024]{2,1,0:T(8,128)(2,1)}, bf16[2,256,1024]{2,1,0:T(8,128)(2,1)S(1)}, u32[]{:S(2)}, u32[]{:S(2)}) %collective-permute-start.13) | collective-permute-done | bytes 1048608 | tf_op jit(solution)/shard_map/ppermute | solution.py:39
  82.3 0.7 collective-permute-start.14
  83.0 3.5 %collective-permute-done.14 = f32[20,512]{1,0:T(8,128)S(1)} collective-permute-done((f32[20,512]{1,0:T(8,128)S(1)}, f32[20,512]{1,0:T(8,128)S(1)}, u32[]{:S(2)}, u32[]{:S(2)}) %collective-permute-start.14) | collective-permute-done | bytes 40992 | tf_op jit(solution)/shard_map/ppermute | solution.py:39
  87.0 1.7 %collective-permute-start.21 = (bf16[2,256,1024]{2,1,0:T(8,128)(2,1)S(1)}, bf16[2,256,1024]{2,1,0:T(8,128)(2,1)}, u32[]{:S(2)}, u32[]{:S(2)}) collective-permute-start(bf16[2,256,1024]{2,1,0:T(8,128)(2,1)S(1)} %collective-permute-done.13.refs_0_), channel_id=1, source_target_pairs={{0,3},{1,2},{2,1},{3,0},{4,7},{5,6},{6,5},{7,4},{8,11},{9,10},{10,... | collective-permute-start | bytes 3145736 | tf_op jit(solution)/shard_map/ppermute | solution.py:39
  88.7 2.1 %collective-permute-start.22 = (bf16[2,256,1024]{2,1,0:T(8,128)(2,1)S(1)}, bf16[2,256,1024]{2,1,0:T(8,128)(2,1)}, u32[]{:S(2)}, u32[]{:S(2)}) collective-permute-start(bf16[2,256,1024]{2,1,0:T(8,128)(2,1)S(1)} %collective-permute-done.13.refs_0_), channel_id=1, source_target_pairs={{0,12},{1,13},{2,14},{3,15},{4,8},{5,9},{6,10},{7,11},{8,4},{9,5},... | collective-permute-start | bytes 3145736 | tf_op jit(solution)/shard_map/ppermute | solution.py:39
  91.5 1.3 collective-permute-start.23
  94.5 2.0 %collective-permute-start.17 = (f32[1,512]{1,0:T(1,128)S(1)}, f32[1,512]{1,0:T(1,128)S(1)}, u32[]{:S(2)}, u32[]{:S(2)}) collective-permute-start(f32[1,512]{1,0:T(1,128)S(1)} %add.183), channel_id=1, source_target_pairs={{0,32},{16,48},{32,0},{48,16},{64,96},{80,112},{96,64},{112,80},{1... | collective-permute-start | bytes 6152 | tf_op jit(solution)/shard_map/ppermute | solution.py:43
  97.0 1.2 collective-permute-done.17
  98.2 3.3 %collective-permute-start.18 = (f32[1,512]{1,0:T(1,128)S(1)}, f32[1,512]{1,0:T(1,128)S(1)}, u32[]{:S(2)}, u32[]{:S(2)}) collective-permute-start(f32[1,512]{1,0:T(1,128)S(1)} %add.184), channel_id=1, source_target_pairs={{0,64},{16,80},{32,96},{48,112},{64,0},{80,16},{96,32},{112,48},{1... | collective-permute-start | bytes 6152 | tf_op jit(solution)/shard_map/ppermute | solution.py:43
  103.0 6.8 %collective-permute-start.19 = (f32[1,512]{1,0:T(1,128)S(1)}, f32[1,512]{1,0:T(1,128)S(1)}, u32[]{:S(2)}, u32[]{:S(2)}) collective-permute-start(f32[1,512]{1,0:T(1,128)S(1)} %add.185), channel_id=1, source_target_pairs={{0,128},{16,144},{32,160},{48,176},{64,192},{80,208},{96,224},{112... | collective-permute-start | bytes 6152 | tf_op jit(solution)/shard_map/ppermute | solution.py:43
  109.9 1.5 collective-permute-done.19
  111.5 1.6 %copy-done.1 = bf16[512,2048]{1,0:T(8,128)(2,1)S(1)} copy-done((bf16[512,2048]{1,0:T(8,128)(2,1)S(1)}, bf16[512,2048]{1,0:T(8,128)(2,1)}, u32[]{:S(2)}) %copy-start.1) | copy-done | bytes 2097176
  113.1 1.2 shard_map.126
  114.3 1.7 %collective-permute-start.20 = (f32[1,2048]{1,0:T(1,128)S(1)}, f32[1,2048]{1,0:T(1,128)S(1)}, u32[]{:S(2)}, u32[]{:S(2)}) collective-permute-start(f32[1,2048]{1,0:T(1,128)S(1)} %get-tuple-element.64.scale_ref), channel_id=1, source_target_pairs={{0,5},{1,4},{2,7},{3,6},{4,1},{5,0},{6,3},{7,2},{8,13},{9,12},{10,... | collective-permute-start | bytes 24584 | tf_op jit(solution)/shard_map/ppermute | solution.py:39
  116.0 1.3 slice_add_fusion.3
  117.3 10.3 %shard_map.127 = (f32[32,128,128]{2,1,0:T(8,128)}, f32[32,128,128]{2,1,0:T(8,128)}) custom-call(s32[4,32]{1,0:T(4,128)} %fusion.8.codes_ref, s32[4]{0:T(128)} %and_select_fusion.6.counts_ref, s32[8,8]{1,0:T(8,128)} %bitcast.57, f32[1,2048]{1,0:T(1,128)} %copy-done.5, bf16[2,256,1024]{2,1,0:T(8,128)(2,1)} %refs_0_.1, bf16[2,256,1024]{2,1,0:T(8,128)(2,1)} %copy-done.6, ...), custom_call_target="tpu_custom_call" | custom-call | flops 1000000 | bytes 10000 | tf_op jit(solution)/shard_map/pallas_call | solution.py:446
  128.2 7.7 %shard_map.129 = (bf16[16,128,128]{2,1,0:T(8,128)(2,1)}, bf16[16,128,128]{2,1,0:T(8,128)(2,1)}) custom-call(s32[4,32]{1,0:T(4,128)} %fusion.10.codes_ref, s32[4]{0:T(128)} %and_select_fusion.4.counts_ref, s32[8,8]{1,0:T(8,128)} %bitcast.60, f32[1,2048]{1,0:T(1,128)} %copy-done.15, bf16[2,256,1024]{2,1,0:T(8,128)(2,1)} %copy-done.11, ...), custom_call_target="tpu_custom_call" | custom-call | flops 1000000 | bytes 10000 | tf_op jit(solution)/shard_map/pallas_call | solution.py:446
  135.9 2.7 %collective-permute-start.24 = (bf16[16,128,128]{2,1,0:T(8,128)(2,1)}, bf16[16,128,128]{2,1,0:T(8,128)(2,1)S(1)}, u32[]{:S(2)}, u32[]{:S(2)}) collective-permute-start(bf16[16,128,128]{2,1,0:T(8,128)(2,1)} %get-tuple-element.73), channel_id=1, source_target_pairs={{0,1},{1,0},{2,3},{3,2},{4,5},{5,4},{6,7},{7,6},{8,9},{9,8},{10,11... | collective-permute-start | bytes 1572872 | tf_op jit(solution)/shard_map/ppermute | solution.py:39
  138.6 1.1 collective-permute-start.25
  139.8 8.7 %shard_map.128.own_ref = f32[32,128,128]{2,1,0:T(8,128)} custom-call(s32[4,32]{1,0:T(4,128)} %fusion.9.codes_ref, s32[4]{0:T(128)} %and_select_fusion.5.counts_ref, s32[8,8]{1,0:T(8,128)} %bitcast.61, f32[1,2048]{1,0:T(1,128)} %copy-done.15, bf16[2,256,1024]{2,1,0:T(8,128)(2,1)} %copy-done.11, bf16[2,256,1024]{2,1,0:T(8,128)(2,1)} %collective-permute-done.21.refs_1_, ...), custom_call_target="tpu_custom_call" | custom-call | flops 20000000000 | bytes 10000 | tf_op jit(solution)/shard_map/pallas_call | solution.py:446
  149.1 1.6 %copy-done.2 = f32[32,128,128]{2,1,0:T(8,128)S(1)} copy-done((f32[32,128,128]{2,1,0:T(8,128)S(1)}, f32[32,128,128]{2,1,0:T(8,128)}, u32[]{:S(2)}) %copy-start.2) | copy-done | bytes 2097176
  150.7 1.7 %shard_map.130 = bf16[32,128,128]{2,1,0:T(8,128)(2,1)} custom-call(f32[32,128,128]{2,1,0:T(8,128)S(1)} %copy-done.2, bf16[16,128,128]{2,1,0:T(8,128)(2,1)S(1)} %collective-permute-done.24.x_ref, bf16[16,128,128]{2,1,0:T(8,128)(2,1)S(1)} %collective-permute-done.25.y_ref), custom_call_target="tpu_custom_call" | custom-call | flops 1000000 | bytes 10000 | tf_op jit(solution)/shard_map/pallas_call | solution.py:473
  (129 shorter events, 15.2 us)
Async XLA Ops:
  2.1 9.6 %collective-permute-start = (f32[6,512]{1,0:T(8,128)}, f32[6,512]{1,0:T(8,128)S(1)}, u32[]{:S(2)}, u32[]{:S(2)}) collective-permute-start(f32[6,512]{1,0:T(8,128)} %shard_map.122), channel_id=1, source_target_pairs={{0,3},{1,2},{2,1},{3,0},{4,7},{5,6},{6,5},{7,4},{8,11},{9,10},{10,... | collective-permute-start | bytes 36872 | tf_op jit(solution)/shard_map/ppermute | solution.py:39
  3.7 8.0 %collective-permute-start.1 = (f32[6,512]{1,0:T(8,128)}, f32[6,512]{1,0:T(8,128)S(1)}, u32[]{:S(2)}, u32[]{:S(2)}) collective-permute-start(f32[6,512]{1,0:T(8,128)} %shard_map.122), channel_id=1, source_target_pairs={{0,12},{1,13},{2,14},{3,15},{4,8},{5,9},{6,10},{7,11},{8,4},{9,5},... | collective-permute-start | bytes 36872 | tf_op jit(solution)/shard_map/ppermute | solution.py:39
  6.7 6.1 %collective-permute-start.2 = (f32[6,512]{1,0:T(8,128)}, f32[6,512]{1,0:T(8,128)S(1)}, u32[]{:S(2)}, u32[]{:S(2)}) collective-permute-start(f32[6,512]{1,0:T(8,128)} %shard_map.122), channel_id=1, source_target_pairs={{0,15},{1,14},{2,13},{3,12},{4,11},{5,10},{6,9},{7,8},{8,7},{9,6},... | collective-permute-start | bytes 36872 | tf_op jit(solution)/shard_map/ppermute | solution.py:39
  6.9 24.4 %collective-permute-start.4 = (bf16[32,128,128]{2,1,0:T(8,128)(2,1)}, bf16[32,128,128]{2,1,0:T(8,128)(2,1)S(1)}, u32[]{:S(2)}, u32[]{:S(2)}) collective-permute-start(bf16[32,128,128]{2,1,0:T(8,128)(2,1)} %own_tile.3), channel_id=1, source_target_pairs={{0,4},{1,5},{2,6},{3,7},{4,0},{5,1},{6,2},{7,3},{8,12},{9,13},{10,... | collective-permute-start | bytes 3145736 | tf_op jit(solution)/shard_map/ppermute | solution.py:39
  7.2 26.7 %collective-permute-start.3 = (bf16[32,128,128]{2,1,0:T(8,128)(2,1)}, bf16[32,128,128]{2,1,0:T(8,128)(2,1)}, u32[]{:S(2)}, u32[]{:S(2)}) collective-permute-start(bf16[32,128,128]{2,1,0:T(8,128)(2,1)} %own_tile.3), channel_id=1, source_target_pairs={{0,1},{1,0},{2,3},{3,2},{4,5},{5,4},{6,7},{7,6},{8,9},{9,8},{10,11... | collective-permute-start | bytes 3145736 | tf_op jit(solution)/shard_map/ppermute | solution.py:39
  10.4 4.8 %copy-start.13 = (f32[6,512]{1,0:T(8,128)S(1)}, f32[6,512]{1,0:T(8,128)}, u32[]{:S(2)}) copy-start(f32[6,512]{1,0:T(8,128)} %shard_map.122) | copy-start | bytes 36868
  11.7 9.8 %copy-start.16 = (f32[3,16]{1,0:T(4,128)S(1)}, f32[3,16]{1,0:T(4,128)}, u32[]{:S(2)}) copy-start(f32[3,16]{1,0:T(4,128)} %shard_map.121) | copy-start | bytes 580
  12.7 30.9 %collective-permute-start.7 = (bf16[2,256,1024]{2,1,0:T(8,128)(2,1)}, bf16[2,256,1024]{2,1,0:T(8,128)(2,1)S(1)}, u32[]{:S(2)}, u32[]{:S(2)}) collective-permute-start(bf16[2,256,1024]{2,1,0:T(8,128)(2,1)} %refs_0_.1), channel_id=1, source_target_pairs={{0,3},{1,2},{2,1},{3,0},{4,7},{5,6},{6,5},{7,4},{8,11},{9,10},{10,... | collective-permute-start | bytes 3145736 | tf_op jit(solution)/shard_map/ppermute | solution.py:39
  13.3 33.4 %collective-permute-start.8 = (bf16[2,256,1024]{2,1,0:T(8,128)(2,1)}, bf16[2,256,1024]{2,1,0:T(8,128)(2,1)S(1)}, u32[]{:S(2)}, u32[]{:S(2)}) collective-permute-start(bf16[2,256,1024]{2,1,0:T(8,128)(2,1)} %refs_0_.1), channel_id=1, source_target_pairs={{0,12},{1,13},{2,14},{3,15},{4,8},{5,9},{6,10},{7,11},{8,4},{9,5},... | collective-permute-start | bytes 3145736 | tf_op jit(solution)/shard_map/ppermute | solution.py:39
  31.2 15.5 %copy-start.8 = (bf16[32,128,128]{2,1,0:T(8,128)(2,1)}, bf16[32,128,128]{2,1,0:T(8,128)(2,1)S(1)}, u32[]{:S(2)}) copy-start(bf16[32,128,128]{2,1,0:T(8,128)(2,1)S(1)} %collective-permute-done.4.y_tile) | copy-start | bytes 3145732
  32.1 16.8 %collective-permute-start.5 = (bf16[16,128,128]{2,1,0:T(8,128)(2,1)}, bf16[16,128,128]{2,1,0:T(8,128)(2,1)}, u32[]{:S(2)}, u32[]{:S(2)}) collective-permute-start(bf16[16,128,128]{2,1,0:T(8,128)(2,1)} %slice.142), channel_id=1, source_target_pairs={{0,1},{1,0},{2,3},{3,2},{4,5},{5,4},{6,7},{7,6},{8,9},{9,8},{10,11... | collective-permute-start | bytes 1572872 | tf_op jit(solution)/shard_map/ppermute | solution.py:39
  35.8 13.1 %collective-permute-start.6 = (bf16[16,128,128]{2,1,0:T(8,128)(2,1)}, bf16[16,128,128]{2,1,0:T(8,128)(2,1)}, u32[]{:S(2)}, u32[]{:S(2)}) collective-permute-start(bf16[16,128,128]{2,1,0:T(8,128)(2,1)} %slice.143), channel_id=1, source_target_pairs={{0,4},{1,5},{2,6},{3,7},{4,0},{5,1},{6,2},{7,3},{8,12},{9,13},{10,... | collective-permute-start | bytes 1572872 | tf_op jit(solution)/shard_map/ppermute | solution.py:39
  43.7 5.3 %copy-start.6 = (bf16[2,256,1024]{2,1,0:T(8,128)(2,1)}, bf16[2,256,1024]{2,1,0:T(8,128)(2,1)S(1)}, u32[]{:S(2)}) copy-start(bf16[2,256,1024]{2,1,0:T(8,128)(2,1)S(1)} %collective-permute-done.7.x_orb.refs_1_) | copy-start | bytes 3145732
  43.7 14.0 %collective-permute-start.10 = (bf16[256,1024]{1,0:T(8,128)(2,1)S(1)}, bf16[256,1024]{1,0:T(8,128)(2,1)S(1)}, u32[]{:S(2)}, u32[]{:S(2)}) collective-permute-start(bf16[256,1024]{1,0:T(8,128)(2,1)S(1)} %slice_bitcast_fusion), channel_id=1, source_target_pairs={{0,12},{1,13},{2,14},{3,15},{4,8},{5,9},{6,10},{7,11},{8,4},{9,5},... | collective-permute-start | bytes 1572872 | tf_op jit(solution)/shard_map/ppermute | solution.py:39
  46.6 2.3 %copy-start.7 = (bf16[2,256,1024]{2,1,0:T(8,128)(2,1)}, bf16[2,256,1024]{2,1,0:T(8,128)(2,1)S(1)}, u32[]{:S(2)}) copy-start(bf16[2,256,1024]{2,1,0:T(8,128)(2,1)S(1)} %collective-permute-done.8.y_orb.refs_2_) | copy-start | bytes 3145732
  46.7 11.9 %collective-permute-start.9 = (bf16[256,1024]{1,0:T(8,128)(2,1)S(1)}, bf16[256,1024]{1,0:T(8,128)(2,1)S(1)}, u32[]{:S(2)}, u32[]{:S(2)}) collective-permute-start(bf16[256,1024]{1,0:T(8,128)(2,1)S(1)} %slice_bitcast_fusion.1), channel_id=1, source_target_pairs={{0,3},{1,2},{2,1},{3,0},{4,7},{5,6},{6,5},{7,4},{8,11},{9,10},{10,... | collective-permute-start | bytes 1572872 | tf_op jit(solution)/shard_map/ppermute | solution.py:39
  57.7 2.3 %copy-start.9 = (bf16[256,1024]{1,0:T(8,128)(2,1)}, bf16[256,1024]{1,0:T(8,128)(2,1)S(1)}, u32[]{:S(2)}) copy-start(bf16[256,1024]{1,0:T(8,128)(2,1)S(1)} %collective-permute-done.10.second_orb.refs_4_) | copy-start | bytes 1572868
  58.6 1.4 copy-start.10
  58.6 23.7 %collective-permute-start.13 = (bf16[2,256,1024]{2,1,0:T(8,128)(2,1)}, bf16[2,256,1024]{2,1,0:T(8,128)(2,1)S(1)}, u32[]{:S(2)}, u32[]{:S(2)}) collective-permute-start(bf16[2,256,1024]{2,1,0:T(8,128)(2,1)} %refs_0_.1), channel_id=1, source_target_pairs={{0,5},{1,4},{2,7},{3,6},{4,1},{5,0},{6,3},{7,2},{8,13},{9,12},{10,... | collective-permute-start | bytes 3145736 | tf_op jit(solution)/shard_map/ppermute | solution.py:39
  60.0 31.3 %copy-start.4 = (f32[16,512]{1,0:T(8,128)S(1)}, f32[16,512]{1,0:T(8,128)}, u32[]{:S(2)}) copy-start(f32[16,512]{1,0:T(8,128)} %pad_maximum_fusion.4.trig_ref) | copy-start | bytes 98308
  60.0 49.9 %copy-start.12 = (f32[8,256]{1,0:T(8,128)S(1)}, f32[8,256]{1,0:T(8,128)}, u32[]{:S(2)}) copy-start(f32[8,256]{1,0:T(8,128)} %reshape_squeeze.12.weights_ref) | copy-start | bytes 24580
  60.0 51.4 %copy-start = (bf16[512,2048]{1,0:T(8,128)(2,1)S(1)}, bf16[512,2048]{1,0:T(8,128)(2,1)}, u32[]{:S(2)}) copy-start(bf16[512,2048]{1,0:T(8,128)(2,1)} %get-tuple-element.51.high_hbm.high_ref) | copy-start | bytes 6291460
  60.0 51.4 %copy-start.3 = (f32[16,2048]{1,0:T(8,128)S(1)}, f32[16,2048]{1,0:T(8,128)}, u32[]{:S(2)}) copy-start(f32[16,2048]{1,0:T(8,128)} %exponential_multiply_fusion.spread_ref) | copy-start | bytes 393220
  67.3 4.5 %collective-permute-start.11 = (f32[24,512]{1,0:T(8,128)}, f32[24,512]{1,0:T(8,128)S(1)}, u32[]{:S(2)}, u32[]{:S(2)}) collective-permute-start(f32[24,512]{1,0:T(8,128)} %get-tuple-element.54), channel_id=1, source_target_pairs={{0,3},{1,2},{2,1},{3,0},{4,7},{5,6},{6,5},{7,4},{8,11},{9,10},{10,... | collective-permute-start | bytes 147464 | tf_op jit(solution)/shard_map/ppermute | solution.py:39
  72.7 5.3 %collective-permute-start.12 = (f32[24,512]{1,0:T(8,128)S(1)}, f32[24,512]{1,0:T(8,128)S(1)}, u32[]{:S(2)}, u32[]{:S(2)}) collective-permute-start(f32[24,512]{1,0:T(8,128)S(1)} %add.176), channel_id=1, source_target_pairs={{0,12},{1,13},{2,14},{3,15},{4,8},{5,9},{6,10},{7,11},{8,4},{9,5},... | collective-permute-start | bytes 147464 | tf_op jit(solution)/shard_map/ppermute | solution.py:39
  78.0 0.6 copy-start.14
  82.3 31.9 %copy-start.11 = (bf16[2,256,1024]{2,1,0:T(8,128)(2,1)}, bf16[2,256,1024]{2,1,0:T(8,128)(2,1)S(1)}, u32[]{:S(2)}) copy-start(bf16[2,256,1024]{2,1,0:T(8,128)(2,1)S(1)} %collective-permute-done.13.refs_0_) | copy-start | bytes 3145732
  82.3 4.2 %collective-permute-start.14 = (f32[20,512]{1,0:T(8,128)S(1)}, f32[20,512]{1,0:T(8,128)S(1)}, u32[]{:S(2)}, u32[]{:S(2)}) collective-permute-start(f32[20,512]{1,0:T(8,128)S(1)} %pad_maximum_fusion.2), channel_id=1, source_target_pairs={{0,1},{1,0},{2,3},{3,2},{4,5},{5,4},{6,7},{7,6},{8,9},{9,8},{10,11... | collective-permute-start | bytes 122888 | tf_op jit(solution)/shard_map/ppermute | solution.py:39
  86.5 4.2 %collective-permute-start.15 = (f32[20,512]{1,0:T(8,128)S(1)}, f32[20,512]{1,0:T(8,128)S(1)}, u32[]{:S(2)}, u32[]{:S(2)}) collective-permute-start(f32[20,512]{1,0:T(8,128)S(1)} %pad_maximum_fusion.3), channel_id=1, source_target_pairs={{0,4},{1,5},{2,6},{3,7},{4,0},{5,1},{6,2},{7,3},{8,12},{9,13},{10,... | collective-permute-start | bytes 122888 | tf_op jit(solution)/shard_map/ppermute | solution.py:39
  87.0 40.6 %collective-permute-start.21 = (bf16[2,256,1024]{2,1,0:T(8,128)(2,1)S(1)}, bf16[2,256,1024]{2,1,0:T(8,128)(2,1)}, u32[]{:S(2)}, u32[]{:S(2)}) collective-permute-start(bf16[2,256,1024]{2,1,0:T(8,128)(2,1)S(1)} %collective-permute-done.13.refs_0_), channel_id=1, source_target_pairs={{0,3},{1,2},{2,1},{3,0},{4,7},{5,6},{6,5},{7,4},{8,11},{9,10},{10,... | collective-permute-start | bytes 3145736 | tf_op jit(solution)/shard_map/ppermute | solution.py:39
  88.7 39.0 %collective-permute-start.22 = (bf16[2,256,1024]{2,1,0:T(8,128)(2,1)S(1)}, bf16[2,256,1024]{2,1,0:T(8,128)(2,1)}, u32[]{:S(2)}, u32[]{:S(2)}) collective-permute-start(bf16[2,256,1024]{2,1,0:T(8,128)(2,1)S(1)} %collective-permute-done.13.refs_0_), channel_id=1, source_target_pairs={{0,12},{1,13},{2,14},{3,15},{4,8},{5,9},{6,10},{7,11},{8,4},{9,5},... | collective-permute-start | bytes 3145736 | tf_op jit(solution)/shard_map/ppermute | solution.py:39
  91.4 3.1 %collective-permute-start.16 = (f32[1,512]{1,0:T(1,128)S(1)}, f32[1,512]{1,0:T(1,128)S(1)}, u32[]{:S(2)}, u32[]{:S(2)}) collective-permute-start(f32[1,512]{1,0:T(1,128)S(1)} %bitcast.62), channel_id=1, source_target_pairs={{0,16},{16,0},{32,48},{48,32},{64,80},{80,64},{96,112},{112,96},{1... | collective-permute-start | bytes 6152 | tf_op jit(solution)/shard_map/ppermute | solution.py:43
  91.5 36.2 %collective-permute-start.23 = (bf16[2,256,1024]{2,1,0:T(8,128)(2,1)}, bf16[2,256,1024]{2,1,0:T(8,128)(2,1)}, u32[]{:S(2)}, u32[]{:S(2)}) collective-permute-start(bf16[2,256,1024]{2,1,0:T(8,128)(2,1)} %get-tuple-element.66), channel_id=1, source_target_pairs={{0,5},{1,4},{2,7},{3,6},{4,1},{5,0},{6,3},{7,2},{8,13},{9,12},{10,... | collective-permute-start | bytes 3145736 | tf_op jit(solution)/shard_map/ppermute | solution.py:39
  94.5 3.7 %collective-permute-start.17 = (f32[1,512]{1,0:T(1,128)S(1)}, f32[1,512]{1,0:T(1,128)S(1)}, u32[]{:S(2)}, u32[]{:S(2)}) collective-permute-start(f32[1,512]{1,0:T(1,128)S(1)} %add.183), channel_id=1, source_target_pairs={{0,32},{16,48},{32,0},{48,16},{64,96},{80,112},{96,64},{112,80},{1... | collective-permute-start | bytes 6152 | tf_op jit(solution)/shard_map/ppermute | solution.py:43
  98.2 4.8 %collective-permute-start.18 = (f32[1,512]{1,0:T(1,128)S(1)}, f32[1,512]{1,0:T(1,128)S(1)}, u32[]{:S(2)}, u32[]{:S(2)}) collective-permute-start(f32[1,512]{1,0:T(1,128)S(1)} %add.184), channel_id=1, source_target_pairs={{0,64},{16,80},{32,96},{48,112},{64,0},{80,16},{96,32},{112,48},{1... | collective-permute-start | bytes 6152 | tf_op jit(solution)/shard_map/ppermute | solution.py:43
  103.0 8.4 %collective-permute-start.19 = (f32[1,512]{1,0:T(1,128)S(1)}, f32[1,512]{1,0:T(1,128)S(1)}, u32[]{:S(2)}, u32[]{:S(2)}) collective-permute-start(f32[1,512]{1,0:T(1,128)S(1)} %add.185), channel_id=1, source_target_pairs={{0,128},{16,144},{32,160},{48,176},{64,192},{80,208},{96,224},{112... | collective-permute-start | bytes 6152 | tf_op jit(solution)/shard_map/ppermute | solution.py:43
  111.5 1.6 %copy-start.1 = (bf16[512,2048]{1,0:T(8,128)(2,1)S(1)}, bf16[512,2048]{1,0:T(8,128)(2,1)}, u32[]{:S(2)}) copy-start(bf16[512,2048]{1,0:T(8,128)(2,1)} %get-tuple-element.52.low_hbm.low_ref) | copy-start | bytes 6291460
  114.3 3.0 %copy-start.5 = (f32[1,2048]{1,0:T(1,128)}, f32[1,2048]{1,0:T(1,128)S(1)}, u32[]{:S(2)}) copy-start(f32[1,2048]{1,0:T(1,128)S(1)} %get-tuple-element.64.scale_ref) | copy-start | bytes 24580
  114.3 13.3 %collective-permute-start.20 = (f32[1,2048]{1,0:T(1,128)S(1)}, f32[1,2048]{1,0:T(1,128)S(1)}, u32[]{:S(2)}, u32[]{:S(2)}) collective-permute-start(f32[1,2048]{1,0:T(1,128)S(1)} %get-tuple-element.64.scale_ref), channel_id=1, source_target_pairs={{0,5},{1,4},{2,7},{3,6},{4,1},{5,0},{6,3},{7,2},{8,13},{9,12},{10,... | collective-permute-start | bytes 24584 | tf_op jit(solution)/shard_map/ppermute | solution.py:39
  127.6 0.6 copy-start.15
  135.9 12.6 %collective-permute-start.24 = (bf16[16,128,128]{2,1,0:T(8,128)(2,1)}, bf16[16,128,128]{2,1,0:T(8,128)(2,1)S(1)}, u32[]{:S(2)}, u32[]{:S(2)}) collective-permute-start(bf16[16,128,128]{2,1,0:T(8,128)(2,1)} %get-tuple-element.73), channel_id=1, source_target_pairs={{0,1},{1,0},{2,3},{3,2},{4,5},{5,4},{6,7},{7,6},{8,9},{9,8},{10,11... | collective-permute-start | bytes 1572872 | tf_op jit(solution)/shard_map/ppermute | solution.py:39
  138.6 10.5 %collective-permute-start.25 = (bf16[16,128,128]{2,1,0:T(8,128)(2,1)}, bf16[16,128,128]{2,1,0:T(8,128)(2,1)S(1)}, u32[]{:S(2)}, u32[]{:S(2)}) collective-permute-start(bf16[16,128,128]{2,1,0:T(8,128)(2,1)} %get-tuple-element.74), channel_id=1, source_target_pairs={{0,4},{1,5},{2,6},{3,7},{4,0},{5,1},{6,2},{7,3},{8,12},{9,13},{10,... | collective-permute-start | bytes 1572872 | tf_op jit(solution)/shard_map/ppermute | solution.py:39
  149.1 1.6 %copy-start.2 = (f32[32,128,128]{2,1,0:T(8,128)S(1)}, f32[32,128,128]{2,1,0:T(8,128)}, u32[]{:S(2)}) copy-start(f32[32,128,128]{2,1,0:T(8,128)} %shard_map.128.own_ref) | copy-start | bytes 6291460

commit v5 on v4

--- a/solution.py
+++ b/solution.py
@@ -348,7 +348,7 @@
     )(*parts)
 
 
-def add_ham(codes_ref, counts_ref, blocks_ref, copies, orbs, scale, ham, turned, scaled):
+def add_ham(table_ref, base, copies, orbs, scale, ham, turned, scaled):
     for e in range(LISTERS):
         for copy in copies[e]:
             copy.wait()
@@ -360,7 +360,7 @@
                 factors.append(jnp.broadcast_to(scale[:, at : at + TB], (TB, TB)).T)
             missing = UB * (UB - 1) // 2
             for i in range(BB):
-                block = blocks_ref[BAT_DEV * e + b, i]
+                block = table_ref[e, (2 + b) * TB + i]
                 missing = missing - block
                 turned[block, :, b * PTS : (b + 1) * PTS] = source[:, i * TB : (i + 1) * TB].T
                 for part in range(PTS // TB):
@@ -372,14 +372,14 @@
 
         def some_items(step, unused):
             for item in range(GROUP):
-                code = codes_ref[e, step * GROUP + item]
+                code = table_ref[e, base + step * GROUP + item]
                 tile = code & 255
                 i = (code >> 8) & 15
                 j = code >> 12
                 ham[tile] += jnp.dot(turned[i], scaled[j], preferred_element_type=F32)
             return unused
 
-        lax.fori_loop(0, counts_ref[e], some_items, 0)
+        lax.fori_loop(0, table_ref[e, base + LIST_LEN], some_items, 0)
 
 
 def potential_kernel(
@@ -417,7 +417,7 @@
     )(moments, far, near, trig, spread, weights, wave_high, wave_low)
 
 
-def ham_kernel(n_starts, n_outs, codes_ref, counts_ref, blocks_ref, scale_ref, *refs):
+def ham_kernel(n_starts, n_outs, base, table_ref, scale_ref, *refs):
     n_orbs = len(refs) - n_starts - n_outs - 5
     orb_refs, refs = refs[:n_orbs], refs[n_orbs:]
     starts, outs, (ham, turned, scaled, orbs, sems) = refs[:n_starts], refs[n_starts : n_starts + n_outs], refs[-5:]
@@ -434,18 +434,18 @@
             return unused
 
         lax.fori_loop(0, tiles, clear, 0)
-    add_ham(codes_ref, counts_ref, blocks_ref, copies, orbs, scale_ref[...], ham, turned, scaled)
+    add_ham(table_ref, base, copies, orbs, scale_ref[...], ham, turned, scaled)
     at = 0
     for out in outs:
         out[...] = ham[at : at + out.shape[0]].astype(out.dtype)
         at = at + out.shape[0]
 
 
-def ham_terms(codes, counts, blocks, scale, orbs, starts, outs, flops):
+def ham_terms(table, base, scale, orbs, starts, outs, flops):
     tiles = sum(count for count, unused in outs)
     return pl.pallas_call(
-        functools.partial(ham_kernel, len(starts), len(outs)),
-        in_specs=[SMEM_SPEC] * 3 + [VMEM_SPEC] + [ANY_SPEC] * (len(orbs) + len(starts)),
+        functools.partial(ham_kernel, len(starts), len(outs), base),
+        in_specs=[SMEM_SPEC, VMEM_SPEC] + [ANY_SPEC] * (len(orbs) + len(starts)),
         out_specs=[VMEM_SPEC] * len(outs),
         out_shape=[jax.ShapeDtypeStruct((count, TB, TB), dtype) for count, dtype in outs],
         scratch_shapes=[
@@ -457,7 +457,7 @@
         ],
         compiler_params=pltpu.CompilerParams(vmem_limit_bytes=56 * MIB),
         cost_estimate=pl.CostEstimate(flops=flops, bytes_accessed=10**4, transcendentals=0),
-    )(codes, counts, blocks, scale, *orbs, *starts)
+    )(table, scale, *orbs, *starts)
 
 
 def final_kernel(own_ref, x_ref, y_ref, out_ref):
@@ -497,16 +497,25 @@
     return listed, counts, at
 
 
-def lists_of(owners, slots, me):
+def table_of(lists, blocks):
+    parts = []
+    for listed, groups in lists:
+        part = jnp.concatenate([listed, groups[:, None]], axis=1)
+        parts.append(jnp.pad(part, ((0, 0), (0, TB - part.shape[1]))))
+    blocks = jnp.pad(blocks, ((0, 0), (0, TB - BB))).reshape(LISTERS, BAT_DEV * TB)
+    return jnp.concatenate(parts + [parts[-1]] * (2 - len(parts)) + [blocks], axis=1)
+
+
+def lists_of(owners, slots, me, apart):
     half = TILE_DEV // 2
     away = owners ^ me
     own = away == 0
     shared = ((away == X1) & (slots < half)) | ((away == Y1) & (slots >= half))
     found = []
-    for mine in (own | shared, own, shared):
-        place = jnp.where(own, slots, TILE_DEV + slots) if len(found) == 0 else slots
+    for mine in (own, shared) if apart else (own | shared,):
+        place = slots if apart else jnp.where(own, slots, TILE_DEV + slots)
         listed, counts, at = kept_of(mine, place)
-        dummy = PARTS if len(found) == 0 else TILE_DEV
+        dummy = TILE_DEV if apart else PARTS
         found.append((jnp.where(at[None] < counts[:, None], listed, dummy), (counts + GROUP - 1) // GROUP))
     return found
 
@@ -545,9 +554,6 @@
     half = TILE_DEV // 2
     tile_x, tile_y = swap(dens_tiles, X1), swap(dens_tiles, Y1)
     orb_x, orb_y = swap(sent, X3), swap(sent, Y3)
-    tile_low, tile_high = swap(tile_y[:half], X1), swap(tile_x[half:], Y1)
-    orb_first, orb_second = swap(orb_y[0], X3), swap(orb_x[1], Y3)
-    orbs = (orbitals, orb_x, orb_y, orb_first, orb_second)
 
     facts = jnp.stack(facts)
     coords = facts[:, :3].transpose(1, 0, 2).reshape(3, LIST_PTS)
@@ -558,7 +564,8 @@
     raw_weight = near_by[:, 1].reshape(LISTERS * BAT_DEV, NEAR)
     away = owners ^ me
     tmap = jnp.where((away & 10) == 0, ((away & 1) + ((away >> 2) & 1) * 2) * TILE_DEV + slots, NO_TILE)
-    codes, counts = lists_of(owners, slots, me)[0]
+    table = table_of(lists_of(owners, slots, me, False), blocks)
+    mate_table = table_of(lists_of(owners, slots, me ^ XY, True), blocks).astype(F32)
 
     wave_vecs = wave_table(KM)
     squared = jnp.sum(wave_vecs * wave_vecs, axis=0)
@@ -580,22 +587,26 @@
     spread = (envelope.reshape(ATOM_GRP, LISTERS * BAT_DEV, PTS) * share[:, :, None]).reshape(ATOM_GRP, LIST_PTS)
     wave_high, wave_low = wave_of_points(coords)
     first_tmap, first_blocks = tmap, blocks
-    early = (spread, weights, wave_high, wave_low, trig, codes, counts, tmap, blocks)
-
+
+    wave_high, wave_low, onward = lax.optimization_barrier((wave_high, wave_low, tile_y[:half]))
+    tile_low, tile_high = swap(onward, X1), swap(tile_x[half:], Y1)
+    orb_first, orb_second = swap(orb_y[0], X3), swap(orb_x[1], Y3)
+    orbs = (orbitals, orb_x, orb_y, orb_first, orb_second)
+    early = (spread, weights, wave_high, wave_low, trig, table, mate_table, tmap, blocks)
     tiles = (dens_tiles, tile_x, tile_y, tile_low, tile_high)
     before = first_density(first_tmap, first_blocks, tiles, orbs)
     early, late, *unused = lax.optimization_barrier((early, orbitals, before, tile_low, tile_high, orb_first, orb_second))
-    spread, weights, wave_high, wave_low, trig, codes, counts, tmap, blocks = early
+    spread, weights, wave_high, wave_low, trig, table, mate_table, tmap, blocks = early
     orb_far = swap(late, XY)
     part, orb_diag = density_and_moments(
-        tmap, blocks, tiles, orbs, before, spread, weights, wave_high, wave_low, trig, facts[:, 4]
+        tmap, blocks, tiles, orbs, before, spread, weights, wave_high, wave_low, trig, mate_table
     )
     a = ATOM_GRP
     got = swap(part, X3)
     order = (a + 1, a, a + 3, a + 2)
     part = part + jnp.concatenate([got[:a]] + [got[r : r + 1] for r in order] + [jnp.zeros((LISTERS, KM), F32)])
     got = swap(part, Y3)
-    density = part[a] + got[a + 2]
+    density_got = got[a + 2]
     moments, orb_far = lax.optimization_barrier((part[:a] + got[:a], orb_far))
     orb_far_x, orb_far_y = swap(orb_far, X3), swap(orb_far, Y3)
     got = swap(jnp.concatenate([moments, part[a + LISTERS :]]), X1)
@@ -603,14 +614,10 @@
     got = swap(jnp.concatenate([moments, got[a:]]), Y1)
     orb_diag, moments = lax.optimization_barrier((orb_diag, moments + got[:a]))
     orbs_far = (orb_far, orb_far_x, orb_far_y, swap(orb_diag, XY))
-    far_owners, far_slots, far_blocks = what_is_listed(got[a:])
-    unused, (own_codes, own_counts), (far_codes, far_counts) = lists_of(far_owners, far_slots, me)
+    far_table = got[a:].astype(jnp.int32)
     structure = jnp.sum(moments[:, :1] * trig, axis=0, keepdims=True)
     for bits in (1, 2, 4):
         structure = structure + swap_grp(structure, bits)
-    structure, own_codes, own_counts, far_codes, far_counts, far_blocks = lax.optimization_barrier(
-        (structure, own_codes, own_counts, far_codes, far_counts, far_blocks)
-    )
     structure = structure + swap_grp(structure, 8)
     potential, scale = potential_of(
         moments,
@@ -623,17 +630,14 @@
         wave_low,
     )
     far_scale = swap(scale, XY)
-    own, shared = ham_terms(
-        codes, counts, blocks, scale, orbs, (), ((TILE_DEV, F32), (TILE_DEV, F32)), 10**6
-    )
+    own, shared = ham_terms(table, 0, scale, orbs, (), ((TILE_DEV, F32), (TILE_DEV, F32)), 10**6)
     half = TILE_DEV // 2
     part_x, part_y = ham_terms(
-        far_codes, far_counts, far_blocks, far_scale, orbs_far, (shared,), ((half, BF16), (half, BF16)), 10**6
-    )
-    (own,) = ham_terms(
-        own_codes, own_counts, far_blocks, far_scale, orbs_far, (own,), ((TILE_DEV, F32),), 2 * 10**10
-    )
-    return (density, potential.reshape(-1), final_tiles(own, swap(part_x, X1), swap(part_y, Y1)))
+        far_table, TB, far_scale, orbs_far, (shared,), ((half, BF16), (half, BF16)), 10**6
+    )
+    (own,) = ham_terms(far_table, 0, far_scale, orbs_far, (own,), ((TILE_DEV, F32),), 2 * 10**10)
+    density, other, part_x = lax.optimization_barrier((part[a], density_got, part_x))
+    return (density + other, potential.reshape(-1), final_tiles(own, swap(part_x, X1), swap(part_y, Y1)))
 
 
 def solution(mesh):

time: 154 us -> 185 us (1.20)
  other arithmetic: 12.1 us -> 31.6 us
  local copies, waits for them, and re-layouts: 10.1 us -> 22.5 us
  starting transfers between devices: 46.5 us -> 39 us
  waiting for transfers between devices: 28.4 us -> 31 us
  Pallas kernels: 53.9 us -> 55.9 us
    ppermute x22, starting transfers between devices: 34.4 us -> 25.9 us  [swap(): return lax.ppermute(array, 'dev', [(d, d ^ bits) for d in range(16)])]
    sub x0 -> x3, local copies, waits for them, and re-layouts: none -> 3.94 us  [lists_of(): counts + GROUP - 1]
    reduce_sum x2, other arithmetic: 0.27 us -> 3.2 us  [kept_of(): counts = jnp.sum(mine.astype(jnp.int32), axis=1)]
    div x2, local copies, waits for them, and re-layouts: 0.16 us -> 2.56 us  [on_device(): partition = raw_weight / jnp.sum(raw_weight, axis=1, keepdims=True)]
    sub x0 -> x2, other arithmetic: none -> 2.39 us  [lists_of(): counts + GROUP - 1]
    concatenate x0 -> x3, other arithmetic: none -> 2.26 us  [table_of(): part = jnp.concatenate([listed, groups[:, None]], axis=1)]
    select_n x3, other arithmetic: 1.67 us -> 3.82 us  [lists_of(): (counts + GROUP - 1) // GROUP]
    pallas_call x3, Pallas kernels: 26.7 us -> 28.8 us  [ham_terms(): pl.pallas_call(functools.partial(ham_kernel, len(starts), len(outs), base...]
  transfers between devices with their start and end apart: 26 -> 26, of which waited for: 11 -> 10; matrix products, arithmetic and copies ran while one was open for 12% -> 27% of each run, Pallas kernels for 28% -> 25%
where the time goes in v5:
time: 185 us; the launch traced here: 182 us
  Pallas kernels  55.9 us (30%)
  starting transfers between devices  39 us (21%)
  other arithmetic  31.6 us (17%)
  waiting for transfers between devices  31 us (17%)
  local copies, waits for them, and re-layouts  22.5 us (12%)
    pallas_call x3, Pallas kernels, ham_terms(): pl.pallas_call(functools.partial(ham_kernel, len(starts), len(outs), base...  28.8 us
    ppermute x22, waiting for transfers between devices, swap(): return lax.ppermute(array, 'dev', [(d, d ^ bits) for d in range(16)])  26.4 us
    ppermute x22, starting transfers between devices, swap(): return lax.ppermute(array, 'dev', [(d, d ^ bits) for d in range(16)])  25.9 us
    ppermute x4, starting transfers between devices, swap_grp(): return lax.ppermute(array, 'grp', [(g, g ^ bits) for g in range(16)])  13 us
    pallas_call x1, Pallas kernels, first_density(): pl.pallas_call(first_density_kernel, in_specs=[SMEM_SPEC] * 2 + [ANY_SPEC...  8.71 us
    pallas_call x1, Pallas kernels, density_and_moments(): pl.pallas_call(density_kernel, in_specs=[SMEM_SPEC] * 2 + [ANY_SPEC] * 7...  7.19 us
    pallas_call x1, Pallas kernels, wave_of_points(): pl.pallas_call(wave_kernel, grid=(points // chunk,), in_specs=[pl.BlockSp...  5.69 us
    unnamed x54, local copies, waits for them, and re-layouts  5.56 us
  transfers between devices with their start and end apart: 26, of which 10 were waited for; matrix products, arithmetic and copies ran while one was open for 27% of the time, Pallas kernels for 25%

profile of v5, /device:TPU:2, one launch (start us, length us, event | category | flops | bytes accessed | tf_op | source)
XLA Modules:
  0.0 182.1 jit_solution(5588541778660194716)
XLA Ops:
  0.6 1.4 shard_map.122
  2.1 1.6 collective-permute-start
  3.7 3.0 %collective-permute-start.1 = (f32[6,512]{1,0:T(8,128)}, f32[6,512]{1,0:T(8,128)S(1)}, u32[]{:S(2)}, u32[]{:S(2)}) collective-permute-start(f32[6,512]{1,0:T(8,128)} %shard_map.122), channel_id=1, source_target_pairs={{0,12},{1,13},{2,14},{3,15},{4,8},{5,9},{6,10},{7,11},{8,4},{9,5},... | collective-permute-start | bytes 36872 | tf_op jit(solution)/shard_map/ppermute | solution.py:39
  7.2 3.1 %collective-permute-start.4 = (bf16[32,128,128]{2,1,0:T(8,128)(2,1)}, bf16[32,128,128]{2,1,0:T(8,128)(2,1)}, u32[]{:S(2)}, u32[]{:S(2)}) collective-permute-start(bf16[32,128,128]{2,1,0:T(8,128)(2,1)} %own_tile.3), channel_id=1, source_target_pairs={{0,1},{1,0},{2,3},{3,2},{4,5},{5,4},{6,7},{7,6},{8,9},{9,8},{10,11... | collective-permute-start | bytes 3145736 | tf_op jit(solution)/shard_map/ppermute | solution.py:39
  16.1 2.7 %collective-permute-start.8 = (bf16[2,256,1024]{2,1,0:T(8,128)(2,1)}, bf16[2,256,1024]{2,1,0:T(8,128)(2,1)S(1)}, u32[]{:S(2)}, u32[]{:S(2)}) collective-permute-start(bf16[2,256,1024]{2,1,0:T(8,128)(2,1)} %refs_0_.1), channel_id=1, source_target_pairs={{0,12},{1,13},{2,14},{3,15},{4,8},{5,9},{6,10},{7,11},{8,4},{9,5},... | collective-permute-start | bytes 3145736 | tf_op jit(solution)/shard_map/ppermute | solution.py:39
  21.3 1.9 %convert_reduce_fusion.3 = (s32[4]{0:T(128)}, pred[4,81]{1,0:T(4,128)(4,1)}, pred[4,81]{1,0:T(4,128)(4,1)S(1)}, pred[4,81]{1,0:T(4,128)(4,1)S(1)}, s32[4,81]{1,0...) fusion(s32[]{:T(128)S(6)} %xor.19, s32[4,512]{1,0:T(4,128)S(1)} %get-tuple-element.94, s32[81]{0:T(128)} %fusion.24, ...), kind=kLoop, calls=%fused_computation.79 | loop fusion | flops 5828 | bytes 7152 | tf_op jit(solution)/shard_map/reduce_sum | solution.py:493
  23.2 1.3 convert_reduce_fusion.4
  24.5 1.3 copy.46
  25.8 1.4 copy.51
  27.2 1.3 copy.56
  29.6 1.6 select_reduce_fusion.1
  31.2 1.3 fusion.13
  33.7 1.3 copy.47
  36.3 1.3 fusion.15
  37.6 1.3 copy.52
  41.4 1.3 fusion.17
  42.7 1.3 copy.57
  46.5 1.4 broadcast_divide_fusion
  47.9 1.3 copy.44
  49.2 1.3 copy.42
  57.0 5.7 %shard_map.123 = (bf16[512,2048]{1,0:T(8,128)(2,1)}, bf16[512,2048]{1,0:T(8,128)(2,1)}) custom-call(f32[48,2048]{1,0:T(8,128)} %bitcast.56), custom_call_target="tpu_custom_call" | custom-call | flops 8388608 | bytes 4194304 | tf_op jit(solution)/shard_map/pallas_call | solution.py:87
  65.6 1.9 %slice.127 = bf16[16,128,128]{2,1,0:T(8,128)(2,1)} slice(bf16[32,128,128]{2,1,0:T(8,128)(2,1)} %collective-permute-done.4.x_tile), slice={[16:32], [0:128], [0:128]} | slice | bytes 1048576 | tf_op jit(solution)/shard_map/slice | solution.py:592
  67.5 1.4 collective-permute-start.6
  71.5 1.3 collective-permute-start.9
  72.8 4.4 %collective-permute-done.5.low_tile = bf16[16,128,128]{2,1,0:T(8,128)(2,1)} collective-permute-done((bf16[16,128,128]{2,1,0:T(8,128)(2,1)}, bf16[16,128,128]{2,1,0:T(8,128)(2,1)}, u32[]{:S(2)}, u32[]{:S(2)}) %collective-permute-start.5) | collective-permute-done | bytes 524320 | tf_op jit(solution)/shard_map/ppermute | solution.py:39
  77.3 2.5 %collective-permute-done.6.high_tile = bf16[16,128,128]{2,1,0:T(8,128)(2,1)} collective-permute-done((bf16[16,128,128]{2,1,0:T(8,128)(2,1)}, bf16[16,128,128]{2,1,0:T(8,128)(2,1)}, u32[]{:S(2)}, u32[]{:S(2)}) %collective-permute-start.6) | collective-permute-done | bytes 524320 | tf_op jit(solution)/shard_map/ppermute | solution.py:39
  79.8 8.7 %shard_map.124.before_ref = f32[8,256]{1,0:T(8,128)} custom-call(s32[4,81]{1,0:T(4,128)} %get-tuple-element.50.tmap_ref, s32[8,8]{1,0:T(8,128)} %bitcast.62, bf16[32,128,128]{2,1,0:T(8,128)(2,1)} %own_tile.3, bf16[32,128,128]{2,1,0:T(8,128)(2,1)} %collective-permute-done.4.x_tile, bf16[32,128,128]{2,1,0:T(8,128)(2,1)} %copy-done.8, ...), custom_call_target="tpu_custom_call" | custom-call | flops 20000000000 | bytes 10000 | tf_op jit(solution)/shard_map/pallas_call | solution.py:178
  88.6 2.0 %collective-permute-start.13 = (bf16[2,256,1024]{2,1,0:T(8,128)(2,1)}, bf16[2,256,1024]{2,1,0:T(8,128)(2,1)S(1)}, u32[]{:S(2)}, u32[]{:S(2)}) collective-permute-start(bf16[2,256,1024]{2,1,0:T(8,128)(2,1)} %refs_0_.1), channel_id=1, source_target_pairs={{0,5},{1,4},{2,7},{3,6},{4,1},{5,0},{6,3},{7,2},{8,13},{9,12},{10,... | collective-permute-start | bytes 3145736 | tf_op jit(solution)/shard_map/ppermute | solution.py:39
  90.6 7.2 %shard_map.125 = (f32[24,512]{1,0:T(8,128)}, bf16[2,256,1024]{2,1,0:T(8,128)(2,1)}) custom-call(s32[4,81]{1,0:T(4,128)} %get-tuple-element.50.tmap_ref, s32[8,8]{1,0:T(8,128)} %bitcast.63, bf16[32,128,128]{2,1,0:T(8,128)(2,1)} %own_tile.3, bf16[32,128,128]{2,1,0:T(8,128)(2,1)} %collective-permute-done.4.x_tile, bf16[32,128,128]{2,1,0:T(8,128)(2,1)} %copy-done.8, ...), custom_call_target="tpu_custom_call" | custom-call | flops 1000000 | bytes 10000 | tf_op jit(solution)/shard_map/pallas_call | solution.py:276
  98.3 3.9 %collective-permute-done.11 = f32[24,512]{1,0:T(8,128)S(1)} collective-permute-done((f32[24,512]{1,0:T(8,128)}, f32[24,512]{1,0:T(8,128)S(1)}, u32[]{:S(2)}, u32[]{:S(2)}) %collective-permute-start.11) | collective-permute-done | bytes 49184 | tf_op jit(solution)/shard_map/ppermute | solution.py:39
  104.0 4.4 %collective-permute-done.12 = f32[24,512]{1,0:T(8,128)S(1)} collective-permute-done((f32[24,512]{1,0:T(8,128)S(1)}, f32[24,512]{1,0:T(8,128)S(1)}, u32[]{:S(2)}, u32[]{:S(2)}) %collective-permute-start.12) | collective-permute-done | bytes 49184 | tf_op jit(solution)/shard_map/ppermute | solution.py:39
  108.4 4.4 %collective-permute-done.13.refs_0_ = bf16[2,256,1024]{2,1,0:T(8,128)(2,1)S(1)} collective-permute-done((bf16[2,256,1024]{2,1,0:T(8,128)(2,1)}, bf16[2,256,1024]{2,1,0:T(8,128)(2,1)S(1)}, u32[]{:S(2)}, u32[]{:S(2)}) %collective-permute-start.13) | collective-permute-done | bytes 1048608 | tf_op jit(solution)/shard_map/ppermute | solution.py:39
  113.8 3.2 %collective-permute-done.14 = f32[20,512]{1,0:T(8,128)S(1)} collective-permute-done((f32[20,512]{1,0:T(8,128)S(1)}, f32[20,512]{1,0:T(8,128)S(1)}, u32[]{:S(2)}, u32[]{:S(2)}) %collective-permute-start.14) | collective-permute-done | bytes 40992 | tf_op jit(solution)/shard_map/ppermute | solution.py:39
  117.8 3.4 %collective-permute-done.15 = f32[20,512]{1,0:T(8,128)S(1)} collective-permute-done((f32[20,512]{1,0:T(8,128)S(1)}, f32[20,512]{1,0:T(8,128)S(1)}, u32[]{:S(2)}, u32[]{:S(2)}) %collective-permute-start.15) | collective-permute-done | bytes 40992 | tf_op jit(solution)/shard_map/ppermute | solution.py:39
  122.5 1.4 collective-permute-start.23
  123.9 2.8 %collective-permute-start.17 = (f32[1,512]{1,0:T(1,128)S(1)}, f32[1,512]{1,0:T(1,128)S(1)}, u32[]{:S(2)}, u32[]{:S(2)}) collective-permute-start(f32[1,512]{1,0:T(1,128)S(1)} %add.234), channel_id=1, source_target_pairs={{0,32},{16,48},{32,0},{48,16},{64,96},{80,112},{96,64},{112,80},{1... | collective-permute-start | bytes 6152 | tf_op jit(solution)/shard_map/ppermute | solution.py:43
  126.6 1.6 collective-permute-done.17
  128.2 3.4 %collective-permute-start.18 = (f32[1,512]{1,0:T(1,128)S(1)}, f32[1,512]{1,0:T(1,128)S(1)}, u32[]{:S(2)}, u32[]{:S(2)}) collective-permute-start(f32[1,512]{1,0:T(1,128)S(1)} %add.235), channel_id=1, source_target_pairs={{0,64},{16,80},{32,96},{48,112},{64,0},{80,16},{96,32},{112,48},{1... | collective-permute-start | bytes 6152 | tf_op jit(solution)/shard_map/ppermute | solution.py:43
  131.6 1.6 collective-permute-done.18
  133.2 6.8 %collective-permute-start.19 = (f32[1,512]{1,0:T(1,128)S(1)}, f32[1,512]{1,0:T(1,128)S(1)}, u32[]{:S(2)}, u32[]{:S(2)}) collective-permute-start(f32[1,512]{1,0:T(1,128)S(1)} %add.236), channel_id=1, source_target_pairs={{0,128},{16,144},{32,160},{48,176},{64,192},{80,208},{96,224},{112... | collective-permute-start | bytes 6152 | tf_op jit(solution)/shard_map/ppermute | solution.py:43
  140.1 1.5 collective-permute-done.19
  141.6 1.6 copy-done.1
  145.7 11.2 %shard_map.127 = (f32[32,128,128]{2,1,0:T(8,128)}, f32[32,128,128]{2,1,0:T(8,128)}) custom-call(s32[4,512]{1,0:T(4,128)} %get-tuple-element.66.table_ref, f32[1,2048]{1,0:T(1,128)} %copy-done.5, bf16[2,256,1024]{2,1,0:T(8,128)(2,1)} %refs_0_.1, bf16[2,256,1024]{2,1,0:T(8,128)(2,1)} %copy-done.6, bf16[2,256,1024]{2,1,0:T(8,128)(2,1)} %copy-done.7, ...), custom_call_target="tpu_custom_call" | custom-call | flops 1000000 | bytes 10000 | tf_op jit(solution)/shard_map/pallas_call | solution.py:446
  158.6 7.5 %shard_map.128 = (bf16[16,128,128]{2,1,0:T(8,128)(2,1)}, bf16[16,128,128]{2,1,0:T(8,128)(2,1)}) custom-call(s32[4,512]{1,0:T(4,128)} %slice_convert_fusion.table_ref, f32[1,2048]{1,0:T(1,128)} %copy-done.20, bf16[2,256,1024]{2,1,0:T(8,128)(2,1)} %copy-done.11, bf16[2,256,1024]{2,1,0:T(8,128)(2,1)} %copy-done.12, bf16[2,256,1024]{2,1,0:T(8,128)(2,1)} %copy-done.13, ...), custom_call_target="tpu_custom_call" | custom-call | flops 1000000 | bytes 10000 | tf_op jit(solution)/shard_map/pallas_call | solution.py:446
  166.1 2.0 %collective-permute-start.24 = (bf16[16,128,128]{2,1,0:T(8,128)(2,1)}, bf16[16,128,128]{2,1,0:T(8,128)(2,1)S(1)}, u32[]{:S(2)}, u32[]{:S(2)}) collective-permute-start(bf16[16,128,128]{2,1,0:T(8,128)(2,1)} %get-tuple-element.73), channel_id=1, source_target_pairs={{0,1},{1,0},{2,3},{3,2},{4,5},{5,4},{6,7},{7,6},{8,9},{9,8},{10,11... | collective-permute-start | bytes 1572872 | tf_op jit(solution)/shard_map/ppermute | solution.py:39
  168.1 10.1 %shard_map.129.own_ref = f32[32,128,128]{2,1,0:T(8,128)} custom-call(s32[4,512]{1,0:T(4,128)} %slice_convert_fusion.table_ref, f32[1,2048]{1,0:T(1,128)} %copy-done.20, bf16[2,256,1024]{2,1,0:T(8,128)(2,1)} %copy-done.11, bf16[2,256,1024]{2,1,0:T(8,128)(2,1)} %copy-done.12, bf16[2,256,1024]{2,1,0:T(8,128)(2,1)} %copy-done.13, ...), custom_call_target="tpu_custom_call" | custom-call | flops 20000000000 | bytes 10000 | tf_op jit(solution)/shard_map/pallas_call | solution.py:446
  178.8 1.6 copy-done.2
  180.4 1.7 shard_map.130
  (150 shorter events, 39.2 us)
Async XLA Ops:
  2.1 12.9 %collective-permute-start = (f32[6,512]{1,0:T(8,128)}, f32[6,512]{1,0:T(8,128)S(1)}, u32[]{:S(2)}, u32[]{:S(2)}) collective-permute-start(f32[6,512]{1,0:T(8,128)} %shard_map.122), channel_id=1, source_target_pairs={{0,3},{1,2},{2,1},{3,0},{4,7},{5,6},{6,5},{7,4},{8,11},{9,10},{10,... | collective-permute-start | bytes 36872 | tf_op jit(solution)/shard_map/ppermute | solution.py:39
  3.7 11.3 %collective-permute-start.1 = (f32[6,512]{1,0:T(8,128)}, f32[6,512]{1,0:T(8,128)S(1)}, u32[]{:S(2)}, u32[]{:S(2)}) collective-permute-start(f32[6,512]{1,0:T(8,128)} %shard_map.122), channel_id=1, source_target_pairs={{0,12},{1,13},{2,14},{3,15},{4,8},{5,9},{6,10},{7,11},{8,4},{9,5},... | collective-permute-start | bytes 36872 | tf_op jit(solution)/shard_map/ppermute | solution.py:39
  6.7 8.3 %collective-permute-start.2 = (f32[6,512]{1,0:T(8,128)}, f32[6,512]{1,0:T(8,128)S(1)}, u32[]{:S(2)}, u32[]{:S(2)}) collective-permute-start(f32[6,512]{1,0:T(8,128)} %shard_map.122), channel_id=1, source_target_pairs={{0,15},{1,14},{2,13},{3,12},{4,11},{5,10},{6,9},{7,8},{8,7},{9,6},... | collective-permute-start | bytes 36872 | tf_op jit(solution)/shard_map/ppermute | solution.py:39
  6.9 57.2 %collective-permute-start.3 = (bf16[32,128,128]{2,1,0:T(8,128)(2,1)}, bf16[32,128,128]{2,1,0:T(8,128)(2,1)S(1)}, u32[]{:S(2)}, u32[]{:S(2)}) collective-permute-start(bf16[32,128,128]{2,1,0:T(8,128)(2,1)} %own_tile.3), channel_id=1, source_target_pairs={{0,4},{1,5},{2,6},{3,7},{4,0},{5,1},{6,2},{7,3},{8,12},{9,13},{10,... | collective-permute-start | bytes 3145736 | tf_op jit(solution)/shard_map/ppermute | solution.py:39
  7.2 58.3 %collective-permute-start.4 = (bf16[32,128,128]{2,1,0:T(8,128)(2,1)}, bf16[32,128,128]{2,1,0:T(8,128)(2,1)}, u32[]{:S(2)}, u32[]{:S(2)}) collective-permute-start(bf16[32,128,128]{2,1,0:T(8,128)(2,1)} %own_tile.3), channel_id=1, source_target_pairs={{0,1},{1,0},{2,3},{3,2},{4,5},{5,4},{6,7},{7,6},{8,9},{9,8},{10,11... | collective-permute-start | bytes 3145736 | tf_op jit(solution)/shard_map/ppermute | solution.py:39
  12.6 1.2 copy-start.22
  12.6 2.4 %copy-start.17 = (f32[6,512]{1,0:T(8,128)S(1)}, f32[6,512]{1,0:T(8,128)}, u32[]{:S(2)}) copy-start(f32[6,512]{1,0:T(8,128)} %shard_map.122) | copy-start | bytes 36868
  15.2 55.5 %collective-permute-start.7 = (bf16[2,256,1024]{2,1,0:T(8,128)(2,1)}, bf16[2,256,1024]{2,1,0:T(8,128)(2,1)S(1)}, u32[]{:S(2)}, u32[]{:S(2)}) collective-permute-start(bf16[2,256,1024]{2,1,0:T(8,128)(2,1)} %refs_0_.1), channel_id=1, source_target_pairs={{0,3},{1,2},{2,1},{3,0},{4,7},{5,6},{6,5},{7,4},{8,11},{9,10},{10,... | collective-permute-start | bytes 3145736 | tf_op jit(solution)/shard_map/ppermute | solution.py:39
  16.1 55.4 %collective-permute-start.8 = (bf16[2,256,1024]{2,1,0:T(8,128)(2,1)}, bf16[2,256,1024]{2,1,0:T(8,128)(2,1)S(1)}, u32[]{:S(2)}, u32[]{:S(2)}) collective-permute-start(bf16[2,256,1024]{2,1,0:T(8,128)(2,1)} %refs_0_.1), channel_id=1, source_target_pairs={{0,12},{1,13},{2,14},{3,15},{4,8},{5,9},{6,10},{7,11},{8,4},{9,5},... | collective-permute-start | bytes 3145736 | tf_op jit(solution)/shard_map/ppermute | solution.py:39
  20.0 0.6 copy-start.15
  64.0 7.5 %copy-start.8 = (bf16[32,128,128]{2,1,0:T(8,128)(2,1)}, bf16[32,128,128]{2,1,0:T(8,128)(2,1)S(1)}, u32[]{:S(2)}) copy-start(bf16[32,128,128]{2,1,0:T(8,128)(2,1)S(1)} %collective-permute-done.3.y_tile) | copy-start | bytes 3145732
  65.0 12.3 %collective-permute-start.5 = (bf16[16,128,128]{2,1,0:T(8,128)(2,1)}, bf16[16,128,128]{2,1,0:T(8,128)(2,1)}, u32[]{:S(2)}, u32[]{:S(2)}) collective-permute-start(bf16[16,128,128]{2,1,0:T(8,128)(2,1)} %slice.123), channel_id=1, source_target_pairs={{0,1},{1,0},{2,3},{3,2},{4,5},{5,4},{6,7},{7,6},{8,9},{9,8},{10,11... | collective-permute-start | bytes 1572872 | tf_op jit(solution)/shard_map/ppermute | solution.py:39
  67.5 12.3 %collective-permute-start.6 = (bf16[16,128,128]{2,1,0:T(8,128)(2,1)}, bf16[16,128,128]{2,1,0:T(8,128)(2,1)}, u32[]{:S(2)}, u32[]{:S(2)}) collective-permute-start(bf16[16,128,128]{2,1,0:T(8,128)(2,1)} %slice.127), channel_id=1, source_target_pairs={{0,4},{1,5},{2,6},{3,7},{4,0},{5,1},{6,2},{7,3},{8,12},{9,13},{10,... | collective-permute-start | bytes 1572872 | tf_op jit(solution)/shard_map/ppermute | solution.py:39
  70.7 9.1 %copy-start.6 = (bf16[2,256,1024]{2,1,0:T(8,128)(2,1)}, bf16[2,256,1024]{2,1,0:T(8,128)(2,1)S(1)}, u32[]{:S(2)}) copy-start(bf16[2,256,1024]{2,1,0:T(8,128)(2,1)S(1)} %collective-permute-done.7.x_orb.refs_1_) | copy-start | bytes 3145732
  70.8 17.7 %collective-permute-start.10 = (bf16[256,1024]{1,0:T(8,128)(2,1)S(1)}, bf16[256,1024]{1,0:T(8,128)(2,1)S(1)}, u32[]{:S(2)}, u32[]{:S(2)}) collective-permute-start(bf16[256,1024]{1,0:T(8,128)(2,1)S(1)} %slice_bitcast_fusion), channel_id=1, source_target_pairs={{0,12},{1,13},{2,14},{3,15},{4,8},{5,9},{6,10},{7,11},{8,4},{9,5},... | collective-permute-start | bytes 1572872 | tf_op jit(solution)/shard_map/ppermute | solution.py:39
  71.5 8.3 %copy-start.7 = (bf16[2,256,1024]{2,1,0:T(8,128)(2,1)}, bf16[2,256,1024]{2,1,0:T(8,128)(2,1)S(1)}, u32[]{:S(2)}) copy-start(bf16[2,256,1024]{2,1,0:T(8,128)(2,1)S(1)} %collective-permute-done.8.y_orb.refs_2_) | copy-start | bytes 3145732
  71.5 17.0 %collective-permute-start.9 = (bf16[256,1024]{1,0:T(8,128)(2,1)S(1)}, bf16[256,1024]{1,0:T(8,128)(2,1)S(1)}, u32[]{:S(2)}, u32[]{:S(2)}) collective-permute-start(bf16[256,1024]{1,0:T(8,128)(2,1)S(1)} %slice_bitcast_fusion.1), channel_id=1, source_target_pairs={{0,3},{1,2},{2,1},{3,0},{4,7},{5,6},{6,5},{7,4},{8,11},{9,10},{10,... | collective-permute-start | bytes 1572872 | tf_op jit(solution)/shard_map/ppermute | solution.py:39
  88.5 2.1 %copy-start.9 = (bf16[256,1024]{1,0:T(8,128)(2,1)}, bf16[256,1024]{1,0:T(8,128)(2,1)S(1)}, u32[]{:S(2)}) copy-start(bf16[256,1024]{1,0:T(8,128)(2,1)S(1)} %collective-permute-done.10.second_orb.refs_4_) | copy-start | bytes 1572868
  88.6 2.1 %copy-start.10 = (bf16[256,1024]{1,0:T(8,128)(2,1)}, bf16[256,1024]{1,0:T(8,128)(2,1)S(1)}, u32[]{:S(2)}) copy-start(bf16[256,1024]{1,0:T(8,128)(2,1)S(1)} %collective-permute-done.9.first_orb.refs_3_) | copy-start | bytes 1572868
  88.6 32.8 %copy-start.4 = (f32[16,512]{1,0:T(8,128)S(1)}, f32[16,512]{1,0:T(8,128)}, u32[]{:S(2)}) copy-start(f32[16,512]{1,0:T(8,128)} %pad_maximum_fusion.4.trig_ref) | copy-start | bytes 98308
  88.6 32.9 %copy-start.18 = (s32[1,256]{1,0:T(1,128)S(1)}, s32[1,256]{1,0:T(1,128)}, u32[]{:S(2)}) copy-start(s32[1,256]{1,0:T(1,128)} %get-tuple-element.118) | copy-start | bytes 3076
  88.6 32.9 %copy-start.19 = (s32[1,256]{1,0:T(1,128)S(1)}, s32[1,256]{1,0:T(1,128)}, u32[]{:S(2)}) copy-start(s32[1,256]{1,0:T(1,128)} %get-tuple-element.119) | copy-start | bytes 3076
  88.6 32.9 %copy-start.21 = (s32[1,256]{1,0:T(1,128)S(1)}, s32[1,256]{1,0:T(1,128)}, u32[]{:S(2)}) copy-start(s32[1,256]{1,0:T(1,128)} %and_select_fusion.3) | copy-start | bytes 3076
  88.6 51.4 %copy-start.16 = (f32[8,256]{1,0:T(8,128)S(1)}, f32[8,256]{1,0:T(8,128)}, u32[]{:S(2)}) copy-start(f32[8,256]{1,0:T(8,128)} %reshape_squeeze.12.weights_ref) | copy-start | bytes 24580
  88.6 52.9 %copy-start.3 = (f32[16,2048]{1,0:T(8,128)S(1)}, f32[16,2048]{1,0:T(8,128)}, u32[]{:S(2)}) copy-start(f32[16,2048]{1,0:T(8,128)} %exponential_multiply_fusion.spread_ref) | copy-start | bytes 393220
  88.6 24.2 %collective-permute-start.13 = (bf16[2,256,1024]{2,1,0:T(8,128)(2,1)}, bf16[2,256,1024]{2,1,0:T(8,128)(2,1)S(1)}, u32[]{:S(2)}, u32[]{:S(2)}) collective-permute-start(bf16[2,256,1024]{2,1,0:T(8,128)(2,1)} %refs_0_.1), channel_id=1, source_target_pairs={{0,5},{1,4},{2,7},{3,6},{4,1},{5,0},{6,3},{7,2},{8,13},{9,12},{10,... | collective-permute-start | bytes 3145736 | tf_op jit(solution)/shard_map/ppermute | solution.py:39
  90.6 51.0 %copy-start = (bf16[512,2048]{1,0:T(8,128)(2,1)S(1)}, bf16[512,2048]{1,0:T(8,128)(2,1)}, u32[]{:S(2)}) copy-start(bf16[512,2048]{1,0:T(8,128)(2,1)} %get-tuple-element.54.high_hbm.high_ref) | copy-start | bytes 6291460
  97.8 4.4 %collective-permute-start.11 = (f32[24,512]{1,0:T(8,128)}, f32[24,512]{1,0:T(8,128)S(1)}, u32[]{:S(2)}, u32[]{:S(2)}) collective-permute-start(f32[24,512]{1,0:T(8,128)} %get-tuple-element.58), channel_id=1, source_target_pairs={{0,3},{1,2},{2,1},{3,0},{4,7},{5,6},{6,5},{7,4},{8,11},{9,10},{10,... | collective-permute-start | bytes 147464 | tf_op jit(solution)/shard_map/ppermute | solution.py:39
  103.1 5.3 %collective-permute-start.12 = (f32[24,512]{1,0:T(8,128)S(1)}, f32[24,512]{1,0:T(8,128)S(1)}, u32[]{:S(2)}, u32[]{:S(2)}) collective-permute-start(f32[24,512]{1,0:T(8,128)S(1)} %add.229), channel_id=1, source_target_pairs={{0,12},{1,13},{2,14},{3,15},{4,8},{5,9},{6,10},{7,11},{8,4},{9,5},... | collective-permute-start | bytes 147464 | tf_op jit(solution)/shard_map/ppermute | solution.py:39
  112.8 31.5 %copy-start.11 = (bf16[2,256,1024]{2,1,0:T(8,128)(2,1)}, bf16[2,256,1024]{2,1,0:T(8,128)(2,1)S(1)}, u32[]{:S(2)}) copy-start(bf16[2,256,1024]{2,1,0:T(8,128)(2,1)S(1)} %collective-permute-done.13.refs_0_) | copy-start | bytes 3145732
  112.8 4.2 %collective-permute-start.14 = (f32[20,512]{1,0:T(8,128)S(1)}, f32[20,512]{1,0:T(8,128)S(1)}, u32[]{:S(2)}, u32[]{:S(2)}) collective-permute-start(f32[20,512]{1,0:T(8,128)S(1)} %pad_maximum_fusion.2), channel_id=1, source_target_pairs={{0,1},{1,0},{2,3},{3,2},{4,5},{5,4},{6,7},{7,6},{8,9},{9,8},{10,11... | collective-permute-start | bytes 122888 | tf_op jit(solution)/shard_map/ppermute | solution.py:39
  117.0 4.2 %collective-permute-start.15 = (f32[20,512]{1,0:T(8,128)S(1)}, f32[20,512]{1,0:T(8,128)S(1)}, u32[]{:S(2)}, u32[]{:S(2)}) collective-permute-start(f32[20,512]{1,0:T(8,128)S(1)} %pad_maximum_fusion.3), channel_id=1, source_target_pairs={{0,4},{1,5},{2,6},{3,7},{4,0},{5,1},{6,2},{7,3},{8,12},{9,13},{10,... | collective-permute-start | bytes 122888 | tf_op jit(solution)/shard_map/ppermute | solution.py:39
  121.4 2.4 %collective-permute-start.16 = (f32[1,512]{1,0:T(1,128)S(1)}, f32[1,512]{1,0:T(1,128)S(1)}, u32[]{:S(2)}, u32[]{:S(2)}) collective-permute-start(f32[1,512]{1,0:T(1,128)S(1)} %bitcast.66), channel_id=1, source_target_pairs={{0,16},{16,0},{32,48},{48,32},{64,80},{80,64},{96,112},{112,96},{1... | collective-permute-start | bytes 6152 | tf_op jit(solution)/shard_map/ppermute | solution.py:43
  121.5 35.3 %collective-permute-start.21 = (bf16[2,256,1024]{2,1,0:T(8,128)(2,1)S(1)}, bf16[2,256,1024]{2,1,0:T(8,128)(2,1)S(1)}, u32[]{:S(2)}, u32[]{:S(2)}) collective-permute-start(bf16[2,256,1024]{2,1,0:T(8,128)(2,1)S(1)} %collective-permute-done.13.refs_0_), channel_id=1, source_target_pairs={{0,3},{1,2},{2,1},{3,0},{4,7},{5,6},{6,5},{7,4},{8,11},{9,10},{10,... | collective-permute-start | bytes 3145736 | tf_op jit(solution)/shard_map/ppermute | solution.py:39
  121.6 35.3 %collective-permute-start.22 = (bf16[2,256,1024]{2,1,0:T(8,128)(2,1)S(1)}, bf16[2,256,1024]{2,1,0:T(8,128)(2,1)S(1)}, u32[]{:S(2)}, u32[]{:S(2)}) collective-permute-start(bf16[2,256,1024]{2,1,0:T(8,128)(2,1)S(1)} %collective-permute-done.13.refs_0_), channel_id=1, source_target_pairs={{0,12},{1,13},{2,14},{3,15},{4,8},{5,9},{6,10},{7,11},{8,4},{9,5},... | collective-permute-start | bytes 3145736 | tf_op jit(solution)/shard_map/ppermute | solution.py:39
  122.5 34.5 %collective-permute-start.23 = (bf16[2,256,1024]{2,1,0:T(8,128)(2,1)}, bf16[2,256,1024]{2,1,0:T(8,128)(2,1)S(1)}, u32[]{:S(2)}, u32[]{:S(2)}) collective-permute-start(bf16[2,256,1024]{2,1,0:T(8,128)(2,1)} %get-tuple-element.65), channel_id=1, source_target_pairs={{0,5},{1,4},{2,7},{3,6},{4,1},{5,0},{6,3},{7,2},{8,13},{9,12},{10,... | collective-permute-start | bytes 3145736 | tf_op jit(solution)/shard_map/ppermute | solution.py:39
  123.9 4.3 %collective-permute-start.17 = (f32[1,512]{1,0:T(1,128)S(1)}, f32[1,512]{1,0:T(1,128)S(1)}, u32[]{:S(2)}, u32[]{:S(2)}) collective-permute-start(f32[1,512]{1,0:T(1,128)S(1)} %add.234), channel_id=1, source_target_pairs={{0,32},{16,48},{32,0},{48,16},{64,96},{80,112},{96,64},{112,80},{1... | collective-permute-start | bytes 6152 | tf_op jit(solution)/shard_map/ppermute | solution.py:43
  128.2 5.0 %collective-permute-start.18 = (f32[1,512]{1,0:T(1,128)S(1)}, f32[1,512]{1,0:T(1,128)S(1)}, u32[]{:S(2)}, u32[]{:S(2)}) collective-permute-start(f32[1,512]{1,0:T(1,128)S(1)} %add.235), channel_id=1, source_target_pairs={{0,64},{16,80},{32,96},{48,112},{64,0},{80,16},{96,32},{112,48},{1... | collective-permute-start | bytes 6152 | tf_op jit(solution)/shard_map/ppermute | solution.py:43
  133.2 8.4 %collective-permute-start.19 = (f32[1,512]{1,0:T(1,128)S(1)}, f32[1,512]{1,0:T(1,128)S(1)}, u32[]{:S(2)}, u32[]{:S(2)}) collective-permute-start(f32[1,512]{1,0:T(1,128)S(1)} %add.236), channel_id=1, source_target_pairs={{0,128},{16,144},{32,160},{48,176},{64,192},{80,208},{96,224},{112... | collective-permute-start | bytes 6152 | tf_op jit(solution)/shard_map/ppermute | solution.py:43
  141.6 1.6 copy-start.1
  144.4 1.3 copy-start.5
  144.4 12.5 %collective-permute-start.20 = (f32[1,2048]{1,0:T(1,128)S(1)}, f32[1,2048]{1,0:T(1,128)S(1)}, u32[]{:S(2)}, u32[]{:S(2)}) collective-permute-start(f32[1,2048]{1,0:T(1,128)S(1)} %get-tuple-element.63.scale_ref), channel_id=1, source_target_pairs={{0,5},{1,4},{2,7},{3,6},{4,1},{5,0},{6,3},{7,2},{8,13},{9,12},{10,... | collective-permute-start | bytes 24584 | tf_op jit(solution)/shard_map/ppermute | solution.py:39
  156.9 1.0 copy-start.12
  156.9 1.3 copy-start.13
  156.9 1.6 copy-start.14
  166.1 12.8 %collective-permute-start.24 = (bf16[16,128,128]{2,1,0:T(8,128)(2,1)}, bf16[16,128,128]{2,1,0:T(8,128)(2,1)S(1)}, u32[]{:S(2)}, u32[]{:S(2)}) collective-permute-start(bf16[16,128,128]{2,1,0:T(8,128)(2,1)} %get-tuple-element.73), channel_id=1, source_target_pairs={{0,1},{1,0},{2,3},{3,2},{4,5},{5,4},{6,7},{7,6},{8,9},{9,8},{10,11... | collective-permute-start | bytes 1572872 | tf_op jit(solution)/shard_map/ppermute | solution.py:39
  168.1 10.7 %collective-permute-start.25 = (bf16[16,128,128]{2,1,0:T(8,128)(2,1)}, bf16[16,128,128]{2,1,0:T(8,128)(2,1)S(1)}, u32[]{:S(2)}, u32[]{:S(2)}) collective-permute-start(bf16[16,128,128]{2,1,0:T(8,128)(2,1)} %get-tuple-element.74), channel_id=1, source_target_pairs={{0,4},{1,5},{2,6},{3,7},{4,0},{5,1},{6,2},{7,3},{8,12},{9,13},{10,... | collective-permute-start | bytes 1572872 | tf_op jit(solution)/shard_map/ppermute | solution.py:39
  178.8 1.6 copy-start.2
  (1 other events, 0.6 us)

commit v6 on v4

--- a/solution.py
+++ b/solution.py
@@ -545,9 +545,6 @@
     half = TILE_DEV // 2
     tile_x, tile_y = swap(dens_tiles, X1), swap(dens_tiles, Y1)
     orb_x, orb_y = swap(sent, X3), swap(sent, Y3)
-    tile_low, tile_high = swap(tile_y[:half], X1), swap(tile_x[half:], Y1)
-    orb_first, orb_second = swap(orb_y[0], X3), swap(orb_x[1], Y3)
-    orbs = (orbitals, orb_x, orb_y, orb_first, orb_second)
 
     facts = jnp.stack(facts)
     coords = facts[:, :3].transpose(1, 0, 2).reshape(3, LIST_PTS)
@@ -579,6 +576,10 @@
     envelope = jnp.exp(-2.0 * jnp.sum(displace * displace, axis=0) / (GRIDN * GRIDN))
     spread = (envelope.reshape(ATOM_GRP, LISTERS * BAT_DEV, PTS) * share[:, :, None]).reshape(ATOM_GRP, LIST_PTS)
     wave_high, wave_low = wave_of_points(coords)
+    wave_high, wave_low, onward = lax.optimization_barrier((wave_high, wave_low, tile_y[:half]))
+    tile_low, tile_high = swap(onward, X1), swap(tile_x[half:], Y1)
+    orb_first, orb_second = swap(orb_y[0], X3), swap(orb_x[1], Y3)
+    orbs = (orbitals, orb_x, orb_y, orb_first, orb_second)
     first_tmap, first_blocks = tmap, blocks
     early = (spread, weights, wave_high, wave_low, trig, codes, counts, tmap, blocks)
 
@@ -595,7 +596,7 @@
     order = (a + 1, a, a + 3, a + 2)
     part = part + jnp.concatenate([got[:a]] + [got[r : r + 1] for r in order] + [jnp.zeros((LISTERS, KM), F32)])
     got = swap(part, Y3)
-    density = part[a] + got[a + 2]
+    density_got = got[a + 2]
     moments, orb_far = lax.optimization_barrier((part[:a] + got[:a], orb_far))
     orb_far_x, orb_far_y = swap(orb_far, X3), swap(orb_far, Y3)
     got = swap(jnp.concatenate([moments, part[a + LISTERS :]]), X1)
@@ -608,9 +609,6 @@
     structure = jnp.sum(moments[:, :1] * trig, axis=0, keepdims=True)
     for bits in (1, 2, 4):
         structure = structure + swap_grp(structure, bits)
-    structure, own_codes, own_counts, far_codes, far_counts, far_blocks = lax.optimization_barrier(
-        (structure, own_codes, own_counts, far_codes, far_counts, far_blocks)
-    )
     structure = structure + swap_grp(structure, 8)
     potential, scale = potential_of(
         moments,
@@ -633,7 +631,8 @@
     (own,) = ham_terms(
         own_codes, own_counts, far_blocks, far_scale, orbs_far, (own,), ((TILE_DEV, F32),), 2 * 10**10
     )
-    return (density, potential.reshape(-1), final_tiles(own, swap(part_x, X1), swap(part_y, Y1)))
+    density, other, part_x = lax.optimization_barrier((part[a], density_got, part_x))
+    return (density + other, potential.reshape(-1), final_tiles(own, swap(part_x, X1), swap(part_y, Y1)))
 
 
 def solution(mesh):

time: 154 us -> 159 us (1.032)
  other arithmetic: 12.1 us -> 20.3 us
  waiting for transfers between devices: 28.4 us -> 23.9 us
  starting transfers between devices: 46.5 us -> 42.4 us
  local copies, waits for them, and re-layouts: 10.1 us -> 12.7 us
  Pallas kernels: 53.9 us -> 56.2 us
    ppermute x22, waiting for transfers between devices: 25.3 us -> 21 us  [swap(): return lax.ppermute(array, 'dev', [(d, d ^ bits) for d in range(16)])]
    ppermute x22, starting transfers between devices: 34.4 us -> 30.2 us  [swap(): return lax.ppermute(array, 'dev', [(d, d ^ bits) for d in range(16)])]
    pallas_call x3, Pallas kernels: 26.7 us -> 28.9 us  [ham_terms(): pl.pallas_call(functools.partial(ham_kernel, len(starts), len(outs)), in_...]
    reduce_sum x2, other arithmetic: 0.27 us -> 2.12 us  [kept_of(): counts = jnp.sum(mine.astype(jnp.int32), axis=1)]
    unnamed x42 -> x54, local copies, waits for them, and re-layouts: 4.46 us -> 4.49 us
  transfers between devices with their start and end apart: 26 -> 26, of which waited for: 11 -> 11; matrix products, arithmetic and copies ran while one was open for 12% -> 19% of each run, Pallas kernels for 28% -> 29%
where the time goes in v6:
time: 159 us; the launch traced here: 158 us
  Pallas kernels  56.2 us (35%)
  starting transfers between devices  42.4 us (27%)
  waiting for transfers between devices  23.9 us (15%)
  other arithmetic  20.3 us (13%)
  local copies, waits for them, and re-layouts  12.7 us (8%)
    ppermute x22, starting transfers between devices, swap(): return lax.ppermute(array, 'dev', [(d, d ^ bits) for d in range(16)])  30.2 us
    pallas_call x3, Pallas kernels, ham_terms(): pl.pallas_call(functools.partial(ham_kernel, len(starts), len(outs)), in_...  28.9 us
    ppermute x22, waiting for transfers between devices, swap(): return lax.ppermute(array, 'dev', [(d, d ^ bits) for d in range(16)])  21 us
    ppermute x4, starting transfers between devices, swap_grp(): return lax.ppermute(array, 'grp', [(g, g ^ bits) for g in range(16)])  12.2 us
    pallas_call x1, Pallas kernels, first_density(): pl.pallas_call(first_density_kernel, in_specs=[SMEM_SPEC] * 2 + [ANY_SPEC...  8.73 us
    pallas_call x1, Pallas kernels, density_and_moments(): pl.pallas_call(density_kernel, in_specs=[SMEM_SPEC] * 2 + [ANY_SPEC] * 7...  7.2 us
    pallas_call x1, Pallas kernels, wave_of_points(): pl.pallas_call(wave_kernel, grid=(points // chunk,), in_specs=[pl.BlockSp...  5.72 us
    unnamed x54, local copies, waits for them, and re-layouts  4.49 us
  transfers between devices with their start and end apart: 26, of which 11 were waited for; matrix products, arithmetic and copies ran while one was open for 19% of the time, Pallas kernels for 29%

profile of v6, /device:TPU:2, one launch (start us, length us, event | category | flops | bytes accessed | tf_op | source)
XLA Modules:
  0.0 157.6 jit_solution(8193181710369345498)
XLA Ops:
  0.6 1.4 shard_map.122
  2.1 1.6 %collective-permute-start = (f32[6,512]{1,0:T(8,128)}, f32[6,512]{1,0:T(8,128)S(1)}, u32[]{:S(2)}, u32[]{:S(2)}) collective-permute-start(f32[6,512]{1,0:T(8,128)} %shard_map.122), channel_id=1, source_target_pairs={{0,3},{1,2},{2,1},{3,0},{4,7},{5,6},{6,5},{7,4},{8,11},{9,10},{10,... | collective-permute-start | bytes 36872 | tf_op jit(solution)/shard_map/ppermute | solution.py:39
  3.7 3.0 %collective-permute-start.1 = (f32[6,512]{1,0:T(8,128)}, f32[6,512]{1,0:T(8,128)S(1)}, u32[]{:S(2)}, u32[]{:S(2)}) collective-permute-start(f32[6,512]{1,0:T(8,128)} %shard_map.122), channel_id=1, source_target_pairs={{0,12},{1,13},{2,14},{3,15},{4,8},{5,9},{6,10},{7,11},{8,4},{9,5},... | collective-permute-start | bytes 36872 | tf_op jit(solution)/shard_map/ppermute | solution.py:39
  7.2 3.1 %collective-permute-start.4 = (bf16[32,128,128]{2,1,0:T(8,128)(2,1)}, bf16[32,128,128]{2,1,0:T(8,128)(2,1)}, u32[]{:S(2)}, u32[]{:S(2)}) collective-permute-start(bf16[32,128,128]{2,1,0:T(8,128)(2,1)} %own_tile.3), channel_id=1, source_target_pairs={{0,1},{1,0},{2,3},{3,2},{4,5},{5,4},{6,7},{7,6},{8,9},{9,8},{10,11... | collective-permute-start | bytes 3145736 | tf_op jit(solution)/shard_map/ppermute | solution.py:39
  11.5 1.3 shard_map.121
  15.0 2.7 %collective-permute-start.8 = (bf16[2,256,1024]{2,1,0:T(8,128)(2,1)}, bf16[2,256,1024]{2,1,0:T(8,128)(2,1)S(1)}, u32[]{:S(2)}, u32[]{:S(2)}) collective-permute-start(bf16[2,256,1024]{2,1,0:T(8,128)(2,1)} %refs_0_.1), channel_id=1, source_target_pairs={{0,12},{1,13},{2,14},{3,15},{4,8},{5,9},{6,10},{7,11},{8,4},{9,5},... | collective-permute-start | bytes 3145736 | tf_op jit(solution)/shard_map/ppermute | solution.py:39
  20.2 2.0 %convert_reduce_fusion.5 = (s32[4]{0:T(128)}, pred[4,81]{1,0:T(4,128)(4,1)}, pred[4,81]{1,0:T(4,128)(4,1)}) fusion(s32[4,512]{1,0:T(4,128)} %get-tuple-element.86, s32[]{:T(128)S(6)} %axis_index.12), kind=kLoop, calls=%fused_computation.62 | loop fusion | flops 3884 | bytes 3260 | tf_op jit(solution)/shard_map/reduce_sum | solution.py:493
  22.2 1.3 copy.22
  23.5 1.4 div.97
  25.7 0.9 convert_reduce_fusion.2
  26.6 1.3 add_select_fusion.1
  28.6 1.3 fusion.8.codes_ref
  30.7 1.3 and_select_fusion.6.counts_ref
  32.1 0.9 multiply_reduce_fusion
  33.3 5.7 %shard_map.123 = (bf16[512,2048]{1,0:T(8,128)(2,1)}, bf16[512,2048]{1,0:T(8,128)(2,1)}) custom-call(f32[48,2048]{1,0:T(8,128)} %bitcast.50), custom_call_target="tpu_custom_call" | custom-call | flops 8388608 | bytes 4194304 | tf_op jit(solution)/shard_map/pallas_call | solution.py:87
  39.1 1.0 fusion.23
  40.7 0.9 slice.139
  41.6 1.3 collective-permute-start.5
  43.0 1.9 %slice.143 = bf16[16,128,128]{2,1,0:T(8,128)(2,1)} slice(bf16[32,128,128]{2,1,0:T(8,128)(2,1)} %collective-permute-done.4.x_tile), slice={[16:32], [0:128], [0:128]} | slice | bytes 1048576 | tf_op jit(solution)/shard_map/slice | solution.py:580
  48.2 2.2 %collective-permute-start.9 = (bf16[256,1024]{1,0:T(8,128)(2,1)S(1)}, bf16[256,1024]{1,0:T(8,128)(2,1)S(1)}, u32[]{:S(2)}, u32[]{:S(2)}) collective-permute-start(bf16[256,1024]{1,0:T(8,128)(2,1)S(1)} %slice_bitcast_fusion.1), channel_id=1, source_target_pairs={{0,3},{1,2},{2,1},{3,0},{4,7},{5,6},{6,5},{7,4},{8,11},{9,10},{10,... | collective-permute-start | bytes 1572872 | tf_op jit(solution)/shard_map/ppermute | solution.py:39
  50.4 3.5 %collective-permute-done.5.low_tile = bf16[16,128,128]{2,1,0:T(8,128)(2,1)} collective-permute-done((bf16[16,128,128]{2,1,0:T(8,128)(2,1)}, bf16[16,128,128]{2,1,0:T(8,128)(2,1)}, u32[]{:S(2)}, u32[]{:S(2)}) %collective-permute-start.5) | collective-permute-done | bytes 524320 | tf_op jit(solution)/shard_map/ppermute | solution.py:39
  53.9 2.5 %collective-permute-done.6.high_tile = bf16[16,128,128]{2,1,0:T(8,128)(2,1)} collective-permute-done((bf16[16,128,128]{2,1,0:T(8,128)(2,1)}, bf16[16,128,128]{2,1,0:T(8,128)(2,1)}, u32[]{:S(2)}, u32[]{:S(2)}) %collective-permute-start.6) | collective-permute-done | bytes 524320 | tf_op jit(solution)/shard_map/ppermute | solution.py:39
  56.5 8.7 %shard_map.124.before_ref = f32[8,256]{1,0:T(8,128)} custom-call(s32[4,81]{1,0:T(4,128)} %get-tuple-element.50.tmap_ref, s32[8,8]{1,0:T(8,128)} %bitcast.56, bf16[32,128,128]{2,1,0:T(8,128)(2,1)} %own_tile.3, bf16[32,128,128]{2,1,0:T(8,128)(2,1)} %collective-permute-done.4.x_tile, bf16[32,128,128]{2,1,0:T(8,128)(2,1)} %copy-done.8, ...), custom_call_target="tpu_custom_call" | custom-call | flops 20000000000 | bytes 10000 | tf_op jit(solution)/shard_map/pallas_call | solution.py:178
  65.2 2.0 %collective-permute-start.13 = (bf16[2,256,1024]{2,1,0:T(8,128)(2,1)}, bf16[2,256,1024]{2,1,0:T(8,128)(2,1)S(1)}, u32[]{:S(2)}, u32[]{:S(2)}) collective-permute-start(bf16[2,256,1024]{2,1,0:T(8,128)(2,1)} %refs_0_.1), channel_id=1, source_target_pairs={{0,5},{1,4},{2,7},{3,6},{4,1},{5,0},{6,3},{7,2},{8,13},{9,12},{10,... | collective-permute-start | bytes 3145736 | tf_op jit(solution)/shard_map/ppermute | solution.py:39
  67.3 7.2 %shard_map.125 = (f32[24,512]{1,0:T(8,128)}, bf16[2,256,1024]{2,1,0:T(8,128)(2,1)}) custom-call(s32[4,81]{1,0:T(4,128)} %get-tuple-element.50.tmap_ref, s32[8,8]{1,0:T(8,128)} %bitcast.57, bf16[32,128,128]{2,1,0:T(8,128)(2,1)} %own_tile.3, bf16[32,128,128]{2,1,0:T(8,128)(2,1)} %collective-permute-done.4.x_tile, bf16[32,128,128]{2,1,0:T(8,128)(2,1)} %copy-done.8, ...), custom_call_target="tpu_custom_call" | custom-call | flops 1000000 | bytes 10000 | tf_op jit(solution)/shard_map/pallas_call | solution.py:276
  74.9 4.0 %collective-permute-done.11 = f32[24,512]{1,0:T(8,128)S(1)} collective-permute-done((f32[24,512]{1,0:T(8,128)}, f32[24,512]{1,0:T(8,128)S(1)}, u32[]{:S(2)}, u32[]{:S(2)}) %collective-permute-start.11) | collective-permute-done | bytes 49184 | tf_op jit(solution)/shard_map/ppermute | solution.py:39
  79.8 0.9 collective-permute-start.12
  80.7 4.4 %collective-permute-done.12 = f32[24,512]{1,0:T(8,128)S(1)} collective-permute-done((f32[24,512]{1,0:T(8,128)S(1)}, f32[24,512]{1,0:T(8,128)S(1)}, u32[]{:S(2)}, u32[]{:S(2)}) %collective-permute-start.12) | collective-permute-done | bytes 49184 | tf_op jit(solution)/shard_map/ppermute | solution.py:39
  85.1 3.3 %collective-permute-done.13.refs_0_ = bf16[2,256,1024]{2,1,0:T(8,128)(2,1)S(1)} collective-permute-done((bf16[2,256,1024]{2,1,0:T(8,128)(2,1)}, bf16[2,256,1024]{2,1,0:T(8,128)(2,1)S(1)}, u32[]{:S(2)}, u32[]{:S(2)}) %collective-permute-start.13) | collective-permute-done | bytes 1048608 | tf_op jit(solution)/shard_map/ppermute | solution.py:39
  88.4 2.0 %collective-permute-start.14 = (f32[20,512]{1,0:T(8,128)S(1)}, f32[20,512]{1,0:T(8,128)S(1)}, u32[]{:S(2)}, u32[]{:S(2)}) collective-permute-start(f32[20,512]{1,0:T(8,128)S(1)} %pad_maximum_fusion.2), channel_id=1, source_target_pairs={{0,1},{1,0},{2,3},{3,2},{4,5},{5,4},{6,7},{7,6},{8,9},{9,8},{10,11... | collective-permute-start | bytes 122888 | tf_op jit(solution)/shard_map/ppermute | solution.py:39
  90.4 2.2 %collective-permute-done.14 = f32[20,512]{1,0:T(8,128)S(1)} collective-permute-done((f32[20,512]{1,0:T(8,128)S(1)}, f32[20,512]{1,0:T(8,128)S(1)}, u32[]{:S(2)}, u32[]{:S(2)}) %collective-permute-start.14) | collective-permute-done | bytes 40992 | tf_op jit(solution)/shard_map/ppermute | solution.py:39
  92.6 2.0 %collective-permute-start.15 = (f32[20,512]{1,0:T(8,128)S(1)}, f32[20,512]{1,0:T(8,128)S(1)}, u32[]{:S(2)}, u32[]{:S(2)}) collective-permute-start(f32[20,512]{1,0:T(8,128)S(1)} %pad_maximum_fusion.3), channel_id=1, source_target_pairs={{0,4},{1,5},{2,6},{3,7},{4,0},{5,1},{6,2},{7,3},{8,12},{9,13},{10,... | collective-permute-start | bytes 122888 | tf_op jit(solution)/shard_map/ppermute | solution.py:39
  94.8 2.1 %collective-permute-start.22 = (bf16[2,256,1024]{2,1,0:T(8,128)(2,1)S(1)}, bf16[2,256,1024]{2,1,0:T(8,128)(2,1)}, u32[]{:S(2)}, u32[]{:S(2)}) collective-permute-start(bf16[2,256,1024]{2,1,0:T(8,128)(2,1)S(1)} %collective-permute-done.13.refs_0_), channel_id=1, source_target_pairs={{0,12},{1,13},{2,14},{3,15},{4,8},{5,9},{6,10},{7,11},{8,4},{9,5},... | collective-permute-start | bytes 3145736 | tf_op jit(solution)/shard_map/ppermute | solution.py:39
  97.6 2.2 %collective-permute-start.23 = (bf16[2,256,1024]{2,1,0:T(8,128)(2,1)}, bf16[2,256,1024]{2,1,0:T(8,128)(2,1)}, u32[]{:S(2)}, u32[]{:S(2)}) collective-permute-start(bf16[2,256,1024]{2,1,0:T(8,128)(2,1)} %get-tuple-element.64), channel_id=1, source_target_pairs={{0,5},{1,4},{2,7},{3,6},{4,1},{5,0},{6,3},{7,2},{8,13},{9,12},{10,... | collective-permute-start | bytes 3145736 | tf_op jit(solution)/shard_map/ppermute | solution.py:39
  100.3 2.0 %collective-permute-start.17 = (f32[1,512]{1,0:T(1,128)S(1)}, f32[1,512]{1,0:T(1,128)S(1)}, u32[]{:S(2)}, u32[]{:S(2)}) collective-permute-start(f32[1,512]{1,0:T(1,128)S(1)} %add.180), channel_id=1, source_target_pairs={{0,32},{16,48},{32,0},{48,16},{64,96},{80,112},{96,64},{112,80},{1... | collective-permute-start | bytes 6152 | tf_op jit(solution)/shard_map/ppermute | solution.py:43
  102.9 1.0 collective-permute-done.17
  104.0 3.3 %collective-permute-start.18 = (f32[1,512]{1,0:T(1,128)S(1)}, f32[1,512]{1,0:T(1,128)S(1)}, u32[]{:S(2)}, u32[]{:S(2)}) collective-permute-start(f32[1,512]{1,0:T(1,128)S(1)} %add.181), channel_id=1, source_target_pairs={{0,64},{16,80},{32,96},{48,112},{64,0},{80,16},{96,32},{112,48},{1... | collective-permute-start | bytes 6152 | tf_op jit(solution)/shard_map/ppermute | solution.py:43
  107.9 0.9 collective-permute-done.18
  108.8 6.8 %collective-permute-start.19 = (f32[1,512]{1,0:T(1,128)S(1)}, f32[1,512]{1,0:T(1,128)S(1)}, u32[]{:S(2)}, u32[]{:S(2)}) collective-permute-start(f32[1,512]{1,0:T(1,128)S(1)} %add.182), channel_id=1, source_target_pairs={{0,128},{16,144},{32,160},{48,176},{64,192},{80,208},{96,224},{112... | collective-permute-start | bytes 6152 | tf_op jit(solution)/shard_map/ppermute | solution.py:43
  116.2 1.0 collective-permute-done.19
  117.2 1.6 %copy-done.1 = bf16[512,2048]{1,0:T(8,128)(2,1)S(1)} copy-done((bf16[512,2048]{1,0:T(8,128)(2,1)S(1)}, bf16[512,2048]{1,0:T(8,128)(2,1)}, u32[]{:S(2)}) %copy-start.1) | copy-done | bytes 2097176
  118.8 1.2 shard_map.126
  120.0 1.8 %collective-permute-start.20 = (f32[1,2048]{1,0:T(1,128)S(1)}, f32[1,2048]{1,0:T(1,128)S(1)}, u32[]{:S(2)}, u32[]{:S(2)}) collective-permute-start(f32[1,2048]{1,0:T(1,128)S(1)} %get-tuple-element.62.scale_ref), channel_id=1, source_target_pairs={{0,5},{1,4},{2,7},{3,6},{4,1},{5,0},{6,3},{7,2},{8,13},{9,12},{10,... | collective-permute-start | bytes 24584 | tf_op jit(solution)/shard_map/ppermute | solution.py:39
  122.9 11.1 %shard_map.127 = (f32[32,128,128]{2,1,0:T(8,128)}, f32[32,128,128]{2,1,0:T(8,128)}) custom-call(s32[4,32]{1,0:T(4,128)} %fusion.8.codes_ref, s32[4]{0:T(128)} %and_select_fusion.6.counts_ref, s32[8,8]{1,0:T(8,128)} %bitcast.58, f32[1,2048]{1,0:T(1,128)} %copy-done.5, bf16[2,256,1024]{2,1,0:T(8,128)(2,1)} %refs_0_.1, bf16[2,256,1024]{2,1,0:T(8,128)(2,1)} %copy-done.6, ...), custom_call_target="tpu_custom_call" | custom-call | flops 1000000 | bytes 10000 | tf_op jit(solution)/shard_map/pallas_call | solution.py:446
  134.7 7.7 %shard_map.128 = (bf16[16,128,128]{2,1,0:T(8,128)(2,1)}, bf16[16,128,128]{2,1,0:T(8,128)(2,1)}) custom-call(s32[4,32]{1,0:T(4,128)} %fusion.9.codes_ref, s32[4]{0:T(128)} %and_select_fusion.5.counts_ref, s32[8,8]{1,0:T(8,128)} %bitcast.61, f32[1,2048]{1,0:T(1,128)} %copy-done.19, bf16[2,256,1024]{2,1,0:T(8,128)(2,1)} %copy-done.11, ...), custom_call_target="tpu_custom_call" | custom-call | flops 1000000 | bytes 10000 | tf_op jit(solution)/shard_map/pallas_call | solution.py:446
  142.6 10.1 %shard_map.129.own_ref = f32[32,128,128]{2,1,0:T(8,128)} custom-call(s32[4,32]{1,0:T(4,128)} %fusion.10.codes_ref, s32[4]{0:T(128)} %and_select_fusion.4.counts_ref, s32[8,8]{1,0:T(8,128)} %bitcast.62, f32[1,2048]{1,0:T(1,128)} %copy-done.19, bf16[2,256,1024]{2,1,0:T(8,128)(2,1)} %copy-done.11, bf16[2,256,1024]{2,1,0:T(8,128)(2,1)} %collective-permute-done.21.refs_1_, ...), custom_call_target="tpu_custom_call" | custom-call | flops 20000000000 | bytes 10000 | tf_op jit(solution)/shard_map/pallas_call | solution.py:446
  154.3 1.6 %copy-done.2 = f32[32,128,128]{2,1,0:T(8,128)S(1)} copy-done((f32[32,128,128]{2,1,0:T(8,128)S(1)}, f32[32,128,128]{2,1,0:T(8,128)}, u32[]{:S(2)}) %copy-start.2) | copy-done | bytes 2097176
  155.9 1.7 %shard_map.130 = bf16[32,128,128]{2,1,0:T(8,128)(2,1)} custom-call(f32[32,128,128]{2,1,0:T(8,128)S(1)} %copy-done.2, bf16[16,128,128]{2,1,0:T(8,128)(2,1)S(1)} %collective-permute-done.24.x_ref, bf16[16,128,128]{2,1,0:T(8,128)(2,1)S(1)} %collective-permute-done.25.y_ref), custom_call_target="tpu_custom_call" | custom-call | flops 1000000 | bytes 10000 | tf_op jit(solution)/shard_map/pallas_call | solution.py:473
  (143 shorter events, 21.1 us)
Async XLA Ops:
  2.1 11.3 %collective-permute-start = (f32[6,512]{1,0:T(8,128)}, f32[6,512]{1,0:T(8,128)S(1)}, u32[]{:S(2)}, u32[]{:S(2)}) collective-permute-start(f32[6,512]{1,0:T(8,128)} %shard_map.122), channel_id=1, source_target_pairs={{0,3},{1,2},{2,1},{3,0},{4,7},{5,6},{6,5},{7,4},{8,11},{9,10},{10,... | collective-permute-start | bytes 36872 | tf_op jit(solution)/shard_map/ppermute | solution.py:39
  3.7 9.7 %collective-permute-start.1 = (f32[6,512]{1,0:T(8,128)}, f32[6,512]{1,0:T(8,128)S(1)}, u32[]{:S(2)}, u32[]{:S(2)}) collective-permute-start(f32[6,512]{1,0:T(8,128)} %shard_map.122), channel_id=1, source_target_pairs={{0,12},{1,13},{2,14},{3,15},{4,8},{5,9},{6,10},{7,11},{8,4},{9,5},... | collective-permute-start | bytes 36872 | tf_op jit(solution)/shard_map/ppermute | solution.py:39
  6.7 6.7 %collective-permute-start.2 = (f32[6,512]{1,0:T(8,128)}, f32[6,512]{1,0:T(8,128)S(1)}, u32[]{:S(2)}, u32[]{:S(2)}) collective-permute-start(f32[6,512]{1,0:T(8,128)} %shard_map.122), channel_id=1, source_target_pairs={{0,15},{1,14},{2,13},{3,12},{4,11},{5,10},{6,9},{7,8},{8,7},{9,6},... | collective-permute-start | bytes 36872 | tf_op jit(solution)/shard_map/ppermute | solution.py:39
  6.9 33.9 %collective-permute-start.3 = (bf16[32,128,128]{2,1,0:T(8,128)(2,1)}, bf16[32,128,128]{2,1,0:T(8,128)(2,1)S(1)}, u32[]{:S(2)}, u32[]{:S(2)}) collective-permute-start(bf16[32,128,128]{2,1,0:T(8,128)(2,1)} %own_tile.3), channel_id=1, source_target_pairs={{0,4},{1,5},{2,6},{3,7},{4,0},{5,1},{6,2},{7,3},{8,12},{9,13},{10,... | collective-permute-start | bytes 3145736 | tf_op jit(solution)/shard_map/ppermute | solution.py:39
  7.2 35.7 %collective-permute-start.4 = (bf16[32,128,128]{2,1,0:T(8,128)(2,1)}, bf16[32,128,128]{2,1,0:T(8,128)(2,1)}, u32[]{:S(2)}, u32[]{:S(2)}) collective-permute-start(bf16[32,128,128]{2,1,0:T(8,128)(2,1)} %own_tile.3), channel_id=1, source_target_pairs={{0,1},{1,0},{2,3},{3,2},{4,5},{5,4},{6,7},{7,6},{8,9},{9,8},{10,11... | collective-permute-start | bytes 3145736 | tf_op jit(solution)/shard_map/ppermute | solution.py:39
  11.5 1.9 %copy-start.14 = (f32[6,512]{1,0:T(8,128)S(1)}, f32[6,512]{1,0:T(8,128)}, u32[]{:S(2)}) copy-start(f32[6,512]{1,0:T(8,128)} %shard_map.122) | copy-start | bytes 36868
  14.2 33.2 %collective-permute-start.7 = (bf16[2,256,1024]{2,1,0:T(8,128)(2,1)}, bf16[2,256,1024]{2,1,0:T(8,128)(2,1)S(1)}, u32[]{:S(2)}, u32[]{:S(2)}) collective-permute-start(bf16[2,256,1024]{2,1,0:T(8,128)(2,1)} %refs_0_.1), channel_id=1, source_target_pairs={{0,3},{1,2},{2,1},{3,0},{4,7},{5,6},{6,5},{7,4},{8,11},{9,10},{10,... | collective-permute-start | bytes 3145736 | tf_op jit(solution)/shard_map/ppermute | solution.py:39
  15.0 33.2 %collective-permute-start.8 = (bf16[2,256,1024]{2,1,0:T(8,128)(2,1)}, bf16[2,256,1024]{2,1,0:T(8,128)(2,1)S(1)}, u32[]{:S(2)}, u32[]{:S(2)}) collective-permute-start(bf16[2,256,1024]{2,1,0:T(8,128)(2,1)} %refs_0_.1), channel_id=1, source_target_pairs={{0,12},{1,13},{2,14},{3,15},{4,8},{5,9},{6,10},{7,11},{8,4},{9,5},... | collective-permute-start | bytes 3145736 | tf_op jit(solution)/shard_map/ppermute | solution.py:39
  18.9 0.6 copy-start.12
  25.7 20.5 %copy-start.15 = (s32[4,512]{1,0:T(4,128)S(1)}, s32[4,512]{1,0:T(4,128)}, u32[]{:S(2)}) copy-start(s32[4,512]{1,0:T(4,128)} %get-tuple-element.86) | copy-start | bytes 24580
  25.7 21.1 %copy-start.16 = (f32[4,1,512]{2,0,1:T(4,128)S(1)}, f32[4,1,512]{2,0,1:T(4,128)}, u32[]{:S(2)}) copy-start(f32[4,1,512]{2,0,1:T(4,128)} %get-tuple-element.92) | copy-start | bytes 24580
  40.7 7.5 %copy-start.8 = (bf16[32,128,128]{2,1,0:T(8,128)(2,1)}, bf16[32,128,128]{2,1,0:T(8,128)(2,1)S(1)}, u32[]{:S(2)}) copy-start(bf16[32,128,128]{2,1,0:T(8,128)(2,1)S(1)} %collective-permute-done.3.y_tile) | copy-start | bytes 3145732
  41.6 12.3 %collective-permute-start.5 = (bf16[16,128,128]{2,1,0:T(8,128)(2,1)}, bf16[16,128,128]{2,1,0:T(8,128)(2,1)}, u32[]{:S(2)}, u32[]{:S(2)}) collective-permute-start(bf16[16,128,128]{2,1,0:T(8,128)(2,1)} %slice.139), channel_id=1, source_target_pairs={{0,1},{1,0},{2,3},{3,2},{4,5},{5,4},{6,7},{7,6},{8,9},{9,8},{10,11... | collective-permute-start | bytes 1572872 | tf_op jit(solution)/shard_map/ppermute | solution.py:39
  44.9 11.6 %collective-permute-start.6 = (bf16[16,128,128]{2,1,0:T(8,128)(2,1)}, bf16[16,128,128]{2,1,0:T(8,128)(2,1)}, u32[]{:S(2)}, u32[]{:S(2)}) collective-permute-start(bf16[16,128,128]{2,1,0:T(8,128)(2,1)} %slice.143), channel_id=1, source_target_pairs={{0,4},{1,5},{2,6},{3,7},{4,0},{5,1},{6,2},{7,3},{8,12},{9,13},{10,... | collective-permute-start | bytes 1572872 | tf_op jit(solution)/shard_map/ppermute | solution.py:39
  47.4 9.1 %copy-start.6 = (bf16[2,256,1024]{2,1,0:T(8,128)(2,1)}, bf16[2,256,1024]{2,1,0:T(8,128)(2,1)S(1)}, u32[]{:S(2)}) copy-start(bf16[2,256,1024]{2,1,0:T(8,128)(2,1)S(1)} %collective-permute-done.7.x_orb.refs_1_) | copy-start | bytes 3145732
  47.4 17.8 %collective-permute-start.10 = (bf16[256,1024]{1,0:T(8,128)(2,1)S(1)}, bf16[256,1024]{1,0:T(8,128)(2,1)S(1)}, u32[]{:S(2)}, u32[]{:S(2)}) collective-permute-start(bf16[256,1024]{1,0:T(8,128)(2,1)S(1)} %slice_bitcast_fusion), channel_id=1, source_target_pairs={{0,12},{1,13},{2,14},{3,15},{4,8},{5,9},{6,10},{7,11},{8,4},{9,5},... | collective-permute-start | bytes 1572872 | tf_op jit(solution)/shard_map/ppermute | solution.py:39
  48.1 8.3 %copy-start.7 = (bf16[2,256,1024]{2,1,0:T(8,128)(2,1)}, bf16[2,256,1024]{2,1,0:T(8,128)(2,1)S(1)}, u32[]{:S(2)}) copy-start(bf16[2,256,1024]{2,1,0:T(8,128)(2,1)S(1)} %collective-permute-done.8.y_orb.refs_2_) | copy-start | bytes 3145732
  48.2 17.0 %collective-permute-start.9 = (bf16[256,1024]{1,0:T(8,128)(2,1)S(1)}, bf16[256,1024]{1,0:T(8,128)(2,1)S(1)}, u32[]{:S(2)}, u32[]{:S(2)}) collective-permute-start(bf16[256,1024]{1,0:T(8,128)(2,1)S(1)} %slice_bitcast_fusion.1), channel_id=1, source_target_pairs={{0,3},{1,2},{2,1},{3,0},{4,7},{5,6},{6,5},{7,4},{8,11},{9,10},{10,... | collective-permute-start | bytes 1572872 | tf_op jit(solution)/shard_map/ppermute | solution.py:39
  65.2 2.0 %copy-start.9 = (bf16[256,1024]{1,0:T(8,128)(2,1)}, bf16[256,1024]{1,0:T(8,128)(2,1)S(1)}, u32[]{:S(2)}) copy-start(bf16[256,1024]{1,0:T(8,128)(2,1)S(1)} %collective-permute-done.10.second_orb.refs_4_) | copy-start | bytes 1572868
  65.2 2.0 %copy-start.10 = (bf16[256,1024]{1,0:T(8,128)(2,1)}, bf16[256,1024]{1,0:T(8,128)(2,1)S(1)}, u32[]{:S(2)}) copy-start(bf16[256,1024]{1,0:T(8,128)(2,1)S(1)} %collective-permute-done.9.first_orb.refs_3_) | copy-start | bytes 1572868
  65.2 23.2 %collective-permute-start.13 = (bf16[2,256,1024]{2,1,0:T(8,128)(2,1)}, bf16[2,256,1024]{2,1,0:T(8,128)(2,1)S(1)}, u32[]{:S(2)}, u32[]{:S(2)}) collective-permute-start(bf16[2,256,1024]{2,1,0:T(8,128)(2,1)} %refs_0_.1), channel_id=1, source_target_pairs={{0,5},{1,4},{2,7},{3,6},{4,1},{5,0},{6,3},{7,2},{8,13},{9,12},{10,... | collective-permute-start | bytes 3145736 | tf_op jit(solution)/shard_map/ppermute | solution.py:39
  67.2 7.7 %copy-start.17 = (s32[1,256]{1,0:T(1,128)S(1)}, s32[1,256]{1,0:T(1,128)}, u32[]{:S(2)}) copy-start(s32[1,256]{1,0:T(1,128)} %get-tuple-element.108) | copy-start | bytes 3076
  67.2 7.7 %copy-start.18 = (s32[1,256]{1,0:T(1,128)S(1)}, s32[1,256]{1,0:T(1,128)}, u32[]{:S(2)}) copy-start(s32[1,256]{1,0:T(1,128)} %get-tuple-element.109) | copy-start | bytes 3076
  67.2 7.7 %copy-start.20 = (s32[1,256]{1,0:T(1,128)S(1)}, s32[1,256]{1,0:T(1,128)}, u32[]{:S(2)}) copy-start(s32[1,256]{1,0:T(1,128)} %and_select_fusion.3) | copy-start | bytes 3076
  67.2 27.4 %copy-start.13 = (f32[8,256]{1,0:T(8,128)S(1)}, f32[8,256]{1,0:T(8,128)}, u32[]{:S(2)}) copy-start(f32[8,256]{1,0:T(8,128)} %reshape_squeeze.12.weights_ref) | copy-start | bytes 24580
  67.2 29.6 %copy-start.21 = (s32[81]{0:T(128)S(1)}, s32[81]{0:T(128)}, u32[]{:S(2)}) copy-start(s32[81]{0:T(128)} %get-tuple-element.110) | copy-start | bytes 976
  67.3 29.6 %copy-start.22 = (s32[81]{0:T(128)S(1)}, s32[81]{0:T(128)}, u32[]{:S(2)}) copy-start(s32[81]{0:T(128)} %get-tuple-element.111) | copy-start | bytes 976
  67.3 30.2 %copy-start.4 = (f32[16,512]{1,0:T(8,128)S(1)}, f32[16,512]{1,0:T(8,128)}, u32[]{:S(2)}) copy-start(f32[16,512]{1,0:T(8,128)} %pad_maximum_fusion.4.trig_ref) | copy-start | bytes 98308
  67.3 49.9 %copy-start = (bf16[512,2048]{1,0:T(8,128)(2,1)S(1)}, bf16[512,2048]{1,0:T(8,128)(2,1)}, u32[]{:S(2)}) copy-start(bf16[512,2048]{1,0:T(8,128)(2,1)} %get-tuple-element.54.high_hbm.high_ref) | copy-start | bytes 6291460
  67.3 49.9 %copy-start.3 = (f32[16,2048]{1,0:T(8,128)S(1)}, f32[16,2048]{1,0:T(8,128)}, u32[]{:S(2)}) copy-start(f32[16,2048]{1,0:T(8,128)} %exponential_multiply_fusion.spread_ref) | copy-start | bytes 393220
  74.5 4.4 %collective-permute-start.11 = (f32[24,512]{1,0:T(8,128)}, f32[24,512]{1,0:T(8,128)S(1)}, u32[]{:S(2)}, u32[]{:S(2)}) collective-permute-start(f32[24,512]{1,0:T(8,128)} %get-tuple-element.57), channel_id=1, source_target_pairs={{0,3},{1,2},{2,1},{3,0},{4,7},{5,6},{6,5},{7,4},{8,11},{9,10},{10,... | collective-permute-start | bytes 147464 | tf_op jit(solution)/shard_map/ppermute | solution.py:39
  79.8 5.3 %collective-permute-start.12 = (f32[24,512]{1,0:T(8,128)S(1)}, f32[24,512]{1,0:T(8,128)S(1)}, u32[]{:S(2)}, u32[]{:S(2)}) collective-permute-start(f32[24,512]{1,0:T(8,128)S(1)} %add.173), channel_id=1, source_target_pairs={{0,12},{1,13},{2,14},{3,15},{4,8},{5,9},{6,10},{7,11},{8,4},{9,5},... | collective-permute-start | bytes 147464 | tf_op jit(solution)/shard_map/ppermute | solution.py:39
  88.4 31.6 %copy-start.11 = (bf16[2,256,1024]{2,1,0:T(8,128)(2,1)}, bf16[2,256,1024]{2,1,0:T(8,128)(2,1)S(1)}, u32[]{:S(2)}) copy-start(bf16[2,256,1024]{2,1,0:T(8,128)(2,1)S(1)} %collective-permute-done.13.refs_0_) | copy-start | bytes 3145732
  88.4 4.2 %collective-permute-start.14 = (f32[20,512]{1,0:T(8,128)S(1)}, f32[20,512]{1,0:T(8,128)S(1)}, u32[]{:S(2)}, u32[]{:S(2)}) collective-permute-start(f32[20,512]{1,0:T(8,128)S(1)} %pad_maximum_fusion.2), channel_id=1, source_target_pairs={{0,1},{1,0},{2,3},{3,2},{4,5},{5,4},{6,7},{7,6},{8,9},{9,8},{10,11... | collective-permute-start | bytes 122888 | tf_op jit(solution)/shard_map/ppermute | solution.py:39
  92.6 4.3 %collective-permute-start.15 = (f32[20,512]{1,0:T(8,128)S(1)}, f32[20,512]{1,0:T(8,128)S(1)}, u32[]{:S(2)}, u32[]{:S(2)}) collective-permute-start(f32[20,512]{1,0:T(8,128)S(1)} %pad_maximum_fusion.3), channel_id=1, source_target_pairs={{0,4},{1,5},{2,6},{3,7},{4,0},{5,1},{6,2},{7,3},{8,12},{9,13},{10,... | collective-permute-start | bytes 122888 | tf_op jit(solution)/shard_map/ppermute | solution.py:39
  94.7 39.4 %collective-permute-start.21 = (bf16[2,256,1024]{2,1,0:T(8,128)(2,1)S(1)}, bf16[2,256,1024]{2,1,0:T(8,128)(2,1)}, u32[]{:S(2)}, u32[]{:S(2)}) collective-permute-start(bf16[2,256,1024]{2,1,0:T(8,128)(2,1)S(1)} %collective-permute-done.13.refs_0_), channel_id=1, source_target_pairs={{0,3},{1,2},{2,1},{3,0},{4,7},{5,6},{6,5},{7,4},{8,11},{9,10},{10,... | collective-permute-start | bytes 3145736 | tf_op jit(solution)/shard_map/ppermute | solution.py:39
  94.8 39.3 %collective-permute-start.22 = (bf16[2,256,1024]{2,1,0:T(8,128)(2,1)S(1)}, bf16[2,256,1024]{2,1,0:T(8,128)(2,1)}, u32[]{:S(2)}, u32[]{:S(2)}) collective-permute-start(bf16[2,256,1024]{2,1,0:T(8,128)(2,1)S(1)} %collective-permute-done.13.refs_0_), channel_id=1, source_target_pairs={{0,12},{1,13},{2,14},{3,15},{4,8},{5,9},{6,10},{7,11},{8,4},{9,5},... | collective-permute-start | bytes 3145736 | tf_op jit(solution)/shard_map/ppermute | solution.py:39
  97.5 2.7 %collective-permute-start.16 = (f32[1,512]{1,0:T(1,128)S(1)}, f32[1,512]{1,0:T(1,128)S(1)}, u32[]{:S(2)}, u32[]{:S(2)}) collective-permute-start(f32[1,512]{1,0:T(1,128)S(1)} %bitcast.63), channel_id=1, source_target_pairs={{0,16},{16,0},{32,48},{48,32},{64,80},{80,64},{96,112},{112,96},{1... | collective-permute-start | bytes 6152 | tf_op jit(solution)/shard_map/ppermute | solution.py:43
  97.6 36.5 %collective-permute-start.23 = (bf16[2,256,1024]{2,1,0:T(8,128)(2,1)}, bf16[2,256,1024]{2,1,0:T(8,128)(2,1)}, u32[]{:S(2)}, u32[]{:S(2)}) collective-permute-start(bf16[2,256,1024]{2,1,0:T(8,128)(2,1)} %get-tuple-element.64), channel_id=1, source_target_pairs={{0,5},{1,4},{2,7},{3,6},{4,1},{5,0},{6,3},{7,2},{8,13},{9,12},{10,... | collective-permute-start | bytes 3145736 | tf_op jit(solution)/shard_map/ppermute | solution.py:39
  100.3 3.7 %collective-permute-start.17 = (f32[1,512]{1,0:T(1,128)S(1)}, f32[1,512]{1,0:T(1,128)S(1)}, u32[]{:S(2)}, u32[]{:S(2)}) collective-permute-start(f32[1,512]{1,0:T(1,128)S(1)} %add.180), channel_id=1, source_target_pairs={{0,32},{16,48},{32,0},{48,16},{64,96},{80,112},{96,64},{112,80},{1... | collective-permute-start | bytes 6152 | tf_op jit(solution)/shard_map/ppermute | solution.py:43
  104.0 4.8 %collective-permute-start.18 = (f32[1,512]{1,0:T(1,128)S(1)}, f32[1,512]{1,0:T(1,128)S(1)}, u32[]{:S(2)}, u32[]{:S(2)}) collective-permute-start(f32[1,512]{1,0:T(1,128)S(1)} %add.181), channel_id=1, source_target_pairs={{0,64},{16,80},{32,96},{48,112},{64,0},{80,16},{96,32},{112,48},{1... | collective-permute-start | bytes 6152 | tf_op jit(solution)/shard_map/ppermute | solution.py:43
  108.8 8.4 %collective-permute-start.19 = (f32[1,512]{1,0:T(1,128)S(1)}, f32[1,512]{1,0:T(1,128)S(1)}, u32[]{:S(2)}, u32[]{:S(2)}) collective-permute-start(f32[1,512]{1,0:T(1,128)S(1)} %add.182), channel_id=1, source_target_pairs={{0,128},{16,144},{32,160},{48,176},{64,192},{80,208},{96,224},{112... | collective-permute-start | bytes 6152 | tf_op jit(solution)/shard_map/ppermute | solution.py:43
  117.2 1.6 %copy-start.1 = (bf16[512,2048]{1,0:T(8,128)(2,1)S(1)}, bf16[512,2048]{1,0:T(8,128)(2,1)}, u32[]{:S(2)}) copy-start(bf16[512,2048]{1,0:T(8,128)(2,1)} %get-tuple-element.55.low_hbm.low_ref) | copy-start | bytes 6291460
  120.0 2.9 %copy-start.5 = (f32[1,2048]{1,0:T(1,128)}, f32[1,2048]{1,0:T(1,128)S(1)}, u32[]{:S(2)}) copy-start(f32[1,2048]{1,0:T(1,128)S(1)} %get-tuple-element.62.scale_ref) | copy-start | bytes 24580
  120.0 14.1 %collective-permute-start.20 = (f32[1,2048]{1,0:T(1,128)S(1)}, f32[1,2048]{1,0:T(1,128)S(1)}, u32[]{:S(2)}, u32[]{:S(2)}) collective-permute-start(f32[1,2048]{1,0:T(1,128)S(1)} %get-tuple-element.62.scale_ref), channel_id=1, source_target_pairs={{0,5},{1,4},{2,7},{3,6},{4,1},{5,0},{6,3},{7,2},{8,13},{9,12},{10,... | collective-permute-start | bytes 24584 | tf_op jit(solution)/shard_map/ppermute | solution.py:39
  142.4 11.0 %collective-permute-start.24 = (bf16[16,128,128]{2,1,0:T(8,128)(2,1)}, bf16[16,128,128]{2,1,0:T(8,128)(2,1)S(1)}, u32[]{:S(2)}, u32[]{:S(2)}) collective-permute-start(bf16[16,128,128]{2,1,0:T(8,128)(2,1)} %get-tuple-element.73), channel_id=1, source_target_pairs={{0,1},{1,0},{2,3},{3,2},{4,5},{5,4},{6,7},{7,6},{8,9},{9,8},{10,11... | collective-permute-start | bytes 1572872 | tf_op jit(solution)/shard_map/ppermute | solution.py:39
  142.5 11.8 %collective-permute-start.25 = (bf16[16,128,128]{2,1,0:T(8,128)(2,1)}, bf16[16,128,128]{2,1,0:T(8,128)(2,1)S(1)}, u32[]{:S(2)}, u32[]{:S(2)}) collective-permute-start(bf16[16,128,128]{2,1,0:T(8,128)(2,1)} %get-tuple-element.74), channel_id=1, source_target_pairs={{0,4},{1,5},{2,6},{3,7},{4,0},{5,1},{6,2},{7,3},{8,12},{9,13},{10,... | collective-permute-start | bytes 1572872 | tf_op jit(solution)/shard_map/ppermute | solution.py:39
  154.3 1.6 %copy-start.2 = (f32[32,128,128]{2,1,0:T(8,128)S(1)}, f32[32,128,128]{2,1,0:T(8,128)}, u32[]{:S(2)}) copy-start(f32[32,128,128]{2,1,0:T(8,128)} %shard_map.129.own_ref) | copy-start | bytes 6291460
  (1 other events, 0.6 us)

commit v7 on v3

--- a/solution.py
+++ b/solution.py
@@ -482,10 +482,10 @@
         batch_weights,
     )
     facts = (facts, swap(facts, X3), swap(facts, Y3), swap(facts, X3 ^ Y3))
-    location, sent, *facts = lax.optimization_barrier((atom_places(atom_grid_index), dens_tiles, *facts))
+    location, sent, *facts = lax.optimization_barrier((atom_places(atom_grid_index), orbitals, *facts))
     half = TILE_DEV // 2
-    tile_x, tile_y = swap(sent, X1), swap(sent, Y1)
-    orb_x, orb_y = swap(orbitals, X3), swap(orbitals, Y3)
+    tile_x, tile_y = swap(dens_tiles, X1), swap(dens_tiles, Y1)
+    orb_x, orb_y = swap(sent, X3), swap(sent, Y3)
     tile_low, tile_high = swap(tile_y[:half], X1), swap(tile_x[half:], Y1)
     orb_first, orb_second = swap(orb_y[0], X3), swap(orb_x[1], Y3)
     orbs = (orbitals, orb_x, orb_y, orb_first, orb_second)
@@ -542,7 +542,7 @@
     order = (a + 1, a, a + 3, a + 2)
     part = part + jnp.concatenate([got[:a]] + [got[r : r + 1] for r in order] + [jnp.zeros((LISTERS, KM), F32)])
     got = swap(part, Y3)
-    density = part[a] + got[a + 2]
+    density_got = got[a + 2]
     moments, orb_far = lax.optimization_barrier((part[:a] + got[:a], orb_far))
     orb_far_x, orb_far_y = swap(orb_far, X3), swap(orb_far, Y3)
     got = swap(jnp.concatenate([moments, part[a + LISTERS :]]), X1)
@@ -555,9 +555,6 @@
     structure = jnp.sum(moments[:, :1] * trig, axis=0, keepdims=True)
     for bits in (1, 2, 4, 8):
         structure = structure + swap_grp(structure, bits)
-    structure, own_codes, own_counts, far_codes, far_counts, far_blocks = lax.optimization_barrier(
-        (structure, own_codes, own_counts, far_codes, far_counts, far_blocks)
-    )
     potential, scale = potential_of(
         moments,
         far_gain * structure,
@@ -570,7 +567,7 @@
     )
     far_scale = swap(scale, XY)
     own, shared = ham_terms(
-        codes, counts, blocks, scale, orbs, (), ((TILE_DEV, F32), (TILE_DEV, F32)), 2 * 10**10
+        codes, counts, blocks, scale, orbs, (), ((TILE_DEV, F32), (TILE_DEV, F32)), 10**6
     )
     half = TILE_DEV // 2
     part_x, part_y = ham_terms(
@@ -579,7 +576,8 @@
     (own,) = ham_terms(
         own_codes, own_counts, far_blocks, far_scale, orbs_far, (own,), ((TILE_DEV, F32),), 2 * 10**10
     )
-    return (density, potential.reshape(-1), final_tiles(own, swap(part_x, X1), swap(part_y, Y1)))
+    density, other, part_x = lax.optimization_barrier((part[a], density_got, part_x))
+    return (density + other, potential.reshape(-1), final_tiles(own, swap(part_x, X1), swap(part_y, Y1)))
 
 
 def solution(mesh):

time: 167 us -> 149 us (0.89); the launches traced: 166 us -> 146 us
  waiting for transfers between devices: 49.6 us -> 26.7 us
  starting transfers between devices: 42.3 us -> 50.9 us
  Pallas kernels: 52.6 us -> 48.6 us
    ppermute x22, waiting for transfers between devices: 47.7 us -> 23.8 us  [swap(): return lax.ppermute(array, 'dev', [(d, d ^ bits) for d in range(16)])]
    ppermute x22, starting transfers between devices: 30.2 us -> 38.7 us  [swap(): return lax.ppermute(array, 'dev', [(d, d ^ bits) for d in range(16)])]
    pallas_call x3, Pallas kernels: 29.3 us -> 25.3 us  [ham_terms(): pl.pallas_call(functools.partial(ham_kernel, len(starts), len(outs)), in_...]
  transfers between devices with their start and end apart: 26 -> 26, of which waited for: 15 -> 16; matrix products, arithmetic and copies ran while one was open for 9% -> 10% of each run, Pallas kernels for 25% -> 26%
where the time goes in v7:
time: 149 us; the launch traced here: 146 us
  starting transfers between devices  50.9 us (34%)
  Pallas kernels  48.6 us (33%)
  waiting for transfers between devices  26.7 us (18%)
  other arithmetic  10.6 us (7%)
  local copies, waits for them, and re-layouts  8.28 us (6%)
    ppermute x22, starting transfers between devices, swap(): return lax.ppermute(array, 'dev', [(d, d ^ bits) for d in range(16)])  38.7 us
    pallas_call x3, Pallas kernels, ham_terms(): pl.pallas_call(functools.partial(ham_kernel, len(starts), len(outs)), in_...  25.3 us
    ppermute x22, waiting for transfers between devices, swap(): return lax.ppermute(array, 'dev', [(d, d ^ bits) for d in range(16)])  23.8 us
    ppermute x4, starting transfers between devices, swap_grp(): return lax.ppermute(array, 'grp', [(g, g ^ bits) for g in range(16)])  12.2 us
    pallas_call x1, Pallas kernels, density_and_moments(): pl.pallas_call(density_kernel, in_specs=[SMEM_SPEC] * 2 + [ANY_SPEC] * 10...  12 us
    pallas_call x1, Pallas kernels, wave_of_points(): pl.pallas_call(wave_kernel, grid=(points // chunk,), in_specs=[pl.BlockSp...  5.74 us
    unnamed x44, local copies, waits for them, and re-layouts  4.26 us
  transfers between devices with their start and end apart: 26, of which 16 were waited for; matrix products, arithmetic and copies ran while one was open for 10% of the time, Pallas kernels for 26%

profile of v7, /device:TPU:2, one launch (start us, length us, event | category | flops | bytes accessed | tf_op | source)
XLA Modules:
  0.0 146.4 jit_solution(6285933724024045824)
XLA Ops:
  0.6 1.4 shard_map.122
  2.1 1.6 %collective-permute-start = (f32[6,512]{1,0:T(8,128)}, f32[6,512]{1,0:T(8,128)S(1)}, u32[]{:S(2)}, u32[]{:S(2)}) collective-permute-start(f32[6,512]{1,0:T(8,128)} %shard_map.122), channel_id=1, source_target_pairs={{0,3},{1,2},{2,1},{3,0},{4,7},{5,6},{6,5},{7,4},{8,11},{9,10},{10,... | collective-permute-start | bytes 36872 | tf_op jit(solution)/shard_map/ppermute | solution.py:39
  3.7 3.0 %collective-permute-start.1 = (f32[6,512]{1,0:T(8,128)}, f32[6,512]{1,0:T(8,128)S(1)}, u32[]{:S(2)}, u32[]{:S(2)}) collective-permute-start(f32[6,512]{1,0:T(8,128)} %shard_map.122), channel_id=1, source_target_pairs={{0,12},{1,13},{2,14},{3,15},{4,8},{5,9},{6,10},{7,11},{8,4},{9,5},... | collective-permute-start | bytes 36872 | tf_op jit(solution)/shard_map/ppermute | solution.py:39
  7.2 3.1 %collective-permute-start.5 = (bf16[32,128,128]{2,1,0:T(8,128)(2,1)}, bf16[32,128,128]{2,1,0:T(8,128)(2,1)}, u32[]{:S(2)}, u32[]{:S(2)}) collective-permute-start(bf16[32,128,128]{2,1,0:T(8,128)(2,1)} %own_tile.1), channel_id=1, source_target_pairs={{0,1},{1,0},{2,3},{3,2},{4,5},{5,4},{6,7},{7,6},{8,9},{9,8},{10,11... | collective-permute-start | bytes 3145736 | tf_op jit(solution)/shard_map/ppermute | solution.py:39
  10.4 1.3 shard_map.121
  11.7 1.0 collective-permute-done.2
  14.2 1.9 %collective-permute-start.7 = (bf16[2,256,1024]{2,1,0:T(8,128)(2,1)}, bf16[2,256,1024]{2,1,0:T(8,128)(2,1)S(1)}, u32[]{:S(2)}, u32[]{:S(2)}) collective-permute-start(bf16[2,256,1024]{2,1,0:T(8,128)(2,1)} %refs_0_.1), channel_id=1, source_target_pairs={{0,12},{1,13},{2,14},{3,15},{4,8},{5,9},{6,10},{7,11},{8,4},{9,5},... | collective-permute-start | bytes 3145736 | tf_op jit(solution)/shard_map/ppermute | solution.py:39
  16.5 0.7 fusion.1
  17.3 0.8 pad_maximum_fusion
  20.6 5.7 %shard_map.123 = (bf16[512,2048]{1,0:T(8,128)(2,1)}, bf16[512,2048]{1,0:T(8,128)(2,1)}) custom-call(f32[48,2048]{1,0:T(8,128)} %bitcast.50), custom_call_target="tpu_custom_call" | custom-call | flops 8388608 | bytes 4194304 | tf_op jit(solution)/shard_map/pallas_call | solution.py:87
  27.9 3.3 %collective-permute-done.3.y_tile = bf16[32,128,128]{2,1,0:T(8,128)(2,1)S(1)} collective-permute-done((bf16[32,128,128]{2,1,0:T(8,128)(2,1)}, bf16[32,128,128]{2,1,0:T(8,128)(2,1)S(1)}, u32[]{:S(2)}, u32[]{:S(2)}) %collective-permute-start.3) | collective-permute-done | bytes 1048608 | tf_op jit(solution)/shard_map/ppermute | solution.py:39
  31.3 1.9 %collective-permute-start.4 = (bf16[16,128,128]{2,1,0:T(8,128)(2,1)S(1)}, bf16[16,128,128]{2,1,0:T(8,128)(2,1)S(1)}, u32[]{:S(2)}, u32[]{:S(2)}) collective-permute-start(bf16[16,128,128]{2,1,0:T(8,128)(2,1)S(1)} %slice.142), channel_id=1, source_target_pairs={{0,1},{1,0},{2,3},{3,2},{4,5},{5,4},{6,7},{7,6},{8,9},{9,8},{10,11... | collective-permute-start | bytes 1572872 | tf_op jit(solution)/shard_map/ppermute | solution.py:39
  33.2 1.1 slice.143
  34.3 1.1 collective-permute-start.6
  35.4 1.7 %collective-permute-done.9.x_orb.refs_1_ = bf16[2,256,1024]{2,1,0:T(8,128)(2,1)S(1)} collective-permute-done((bf16[2,256,1024]{2,1,0:T(8,128)(2,1)}, bf16[2,256,1024]{2,1,0:T(8,128)(2,1)S(1)}, u32[]{:S(2)}, u32[]{:S(2)}) %collective-permute-start.9) | collective-permute-done | bytes 1048608 | tf_op jit(solution)/shard_map/ppermute | solution.py:39
  37.1 1.4 collective-permute-start.10
  38.9 2.4 %collective-permute-start.8 = (bf16[256,1024]{1,0:T(8,128)(2,1)S(1)}, bf16[256,1024]{1,0:T(8,128)(2,1)S(1)}, u32[]{:S(2)}, u32[]{:S(2)}) collective-permute-start(bf16[256,1024]{1,0:T(8,128)(2,1)S(1)} %slice_bitcast_fusion.1), channel_id=1, source_target_pairs={{0,3},{1,2},{2,1},{3,0},{4,7},{5,6},{6,5},{7,4},{8,11},{9,10},{10,... | collective-permute-start | bytes 1572872 | tf_op jit(solution)/shard_map/ppermute | solution.py:39
  42.6 0.9 collective-permute-done.4.low_tile
  43.5 1.4 collective-permute-done.6.high_tile
  44.9 4.9 %collective-permute-done.10.second_orb.refs_4_ = bf16[256,1024]{1,0:T(8,128)(2,1)S(1)} collective-permute-done((bf16[256,1024]{1,0:T(8,128)(2,1)S(1)}, bf16[256,1024]{1,0:T(8,128)(2,1)S(1)}, u32[]{:S(2)}, u32[]{:S(2)}) %collective-permute-start.10) | collective-permute-done | bytes 524320 | tf_op jit(solution)/shard_map/ppermute | solution.py:39
  50.2 2.4 %collective-permute-start.13 = (bf16[2,256,1024]{2,1,0:T(8,128)(2,1)}, bf16[2,256,1024]{2,1,0:T(8,128)(2,1)}, u32[]{:S(2)}, u32[]{:S(2)}) collective-permute-start(bf16[2,256,1024]{2,1,0:T(8,128)(2,1)} %refs_0_.1), channel_id=1, source_target_pairs={{0,5},{1,4},{2,7},{3,6},{4,1},{5,0},{6,3},{7,2},{8,13},{9,12},{10,... | collective-permute-start | bytes 3145736 | tf_op jit(solution)/shard_map/ppermute | solution.py:39
  52.7 12.0 %shard_map.124 = (f32[24,512]{1,0:T(8,128)}, bf16[2,256,1024]{2,1,0:T(8,128)(2,1)}) custom-call(s32[4,81]{1,0:T(4,128)} %get-tuple-element.44.tmap_ref, s32[8,8]{1,0:T(8,128)} %bitcast.56, bf16[32,128,128]{2,1,0:T(8,128)(2,1)} %own_tile.1, bf16[32,128,128]{2,1,0:T(8,128)(2,1)} %collective-permute-done.5.x_tile, bf16[32,128,128]{2,1,0:T(8,128)(2,1)} %copy-done.8, ...), custom_call_target="tpu_custom_call" | custom-call | flops 1000000 | bytes 10000 | tf_op jit(solution)/shard_map/pallas_call | solution.py:217
  64.7 2.4 %collective-permute-start.11 = (f32[24,512]{1,0:T(8,128)}, f32[24,512]{1,0:T(8,128)S(1)}, u32[]{:S(2)}, u32[]{:S(2)}) collective-permute-start(f32[24,512]{1,0:T(8,128)} %get-tuple-element.51), channel_id=1, source_target_pairs={{0,3},{1,2},{2,1},{3,0},{4,7},{5,6},{6,5},{7,4},{8,11},{9,10},{10,... | collective-permute-start | bytes 147464 | tf_op jit(solution)/shard_map/ppermute | solution.py:39
  67.2 2.3 %collective-permute-done.11 = f32[24,512]{1,0:T(8,128)S(1)} collective-permute-done((f32[24,512]{1,0:T(8,128)}, f32[24,512]{1,0:T(8,128)S(1)}, u32[]{:S(2)}, u32[]{:S(2)}) %collective-permute-start.11) | collective-permute-done | bytes 49184 | tf_op jit(solution)/shard_map/ppermute | solution.py:39
  69.5 0.8 add.173
  70.3 1.6 %collective-permute-start.12 = (f32[24,512]{1,0:T(8,128)S(1)}, f32[24,512]{1,0:T(8,128)S(1)}, u32[]{:S(2)}, u32[]{:S(2)}) collective-permute-start(f32[24,512]{1,0:T(8,128)S(1)} %add.173), channel_id=1, source_target_pairs={{0,12},{1,13},{2,14},{3,15},{4,8},{5,9},{6,10},{7,11},{8,4},{9,5},... | collective-permute-start | bytes 147464 | tf_op jit(solution)/shard_map/ppermute | solution.py:39
  71.9 3.7 %collective-permute-done.12 = f32[24,512]{1,0:T(8,128)S(1)} collective-permute-done((f32[24,512]{1,0:T(8,128)S(1)}, f32[24,512]{1,0:T(8,128)S(1)}, u32[]{:S(2)}, u32[]{:S(2)}) %collective-permute-start.12) | collective-permute-done | bytes 49184 | tf_op jit(solution)/shard_map/ppermute | solution.py:39
  75.6 3.0 %collective-permute-start.14 = (f32[20,512]{1,0:T(8,128)S(1)}, f32[20,512]{1,0:T(8,128)S(1)}, u32[]{:S(2)}, u32[]{:S(2)}) collective-permute-start(f32[20,512]{1,0:T(8,128)S(1)} %pad_maximum_fusion.2), channel_id=1, source_target_pairs={{0,1},{1,0},{2,3},{3,2},{4,5},{5,4},{6,7},{7,6},{8,9},{9,8},{10,11... | collective-permute-start | bytes 122888 | tf_op jit(solution)/shard_map/ppermute | solution.py:39
  78.6 2.1 %collective-permute-done.14 = f32[20,512]{1,0:T(8,128)S(1)} collective-permute-done((f32[20,512]{1,0:T(8,128)S(1)}, f32[20,512]{1,0:T(8,128)S(1)}, u32[]{:S(2)}, u32[]{:S(2)}) %collective-permute-start.14) | collective-permute-done | bytes 40992 | tf_op jit(solution)/shard_map/ppermute | solution.py:39
  81.4 1.7 %collective-permute-start.21 = (bf16[2,256,1024]{2,1,0:T(8,128)(2,1)}, bf16[2,256,1024]{2,1,0:T(8,128)(2,1)S(1)}, u32[]{:S(2)}, u32[]{:S(2)}) collective-permute-start(bf16[2,256,1024]{2,1,0:T(8,128)(2,1)} %collective-permute-done.13.refs_0_), channel_id=1, source_target_pairs={{0,3},{1,2},{2,1},{3,0},{4,7},{5,6},{6,5},{7,4},{8,11},{9,10},{10,... | collective-permute-start | bytes 3145736 | tf_op jit(solution)/shard_map/ppermute | solution.py:39
  83.1 1.1 collective-permute-start.22
  85.6 2.4 %collective-permute-start.23 = (bf16[2,256,1024]{2,1,0:T(8,128)(2,1)}, bf16[2,256,1024]{2,1,0:T(8,128)(2,1)}, u32[]{:S(2)}, u32[]{:S(2)}) collective-permute-start(bf16[2,256,1024]{2,1,0:T(8,128)(2,1)} %get-tuple-element.58), channel_id=1, source_target_pairs={{0,5},{1,4},{2,7},{3,6},{4,1},{5,0},{6,3},{7,2},{8,13},{9,12},{10,... | collective-permute-start | bytes 3145736 | tf_op jit(solution)/shard_map/ppermute | solution.py:39
  88.4 2.0 %collective-permute-start.17 = (f32[1,512]{1,0:T(1,128)S(1)}, f32[1,512]{1,0:T(1,128)S(1)}, u32[]{:S(2)}, u32[]{:S(2)}) collective-permute-start(f32[1,512]{1,0:T(1,128)S(1)} %add.180), channel_id=1, source_target_pairs={{0,32},{16,48},{32,0},{48,16},{64,96},{80,112},{96,64},{112,80},{1... | collective-permute-start | bytes 6152 | tf_op jit(solution)/shard_map/ppermute | solution.py:43
  91.1 1.0 collective-permute-done.17
  92.1 3.3 %collective-permute-start.18 = (f32[1,512]{1,0:T(1,128)S(1)}, f32[1,512]{1,0:T(1,128)S(1)}, u32[]{:S(2)}, u32[]{:S(2)}) collective-permute-start(f32[1,512]{1,0:T(1,128)S(1)} %add.181), channel_id=1, source_target_pairs={{0,64},{16,80},{32,96},{48,112},{64,0},{80,16},{96,32},{112,48},{1... | collective-permute-start | bytes 6152 | tf_op jit(solution)/shard_map/ppermute | solution.py:43
  96.0 0.9 collective-permute-done.18
  97.0 6.8 %collective-permute-start.19 = (f32[1,512]{1,0:T(1,128)S(1)}, f32[1,512]{1,0:T(1,128)S(1)}, u32[]{:S(2)}, u32[]{:S(2)}) collective-permute-start(f32[1,512]{1,0:T(1,128)S(1)} %add.182), channel_id=1, source_target_pairs={{0,128},{16,144},{32,160},{48,176},{64,192},{80,208},{96,224},{112... | collective-permute-start | bytes 6152 | tf_op jit(solution)/shard_map/ppermute | solution.py:43
  104.4 1.0 collective-permute-done.19
  105.4 1.6 %copy-done.1 = bf16[512,2048]{1,0:T(8,128)(2,1)S(1)} copy-done((bf16[512,2048]{1,0:T(8,128)(2,1)S(1)}, bf16[512,2048]{1,0:T(8,128)(2,1)}, u32[]{:S(2)}) %copy-start.1) | copy-done | bytes 2097176
  107.0 1.2 shard_map.125
  109.9 9.4 %shard_map.126 = (f32[32,128,128]{2,1,0:T(8,128)}, f32[32,128,128]{2,1,0:T(8,128)}) custom-call(s32[4,32]{1,0:T(4,128)} %fusion.8.codes_ref, s32[4]{0:T(128)} %and_select_fusion.6.counts_ref, s32[8,8]{1,0:T(8,128)} %bitcast.57, f32[1,2048]{1,0:T(1,128)} %copy-done.5, bf16[2,256,1024]{2,1,0:T(8,128)(2,1)} %refs_0_.1, bf16[2,256,1024]{2,1,0:T(8,128)(2,1)} %copy-done.6, ...), custom_call_target="tpu_custom_call" | custom-call | flops 1000000 | bytes 10000 | tf_op jit(solution)/shard_map/pallas_call | solution.py:387
  120.3 8.0 %shard_map.127 = (bf16[16,128,128]{2,1,0:T(8,128)(2,1)}, bf16[16,128,128]{2,1,0:T(8,128)(2,1)}) custom-call(s32[4,32]{1,0:T(4,128)} %fusion.9.codes_ref, s32[4]{0:T(128)} %and_select_fusion.5.counts_ref, s32[8,8]{1,0:T(8,128)} %bitcast.60, f32[1,2048]{1,0:T(1,128)} %copy-done.16, bf16[2,256,1024]{2,1,0:T(8,128)(2,1)} %collective-permute-done.13.refs_0_, ...), custom_call_target="tpu_custom_call" | custom-call | flops 1000000 | bytes 10000 | tf_op jit(solution)/shard_map/pallas_call | solution.py:387
  128.4 3.0 %collective-permute-start.24 = (bf16[16,128,128]{2,1,0:T(8,128)(2,1)}, bf16[16,128,128]{2,1,0:T(8,128)(2,1)S(1)}, u32[]{:S(2)}, u32[]{:S(2)}) collective-permute-start(bf16[16,128,128]{2,1,0:T(8,128)(2,1)} %get-tuple-element.67), channel_id=1, source_target_pairs={{0,1},{1,0},{2,3},{3,2},{4,5},{5,4},{6,7},{7,6},{8,9},{9,8},{10,11... | collective-permute-start | bytes 1572872 | tf_op jit(solution)/shard_map/ppermute | solution.py:39
  131.3 2.3 %collective-permute-start.25 = (bf16[16,128,128]{2,1,0:T(8,128)(2,1)}, bf16[16,128,128]{2,1,0:T(8,128)(2,1)S(1)}, u32[]{:S(2)}, u32[]{:S(2)}) collective-permute-start(bf16[16,128,128]{2,1,0:T(8,128)(2,1)} %get-tuple-element.68), channel_id=1, source_target_pairs={{0,4},{1,5},{2,6},{3,7},{4,0},{5,1},{6,2},{7,3},{8,12},{9,13},{10,... | collective-permute-start | bytes 1572872 | tf_op jit(solution)/shard_map/ppermute | solution.py:39
  133.6 7.8 %shard_map.128.own_ref = f32[32,128,128]{2,1,0:T(8,128)} custom-call(s32[4,32]{1,0:T(4,128)} %fusion.10.codes_ref, s32[4]{0:T(128)} %and_select_fusion.4.counts_ref, s32[8,8]{1,0:T(8,128)} %bitcast.61, f32[1,2048]{1,0:T(1,128)} %copy-done.16, bf16[2,256,1024]{2,1,0:T(8,128)(2,1)} %collective-permute-done.13.refs_0_, bf16[2,256,1024]{2,1,0:T(8,128)(2,1)} %copy-done.11, ...), custom_call_target="tpu_custom_call" | custom-call | flops 20000000000 | bytes 10000 | tf_op jit(solution)/shard_map/pallas_call | solution.py:387
  142.1 1.1 collective-permute-done.25.y_ref
  143.2 1.6 %copy-done.2 = f32[32,128,128]{2,1,0:T(8,128)S(1)} copy-done((f32[32,128,128]{2,1,0:T(8,128)S(1)}, f32[32,128,128]{2,1,0:T(8,128)}, u32[]{:S(2)}) %copy-start.2) | copy-done | bytes 2097176
  144.8 1.7 %shard_map.129 = bf16[32,128,128]{2,1,0:T(8,128)(2,1)} custom-call(f32[32,128,128]{2,1,0:T(8,128)S(1)} %copy-done.2, bf16[16,128,128]{2,1,0:T(8,128)(2,1)S(1)} %collective-permute-done.24.x_ref, bf16[16,128,128]{2,1,0:T(8,128)(2,1)S(1)} %collective-permute-done.25.y_ref), custom_call_target="tpu_custom_call" | custom-call | flops 1000000 | bytes 10000 | tf_op jit(solution)/shard_map/pallas_call | solution.py:414
  (132 shorter events, 16.6 us)
Async XLA Ops:
  2.1 9.6 %collective-permute-start = (f32[6,512]{1,0:T(8,128)}, f32[6,512]{1,0:T(8,128)S(1)}, u32[]{:S(2)}, u32[]{:S(2)}) collective-permute-start(f32[6,512]{1,0:T(8,128)} %shard_map.122), channel_id=1, source_target_pairs={{0,3},{1,2},{2,1},{3,0},{4,7},{5,6},{6,5},{7,4},{8,11},{9,10},{10,... | collective-permute-start | bytes 36872 | tf_op jit(solution)/shard_map/ppermute | solution.py:39
  3.7 8.0 %collective-permute-start.1 = (f32[6,512]{1,0:T(8,128)}, f32[6,512]{1,0:T(8,128)S(1)}, u32[]{:S(2)}, u32[]{:S(2)}) collective-permute-start(f32[6,512]{1,0:T(8,128)} %shard_map.122), channel_id=1, source_target_pairs={{0,12},{1,13},{2,14},{3,15},{4,8},{5,9},{6,10},{7,11},{8,4},{9,5},... | collective-permute-start | bytes 36872 | tf_op jit(solution)/shard_map/ppermute | solution.py:39
  6.7 6.1 %collective-permute-start.2 = (f32[6,512]{1,0:T(8,128)}, f32[6,512]{1,0:T(8,128)S(1)}, u32[]{:S(2)}, u32[]{:S(2)}) collective-permute-start(f32[6,512]{1,0:T(8,128)} %shard_map.122), channel_id=1, source_target_pairs={{0,15},{1,14},{2,13},{3,12},{4,11},{5,10},{6,9},{7,8},{8,7},{9,6},... | collective-permute-start | bytes 36872 | tf_op jit(solution)/shard_map/ppermute | solution.py:39
  6.9 24.4 %collective-permute-start.3 = (bf16[32,128,128]{2,1,0:T(8,128)(2,1)}, bf16[32,128,128]{2,1,0:T(8,128)(2,1)S(1)}, u32[]{:S(2)}, u32[]{:S(2)}) collective-permute-start(bf16[32,128,128]{2,1,0:T(8,128)(2,1)} %own_tile.1), channel_id=1, source_target_pairs={{0,4},{1,5},{2,6},{3,7},{4,0},{5,1},{6,2},{7,3},{8,12},{9,13},{10,... | collective-permute-start | bytes 3145736 | tf_op jit(solution)/shard_map/ppermute | solution.py:39
  7.2 25.9 %collective-permute-start.5 = (bf16[32,128,128]{2,1,0:T(8,128)(2,1)}, bf16[32,128,128]{2,1,0:T(8,128)(2,1)}, u32[]{:S(2)}, u32[]{:S(2)}) collective-permute-start(bf16[32,128,128]{2,1,0:T(8,128)(2,1)} %own_tile.1), channel_id=1, source_target_pairs={{0,1},{1,0},{2,3},{3,2},{4,5},{5,4},{6,7},{7,6},{8,9},{9,8},{10,11... | collective-permute-start | bytes 3145736 | tf_op jit(solution)/shard_map/ppermute | solution.py:39
  10.4 2.3 %copy-start.15 = (f32[6,512]{1,0:T(8,128)S(1)}, f32[6,512]{1,0:T(8,128)}, u32[]{:S(2)}) copy-start(f32[6,512]{1,0:T(8,128)} %shard_map.122) | copy-start | bytes 36868
  11.7 14.7 %copy-start.17 = (f32[3,16]{1,0:T(4,128)S(1)}, f32[3,16]{1,0:T(4,128)}, u32[]{:S(2)}) copy-start(f32[3,16]{1,0:T(4,128)} %shard_map.121) | copy-start | bytes 580
  13.6 23.5 %collective-permute-start.9 = (bf16[2,256,1024]{2,1,0:T(8,128)(2,1)}, bf16[2,256,1024]{2,1,0:T(8,128)(2,1)S(1)}, u32[]{:S(2)}, u32[]{:S(2)}) collective-permute-start(bf16[2,256,1024]{2,1,0:T(8,128)(2,1)} %refs_0_.1), channel_id=1, source_target_pairs={{0,3},{1,2},{2,1},{3,0},{4,7},{5,6},{6,5},{7,4},{8,11},{9,10},{10,... | collective-permute-start | bytes 3145736 | tf_op jit(solution)/shard_map/ppermute | solution.py:39
  14.2 24.6 %collective-permute-start.7 = (bf16[2,256,1024]{2,1,0:T(8,128)(2,1)}, bf16[2,256,1024]{2,1,0:T(8,128)(2,1)S(1)}, u32[]{:S(2)}, u32[]{:S(2)}) collective-permute-start(bf16[2,256,1024]{2,1,0:T(8,128)(2,1)} %refs_0_.1), channel_id=1, source_target_pairs={{0,12},{1,13},{2,14},{3,15},{4,8},{5,9},{6,10},{7,11},{8,4},{9,5},... | collective-permute-start | bytes 3145736 | tf_op jit(solution)/shard_map/ppermute | solution.py:39
  31.2 7.6 %copy-start.8 = (bf16[32,128,128]{2,1,0:T(8,128)(2,1)}, bf16[32,128,128]{2,1,0:T(8,128)(2,1)S(1)}, u32[]{:S(2)}) copy-start(bf16[32,128,128]{2,1,0:T(8,128)(2,1)S(1)} %collective-permute-done.3.y_tile) | copy-start | bytes 3145732
  31.3 12.2 %collective-permute-start.4 = (bf16[16,128,128]{2,1,0:T(8,128)(2,1)S(1)}, bf16[16,128,128]{2,1,0:T(8,128)(2,1)S(1)}, u32[]{:S(2)}, u32[]{:S(2)}) collective-permute-start(bf16[16,128,128]{2,1,0:T(8,128)(2,1)S(1)} %slice.142), channel_id=1, source_target_pairs={{0,1},{1,0},{2,3},{3,2},{4,5},{5,4},{6,7},{7,6},{8,9},{9,8},{10,11... | collective-permute-start | bytes 1572872 | tf_op jit(solution)/shard_map/ppermute | solution.py:39
  34.3 10.6 %collective-permute-start.6 = (bf16[16,128,128]{2,1,0:T(8,128)(2,1)S(1)}, bf16[16,128,128]{2,1,0:T(8,128)(2,1)S(1)}, u32[]{:S(2)}, u32[]{:S(2)}) collective-permute-start(bf16[16,128,128]{2,1,0:T(8,128)(2,1)S(1)} %slice.143), channel_id=1, source_target_pairs={{0,4},{1,5},{2,6},{3,7},{4,0},{5,1},{6,2},{7,3},{8,12},{9,13},{10,... | collective-permute-start | bytes 1572872 | tf_op jit(solution)/shard_map/ppermute | solution.py:39
  37.1 15.6 %copy-start.6 = (bf16[2,256,1024]{2,1,0:T(8,128)(2,1)}, bf16[2,256,1024]{2,1,0:T(8,128)(2,1)S(1)}, u32[]{:S(2)}) copy-start(bf16[2,256,1024]{2,1,0:T(8,128)(2,1)S(1)} %collective-permute-done.9.x_orb.refs_1_) | copy-start | bytes 3145732
  37.1 12.7 %collective-permute-start.10 = (bf16[256,1024]{1,0:T(8,128)(2,1)S(1)}, bf16[256,1024]{1,0:T(8,128)(2,1)S(1)}, u32[]{:S(2)}, u32[]{:S(2)}) collective-permute-start(bf16[256,1024]{1,0:T(8,128)(2,1)S(1)} %slice_bitcast_fusion), channel_id=1, source_target_pairs={{0,12},{1,13},{2,14},{3,15},{4,8},{5,9},{6,10},{7,11},{8,4},{9,5},... | collective-permute-start | bytes 1572872 | tf_op jit(solution)/shard_map/ppermute | solution.py:39
  38.8 13.8 %copy-start.7 = (bf16[2,256,1024]{2,1,0:T(8,128)(2,1)}, bf16[2,256,1024]{2,1,0:T(8,128)(2,1)S(1)}, u32[]{:S(2)}) copy-start(bf16[2,256,1024]{2,1,0:T(8,128)(2,1)S(1)} %collective-permute-done.7.y_orb.refs_2_) | copy-start | bytes 3145732
  38.9 11.4 %collective-permute-start.8 = (bf16[256,1024]{1,0:T(8,128)(2,1)S(1)}, bf16[256,1024]{1,0:T(8,128)(2,1)S(1)}, u32[]{:S(2)}, u32[]{:S(2)}) collective-permute-start(bf16[256,1024]{1,0:T(8,128)(2,1)S(1)} %slice_bitcast_fusion.1), channel_id=1, source_target_pairs={{0,3},{1,2},{2,1},{3,0},{4,7},{5,6},{6,5},{7,4},{8,11},{9,10},{10,... | collective-permute-start | bytes 1572872 | tf_op jit(solution)/shard_map/ppermute | solution.py:39
  43.5 9.2 %copy-start.12 = (bf16[16,128,128]{2,1,0:T(8,128)(2,1)}, bf16[16,128,128]{2,1,0:T(8,128)(2,1)S(1)}, u32[]{:S(2)}) copy-start(bf16[16,128,128]{2,1,0:T(8,128)(2,1)S(1)} %collective-permute-done.4.low_tile) | copy-start | bytes 1572868
  44.9 7.8 %copy-start.13 = (bf16[16,128,128]{2,1,0:T(8,128)(2,1)}, bf16[16,128,128]{2,1,0:T(8,128)(2,1)S(1)}, u32[]{:S(2)}) copy-start(bf16[16,128,128]{2,1,0:T(8,128)(2,1)S(1)} %collective-permute-done.6.high_tile) | copy-start | bytes 1572868
  49.8 2.9 %copy-start.9 = (bf16[256,1024]{1,0:T(8,128)(2,1)}, bf16[256,1024]{1,0:T(8,128)(2,1)S(1)}, u32[]{:S(2)}) copy-start(bf16[256,1024]{1,0:T(8,128)(2,1)S(1)} %collective-permute-done.10.second_orb.refs_4_) | copy-start | bytes 1572868
  50.2 2.4 %copy-start.10 = (bf16[256,1024]{1,0:T(8,128)(2,1)}, bf16[256,1024]{1,0:T(8,128)(2,1)S(1)}, u32[]{:S(2)}) copy-start(bf16[256,1024]{1,0:T(8,128)(2,1)S(1)} %collective-permute-done.8.first_orb.refs_3_) | copy-start | bytes 1572868
  50.2 25.3 %collective-permute-start.13 = (bf16[2,256,1024]{2,1,0:T(8,128)(2,1)}, bf16[2,256,1024]{2,1,0:T(8,128)(2,1)}, u32[]{:S(2)}, u32[]{:S(2)}) collective-permute-start(bf16[2,256,1024]{2,1,0:T(8,128)(2,1)} %refs_0_.1), channel_id=1, source_target_pairs={{0,5},{1,4},{2,7},{3,6},{4,1},{5,0},{6,3},{7,2},{8,13},{9,12},{10,... | collective-permute-start | bytes 3145736 | tf_op jit(solution)/shard_map/ppermute | solution.py:39
  52.7 28.7 %copy-start.14 = (f32[8,256]{1,0:T(8,128)S(1)}, f32[8,256]{1,0:T(8,128)}, u32[]{:S(2)}) copy-start(f32[8,256]{1,0:T(8,128)} %reshape_squeeze.12.weights_ref) | copy-start | bytes 24580
  52.7 32.7 %copy-start.4 = (f32[16,512]{1,0:T(8,128)S(1)}, f32[16,512]{1,0:T(8,128)}, u32[]{:S(2)}) copy-start(f32[16,512]{1,0:T(8,128)} %pad_maximum_fusion.4.trig_ref) | copy-start | bytes 98308
  52.7 52.7 %copy-start = (bf16[512,2048]{1,0:T(8,128)(2,1)S(1)}, bf16[512,2048]{1,0:T(8,128)(2,1)}, u32[]{:S(2)}) copy-start(bf16[512,2048]{1,0:T(8,128)(2,1)} %get-tuple-element.48.high_hbm.high_ref) | copy-start | bytes 6291460
  52.7 52.7 %copy-start.3 = (f32[16,2048]{1,0:T(8,128)S(1)}, f32[16,2048]{1,0:T(8,128)}, u32[]{:S(2)}) copy-start(f32[16,2048]{1,0:T(8,128)} %exponential_multiply_fusion.spread_ref) | copy-start | bytes 393220
  64.7 4.7 %collective-permute-start.11 = (f32[24,512]{1,0:T(8,128)}, f32[24,512]{1,0:T(8,128)S(1)}, u32[]{:S(2)}, u32[]{:S(2)}) collective-permute-start(f32[24,512]{1,0:T(8,128)} %get-tuple-element.51), channel_id=1, source_target_pairs={{0,3},{1,2},{2,1},{3,0},{4,7},{5,6},{6,5},{7,4},{8,11},{9,10},{10,... | collective-permute-start | bytes 147464 | tf_op jit(solution)/shard_map/ppermute | solution.py:39
  70.3 5.3 %collective-permute-start.12 = (f32[24,512]{1,0:T(8,128)S(1)}, f32[24,512]{1,0:T(8,128)S(1)}, u32[]{:S(2)}, u32[]{:S(2)}) collective-permute-start(f32[24,512]{1,0:T(8,128)S(1)} %add.173), channel_id=1, source_target_pairs={{0,12},{1,13},{2,14},{3,15},{4,8},{5,9},{6,10},{7,11},{8,4},{9,5},... | collective-permute-start | bytes 147464 | tf_op jit(solution)/shard_map/ppermute | solution.py:39
  75.6 5.0 %collective-permute-start.14 = (f32[20,512]{1,0:T(8,128)S(1)}, f32[20,512]{1,0:T(8,128)S(1)}, u32[]{:S(2)}, u32[]{:S(2)}) collective-permute-start(f32[20,512]{1,0:T(8,128)S(1)} %pad_maximum_fusion.2), channel_id=1, source_target_pairs={{0,1},{1,0},{2,3},{3,2},{4,5},{5,4},{6,7},{7,6},{8,9},{9,8},{10,11... | collective-permute-start | bytes 122888 | tf_op jit(solution)/shard_map/ppermute | solution.py:39
  80.7 4.2 %collective-permute-start.15 = (f32[20,512]{1,0:T(8,128)S(1)}, f32[20,512]{1,0:T(8,128)S(1)}, u32[]{:S(2)}, u32[]{:S(2)}) collective-permute-start(f32[20,512]{1,0:T(8,128)S(1)} %pad_maximum_fusion.3), channel_id=1, source_target_pairs={{0,4},{1,5},{2,6},{3,7},{4,0},{5,1},{6,2},{7,3},{8,12},{9,13},{10,... | collective-permute-start | bytes 122888 | tf_op jit(solution)/shard_map/ppermute | solution.py:39
  81.4 37.9 %collective-permute-start.21 = (bf16[2,256,1024]{2,1,0:T(8,128)(2,1)}, bf16[2,256,1024]{2,1,0:T(8,128)(2,1)S(1)}, u32[]{:S(2)}, u32[]{:S(2)}) collective-permute-start(bf16[2,256,1024]{2,1,0:T(8,128)(2,1)} %collective-permute-done.13.refs_0_), channel_id=1, source_target_pairs={{0,3},{1,2},{2,1},{3,0},{4,7},{5,6},{6,5},{7,4},{8,11},{9,10},{10,... | collective-permute-start | bytes 3145736 | tf_op jit(solution)/shard_map/ppermute | solution.py:39
  83.1 36.2 %collective-permute-start.22 = (bf16[2,256,1024]{2,1,0:T(8,128)(2,1)}, bf16[2,256,1024]{2,1,0:T(8,128)(2,1)}, u32[]{:S(2)}, u32[]{:S(2)}) collective-permute-start(bf16[2,256,1024]{2,1,0:T(8,128)(2,1)} %collective-permute-done.13.refs_0_), channel_id=1, source_target_pairs={{0,12},{1,13},{2,14},{3,15},{4,8},{5,9},{6,10},{7,11},{8,4},{9,5},... | collective-permute-start | bytes 3145736 | tf_op jit(solution)/shard_map/ppermute | solution.py:39
  85.5 2.9 %collective-permute-start.16 = (f32[1,512]{1,0:T(1,128)S(1)}, f32[1,512]{1,0:T(1,128)S(1)}, u32[]{:S(2)}, u32[]{:S(2)}) collective-permute-start(f32[1,512]{1,0:T(1,128)S(1)} %bitcast.62), channel_id=1, source_target_pairs={{0,16},{16,0},{32,48},{48,32},{64,80},{80,64},{96,112},{112,96},{1... | collective-permute-start | bytes 6152 | tf_op jit(solution)/shard_map/ppermute | solution.py:43
  85.6 33.8 %collective-permute-start.23 = (bf16[2,256,1024]{2,1,0:T(8,128)(2,1)}, bf16[2,256,1024]{2,1,0:T(8,128)(2,1)}, u32[]{:S(2)}, u32[]{:S(2)}) collective-permute-start(bf16[2,256,1024]{2,1,0:T(8,128)(2,1)} %get-tuple-element.58), channel_id=1, source_target_pairs={{0,5},{1,4},{2,7},{3,6},{4,1},{5,0},{6,3},{7,2},{8,13},{9,12},{10,... | collective-permute-start | bytes 3145736 | tf_op jit(solution)/shard_map/ppermute | solution.py:39
  88.4 3.7 %collective-permute-start.17 = (f32[1,512]{1,0:T(1,128)S(1)}, f32[1,512]{1,0:T(1,128)S(1)}, u32[]{:S(2)}, u32[]{:S(2)}) collective-permute-start(f32[1,512]{1,0:T(1,128)S(1)} %add.180), channel_id=1, source_target_pairs={{0,32},{16,48},{32,0},{48,16},{64,96},{80,112},{96,64},{112,80},{1... | collective-permute-start | bytes 6152 | tf_op jit(solution)/shard_map/ppermute | solution.py:43
  92.1 4.8 %collective-permute-start.18 = (f32[1,512]{1,0:T(1,128)S(1)}, f32[1,512]{1,0:T(1,128)S(1)}, u32[]{:S(2)}, u32[]{:S(2)}) collective-permute-start(f32[1,512]{1,0:T(1,128)S(1)} %add.181), channel_id=1, source_target_pairs={{0,64},{16,80},{32,96},{48,112},{64,0},{80,16},{96,32},{112,48},{1... | collective-permute-start | bytes 6152 | tf_op jit(solution)/shard_map/ppermute | solution.py:43
  97.0 8.4 %collective-permute-start.19 = (f32[1,512]{1,0:T(1,128)S(1)}, f32[1,512]{1,0:T(1,128)S(1)}, u32[]{:S(2)}, u32[]{:S(2)}) collective-permute-start(f32[1,512]{1,0:T(1,128)S(1)} %add.182), channel_id=1, source_target_pairs={{0,128},{16,144},{32,160},{48,176},{64,192},{80,208},{96,224},{112... | collective-permute-start | bytes 6152 | tf_op jit(solution)/shard_map/ppermute | solution.py:43
  105.4 1.6 %copy-start.1 = (bf16[512,2048]{1,0:T(8,128)(2,1)S(1)}, bf16[512,2048]{1,0:T(8,128)(2,1)}, u32[]{:S(2)}) copy-start(bf16[512,2048]{1,0:T(8,128)(2,1)} %get-tuple-element.49.low_hbm.low_ref) | copy-start | bytes 6291460
  108.2 1.7 %copy-start.5 = (f32[1,2048]{1,0:T(1,128)}, f32[1,2048]{1,0:T(1,128)S(1)}, u32[]{:S(2)}) copy-start(f32[1,2048]{1,0:T(1,128)S(1)} %get-tuple-element.56.scale_ref) | copy-start | bytes 24580
  108.2 11.1 %collective-permute-start.20 = (f32[1,2048]{1,0:T(1,128)S(1)}, f32[1,2048]{1,0:T(1,128)S(1)}, u32[]{:S(2)}, u32[]{:S(2)}) collective-permute-start(f32[1,2048]{1,0:T(1,128)S(1)} %get-tuple-element.56.scale_ref), channel_id=1, source_target_pairs={{0,5},{1,4},{2,7},{3,6},{4,1},{5,0},{6,3},{7,2},{8,13},{9,12},{10,... | collective-permute-start | bytes 24584 | tf_op jit(solution)/shard_map/ppermute | solution.py:39
  119.3 0.6 copy-start.16
  119.3 1.0 copy-start.11
  128.4 13.7 %collective-permute-start.24 = (bf16[16,128,128]{2,1,0:T(8,128)(2,1)}, bf16[16,128,128]{2,1,0:T(8,128)(2,1)S(1)}, u32[]{:S(2)}, u32[]{:S(2)}) collective-permute-start(bf16[16,128,128]{2,1,0:T(8,128)(2,1)} %get-tuple-element.67), channel_id=1, source_target_pairs={{0,1},{1,0},{2,3},{3,2},{4,5},{5,4},{6,7},{7,6},{8,9},{9,8},{10,11... | collective-permute-start | bytes 1572872 | tf_op jit(solution)/shard_map/ppermute | solution.py:39
  131.3 11.8 %collective-permute-start.25 = (bf16[16,128,128]{2,1,0:T(8,128)(2,1)}, bf16[16,128,128]{2,1,0:T(8,128)(2,1)S(1)}, u32[]{:S(2)}, u32[]{:S(2)}) collective-permute-start(bf16[16,128,128]{2,1,0:T(8,128)(2,1)} %get-tuple-element.68), channel_id=1, source_target_pairs={{0,4},{1,5},{2,6},{3,7},{4,0},{5,1},{6,2},{7,3},{8,12},{9,13},{10,... | collective-permute-start | bytes 1572872 | tf_op jit(solution)/shard_map/ppermute | solution.py:39
  143.2 1.6 %copy-start.2 = (f32[32,128,128]{2,1,0:T(8,128)S(1)}, f32[32,128,128]{2,1,0:T(8,128)}, u32[]{:S(2)}) copy-start(f32[32,128,128]{2,1,0:T(8,128)} %shard_map.128.own_ref) | copy-start | bytes 6291460
